TPU v7x, 32 devices: a whole 2x2x4 slice. The times are simulated.
32 devices in a mesh: dp: 8 (over z, core), tensor: 4 (over y, x).
Axes of the slice: x: 2, y: 2, z: 4, core: 2. Of those that a mesh axis runs over, the one named last changes fastest.
Arguments:
- tokens: bfloat16 [16384, 2560], P(('dp', 'tensor')), may hold values from -6 to 6
- segments: int32 [16, 1024], P('dp'), may hold values from -1 to 16, as said below
- attn_gain: bfloat16 [2560], P('dp'), may hold values from 0.5 to 1.5
- w_query: bfloat16 [2560, 2560], P('dp', 'tensor'), may hold values from -0.125 to 0.125
- w_key: bfloat16 [2560, 640], P('dp', 'tensor'), may hold values from -0.125 to 0.125
- w_value: bfloat16 [2560, 640], P('dp', 'tensor'), may hold values from -0.125 to 0.125
- w_out: bfloat16 [2560, 2560], P('tensor', 'dp'), may hold values from -1 to 1
- mlp_gain: bfloat16 [2560], P('dp'), may hold values from 0.5 to 1.5
- w_gate: bfloat16 [2560, 6912], P('dp', 'tensor'), may hold values from -0.125 to 0.125
- w_up: bfloat16 [2560, 6912], P('dp', 'tensor'), may hold values from -0.125 to 0.125
- w_down: bfloat16 [6912, 2560], P('tensor', 'dp'), may hold values from -0.078125 to 0.078125
- out_grad: bfloat16 [16384, 2560], P(('dp', 'tensor')), may hold values from -6 to 6
Outputs:
- output: bfloat16 [16384, 2560], P(('dp', 'tensor'))
- input_grad: float32 [16384, 2560], P(('dp', 'tensor'))
- attn_gain_grad: float32 [2560], P(('dp', 'tensor'))
- w_query_grad: float32 [2560, 2560], P('dp', 'tensor')
- w_key_grad: float32 [2560, 640], P('dp', 'tensor')
- w_value_grad: float32 [2560, 640], P('dp', 'tensor')
- w_out_grad: float32 [2560, 2560], P('tensor', 'dp')
- mlp_gain_grad: float32 [2560], P(('dp', 'tensor'))
- w_gate_grad: float32 [2560, 6912], P('dp', 'tensor')
- w_up_grad: float32 [2560, 6912], P('dp', 'tensor')
- w_down_grad: float32 [6912, 2560], P('tensor', 'dp')
Inputs may be any that keep to these rules, and one draw needn't show every extreme that they name: `segments`: in each sequence the segment numbers start at 0 and rise by one from document to document; padding, marked -1, fills only the end; each document has 60 to 800 tokens.
All inputs are finite; a program needn't handle non-finite values.
Results may differ from a plain program's by a relative error of at most 0.023.
Values may be sent and summed in bfloat16 or wider, within the bound.
No kernel may reach another device: no remote copies, remote signals or barrier semaphores. Data moves between devices by JAX's collectives and lax.ppermute only.
A program may use at most 320 MiB of HBM per device.

v0:
```python
import jax
import jax.numpy as jnp
from jax import lax
from jax.sharding import PartitionSpec as P

HD = 80
WINDOW = 4096


EPS = 1e-05
THETA = 10000.0
NEG = -1e30


def scaled_norm(inputs, gain_row):
    return inputs * lax.rsqrt(jnp.mean(inputs * inputs, axis=-1, keepdims=True) + EPS) * gain_row


def doc_positions(seg_table):
    places = jnp.arange(seg_table.shape[-1], dtype=jnp.int32)
    previous = jnp.concatenate([seg_table[:, :1] - 1, seg_table[:, :-1]], axis=1)
    doc_start = lax.cummax(jnp.where(seg_table != previous, places[None, :], 0), axis=1)
    return places[None, :] - doc_start


def rope_tables(positions, head_size):
    half_width = head_size // 2
    frequency = THETA ** (-(jnp.arange(half_width, dtype=jnp.float32) * 2.0 / head_size))
    angles = positions.astype(jnp.float32)[..., None] * frequency
    return (jnp.cos(angles), jnp.sin(angles))


def rotate(inputs, cosine, sine_table):
    half_width = inputs.shape[-1] // 2
    first_half, second_half = (inputs[..., :half_width], inputs[..., half_width:])
    return jnp.concatenate(
        [
            first_half * cosine - second_half * sine_table,
            second_half * cosine + first_half * sine_table,
        ],
        axis=-1,
    )


def rotate_back(grads_in, cosine, sine_table):
    half_width = grads_in.shape[-1] // 2
    first_half, second_half = (grads_in[..., :half_width], grads_in[..., half_width:])
    return jnp.concatenate(
        [
            first_half * cosine + second_half * sine_table,
            second_half * cosine - first_half * sine_table,
        ],
        axis=-1,
    )


def allowed(seg_row):
    places = jnp.arange(seg_row.shape[0], dtype=jnp.int32)
    causal = (places[None, :] <= places[:, None]) & (places[:, None] - places[None, :] < WINDOW)
    return causal & (seg_row[:, None] == seg_row[None, :])


def masked_scores(q_seq, k_seq, seg_seq, soft_scale):
    scores = (
        jnp.einsum("qkgd,skd->kgqs", q_seq, k_seq, preferred_element_type=jnp.float32) * soft_scale
    )
    return jnp.where(allowed(seg_seq), scores, NEG)


def body(
    tokens,
    segments,
    attn_gain,
    w_query,
    w_key,
    w_value,
    w_out,
    mlp_gain,
    w_gate,
    w_up,
    w_down,
    out_grad,
):
    head_size = HD
    q_local = w_query.shape[1] // head_size
    kv_local = w_key.shape[1] // head_size
    groups = q_local // kv_local
    q_width = q_local * head_size
    k_width = kv_local * head_size
    row_count = tokens.shape[0]
    seq_count, length = segments.shape
    group_rows = seq_count * length
    ff_local = w_gate.shape[1]
    tensor_index = lax.axis_index("tensor")
    soft_scale = head_size ** (-0.5)
    query_w, key_w, value_w, out_w, gain_one = (
        lax.all_gather(w_query, "dp", axis=0, tiled=True),
        lax.all_gather(w_key, "dp", axis=0, tiled=True),
        lax.all_gather(w_value, "dp", axis=0, tiled=True),
        lax.all_gather(w_out, "dp", axis=1, tiled=True),
        lax.all_gather(attn_gain, "dp", axis=0, tiled=True),
    )
    gain_one = gain_one.astype(jnp.float32)
    token_rows = tokens.astype(jnp.float32)
    normed_one = scaled_norm(token_rows, gain_one).astype(jnp.bfloat16)
    rows_one = lax.all_gather(normed_one, "tensor", axis=0, tiled=True)
    proj_weight = jnp.concatenate([query_w, key_w, value_w], axis=1)
    projected = jnp.dot(rows_one, proj_weight, preferred_element_type=jnp.float32).reshape(
        seq_count, length, -1
    )
    cosine, sine_table = rope_tables(doc_positions(segments), head_size)
    queries = projected[..., :q_width].reshape(seq_count, length, kv_local, groups, head_size)
    keys_raw = projected[..., q_width : q_width + k_width].reshape(
        seq_count, length, kv_local, head_size
    )
    values_raw = projected[..., q_width + k_width :].reshape(seq_count, length, kv_local, head_size)
    q_cos, q_sin = (cosine[:, :, None, None, :], sine_table[:, :, None, None, :])
    k_cos, k_sin = (cosine[:, :, None, :], sine_table[:, :, None, :])
    q_rot = rotate(queries, q_cos, q_sin).astype(jnp.bfloat16)
    k_rot = rotate(keys_raw, k_cos, k_sin).astype(jnp.bfloat16)
    v_low = values_raw.astype(jnp.bfloat16)

    def attend(packed):
        q_seq, k_seq, v_seq, seg_seq = packed
        scores = masked_scores(q_seq, k_seq, seg_seq, soft_scale)
        row_top = jnp.max(scores, axis=-1, keepdims=True)
        exp_scores = jnp.exp(scores - row_top)
        row_total = jnp.sum(exp_scores, axis=-1, keepdims=True)
        soft_probs = (exp_scores / row_total).astype(jnp.bfloat16)
        mixed_heads = jnp.einsum(
            "kgqs,skd->qkgd", soft_probs, v_seq, preferred_element_type=jnp.float32
        )
        return (mixed_heads.astype(jnp.bfloat16), (row_top + jnp.log(row_total))[..., 0])

    attn_low, log_total = lax.map(attend, (q_rot, k_rot, v_low, segments))
    attn_flat = attn_low.reshape(group_rows, q_width)
    attn_branch = lax.psum_scatter(
        jnp.dot(attn_flat, out_w, preferred_element_type=jnp.float32).astype(jnp.bfloat16),
        "tensor",
        scatter_dimension=0,
        tiled=True,
    ).astype(jnp.float32)
    residual = token_rows + attn_branch
    gate_w, up_w, down_w, gain_two = (
        lax.all_gather(w_gate, "dp", axis=0, tiled=True),
        lax.all_gather(w_up, "dp", axis=0, tiled=True),
        lax.all_gather(w_down, "dp", axis=1, tiled=True),
        lax.all_gather(mlp_gain, "dp", axis=0, tiled=True),
    )
    gain_two = gain_two.astype(jnp.float32)
    normed_mid = scaled_norm(residual, gain_two).astype(jnp.bfloat16)
    rows_two = lax.all_gather(normed_mid, "tensor", axis=0, tiled=True)
    both_w = jnp.concatenate([gate_w, up_w], axis=1)
    gate_up = jnp.dot(rows_two, both_w, preferred_element_type=jnp.float32)
    gate_part = gate_up[:, :ff_local]
    up_part = gate_up[:, ff_local:]
    hidden = (jax.nn.silu(gate_part) * up_part).astype(jnp.bfloat16)
    mlp_branch = lax.psum_scatter(
        jnp.dot(hidden, down_w, preferred_element_type=jnp.float32).astype(jnp.bfloat16),
        "tensor",
        scatter_dimension=0,
        tiled=True,
    ).astype(jnp.float32)
    output = (residual + mlp_branch).astype(jnp.bfloat16)
    own_segs = lax.dynamic_slice_in_dim(
        segments.reshape(-1), tensor_index * row_count, row_count, 0
    )
    grad_out = out_grad * (own_segs >= 0).astype(jnp.bfloat16)[:, None]
    grads_all = lax.all_gather(grad_out, "tensor", axis=0, tiled=True)
    down_grad = jnp.einsum("gf,gd->fd", hidden, grads_all, preferred_element_type=jnp.float32)
    hidden_grad = jnp.einsum("gd,fd->gf", grads_all, down_w, preferred_element_type=jnp.float32)
    sigmoid_gate = jax.nn.sigmoid(gate_part)
    gate_grad = hidden_grad * up_part * sigmoid_gate * (1.0 + gate_part * (1.0 - sigmoid_gate))
    up_grad = hidden_grad * gate_part * sigmoid_gate
    gu_grad = jnp.concatenate([gate_grad, up_grad], axis=1).astype(jnp.bfloat16)
    both_grad = jnp.einsum("gd,gf->df", rows_two, gu_grad, preferred_element_type=jnp.float32)
    gate_wgrad = both_grad[:, :ff_local]
    up_wgrad = both_grad[:, ff_local:]
    mid_grad = lax.psum_scatter(
        jnp.einsum("gf,df->gd", gu_grad, both_w, preferred_element_type=jnp.float32).astype(
            jnp.bfloat16
        ),
        "tensor",
        scatter_dimension=0,
        tiled=True,
    ).astype(jnp.float32)
    norm_two_out, norm_two_vjp = jax.vjp(scaled_norm, residual, gain_two)
    residual_part, gain_two_grad = norm_two_vjp(mid_grad)
    residual_grad = grad_out.astype(jnp.float32) + residual_part
    residual_low = residual_grad.astype(jnp.bfloat16)
    attn_grads_all = lax.all_gather(residual_low, "tensor", axis=0, tiled=True)
    out_wgrad = jnp.einsum(
        "gc,gd->cd", attn_flat, attn_grads_all, preferred_element_type=jnp.float32
    )
    mixed_grad = jnp.einsum(
        "gd,cd->gc", attn_grads_all, out_w, preferred_element_type=jnp.float32
    ).astype(jnp.bfloat16)
    mixed_grad = mixed_grad.reshape(seq_count, length, kv_local, groups, head_size)

    def attend_back(packed):
        q_seq, k_seq, v_seq, seg_seq, lse_seq, mix_grad = packed
        scores = masked_scores(q_seq, k_seq, seg_seq, soft_scale)
        soft_probs = jnp.exp(scores - lse_seq[..., None])
        probs_low = soft_probs.astype(jnp.bfloat16)
        prob_grad = jnp.einsum(
            "qkgd,skd->kgqs", mix_grad, v_seq, preferred_element_type=jnp.float32
        )
        value_grad = jnp.einsum(
            "kgqs,qkgd->skd", probs_low, mix_grad, preferred_element_type=jnp.float32
        )
        score_grad = soft_probs * (
            prob_grad - jnp.sum(soft_probs * prob_grad, axis=-1, keepdims=True)
        )
        score_grad = score_grad.astype(jnp.bfloat16)
        query_grad = (
            jnp.einsum("kgqs,skd->qkgd", score_grad, k_seq, preferred_element_type=jnp.float32)
            * soft_scale
        )
        key_grad = (
            jnp.einsum("kgqs,qkgd->skd", score_grad, q_seq, preferred_element_type=jnp.float32)
            * soft_scale
        )
        return (query_grad, key_grad, value_grad)

    query_grad, key_grad, value_grad = lax.map(
        attend_back, (q_rot, k_rot, v_low, segments, log_total, mixed_grad)
    )
    query_grad = rotate_back(query_grad, q_cos, q_sin).reshape(group_rows, q_width)
    key_grad = rotate_back(key_grad, k_cos, k_sin).reshape(group_rows, k_width)
    value_grad = value_grad.reshape(group_rows, k_width)
    proj_grad = jnp.concatenate([query_grad, key_grad, value_grad], axis=1).astype(jnp.bfloat16)
    proj_wgrad = jnp.einsum("gd,gc->dc", rows_one, proj_grad, preferred_element_type=jnp.float32)
    query_wgrad = proj_wgrad[:, :q_width]
    key_wgrad = proj_wgrad[:, q_width : q_width + k_width]
    value_wgrad = proj_wgrad[:, q_width + k_width :]
    in_grad = lax.psum_scatter(
        jnp.einsum("gc,dc->gd", proj_grad, proj_weight, preferred_element_type=jnp.float32).astype(
            jnp.bfloat16
        ),
        "tensor",
        scatter_dimension=0,
        tiled=True,
    ).astype(jnp.float32)
    norm_one_out, norm_one_vjp = jax.vjp(scaled_norm, token_rows, gain_one)
    token_part, gain_one_grad = norm_one_vjp(in_grad)
    input_grad = residual_grad + token_part
    gain_one_sum, gain_two_sum = (
        lax.psum_scatter(gain_one_grad, ("dp", "tensor"), scatter_dimension=0, tiled=True),
        lax.psum_scatter(gain_two_grad, ("dp", "tensor"), scatter_dimension=0, tiled=True),
    )
    query_sum, key_sum, value_sum, out_sum, gate_sum, up_sum, down_sum = (
        lax.psum_scatter(
            query_wgrad.astype(jnp.bfloat16), "dp", scatter_dimension=0, tiled=True
        ).astype(jnp.float32),
        lax.psum_scatter(
            key_wgrad.astype(jnp.bfloat16), "dp", scatter_dimension=0, tiled=True
        ).astype(jnp.float32),
        lax.psum_scatter(
            value_wgrad.astype(jnp.bfloat16), "dp", scatter_dimension=0, tiled=True
        ).astype(jnp.float32),
        lax.psum_scatter(
            out_wgrad.astype(jnp.bfloat16), "dp", scatter_dimension=1, tiled=True
        ).astype(jnp.float32),
        lax.psum_scatter(
            gate_wgrad.astype(jnp.bfloat16), "dp", scatter_dimension=0, tiled=True
        ).astype(jnp.float32),
        lax.psum_scatter(
            up_wgrad.astype(jnp.bfloat16), "dp", scatter_dimension=0, tiled=True
        ).astype(jnp.float32),
        lax.psum_scatter(
            down_grad.astype(jnp.bfloat16), "dp", scatter_dimension=1, tiled=True
        ).astype(jnp.float32),
    )
    return (
        output,
        input_grad,
        gain_one_sum,
        query_sum,
        key_sum,
        value_sum,
        out_sum,
        gain_two_sum,
        gate_sum,
        up_sum,
        down_sum,
    )


def solution(mesh):
    in_specs = (
        P(("dp", "tensor"), None),
        P("dp", None),
        P("dp"),
        P("dp", "tensor"),
        P("dp", "tensor"),
        P("dp", "tensor"),
        P("tensor", "dp"),
        P("dp"),
        P("dp", "tensor"),
        P("dp", "tensor"),
        P("tensor", "dp"),
        P(("dp", "tensor"), None),
    )
    out_specs = (
        P(("dp", "tensor"), None),
        P(("dp", "tensor"), None),
        P(("dp", "tensor")),
        P("dp", "tensor"),
        P("dp", "tensor"),
        P("dp", "tensor"),
        P("tensor", "dp"),
        P(("dp", "tensor")),
        P("dp", "tensor"),
        P("dp", "tensor"),
        P("tensor", "dp"),
    )
    return jax.shard_map(body, mesh=mesh, in_specs=in_specs, out_specs=out_specs, check_vma=False)
```

profile of v0, /device:TPU:0, one launch (start us, length us, event | category | flops | bytes accessed | tf_op | source)
XLA Modules:
  0.0 1881.1 jit_solution(1054040442449917918)
XLA Ops:
  11.6 31.4 %all-reduce.5 = (bf16[2560]{0:T(1024)(128)(2,1)S(1)}, bf16[2560]{0:T(1024)(128)(2,1)}) all-reduce(bf16[2560]{0:T(1024)(128)(2,1)S(1)} %dynamic-update-slice, bf16[2560]{0:T(1024)(128)(2,1)S(1)} %dynamic-update-slice.1), channel_id=1, replica_groups=mesh['dp'=8,'tensor'=4] {'dp'}, use_global_device_ids=true, to_apply=%add | all-reduce | flops 5120 | bytes 20480
  51.4 16.1 all-gather
  68.3 17.1 all-gather.1
  88.2 70.4 %all-gather.12.cloned.1.call-done = bf16[2048,2560]{1,0:T(8,128)(2,1)} async-done(((bf16[512,2560]{1,0:T(8,128)(2,1)}), bf16[2048,2560]{1,0:T(8,128)(2,1)}) %all-gather.12.cloned.1.call-update) | async-done | bytes 10485776 | tf_op jit(solution)/shard_map/all_gather | solution.py:106
  158.5 19.1 %fusion.86 = f32[2048,960]{0,1:T(8,128)} fusion(bf16[2048,2560]{1,0:T(8,128)(2,1)} %all-gather.12.cloned.1.call-done, bf16[2560,160]{1,0:T(8,128)(2,1)} %bitcast.265, bf16[2560,160]{1,0:T(8,128)(2,1)S(1)} %bitcast.263, bf16[2560,640]{1,0:T(8,128)(2,1)} %all-gather.14.cloned.1.call-done), kind=kOutput, calls=%fused_computation.121 | convolution fusion | flops 10081075200 | bytes 23265280 | tf_op jit(solution)/shard_map/dot_general | solution.py:108
  177.6 11.5 reshape.163
  197.3 93.3 %while.26 = (s32[]{:T(128)}, bf16[2,1024,2,4,80]{1,4,3,2,0:T(8,128)(2,1)}, f32[2,2,4,1024]{3,2,1,0:T(4,128)S(1)}, bf16[2,1024,2,80]{1,3,2,0:T(8,128)(2,1)}, s32[...) while((s32[]{:T(128)}, ...), condition=%wide.region_6.7_spmd, body=%wide.region_3.6_spmd.sunk | while | flops 2791956480 | bytes 132004024 | solution.py:135
  199.2 13.8 fusion.141
  213.0 14.6 fusion.142
  227.6 14.9 fusion.143
  245.7 13.8 fusion.141
  259.6 14.6 fusion.142
  274.2 14.9 fusion.143
  298.7 13.4 convolution_convert_fusion.5
  313.4 102.5 %reduce-scatter.18.cloned.1.call-done = bf16[512,2560]{1,0:T(8,128)(2,1)} async-done(((bf16[2048,2560]{1,0:T(8,128)(2,1)}), bf16[512,2560]{1,0:T(8,128)(2,1)}) %reduce-scatter.18.cloned.1.call-update) | async-done | bytes 2621456 | tf_op jit(solution)/shard_map/reduce_scatter | solution.py:137
  425.0 81.0 %all-gather.20.cloned.1.call-done = bf16[2560,1728]{1,0:T(8,128)(2,1)} async-done(((bf16[320,1728]{1,0:T(8,128)(2,1)}), bf16[2560,1728]{1,0:T(8,128)(2,1)}) %all-gather.20.cloned.1.call-update) | async-done | bytes 8847376 | tf_op jit(solution)/shard_map/all_gather | solution.py:145
  506.0 88.6 %all-gather.22.cloned.1.call-done = bf16[2560,1728]{1,0:T(8,128)(2,1)} async-done(((bf16[320,1728]{1,0:T(8,128)(2,1)}), bf16[2560,1728]{1,0:T(8,128)(2,1)}) %all-gather.22.cloned.1.call-update) | async-done | bytes 8847376 | tf_op jit(solution)/shard_map/all_gather | solution.py:146
  594.5 106.0 %all-gather.18.cloned.1.call-done = bf16[2048,2560]{1,0:T(8,128)(2,1)} async-done(((bf16[512,2560]{1,0:T(8,128)(2,1)}), bf16[2048,2560]{1,0:T(8,128)(2,1)}) %all-gather.18.cloned.1.call-update) | async-done | bytes 10485776 | tf_op jit(solution)/shard_map/all_gather | solution.py:152
  700.5 47.5 %fusion.73 = f32[2048,3456]{1,0:T(8,128)} fusion(bf16[2048,2560]{1,0:T(8,128)(2,1)} %all-gather.18.cloned.1.call-done, bf16[2560,1728]{1,0:T(8,128)(2,1)} %all-gather.22.cloned.1.call-done, bf16[2560,1728]{1,0:T(8,128)(2,1)} %all-gather.20.cloned.1.call-done), kind=kOutput, calls=%fused_computation.84 | convolution fusion | flops 36274176000 | bytes 56492032 | tf_op jit(solution)/shard_map/dot_general | solution.py:154
  748.0 42.8 %all-gather.24.cloned.1.call-done = bf16[1728,2560]{0,1:T(8,128)(2,1)} async-done(((bf16[1728,320]{0,1:T(8,128)(2,1)}), bf16[1728,2560]{0,1:T(8,128)(2,1)}) %all-gather.24.cloned.1.call-update) | async-done | bytes 8847376 | tf_op jit(solution)/shard_map/all_gather | solution.py:147
  790.7 105.4 %all-gather.26.cloned.1.call-done = bf16[2048,2560]{1,0:T(8,128)(2,1)} async-done(((bf16[512,2560]{1,0:T(8,128)(2,1)}), bf16[2048,2560]{1,0:T(8,128)(2,1)}) %all-gather.26.cloned.1.call-update) | async-done | bytes 10485776 | tf_op jit(solution)/shard_map/all_gather | solution.py:169
  896.2 33.3 %multiply_convert_fusion.1 = (bf16[2048,1728]{1,0:T(8,128)(2,1)}, bf16[2048,1728]{1,0:T(8,128)(2,1)}, bf16[2048,1728]{1,0:T(8,128)(2,1)}) fusion(f32[2048,3456]{1,0:T(8,128)} %fusion.73, bf16[2048,2560]{1,0:T(8,128)(2,1)} %all-gather.26.cloned.1.call-done, bf16[1728,2560]{0,1:T(8,128)(2,1)} %all-gather.24.cloned.1.call-done), kind=kOutput, calls=%fused_computation.75 | convolution fusion | flops 18176016384 | bytes 68878336 | tf_op jit(solution)/shard_map/gd,fd->gf/dot_general | solution.py:171
  929.5 55.4 %convolution_convert_fusion.1 = bf16[2048,2560]{1,0:T(8,128)(2,1)} fusion(bf16[2560,1728]{1,0:T(8,128)(2,1)} %all-gather.22.cloned.1.call-done, bf16[2560,1728]{1,0:T(8,128)(2,1)} %all-gather.20.cloned.1.call-done, bf16[2048,1728]{1,0:T(8,128)(2,1)} %get-tuple-element.218, bf16[2048,1728]{1,0:T(8,128)(2,1)} %get-tuple-element.217), kind=kOutput, calls=%fused_computation.79 | convolution fusion | flops 36307730432 | bytes 42336256 | tf_op jit(solution)/shard_map/gf,df->gd/dot_general | solution.py:180
  985.1 103.5 %reduce-scatter.22.cloned.1.call-done = bf16[512,2560]{1,0:T(8,128)(2,1)} async-done(((bf16[2048,2560]{1,0:T(8,128)(2,1)}), bf16[512,2560]{1,0:T(8,128)(2,1)}) %reduce-scatter.22.cloned.1.call-update) | async-done | bytes 2621456 | tf_op jit(solution)/shard_map/reduce_scatter | solution.py:179
  1099.4 47.3 %convolution_convert_fusion = bf16[2560,3456]{1,0:T(8,128)(2,1)S(1)} fusion(bf16[2048,2560]{1,0:T(8,128)(2,1)} %all-gather.18.cloned.1.call-done, bf16[2048,1728]{1,0:T(8,128)(2,1)} %get-tuple-element.218, bf16[2048,1728]{1,0:T(8,128)(2,1)} %get-tuple-element.217), kind=kOutput, calls=%fused_computation.72 | convolution fusion | flops 36275945472 | bytes 42336256 | tf_op jit(solution)/shard_map/gd,gf->df/dot_general | solution.py:176
  1156.9 25.3 %convolution_convert_fusion.3 = bf16[1728,2560]{0,1:T(8,128)(2,1)} fusion(bf16[2048,1728]{1,0:T(8,128)(2,1)} %get-tuple-element.219, bf16[2048,2560]{1,0:T(8,128)(2,1)} %all-gather.26.cloned.1.call-done), kind=kOutput, calls=%fused_computation.81 | convolution fusion | flops 18123816960 | bytes 26411008 | tf_op jit(solution)/shard_map/gf,gd->fd/dot_general | solution.py:170
  1182.2 22.3 %all-gather.28.cloned.1.call-done = bf16[2048,2560]{1,0:T(8,128)(2,1)} async-done(((bf16[512,2560]{1,0:T(8,128)(2,1)}), bf16[2048,2560]{1,0:T(8,128)(2,1)}) %all-gather.28.cloned.1.call-update) | async-done | bytes 10485776 | tf_op jit(solution)/shard_map/all_gather | solution.py:191
  1204.5 12.0 convolution_convert_fusion.8
  1227.5 214.0 %while.27 = (s32[]{:T(128)}, f32[2,1024,2,4,80]{1,4,3,2,0:T(8,128)}, f32[2,1024,2,80]{1,3,2,0:T(8,128)}, bf16[2,1024,2,80]{1,3,2,0:T(8,128)(2,1)}, bf16[2,1024,2...) while((s32[]{:T(128)}, ...), condition=%wide.region_14.15_spmd, body=%wide.region_12.14_spmd.sunk | while | flops 6793486336 | bytes 274580640 | solution.py:225
  1229.7 14.6 fusion.152
  1244.3 24.4 %fusion.154 = (f32[2,4,1024]{2,1,0:T(4,128)S(1)}, f32[2,4,1024,1024]{2,3,1,0:T(8,128)}) fusion(f32[2,1024,1024,4]{2,1,3,0:T(8,128)} %fusion.152, f32[2,4,1024]{2,1,0:T(4,128)S(1)} %dynamic-slice_bitcast_fusion.2, bf16[2,1024,2,4,80]{1,4,3,2,0:T(8,128)(2,1)S(1)} %copy-done.4, s32[]{:T(128)S(6)} %copy.129, ...), kind=kOutput, calls=%fused_computation.29.clone.1 | convolution fusion | flops 1384112128 | bytes 69862400 | tf_op jit(solution)/shard_map/while/body/eval_jaxpr/qkgd,skd->kgqs/dot_general | solution.py:65
  1268.7 28.7 %fusion.155 = bf16[2,4,1024,1024]{2,3,1,0:T(8,128)(2,1)} fusion(f32[2,4,1024,1024]{2,3,1,0:T(8,128)} %get-tuple-element.346, f32[2,1024,1024,4]{2,1,3,0:T(8,128)} %fusion.152, f32[2,4,1024]{2,1,0:T(4,128)S(1)} %get-tuple-element.347), kind=kLoop, calls=%fused_computation.31.clone.1 | loop fusion | flops 25165824 | bytes 83918848 | tf_op jit(solution)/shard_map/while/body/eval_jaxpr/convert_element_type | solution.py:214
  1297.4 14.2 fusion.157
  1311.6 12.2 fusion.156
  1336.1 14.6 fusion.152
  1350.8 24.4 %fusion.154 = (f32[2,4,1024]{2,1,0:T(4,128)S(1)}, f32[2,4,1024,1024]{2,3,1,0:T(8,128)}) fusion(f32[2,1024,1024,4]{2,1,3,0:T(8,128)} %fusion.152, f32[2,4,1024]{2,1,0:T(4,128)S(1)} %dynamic-slice_bitcast_fusion.2, bf16[2,1024,2,4,80]{1,4,3,2,0:T(8,128)(2,1)S(1)} %copy-done.4, s32[]{:T(128)S(6)} %copy.129, ...), kind=kOutput, calls=%fused_computation.29.clone.1 | convolution fusion | flops 1384112128 | bytes 69862400 | tf_op jit(solution)/shard_map/while/body/eval_jaxpr/qkgd,skd->kgqs/dot_general | solution.py:65
  1375.1 28.5 %fusion.155 = bf16[2,4,1024,1024]{2,3,1,0:T(8,128)(2,1)} fusion(f32[2,4,1024,1024]{2,3,1,0:T(8,128)} %get-tuple-element.346, f32[2,1024,1024,4]{2,1,3,0:T(8,128)} %fusion.152, f32[2,4,1024]{2,1,0:T(4,128)S(1)} %get-tuple-element.347), kind=kLoop, calls=%fused_computation.31.clone.1 | loop fusion | flops 25165824 | bytes 83918848 | tf_op jit(solution)/shard_map/while/body/eval_jaxpr/convert_element_type | solution.py:214
  1403.7 14.8 fusion.157
  1418.5 12.4 fusion.156
  1475.7 13.5 convolution_convert_fusion.7
  1489.3 18.8 convolution_convert_fusion.4
  1508.2 25.8 %convolution_convert_fusion.2 = bf16[2048,2560]{1,0:T(8,128)(2,1)} fusion(bf16[2048,1728]{1,0:T(8,128)(2,1)} %get-tuple-element.219, bf16[1728,2560]{0,1:T(8,128)(2,1)} %all-gather.24.cloned.1.call-done), kind=kOutput, calls=%fused_computation.80 | convolution fusion | flops 18124636160 | bytes 26411008 | tf_op jit(solution)/shard_map/dot_general | solution.py:159
  1544.4 22.0 %reduce-scatter.36.cloned.1.call-done = bf16[320,160]{1,0:T(8,128)(2,1)} async-done(((bf16[2560,160]{1,0:T(8,128)(2,1)}), bf16[320,160]{1,0:T(8,128)(2,1)}) %reduce-scatter.36.cloned.1.call-update) | async-done | bytes 102416
  1568.2 40.5 %reduce-scatter.34.cloned.1.call-done = bf16[320,640]{1,0:T(8,128)(2,1)} async-done(((bf16[2560,640]{1,0:T(8,128)(2,1)}), bf16[320,640]{1,0:T(8,128)(2,1)}) %reduce-scatter.34.cloned.1.call-update) | async-done | bytes 409616
  1611.1 40.1 %reduce-scatter.26.cloned.1.call-done = bf16[640,320]{0,1:T(8,128)(2,1)} async-done(((bf16[640,2560]{0,1:T(8,128)(2,1)}), bf16[640,320]{0,1:T(8,128)(2,1)}) %reduce-scatter.26.cloned.1.call-update) | async-done | bytes 409616 | tf_op jit(solution)/shard_map/reduce_scatter | solution.py:261
  1653.1 103.6 %reduce-scatter.24.cloned.1.call-done = bf16[512,2560]{1,0:T(8,128)(2,1)} async-done(((bf16[2048,2560]{1,0:T(8,128)(2,1)}), bf16[512,2560]{1,0:T(8,128)(2,1)}) %reduce-scatter.24.cloned.1.call-update) | async-done | bytes 2621456 | tf_op jit(solution)/shard_map/reduce_scatter | solution.py:236
  1760.7 40.1 %all-reduce.4 = (f32[2560]{0:T(1024)S(1)}, f32[2560]{0:T(1024)S(1)}) all-reduce(f32[2560]{0:T(1024)S(1)} %get-tuple-element.173, f32[2560]{0:T(1024)S(1)} %copy-done.39), channel_id=6, replica_groups=mesh['dp'=8,'tensor'=4] {'dp','tensor'}, use_global_device_ids=true, to_apply=%region_18.19.clone | all-reduce | flops 5120 | bytes 40960
  1802.0 62.3 %reduce-scatter.20.cloned.1.call-done = bf16[512,2560]{1,0:T(8,128)(2,1)} async-done(((bf16[2048,2560]{1,0:T(8,128)(2,1)}), bf16[512,2560]{1,0:T(8,128)(2,1)}) %reduce-scatter.20.cloned.1.call-update) | async-done | bytes 2621456 | tf_op jit(solution)/shard_map/reduce_scatter | solution.py:158
  (267 shorter events, 170.3 us)
Async XLA Ops:
  7.2 81.0 %all-gather.14.cloned.1.call-start = ((), (), s32[]{:S(2)}) async-start(), calls=%async_computation.12 | async-start | bytes 3686400 | tf_op jit(solution)/shard_map/all_gather | solution.py:97
  7.9 150.6 %all-gather.12.cloned.1.call-start = ((), (), s32[]{:S(2)}) async-start(), calls=%async_computation.11 | async-start | bytes 13107200 | tf_op jit(solution)/shard_map/all_gather | solution.py:106
  45.4 22.9 %copy-start.35 = (bf16[320,160]{0,1:T(8,128)(2,1)S(1)}, bf16[320,160]{0,1:T(8,128)(2,1)}, u32[]{:S(2)}) copy-start(bf16[320,160]{0,1:T(8,128)(2,1)} %param.21) | copy-start | bytes 307204
  49.4 249.3 %all-gather.16.cloned.1.call-start = ((), (), s32[]{:S(2)}) async-start(), calls=%async_computation.13 | async-start | bytes 3686400 | tf_op jit(solution)/shard_map/all_gather | solution.py:100
  50.1 365.8 %reduce-scatter.18.cloned.1.call-start = ((), (), s32[]{:S(2)}) async-start(), calls=%async_computation.14 | async-start | bytes 13107200 | tf_op jit(solution)/shard_map/reduce_scatter | solution.py:137
  68.3 109.4 %copy-start.21 = (bf16[8,320,160]{2,1,0:T(8,128)(2,1)}, bf16[8,320,160]{2,1,0:T(8,128)(2,1)S(1)}, u32[]{:S(2)}) copy-start(bf16[8,320,160]{2,1,0:T(8,128)(2,1)S(1)} %copy.85) | copy-start | bytes 2457604
  88.1 108.6 %copy-start.13 = (f32[2,1024,40]{1,2,0:T(8,128)}, f32[2,1024,40]{1,2,0:T(8,128)S(1)}, u32[]{:S(2)}) copy-start(f32[2,1024,40]{1,2,0:T(8,128)S(1)} %get-tuple-element.234) | copy-start | bytes 983044
  88.1 108.6 %copy-start.15 = (f32[2,1024,40]{1,2,0:T(8,128)}, f32[2,1024,40]{1,2,0:T(8,128)S(1)}, u32[]{:S(2)}) copy-start(f32[2,1024,40]{1,2,0:T(8,128)S(1)} %get-tuple-element.235) | copy-start | bytes 983044
  213.0 14.6 copy-start.17
  213.0 14.6 copy-start.18
  259.6 14.6 copy-start.17
  259.6 14.6 copy-start.18
  312.1 103.8 %copy-start = (bf16[512,2560]{1,0:T(8,128)(2,1)S(1)}, bf16[512,2560]{1,0:T(8,128)(2,1)}, u32[]{:S(2)}) copy-start(bf16[512,2560]{1,0:T(8,128)(2,1)} %param.16) | copy-start | bytes 7864324
  312.2 193.8 %all-gather.20.cloned.1.call-start = ((), (), s32[]{:S(2)}) async-start(), calls=%async_computation.16 | async-start | bytes 10321920 | tf_op jit(solution)/shard_map/all_gather | solution.py:145
  312.8 281.8 %all-gather.22.cloned.1.call-start = ((), (), s32[]{:S(2)}) async-start(), calls=%async_computation.17 | async-start | bytes 10321920 | tf_op jit(solution)/shard_map/all_gather | solution.py:146
  313.3 387.2 %all-gather.18.cloned.1.call-start = ((), (), s32[]{:S(2)}) async-start(), calls=%async_computation.15 | async-start | bytes 13107200 | tf_op jit(solution)/shard_map/all_gather | solution.py:152
  313.4 108.0 %copy-start.29 = (f32[2560]{0:T(1024)}, f32[2560]{0:T(1024)S(1)}, u32[]{:S(2)}) copy-start(f32[2560]{0:T(1024)S(1)} %convert_element_type.126) | copy-start | bytes 30724
  421.5 369.3 %all-gather.24.cloned.1.call-start = ((), (), s32[]{:S(2)}) async-start(), calls=%async_computation.18 | async-start | bytes 10321920 | tf_op jit(solution)/shard_map/all_gather | solution.py:147
  422.2 473.9 %all-gather.26.cloned.1.call-start = ((), (), s32[]{:S(2)}) async-start(), calls=%async_computation.20 | async-start | bytes 13107200 | tf_op jit(solution)/shard_map/all_gather | solution.py:169
  425.0 663.6 %reduce-scatter.22.cloned.1.call-start = ((), (), s32[]{:S(2)}) async-start(), calls=%async_computation.21 | async-start | bytes 13107200 | tf_op jit(solution)/shard_map/reduce_scatter | solution.py:179
  984.9 103.7 %copy-start.1 = (bf16[512,2560]{1,0:T(8,128)(2,1)S(1)}, bf16[512,2560]{1,0:T(8,128)(2,1)}, u32[]{:S(2)}) copy-start(bf16[512,2560]{1,0:T(8,128)(2,1)} %param.16) | copy-start | bytes 7864324
  984.9 103.7 %copy-start.30 = (f32[2560]{0:T(1024)S(1)}, f32[2560]{0:T(1024)}, u32[]{:S(2)}) copy-start(f32[2560]{0:T(1024)} %copy-done.29) | copy-start | bytes 30724
  984.9 103.7 %copy-start.37 = (f32[512]{0:T(512)S(1)}, f32[512]{0:T(512)}, u32[]{:S(2)}) copy-start(f32[512]{0:T(512)} %copy-done.36) | copy-start | bytes 6148
  984.9 110.2 %copy-start.43 = (f32[512]{0:T(512)S(1)}, f32[512]{0:T(512)}, u32[]{:S(2)}) copy-start(f32[512]{0:T(512)} %copy-done.42) | copy-start | bytes 6148
  984.9 110.7 %copy-start.49 = (bf16[512]{0:T(512)(128)(2,1)S(1)}, bf16[512]{0:T(512)(128)(2,1)}, u32[]{:S(2)}) copy-start(bf16[512]{0:T(512)(128)(2,1)} %copy-done.48) | copy-start | bytes 3076
  984.9 219.6 %all-gather.28.cloned.1.call-start = ((), (), s32[]{:S(2)}) async-start(), calls=%async_computation.22 | async-start | bytes 13107200 | tf_op jit(solution)/shard_map/all_gather | solution.py:191
  1099.3 434.7 %reduce-scatter.28.cloned.1.call-start = ((), (), s32[]{:S(2)}) async-start(), calls=%async_computation.25 | async-start | bytes 10321920 | tf_op jit(solution)/shard_map/reduce_scatter | solution.py:264
  1155.9 381.0 %reduce-scatter.30.cloned.1.call-start = ((), (), s32[]{:S(2)}) async-start(), calls=%async_computation.26 | async-start | bytes 10321920 | tf_op jit(solution)/shard_map/reduce_scatter | solution.py:267
  1156.6 383.2 %reduce-scatter.32.cloned.1.call-start = ((), (), s32[]{:S(2)}) async-start(), calls=%async_computation.27 | async-start | bytes 10321920 | tf_op jit(solution)/shard_map/reduce_scatter | solution.py:270
  1182.2 360.5 %reduce-scatter.38.cloned.1.call-start = ((), (), s32[]{:S(2)}) async-start(), calls=%async_computation.30 | async-start | bytes 1474560
  1229.7 14.6 copy-start.4
  1336.1 14.6 copy-start.4
  1469.5 96.9 %reduce-scatter.36.cloned.1.call-start = ((), (), s32[]{:S(2)}) async-start(), calls=%async_computation.29 | async-start | bytes 1474560
  1472.2 136.5 %reduce-scatter.34.cloned.1.call-start = ((), (), s32[]{:S(2)}) async-start(), calls=%async_computation.28 | async-start | bytes 3686400
  1475.6 13.7 copy-start.22
  1475.7 13.7 copy-start.23
  1475.7 175.5 %reduce-scatter.26.cloned.1.call-start = ((), (), s32[]{:S(2)}) async-start(), calls=%async_computation.24 | async-start | bytes 3686400 | tf_op jit(solution)/shard_map/reduce_scatter | solution.py:261
  1489.3 267.4 %reduce-scatter.24.cloned.1.call-start = ((), (), s32[]{:S(2)}) async-start(), calls=%async_computation.23 | async-start | bytes 13107200 | tf_op jit(solution)/shard_map/reduce_scatter | solution.py:236
  1508.1 356.1 %reduce-scatter.20.cloned.1.call-start = ((), (), s32[]{:S(2)}) async-start(), calls=%async_computation.19 | async-start | bytes 13107200 | tf_op jit(solution)/shard_map/reduce_scatter | solution.py:158
  1536.8 219.8 %copy-start.2 = (bf16[512,2560]{1,0:T(8,128)(2,1)S(1)}, bf16[512,2560]{1,0:T(8,128)(2,1)}, u32[]{:S(2)}) copy-start(bf16[512,2560]{1,0:T(8,128)(2,1)} %param.16) | copy-start | bytes 7864324
  1536.8 219.8 %copy-start.33 = (f32[2560]{0:T(1024)S(1)}, f32[2560]{0:T(1024)}, u32[]{:S(2)}) copy-start(f32[2560]{0:T(1024)} %copy-done.32) | copy-start | bytes 30724
  1536.8 219.8 %copy-start.41 = (f32[512]{0:T(512)S(1)}, f32[512]{0:T(512)}, u32[]{:S(2)}) copy-start(f32[512]{0:T(512)} %copy-done.40) | copy-start | bytes 6148
  1542.6 218.1 %copy-start.39 = (f32[2560]{0:T(1024)S(1)}, f32[2560]{0:T(1024)}, u32[]{:S(2)}) copy-start(f32[2560]{0:T(1024)} %get-tuple-element.171) | copy-start | bytes 30724
  1542.6 259.4 %copy-start.45 = (f32[512]{0:T(512)S(1)}, f32[512]{0:T(512)}, u32[]{:S(2)}) copy-start(f32[512]{0:T(512)} %copy-done.44) | copy-start | bytes 6148
  1542.6 321.6 %copy-start.31 = (f32[2560]{0:T(1024)S(1)}, f32[2560]{0:T(1024)}, u32[]{:S(2)}) copy-start(f32[2560]{0:T(1024)} %copy-done.29) | copy-start | bytes 30724
  1542.6 321.6 %copy-start.38 = (f32[512]{0:T(512)S(1)}, f32[512]{0:T(512)}, u32[]{:S(2)}) copy-start(f32[512]{0:T(512)} %copy-done.36) | copy-start | bytes 6148
  1542.6 321.6 %copy-start.47 = (f32[512]{0:T(512)S(1)}, f32[512]{0:T(512)}, u32[]{:S(2)}) copy-start(f32[512]{0:T(512)} %copy-done.46) | copy-start | bytes 6148
  1542.6 321.6 %copy-start.50 = (bf16[512]{0:T(512)(128)(2,1)S(1)}, bf16[512]{0:T(512)(128)(2,1)}, u32[]{:S(2)}) copy-start(bf16[512]{0:T(512)(128)(2,1)} %copy-done.48) | copy-start | bytes 3076
  (34 other events, 161.9 us)
Sparse Core Ops, SparseCore 0:
  9.7 42.4 all-gather.13
  54.6 103.9 all-gather.11
  160.2 39.3 all-gather.15
  312.3 103.5 reduce-scatter.17
  417.4 88.5 all-gather.19
  507.5 87.0 all-gather.21
  596.9 103.5 all-gather.17
  702.2 88.5 all-gather.23
  792.6 103.5 all-gather.25
  985.0 103.5 reduce-scatter.21
  1099.5 105.0 all-gather.27
  1206.7 97.0 reduce-scatter.27
  1306.1 95.3 reduce-scatter.29
  1403.7 95.3 reduce-scatter.31
  1501.3 31.5 reduce-scatter.37
  1535.0 31.3 reduce-scatter.35
  1569.2 39.4 reduce-scatter.33
  1611.0 40.1 reduce-scatter.25
  1654.3 102.3 reduce-scatter.23
  1759.6 104.5 reduce-scatter.19
where the time goes:
time: 1890 us; the launch traced here: 1880 us
  waiting for transfers between devices  995 us (53%)
  matrix products  532 us (28%)
  other arithmetic  151 us (8%)
  blocking collectives  105 us (6%)
  local copies, waits for them, and re-layouts  80.8 us (4%)
    all_gather x1, waiting for transfers between devices, body(): rows_two = lax.all_gather(normed_mid, 'tensor', axis=0, tiled=True)  106 us
    all_gather x1, waiting for transfers between devices, body(): grads_all = lax.all_gather(grad_out, 'tensor', axis=0, tiled=True)  105 us
    reduce_scatter x1, waiting for transfers between devices, body(): lax.psum_scatter(jnp.einsum('gc,dc->gd', proj_grad, proj_weight, preferre...  104 us
    reduce_scatter x1, waiting for transfers between devices, body(): lax.psum_scatter(jnp.einsum('gf,df->gd', gu_grad, both_w, preferred_eleme...  103 us
    reduce_scatter x1, waiting for transfers between devices, body(): lax.psum_scatter(jnp.dot(attn_flat, out_w, preferred_element_type=jnp.flo...  102 us
    all_gather x1, waiting for transfers between devices, body(): lax.all_gather(w_up, 'dp', axis=0, tiled=True)  88.6 us
    all_gather x1, waiting for transfers between devices, body(): lax.all_gather(w_gate, 'dp', axis=0, tiled=True)  81 us
    dot_general x4, matrix products, masked_scores(): jnp.einsum('qkgd,skd->kgqs', q_seq, k_seq, preferred_element_type=jnp.flo...  76.4 us
  transfers between devices with their start and end apart: 20, of which 14 were waited for; matrix products, arithmetic and copies ran while one was open for 34% of the time, Pallas kernels for 0%

commit v1 on v0

v1 whole, which is shorter than its diff:
```python
import functools

import jax
import jax.numpy as jnp
from jax import lax
from jax.experimental import pallas as pl
from jax.experimental.pallas import tpu as pltpu
from jax.sharding import PartitionSpec as P

HD = 80
LANES = 128
WINDOW = 4096
EPS = 1e-05
THETA = 10000.0
NEG = -1e30
LOG2E = 1.4426950408889634
BLK = 256
BF = jnp.bfloat16
F32 = jnp.float32


def turn(x, c, s):
    return x * c + pltpu.roll(x, LANES // 2, 1) * s


def turn_back(x, c, s):
    return x * c - pltpu.roll(x, LANES // 2, 1) * s


def allowed(start, first_row, rows, first_col, cols):
    row = first_row + lax.broadcasted_iota(jnp.int32, (rows, cols), 0)
    col = first_col + lax.broadcasted_iota(jnp.int32, (rows, cols), 1)
    return (col >= start) & (col <= row) & (row - col < WINDOW)


def nt(a, b):
    return lax.dot_general(a, b, (((1,), (1,)), ((), ())), preferred_element_type=F32)


def nn(a, b):
    return lax.dot_general(a, b, (((1,), (0,)), ((), ())), preferred_element_type=F32)


def tn(a, b):
    return lax.dot_general(a, b, (((0,), (0,)), ((), ())), preferred_element_type=F32)


def fwd_kernel(groups, scale, lo_ref, q_ref, k_ref, v_ref, c_ref, s_ref, start_ref,
               o_ref, qr_ref, kr_ref, vb_ref, lse_ref):
    length = q_ref.shape[0]
    c, s = c_ref[...], s_ref[...]
    kr_ref[...] = turn(k_ref[...], c, s).astype(BF)
    vb_ref[...] = v_ref[...].astype(BF)
    for g in range(groups):
        lanes = slice(g * LANES, (g + 1) * LANES)
        qr_ref[:, lanes] = turn(q_ref[:, lanes], c, s).astype(BF)
    for i in range(length // BLK):
        rows = slice(i * BLK, (i + 1) * BLK)
        for j in range(i + 1):
            cols = slice(j * BLK, (i + 1) * BLK)
            width = (i + 1 - j) * BLK

            @pl.when(lo_ref[i] == j)
            def _():
                ok = allowed(start_ref[rows, :], i * BLK, BLK, j * BLK, width)
                for g in range(groups):
                    lanes = slice(g * LANES, (g + 1) * LANES)
                    scores = nt(qr_ref[rows, lanes], kr_ref[cols, :]) * (scale * LOG2E)
                    scores = jnp.where(ok, scores, NEG)
                    top = jnp.max(scores, axis=1, keepdims=True)
                    e = jnp.exp2(scores - top)
                    total = jnp.sum(e, axis=1, keepdims=True)
                    mixed = nn(e.astype(BF), vb_ref[cols, :])
                    o_ref[rows, lanes] = (mixed / total).astype(BF)
                    lse_ref[rows, g:g + 1] = top + jnp.log2(total)


def bwd_kernel(groups, scale, lo_ref, qr_ref, kr_ref, vb_ref, do_ref, c_ref, s_ref, start_ref, lse_ref,
               dq_ref, dk_ref, dv_ref, dk_acc, dv_acc):
    length = qr_ref.shape[0]
    dk_acc[...] = jnp.zeros_like(dk_acc)
    dv_acc[...] = jnp.zeros_like(dv_acc)
    for i in range(length // BLK):
        rows = slice(i * BLK, (i + 1) * BLK)
        for j in range(i + 1):
            cols = slice(j * BLK, (i + 1) * BLK)
            width = (i + 1 - j) * BLK

            @pl.when(lo_ref[i] == j)
            def _():
                ok = allowed(start_ref[rows, :], i * BLK, BLK, j * BLK, width)
                for g in range(groups):
                    lanes = slice(g * LANES, (g + 1) * LANES)
                    q, do = qr_ref[rows, lanes], do_ref[rows, lanes]
                    k, v = kr_ref[cols, :], vb_ref[cols, :]
                    scores = nt(q, k) * (scale * LOG2E)
                    p = jnp.exp2(jnp.where(ok, scores, NEG) - lse_ref[rows, g:g + 1])
                    pd = p * nt(do, v)
                    ds = (pd - p * jnp.sum(pd, axis=1, keepdims=True)).astype(BF)
                    dq = nn(ds, k) * scale
                    dq_ref[rows, lanes] = turn_back(dq, c_ref[rows, :], s_ref[rows, :]).astype(BF)
                    dk_acc[cols, :] += tn(ds, q)
                    dv_acc[cols, :] += tn(p.astype(BF), do)
    dk_ref[...] = turn_back(dk_acc[...] * scale, c_ref[...], s_ref[...]).astype(BF)
    dv_ref[...] = dv_acc[...].astype(BF)


def attend(proj, tables, kv, groups):
    cos_t, sin_t, start, lo = tables
    rows = proj.shape[0]
    whole = lambda width: pl.BlockSpec((rows, width), lambda h, lo: (0, 0))
    at = lambda width, first: pl.BlockSpec((rows, width), lambda h, lo: (0, first + h))
    wide = groups * LANES
    out = lambda width: jax.ShapeDtypeStruct((rows, kv * width), BF)
    return pl.pallas_call(
        functools.partial(fwd_kernel, groups, HD ** -0.5),
        grid_spec=pltpu.PrefetchScalarGridSpec(
            num_scalar_prefetch=1,
            grid=(kv,),
            in_specs=[at(wide, 0), at(LANES, kv * groups), at(LANES, kv * groups + kv),
                      whole(LANES), whole(LANES), whole(1)],
            out_specs=[at(wide, 0), at(wide, 0), at(LANES, 0), at(LANES, 0),
                       pl.BlockSpec((None, rows, groups), lambda h, lo: (h, 0, 0))],
        ),
        out_shape=[out(wide), out(wide), out(LANES), out(LANES),
                   jax.ShapeDtypeStruct((kv, rows, groups), F32)],
        compiler_params=pltpu.CompilerParams(vmem_limit_bytes=48 * 2 ** 20),
        cost_estimate=pl.CostEstimate(flops=int(4 * kv * groups * rows * rows * LANES * 0.6),
                                      bytes_accessed=rows * kv * (groups + 1) * LANES * 10, transcendentals=0),
        name="attend",
    )(lo, proj, proj, proj, cos_t, sin_t, start)


def attend_back(qr, kr, vb, d_o, tables, lse, kv, groups):
    cos_t, sin_t, start, lo = tables
    rows = qr.shape[0]
    whole = lambda width: pl.BlockSpec((rows, width), lambda h, lo: (0, 0))
    at = lambda width: pl.BlockSpec((rows, width), lambda h, lo: (0, h))
    wide = groups * LANES
    out = lambda width: jax.ShapeDtypeStruct((rows, kv * width), BF)
    return pl.pallas_call(
        functools.partial(bwd_kernel, groups, HD ** -0.5),
        grid_spec=pltpu.PrefetchScalarGridSpec(
            num_scalar_prefetch=1,
            grid=(kv,),
            in_specs=[at(wide), at(LANES), at(LANES), at(wide), whole(LANES), whole(LANES), whole(1),
                      pl.BlockSpec((None, rows, groups), lambda h, lo: (h, 0, 0))],
            out_specs=[at(wide), at(LANES), at(LANES)],
            scratch_shapes=[pltpu.VMEM((rows, LANES), F32)] * 2,
        ),
        out_shape=[out(wide), out(LANES), out(LANES)],
        compiler_params=pltpu.CompilerParams(vmem_limit_bytes=48 * 2 ** 20),
        cost_estimate=pl.CostEstimate(flops=int(10 * kv * groups * rows * rows * LANES * 0.6),
                                      bytes_accessed=rows * kv * (groups + 1) * LANES * 10, transcendentals=0),
        name="attend_back",
    )(lo, qr, kr, vb, d_o, cos_t, sin_t, start, lse)


def doc_starts(seg_row):
    places = jnp.arange(seg_row.shape[0], dtype=jnp.int32)
    previous = jnp.concatenate([seg_row[:1] - 1, seg_row[:-1]])
    return lax.cummax(jnp.where(seg_row != previous, places, 0), axis=0)


def head_tables(positions):
    half = HD // 2
    freq = THETA ** (-(jnp.arange(half, dtype=F32) * 2.0 / HD))
    angles = positions.astype(F32)[:, None] * freq
    cosine, sine = jnp.cos(angles), jnp.sin(angles)
    gap = jnp.zeros((positions.shape[0], LANES // 2 - half), F32)
    return (jnp.concatenate([cosine, gap, cosine, gap], axis=1),
            jnp.concatenate([-sine, gap, sine, gap], axis=1))


def spread_matrix(heads):
    row = jnp.arange(heads * HD)
    feature = row % HD
    lane = (row // HD) * LANES + feature + jnp.where(feature >= HD // 2, LANES // 2 - HD // 2, 0)
    return (lane[:, None] == jnp.arange(heads * LANES)[None, :]).astype(BF)


def dot(a, b, out=BF):
    return jnp.dot(a, b, preferred_element_type=F32).astype(out)


def dot_t(a, b, out=BF):
    return lax.dot_general(a, b, (((0,), (0,)), ((), ())), preferred_element_type=F32).astype(out)


def dot_nt(a, b, out=BF):
    return lax.dot_general(a, b, (((1,), (1,)), ((), ())), preferred_element_type=F32).astype(out)


def inverse_rms(v):
    return lax.rsqrt(jnp.mean(v * v, axis=-1, keepdims=True) + EPS)


def norm_back(v, inv, gain, grad):
    scaled = grad * gain
    return inv * scaled - v * (inv * inv * inv * jnp.mean(scaled * v, axis=-1, keepdims=True))


def swap(v, bit):
    return lax.ppermute(v, "tensor", [(i, i ^ bit) for i in range(lax.axis_size("tensor"))])


def groups_of(size):
    return [[first + i for i in range(size)] for first in range(0, lax.axis_size("tensor"), size)]


def gather(mine, size):
    if size == 2:
        return [mine, swap(mine, 1)]
    if size == 4 and lax.axis_size("tensor") == 4:
        half = mine.shape[0] // 2
        from_x, from_y = swap(mine, 1), swap(mine, 2)
        return [mine, from_x, from_y, jnp.concatenate([swap(from_x[:half], 2), swap(from_y[half:], 1)])]
    blocks = lax.all_gather(mine, "tensor", axis=0, tiled=False, axis_index_groups=groups_of(size))
    at = lax.axis_index("tensor") % size
    return [lax.dynamic_index_in_dim(blocks, at ^ r, 0, keepdims=False) for r in range(size)]


def scatter(parts, size):
    if size == 2:
        return swap(parts[1], 1).astype(F32)
    if size == 4 and lax.axis_size("tensor") == 4:
        _, p_x, p_y, p_diag = parts
        half = p_x.shape[0] // 2
        add = lambda a, b: (a.astype(F32) + b.astype(F32)).astype(BF)
        for_y = swap(p_diag[:half], 1)
        for_x = swap(p_diag[half:], 2)
        a1, b1 = swap(p_x[:half], 1), swap(p_y[half:], 2)
        a2, b2 = swap(add(p_x[half:], for_x), 1), swap(add(p_y[:half], for_y), 2)
        low = a1.astype(F32) + b2.astype(F32)
        high = a2.astype(F32) + b1.astype(F32)
        return jnp.concatenate([low, high])
    at = lax.axis_index("tensor") % size
    blocks = jnp.stack([jnp.zeros_like(parts[1])] + list(parts[1:]))[jnp.arange(size) ^ at]
    summed = lax.psum_scatter(blocks, "tensor", scatter_dimension=0, tiled=False, axis_index_groups=groups_of(size))
    return summed.astype(F32)


def in_order(blocks):
    at = lax.axis_index("tensor") % len(blocks)
    if len(blocks) == 2:
        return by_place(at, *blocks)
    return jnp.stack(blocks)[jnp.arange(len(blocks)) ^ at].reshape(-1, *blocks[0].shape[1:])


def by_place(bit, mine, other):
    return jnp.where(bit == 0, jnp.concatenate([mine, other]), jnp.concatenate([other, mine]))


def body(tokens, segments, attn_gain, w_query, w_key, w_value, w_out, mlp_gain, w_gate, w_up, w_down, out_grad):
    q_width, k_width = w_query.shape[1], w_key.shape[1]
    heads, kv = q_width // HD, k_width // HD
    groups = heads // kv
    row_count, width = tokens.shape
    seq_count, length = segments.shape
    ff = w_gate.shape[1]
    place, places = lax.axis_index("tensor"), lax.axis_size("tensor")
    group = places // seq_count
    core = lax.axis_index("dp") % 2

    token_blocks = gather(tokens, group)
    dy_blocks = gather(out_grad, places)
    qkv_shard = jnp.concatenate(
        [w_query, w_key, w_value, attn_gain[:, None], mlp_gain[:, None]], axis=1)
    qkv_all = lax.all_gather(qkv_shard, "dp", axis=0, tiled=True)
    qkv_w = qkv_all[:, :q_width + 2 * k_width]
    gain_one = qkv_all[:, q_width + 2 * k_width].astype(F32)
    gain_two = qkv_all[:, q_width + 2 * k_width + 1].astype(F32)
    out_w = lax.all_gather(w_out, "dp", axis=1, tiled=True)
    gu_w = lax.all_gather(jnp.concatenate([w_gate, w_up], axis=1), "dp", axis=0, tiled=True)
    down_w = lax.all_gather(w_down, "dp", axis=1, tiled=True)

    def swap_shared(v, bit):
        half = v.shape[0] // 2
        got = swap(lax.dynamic_slice_in_dim(v, core * half, half, 0), bit)
        pair = lax.ppermute(got, "dp", [(i, i ^ 1) for i in range(lax.axis_size("dp"))])
        return by_place(core, got, pair)

    others = [group * m for m in range(1, seq_count)]
    qkv_ws = [qkv_w] + [swap_shared(qkv_w, bits) for bits in others]
    out_ws = [out_w] + [swap_shared(out_w, bits) for bits in others]

    seg_row = lax.dynamic_index_in_dim(segments, place // group, 0, keepdims=False)
    start = doc_starts(seg_row)
    cos_t, sin_t = head_tables(jnp.arange(length, dtype=jnp.int32) - start)
    tables = (cos_t, sin_t, start[:, None], start[::BLK] // BLK)

    spread_q, spread_k = spread_matrix(heads), spread_matrix(kv)

    def pad_heads(w):
        return jnp.concatenate([
            dot(w[:, :q_width], spread_q), dot(w[:, q_width:q_width + k_width], spread_k),
            dot(w[:, q_width + k_width:], spread_k)], axis=1)

    x_own = tokens.astype(F32)
    inv_own = inverse_rms(x_own)
    x_pair = in_order(token_blocks).astype(F32)
    inv_pair = inverse_rms(x_pair)
    n1 = (x_pair * inv_pair * gain_one).astype(BF)
    kept = []
    for w in qkv_ws:
        proj = dot(n1, pad_heads(w), F32)
        o, qr, kr, vb, lse = attend(proj, tables, kv, groups)
        kept.append((dot_nt(o, spread_q), qr, kr, vb, lse))
    o_flat = jnp.concatenate([k[0] for k in kept], axis=1)
    out_both = jnp.concatenate(out_ws, axis=0)

    def rows_of(v, bits):
        return lax.dynamic_slice_in_dim(v, ((place % group) ^ bits) * row_count, row_count, 0)

    branch = scatter([None] + [dot(rows_of(o_flat, bits), out_both) for bits in range(1, group)], group)
    h = x_own + dot(rows_of(o_flat, 0), out_both, F32) + branch

    inv_h = inverse_rms(h)
    n2 = (h * inv_h * gain_two).astype(BF)
    n2s = gather(n2, places)
    segs = segments.reshape(-1)

    def masked(v, bits):
        own = lax.dynamic_slice_in_dim(segs, (place ^ bits) * row_count, row_count, 0)
        return v * (own >= 0).astype(BF)[:, None]

    dys = [masked(block, bits) for bits, block in enumerate(dy_blocks)]
    hiddens, gu_grads = [], []
    for n2_c, dy_c in zip(n2s, dys):
        gate_up = dot(n2_c, gu_w, F32)
        d_hidden = dot_nt(dy_c, down_w, F32)
        gate, up = gate_up[:, :ff], gate_up[:, ff:]
        sig = jax.nn.sigmoid(gate)
        act = gate * sig
        hiddens.append((act * up).astype(BF))
        gu_grads.append(jnp.concatenate(
            [(d_hidden * up * sig * (1.0 + gate * (1.0 - sig))).astype(BF), (d_hidden * act).astype(BF)], axis=1))
    d_n2 = scatter([None] + [dot_nt(g, gu_w) for g in gu_grads[1:]], places) + dot_nt(gu_grads[0], gu_w, F32)

    hidden_all, gu_grad_all = jnp.concatenate(hiddens), jnp.concatenate(gu_grads)
    n2_all, dy_all = jnp.concatenate(n2s), jnp.concatenate(dys)
    down_grad = lax.psum_scatter(dot_t(hidden_all, dy_all), "dp", scatter_dimension=1, tiled=True)
    gu_grad = lax.psum_scatter(dot_t(n2_all, gu_grad_all), "dp", scatter_dimension=0, tiled=True)
    mlp = scatter([None] + [dot(v, down_w) for v in hiddens[1:]], places) + dot(hiddens[0], down_w, F32)
    output = (h + mlp).astype(BF)

    gain_two_grad = jnp.sum(d_n2 * h * inv_h, axis=0)
    dh = dys[0].astype(F32) + norm_back(h, inv_h, gain_two, d_n2)

    dhb = dh.astype(BF)
    dhb_pair = in_order(gather(dhb, group))
    back, wgrads = [], []
    for (o, qr, kr, vb, lse), w, w_o in zip(kept[::-1], qkv_ws[::-1], out_ws[::-1]):
        d_o = dot(dot_nt(dhb_pair, w_o), spread_q)
        dq, dk, dv = attend_back(qr, kr, vb, d_o, tables, lse, kv, groups)
        d_proj = jnp.concatenate([dot_nt(dq, spread_q), dot_nt(dk, spread_k), dot_nt(dv, spread_k)], axis=1)
        back.append((d_proj, w))
        wgrads.append((dot_t(n1, d_proj), dot_t(o, dhb_pair)))

    def add_shares(shares):
        total = shares[-1].astype(F32)
        for bits, share in zip(others[::-1], shares):
            total += swap(share, bits).astype(F32)
        return total.astype(BF)

    qkv_grad = lax.psum_scatter(add_shares([g[0] for g in wgrads]), "dp", scatter_dimension=0, tiled=True).astype(F32)
    out_grad_w = lax.psum_scatter(add_shares([g[1] for g in wgrads]), "dp", scatter_dimension=1, tiled=True).astype(F32)

    d_n1_pair = sum(dot_nt(d, w, F32) for d, w in back)
    gain_one_grad = jnp.sum(d_n1_pair * x_pair * inv_pair, axis=0)
    d_n1 = rows_of(d_n1_pair, 0) + scatter(
        [None] + [rows_of(d_n1_pair, bits).astype(BF) for bits in range(1, group)], group)
    input_grad = dh + norm_back(x_own, inv_own, gain_one, d_n1)

    gains = lax.psum_scatter(jnp.stack([gain_one_grad, gain_two_grad], axis=1), ("dp", "tensor"),
                             scatter_dimension=0, tiled=True)
    return (
        output,
        input_grad,
        gains[:, 0],
        qkv_grad[:, :q_width],
        qkv_grad[:, q_width:q_width + k_width],
        qkv_grad[:, q_width + k_width:],
        out_grad_w,
        gains[:, 1],
        gu_grad[:, :ff].astype(F32),
        gu_grad[:, ff:].astype(F32),
        down_grad.astype(F32),
    )


def solution(mesh):
    rows, weight_in, weight_out = P(("dp", "tensor"), None), P("dp", "tensor"), P("tensor", "dp")
    in_specs = (rows, P("dp", None), P("dp"), weight_in, weight_in, weight_in, weight_out, P("dp"),
                weight_in, weight_in, weight_out, rows)
    gain = P(("dp", "tensor"))
    out_specs = (rows, rows, gain, weight_in, weight_in, weight_in, weight_out, gain, weight_in, weight_in, weight_out)
    return jax.shard_map(body, mesh=mesh, in_specs=in_specs, out_specs=out_specs, check_vma=False)
```

time: 1890 us -> 1560 us (0.83)
  waiting for transfers between devices: 995 us -> 783 us
  blocking collectives: 105 us -> 0 us
  matrix products: 532 us -> 446 us
  Pallas kernels: 0 us -> 85.4 us
  other arithmetic: 151 us -> 109 us
  starting transfers between devices: 1.19 us -> 25.6 us
    ppermute x0 -> x30, waiting for transfers between devices: none -> 543 us  [the longest x28 543 us: swap(): lax.ppermute(v, 'tensor', [(i, i ^ bit) for i in range(lax.axis_size('ten...]
    all_gather x9 -> x4, waiting for transfers between devices: 516 us -> 77.6 us  [the longest x1 49.6 us: body(): qkv_all = lax.all_gather(qkv_shard, 'dp', axis=0, tiled=True)]
    reduce_scatter x8 -> x4, waiting for transfers between devices: 412 us -> 162 us  [the longest x1 162 us: body(): lax.psum_scatter(dot_t(n2_all, gu_grad_all), 'dp', scatter_dimension=0, t...]
    dot_general x26 -> x44, matrix products: 532 us -> 446 us  [the longest x20 194 us: dot(): return jnp.dot(a, b, preferred_element_type=F32).astype(out)]
    pallas_call x0 -> x4, Pallas kernels: none -> 85.4 us  [the longest x2 51.1 us: attend_back(): pl.pallas_call(functools.partial(bwd_kernel, groups, HD ** (-0.5)), grid_...]
    unnamed x2 -> x0, blocking collectives: 71.5 us -> none
    unnamed x23 -> x10, waiting for transfers between devices: 66.6 us -> 0.81 us
    convert_element_type x15 -> x12, other arithmetic: 79.5 us -> 34 us  [the longest x2 13.7 us: add_shares(): return total.astype(BF)]
  transfers between devices with their start and end apart: 20 -> 39, of which waited for: 14 -> 19; matrix products, arithmetic and copies ran while one was open for 34% -> 34% of each run, Pallas kernels for 0% -> 2%
where the time goes in v1:
time: 1560 us; the launch traced here: 1550 us
  waiting for transfers between devices  783 us (50%)
  matrix products  446 us (29%)
  other arithmetic  109 us (7%)
  Pallas kernels  85.4 us (5%)
  local copies, waits for them, and re-layouts  85.1 us (5%)
  starting transfers between devices  25.6 us (2%)
    ppermute x28, waiting for transfers between devices, swap(): lax.ppermute(v, 'tensor', [(i, i ^ bit) for i in range(lax.axis_size('ten...  543 us
    dot_general x20, matrix products, dot(): return jnp.dot(a, b, preferred_element_type=F32).astype(out)  194 us
    reduce_scatter x1, waiting for transfers between devices, body(): lax.psum_scatter(dot_t(n2_all, gu_grad_all), 'dp', scatter_dimension=0, t...  162 us
    dot_general x18, matrix products, dot_nt(): lax.dot_general(a, b, (((1,), (1,)), ((), ())), preferred_element_type=F32)  143 us
    dot_general x6, matrix products, dot_t(): lax.dot_general(a, b, (((0,), (0,)), ((), ())), preferred_element_type=F32)  109 us
    pallas_call x2, Pallas kernels, attend_back(): pl.pallas_call(functools.partial(bwd_kernel, groups, HD ** (-0.5)), grid_...  51.1 us
    all_gather x1, waiting for transfers between devices, body(): qkv_all = lax.all_gather(qkv_shard, 'dp', axis=0, tiled=True)  49.6 us
    pallas_call x2, Pallas kernels, attend(): pl.pallas_call(functools.partial(fwd_kernel, groups, HD ** (-0.5)), grid_...  34.3 us
  transfers between devices with their start and end apart: 39, of which 19 were waited for; matrix products, arithmetic and copies ran while one was open for 34% of the time, Pallas kernels for 2%

profile of v1, /device:TPU:0, one launch (start us, length us, event | category | flops | bytes accessed | tf_op | source)
XLA Modules:
  0.0 1549.2 jit_solution(450995783369353698)
XLA Ops:
  23.8 28.0 %all-gather.7.cloned.1.call-done = bf16[640,2560]{0,1:T(8,128)(2,1)} async-done(((bf16[640,320]{0,1:T(8,128)(2,1)}), bf16[640,2560]{0,1:T(8,128)(2,1)}) %all-gather.7.cloned.1.call-update) | async-done | bytes 3276816 | tf_op jit(solution)/shard_map/all_gather | solution.py:273
  59.3 49.6 %all-gather.5.cloned.1.call-done = bf16[2560,962]{1,0:T(8,128)(2,1)} async-done(((bf16[320,962]{1,0:T(8,128)(2,1)}), bf16[2560,962]{1,0:T(8,128)(2,1)}) %all-gather.5.cloned.1.call-update) | async-done | bytes 4925456 | tf_op jit(solution)/shard_map/all_gather | solution.py:269
  142.9 29.6 %collective-permute-done.1 = bf16[1280,960]{0,1:T(8,128)(2,1)} collective-permute-done((bf16[1280,960]{0,1:T(8,128)(2,1)}, bf16[1280,960]{0,1:T(8,128)(2,1)}, u32[]{:S(2)}, u32[]{:S(2)}) %collective-permute-start.1) | collective-permute-done | bytes 2457632 | tf_op jit(solution)/shard_map/ppermute | solution.py:204
  172.6 14.5 fusion.19.q_ref.k_ref.v_ref
  187.0 16.9 %attend.2 = (bf16[1024,1024]{1,0:T(8,128)(2,1)S(1)}, bf16[1024,1024]{1,0:T(8,128)(2,1)}, bf16[1024,256]{1,0:T(8,128)(2,1)S(1)}, bf16[1024,256]{1,0:T(8,128)(2,1)S(1)}, f32[2,1024,4]{2,1,0:T(8,128)S(1)}) custom-call(s32[4]{0:T(128)S(1)} %and_select_fusion.2.lo_ref, f32[1024,1536]{1,0:T(8,128)} %fusion.19.q_ref.k_ref.v_ref, ...), custom_call_target="tpu_custom_call" | custom-call | flops 2576980480 | bytes 13107200 | tf_op jit(solution)/shard_map/attend/pallas_call | solution.py:115
  230.3 14.1 fusion.25.q_ref.k_ref.v_ref
  244.4 17.3 %attend.3 = (bf16[1024,1024]{1,0:T(8,128)(2,1)S(1)}, bf16[1024,1024]{1,0:T(8,128)(2,1)}, bf16[1024,256]{1,0:T(8,128)(2,1)S(1)}, bf16[1024,256]{1,0:T(8,128)(2,1)S(1)}, f32[2,1024,4]{2,1,0:T(8,128)S(1)}) custom-call(s32[4]{0:T(128)S(1)} %and_select_fusion.2.lo_ref, f32[1024,1536]{1,0:T(8,128)} %fusion.25.q_ref.k_ref.v_ref, ...), custom_call_target="tpu_custom_call" | custom-call | flops 2576980480 | bytes 13107200 | tf_op jit(solution)/shard_map/attend/pallas_call | solution.py:115
  271.9 57.9 %collective-permute-done.5 = bf16[512,2560]{1,0:T(8,128)(2,1)} collective-permute-done((bf16[512,2560]{1,0:T(8,128)(2,1)}, bf16[512,2560]{1,0:T(8,128)(2,1)}, u32[]{:S(2)}, u32[]{:S(2)}) %collective-permute-start.5) | collective-permute-done | bytes 2621472 | tf_op jit(solution)/shard_map/ppermute | solution.py:204
  329.8 9.0 multiply_reduce_fusion.2
  349.9 36.1 %collective-permute-done.16 = bf16[512,2560]{1,0:T(8,128)(2,1)} collective-permute-done((bf16[512,2560]{1,0:T(8,128)(2,1)}, bf16[512,2560]{1,0:T(8,128)(2,1)}, u32[]{:S(2)}, u32[]{:S(2)}) %collective-permute-start.16) | collective-permute-done | bytes 2621472 | tf_op jit(solution)/shard_map/ppermute | solution.py:204
  390.9 9.9 collective-permute-done.8
  403.9 38.3 %collective-permute-done.6 = bf16[512,2560]{1,0:T(8,128)(2,1)} collective-permute-done((bf16[512,2560]{1,0:T(8,128)(2,1)}, bf16[512,2560]{1,0:T(8,128)(2,1)}, u32[]{:S(2)}, u32[]{:S(2)}) %collective-permute-start.6) | collective-permute-done | bytes 2621472 | tf_op jit(solution)/shard_map/ppermute | solution.py:204
  447.2 23.0 %collective-permute-done.20 = bf16[256,2560]{1,0:T(8,128)(2,1)S(1)} collective-permute-done((bf16[256,2560]{1,0:T(8,128)(2,1)S(1)}, bf16[256,2560]{1,0:T(8,128)(2,1)S(1)}, u32[]{:S(2)}, u32[]{:S(2)}) %collective-permute-start.20) | collective-permute-done | bytes 1310752 | tf_op jit(solution)/shard_map/ppermute | solution.py:204
  472.1 25.7 %collective-permute-done.10 = bf16[256,2560]{1,0:T(8,128)(2,1)S(1)} collective-permute-done((bf16[256,2560]{1,0:T(8,128)(2,1)S(1)}, bf16[256,2560]{1,0:T(8,128)(2,1)S(1)}, u32[]{:S(2)}, u32[]{:S(2)}) %collective-permute-start.10) | collective-permute-done | bytes 1310752 | tf_op jit(solution)/shard_map/ppermute | solution.py:204
  497.9 16.0 %fusion.51 = f32[512,3456]{1,0:T(8,128)} fusion(bf16[2560,3456]{1,0:T(8,128)(2,1)} %all-gather.9.cloned.1.call-done, bf16[256,2560]{1,0:T(8,128)(2,1)S(1)} %collective-permute-done.10, bf16[256,2560]{1,0:T(8,128)(2,1)} %collective-permute-done.9), kind=kOutput, calls=%fused_computation.118 | convolution fusion | flops 9064939520 | bytes 27394048 | tf_op jit(solution)/shard_map/dot_general | solution.py:183
  513.8 13.2 multiply_convert_fusion.4
  527.9 14.7 convolution_convert_fusion.8
  545.8 9.2 convolution_convert_fusion.11
  559.3 16.7 %fusion.142 = f32[512,3456]{1,0:T(8,128)} fusion(bf16[512,2560]{1,0:T(8,128)(2,1)} %collective-permute-done.6, bf16[2560,3456]{1,0:T(8,128)(2,1)} %all-gather.9.cloned.1.call-done), kind=kOutput, calls=%fused_computation.277 | convolution fusion | flops 9059696640 | bytes 27394048 | tf_op jit(solution)/shard_map/dot_general | solution.py:183
  585.4 14.7 convolution_convert_fusion.10
  604.3 16.9 %fusion.143 = f32[512,3456]{1,0:T(8,128)} fusion(bf16[512,2560]{1,0:T(8,128)(2,1)} %collective-permute-done.8, bf16[2560,3456]{1,0:T(8,128)(2,1)} %all-gather.9.cloned.1.call-done), kind=kOutput, calls=%fused_computation.278 | convolution fusion | flops 9059696640 | bytes 27394048 | tf_op jit(solution)/shard_map/dot_general | solution.py:183
  621.2 8.8 multiply_convert_fusion.6
  632.7 15.9 %fusion.144 = f32[512,3456]{1,0:T(8,128)} fusion(bf16[512,2560]{1,0:T(8,128)(2,1)} %get-tuple-element.105, bf16[2560,3456]{1,0:T(8,128)(2,1)} %all-gather.9.cloned.1.call-done), kind=kOutput, calls=%fused_computation.279 | convolution fusion | flops 9059696640 | bytes 27394048 | tf_op jit(solution)/shard_map/dot_general | solution.py:183
  655.5 15.4 convolution_convert_fusion.9
  670.9 11.9 multiply_convert_fusion.2
  682.9 9.1 convolution_convert_fusion.12
  710.0 21.3 %collective-permute-done.25 = bf16[256,2560]{1,0:T(8,128)(2,1)S(1)} collective-permute-done((bf16[256,2560]{1,0:T(8,128)(2,1)S(1)}, bf16[256,2560]{1,0:T(8,128)(2,1)S(1)}, u32[]{:S(2)}, u32[]{:S(2)}) %collective-permute-start.25) | collective-permute-done | bytes 1310752 | tf_op jit(solution)/shard_map/ppermute | solution.py:204
  731.3 22.9 %collective-permute-done.24 = bf16[256,2560]{1,0:T(8,128)(2,1)S(1)} collective-permute-done((bf16[256,2560]{1,0:T(8,128)(2,1)S(1)}, bf16[256,2560]{1,0:T(8,128)(2,1)S(1)}, u32[]{:S(2)}, u32[]{:S(2)}) %collective-permute-start.24) | collective-permute-done | bytes 1310752 | tf_op jit(solution)/shard_map/ppermute | solution.py:204
  761.4 18.4 %multiply_reduce_fusion = (f32[2560]{0:T(1024)S(1)}, f32[512]{0:T(512)S(1)}, f32[512,2560]{1,0:T(8,128)}) fusion(f32[512,2560]{1,0:T(8,128)} %copy-done.12, f32[512]{0:T(512)S(1)} %copy-done.44, f32[256,2560]{1,0:T(8,128)} %convert_add_fusion.1, f32[256,2560]{1,0:T(8,128)} %convert_add_fusion.2, f32[2560]{0:T(1024)S(1)} %copy-done.37, ...), kind=kOutput, calls=%fused_computation.66 | convolution fusion | flops 9070180352 | bytes 36986880 | tf_op jit(solution)/shard_map/dot_general | solution.py:191
  791.1 21.2 %collective-permute-done.12 = bf16[256,2560]{1,0:T(8,128)(2,1)} collective-permute-done((bf16[256,2560]{1,0:T(8,128)(2,1)}, bf16[256,2560]{1,0:T(8,128)(2,1)}, u32[]{:S(2)}, u32[]{:S(2)}) %collective-permute-start.12) | collective-permute-done | bytes 1310752 | tf_op jit(solution)/shard_map/ppermute | solution.py:204
  816.0 15.1 fusion.136
  832.5 54.4 %collective-permute-done.26 = bf16[512,2560]{1,0:T(8,128)(2,1)} collective-permute-done((bf16[512,2560]{1,0:T(8,128)(2,1)}, bf16[512,2560]{1,0:T(8,128)(2,1)}, u32[]{:S(2)}, u32[]{:S(2)}) %collective-permute-start.26) | collective-permute-done | bytes 2621472 | tf_op jit(solution)/shard_map/ppermute | solution.py:204
  886.9 14.7 fusion.61.do_ref
  904.9 25.6 %attend_back.2 = (bf16[1024,1024]{1,0:T(8,128)(2,1)}, bf16[1024,256]{1,0:T(8,128)(2,1)S(1)}, bf16[1024,256]{1,0:T(8,128)(2,1)S(1)}) custom-call(s32[4]{0:T(128)S(1)} %copy-done.1, bf16[1024,1024]{1,0:T(8,128)(2,1)} %get-tuple-element.29.qr_ref, bf16[1024,256]{1,0:T(8,128)(2,1)S(1)} %copy-done.9, bf16[1024,256]{1,0:T(8,128)(2,1)S(1)} %copy-done.11, ...), custom_call_target="tpu_custom_call" | custom-call | flops 6442450944 | bytes 13107200 | tf_op jit(solution)/shard_map/attend_back/pallas_call | solution.py:141
  934.8 14.7 fusion.62.do_ref
  951.8 25.5 %attend_back.3 = (bf16[1024,1024]{1,0:T(8,128)(2,1)}, bf16[1024,256]{1,0:T(8,128)(2,1)S(1)}, bf16[1024,256]{1,0:T(8,128)(2,1)S(1)}) custom-call(s32[4]{0:T(128)S(1)} %copy-done.1, bf16[1024,1024]{1,0:T(8,128)(2,1)} %get-tuple-element.36.qr_ref, bf16[1024,256]{1,0:T(8,128)(2,1)S(1)} %get-tuple-element.37.kr_ref, bf16[1024,256]{1,0:T(8,128)(2,1)S(1)} %copy-done.7, ...), custom_call_target="tpu_custom_call" | custom-call | flops 6442450944 | bytes 13107200 | tf_op jit(solution)/shard_map/attend_back/pallas_call | solution.py:141
  991.5 8.4 fusion.83
  999.9 14.3 fusion.11
  1023.7 45.3 %collective-permute-done.29 = bf16[640,2560]{0,1:T(8,128)(2,1)} collective-permute-done((bf16[640,2560]{0,1:T(8,128)(2,1)}, bf16[640,2560]{0,1:T(8,128)(2,1)}, u32[]{:S(2)}, u32[]{:S(2)}) %collective-permute-start.29) | collective-permute-done | bytes 3276832 | tf_op jit(solution)/shard_map/ppermute | solution.py:204
  1073.6 26.9 %convolution_convert_fusion.1 = bf16[1728,2560]{0,1:T(8,128)(2,1)} fusion(bf16[512,2560]{1,0:T(8,128)(2,1)} %maximum_multiply_fusion, bf16[512,2560]{1,0:T(8,128)(2,1)} %broadcast_multiply_fusion, bf16[512,2560]{1,0:T(8,128)(2,1)} %broadcast_multiply_fusion.1, bf16[512,2560]{1,0:T(8,128)(2,1)S(1)} %copy-done.16, bf16[512,1728]{1,0:T(8,128)(2,1)} %get-tuple-element.119, ...), kind=kOutput, calls=%fused_computation.11 | convolution fusion | flops 18194071552 | bytes 26411008 | tf_op jit(solution)/shard_map/dot_general | solution.py:187
  1101.9 8.9 convolution_convert_fusion.5
  1121.7 10.7 convolution_convert_fusion.4
  1132.5 91.9 %collective-permute-done.28 = bf16[2560,960]{0,1:T(8,128)(2,1)} collective-permute-done((bf16[2560,960]{0,1:T(8,128)(2,1)S(1)}, bf16[2560,960]{0,1:T(8,128)(2,1)}, u32[]{:S(2)}, u32[]{:S(2)}) %collective-permute-start.28) | collective-permute-done | bytes 4915232 | tf_op jit(solution)/shard_map/ppermute | solution.py:204
  1232.3 9.2 add_convert_fusion
  1243.5 46.4 %convolution_convert_fusion = bf16[2560,3456]{1,0:T(8,128)(2,1)} fusion(bf16[2048,2560]{1,0:T(8,128)(2,1)} %constant_dynamic-update-slice_fusion, bf16[512,3456]{1,0:T(8,128)(2,1)S(1)} %copy-done.19, bf16[512,3456]{1,0:T(8,128)(2,1)} %pad_maximum_fusion.4, bf16[512,3456]{1,0:T(8,128)(2,1)} %copy-done.20, bf16[512,3456]{1,0:T(8,128)(2,1)} %pad_maximum_fusion.6), kind=kOutput, calls=%fused_computation | convolution fusion | flops 36304257024 | bytes 42336256 | tf_op jit(solution)/shard_map/dot_general | solution.py:187
  1297.6 55.5 %collective-permute-done.27 = bf16[512,2560]{1,0:T(8,128)(2,1)} collective-permute-done((bf16[512,2560]{1,0:T(8,128)(2,1)}, bf16[512,2560]{1,0:T(8,128)(2,1)}, u32[]{:S(2)}, u32[]{:S(2)}) %collective-permute-start.27) | collective-permute-done | bytes 2621472 | tf_op jit(solution)/shard_map/ppermute | solution.py:204
  1358.7 8.4 fusion.42
  1376.7 161.6 %reduce-scatter.12.cloned.1.call-done = bf16[320,3456]{1,0:T(8,128)(2,1)} async-done(((bf16[2560,3456]{1,0:T(8,128)(2,1)}), bf16[320,3456]{1,0:T(8,128)(2,1)}) %reduce-scatter.12.cloned.1.call-update) | async-done | bytes 2211856 | tf_op jit(solution)/shard_map/reduce_scatter | solution.py:343
  (333 shorter events, 280.0 us)
Async XLA Ops:
  7.2 44.6 %all-gather.7.cloned.1.call-start = ((), (), s32[]{:S(2)}) async-start(), calls=%async_computation.6 | async-start | bytes 3686400 | tf_op jit(solution)/shard_map/all_gather | solution.py:273
  7.9 101.0 %all-gather.5.cloned.1.call-start = ((), (), s32[]{:S(2)}) async-start(), calls=%async_computation.5 | async-start | bytes 5898240 | tf_op jit(solution)/shard_map/all_gather | solution.py:269
  13.6 484.2 %all-gather.9.cloned.1.call-start = ((), (), s32[]{:S(2)}) async-start(), calls=%async_computation.7 | async-start | bytes 19906560 | tf_op jit(solution)/shard_map/all_gather | solution.py:274
  15.6 498.2 %all-gather.11.cloned.1.call-start = ((), (), s32[]{:S(2)}) async-start(), calls=%async_computation.8 | async-start | bytes 10321920 | tf_op jit(solution)/shard_map/all_gather | solution.py:275
  15.7 103.5 %collective-permute-start = (bf16[512,2560]{1,0:T(8,128)(2,1)}, bf16[512,2560]{1,0:T(8,128)(2,1)}, u32[]{:S(2)}, u32[]{:S(2)}) collective-permute-start(bf16[512,2560]{1,0:T(8,128)(2,1)} %param.12), channel_id=1, source_target_pairs={{0,1},{1,0},{2,3},{3,2},{4,5},{5,4},{6,7},{7,6},{8,9},{9,8},{10,11... | collective-permute-start | bytes 7864328 | tf_op jit(solution)/shard_map/ppermute | solution.py:204
  18.7 1276.8 %reduce-scatter.16.cloned.1.call-start = ((), (), s32[]{:S(2)}) async-start(), calls=%async_computation.13 | async-start | bytes 1351680
  20.8 241.0 %copy-start.54 = (s32[640]{0:T(1024)}, s32[640]{0:T(1024)S(1)}, u32[]{:S(2)}) copy-start(s32[640]{0:T(1024)S(1)} %fusion.103) | copy-start | bytes 7684
  57.8 68.1 %collective-permute-start.3 = (bf16[320,2560]{1,0:T(8,128)(2,1)}, bf16[320,2560]{1,0:T(8,128)(2,1)}, u32[]{:S(2)}, u32[]{:S(2)}) collective-permute-start(bf16[320,2560]{1,0:T(8,128)(2,1)} %copy.109), channel_id=1, source_target_pairs={{0,2},{1,3},{2,0},{3,1},{4,6},{5,7},{6,4},{7,5},{8,10},{9,11},{10,... | collective-permute-start | bytes 4915208 | tf_op jit(solution)/shard_map/ppermute | solution.py:204
  59.3 185.1 %copy-start = (s32[4]{0:T(128)}, s32[4]{0:T(128)S(1)}, u32[]{:S(2)}) copy-start(s32[4]{0:T(128)S(1)} %and_select_fusion.2.lo_ref) | copy-start | bytes 52
  116.8 55.8 %collective-permute-start.1 = (bf16[1280,960]{0,1:T(8,128)(2,1)}, bf16[1280,960]{0,1:T(8,128)(2,1)}, u32[]{:S(2)}, u32[]{:S(2)}) collective-permute-start(bf16[1280,960]{0,1:T(8,128)(2,1)} %copy.107), channel_id=1, source_target_pairs={{0,2},{1,3},{2,0},{3,1},{4,6},{5,7},{6,4},{7,5},{8,10},{9,11},{10,... | collective-permute-start | bytes 7372808 | tf_op jit(solution)/shard_map/ppermute | solution.py:204
  118.2 105.8 %copy-start.47 = (s32[160]{0:T(256)}, s32[160]{0:T(256)S(1)}, u32[]{:S(2)}) copy-start(s32[160]{0:T(256)S(1)} %fusion.119) | copy-start | bytes 1924
  125.9 104.4 %copy-start.52 = (f32[1024]{0:T(1024)}, f32[1024]{0:T(1024)S(1)}, u32[]{:S(2)}) copy-start(f32[1024]{0:T(1024)S(1)} %add_rsqrt_fusion) | copy-start | bytes 12292
  125.9 80.7 %collective-permute-start.4 = (bf16[320,2560]{1,0:T(8,128)(2,1)}, bf16[320,2560]{1,0:T(8,128)(2,1)}, u32[]{:S(2)}, u32[]{:S(2)}) collective-permute-start(bf16[320,2560]{1,0:T(8,128)(2,1)} %collective-permute-done.3), channel_id=1, source_target_pairs={{0,4},{4,0},{8,12},{12,8},{16,20},{20,16},{24,28},{28,24},{1,5},{5... | collective-permute-start | bytes 4915208 | tf_op jit(solution)/shard_map/ppermute | solution.py:280
  132.1 98.2 %copy-start.45 = (f32[2560]{0:T(1024)}, f32[2560]{0:T(1024)S(1)}, u32[]{:S(2)}) copy-start(f32[2560]{0:T(1024)S(1)} %get-tuple-element.101) | copy-start | bytes 30724
  132.2 206.7 %copy-start.36 = (f32[2560]{0:T(1024)}, f32[2560]{0:T(1024)S(1)}, u32[]{:S(2)}) copy-start(f32[2560]{0:T(1024)S(1)} %get-tuple-element.100) | copy-start | bytes 30724
  172.6 44.9 %collective-permute-start.2 = (bf16[1280,960]{0,1:T(8,128)(2,1)}, bf16[1280,960]{0,1:T(8,128)(2,1)}, u32[]{:S(2)}, u32[]{:S(2)}) collective-permute-start(bf16[1280,960]{0,1:T(8,128)(2,1)} %collective-permute-done.1), channel_id=1, source_target_pairs={{0,4},{4,0},{8,12},{12,8},{16,20},{20,16},{24,28},{28,24},{1,5},{5... | collective-permute-start | bytes 7372808 | tf_op jit(solution)/shard_map/ppermute | solution.py:280
  269.8 60.0 %collective-permute-start.5 = (bf16[512,2560]{1,0:T(8,128)(2,1)}, bf16[512,2560]{1,0:T(8,128)(2,1)}, u32[]{:S(2)}, u32[]{:S(2)}) collective-permute-start(bf16[512,2560]{1,0:T(8,128)(2,1)} %convolution_convert_fusion.14), channel_id=1, source_target_pairs={{0,1},{1,0},{2,3},{3,2},{4,5},{5,4},{6,7},{7,6},{8,9},{9,8},{10,11... | collective-permute-start | bytes 7864328 | tf_op jit(solution)/shard_map/ppermute | solution.py:204
  271.3 76.6 %collective-permute-start.18 = (bf16[512,2560]{1,0:T(8,128)(2,1)}, bf16[512,2560]{1,0:T(8,128)(2,1)}, u32[]{:S(2)}, u32[]{:S(2)}) collective-permute-start(bf16[512,2560]{1,0:T(8,128)(2,1)} %param.23), channel_id=1, source_target_pairs={{0,2},{1,3},{2,0},{3,1},{4,6},{5,7},{6,4},{7,5},{8,10},{9,11},{10,... | collective-permute-start | bytes 7864328 | tf_op jit(solution)/shard_map/ppermute | solution.py:204
  271.3 114.7 %collective-permute-start.16 = (bf16[512,2560]{1,0:T(8,128)(2,1)}, bf16[512,2560]{1,0:T(8,128)(2,1)}, u32[]{:S(2)}, u32[]{:S(2)}) collective-permute-start(bf16[512,2560]{1,0:T(8,128)(2,1)} %param.23), channel_id=1, source_target_pairs={{0,1},{1,0},{2,3},{3,2},{4,5},{5,4},{6,7},{7,6},{8,9},{9,8},{10,11... | collective-permute-start | bytes 7864328 | tf_op jit(solution)/shard_map/ppermute | solution.py:204
  342.7 58.2 %collective-permute-start.8 = (bf16[512,2560]{1,0:T(8,128)(2,1)}, bf16[512,2560]{1,0:T(8,128)(2,1)}, u32[]{:S(2)}, u32[]{:S(2)}) collective-permute-start(bf16[512,2560]{1,0:T(8,128)(2,1)} %get-tuple-element.105), channel_id=1, source_target_pairs={{0,2},{1,3},{2,0},{3,1},{4,6},{5,7},{6,4},{7,5},{8,10},{9,11},{10,... | collective-permute-start | bytes 7864328 | tf_op jit(solution)/shard_map/ppermute | solution.py:204
  342.7 99.4 %collective-permute-start.6 = (bf16[512,2560]{1,0:T(8,128)(2,1)}, bf16[512,2560]{1,0:T(8,128)(2,1)}, u32[]{:S(2)}, u32[]{:S(2)}) collective-permute-start(bf16[512,2560]{1,0:T(8,128)(2,1)} %get-tuple-element.105), channel_id=1, source_target_pairs={{0,1},{1,0},{2,3},{3,2},{4,5},{5,4},{6,7},{7,6},{8,9},{9,8},{10,11... | collective-permute-start | bytes 7864328 | tf_op jit(solution)/shard_map/ppermute | solution.py:204
  349.3 120.8 %collective-permute-start.20 = (bf16[256,2560]{1,0:T(8,128)(2,1)S(1)}, bf16[256,2560]{1,0:T(8,128)(2,1)S(1)}, u32[]{:S(2)}, u32[]{:S(2)}) collective-permute-start(bf16[256,2560]{1,0:T(8,128)(2,1)S(1)} %slice.218), channel_id=1, source_target_pairs={{0,1},{1,0},{2,3},{3,2},{4,5},{5,4},{6,7},{7,6},{8,9},{9,8},{10,11... | collective-permute-start | bytes 3932168 | tf_op jit(solution)/shard_map/ppermute | solution.py:204
  387.4 82.8 %collective-permute-start.19 = (bf16[256,2560]{1,0:T(8,128)(2,1)S(1)}, bf16[256,2560]{1,0:T(8,128)(2,1)S(1)}, u32[]{:S(2)}, u32[]{:S(2)}) collective-permute-start(bf16[256,2560]{1,0:T(8,128)(2,1)S(1)} %slice.217), channel_id=1, source_target_pairs={{0,2},{1,3},{2,0},{3,1},{4,6},{5,7},{6,4},{7,5},{8,10},{9,11},{10,... | collective-permute-start | bytes 3932168 | tf_op jit(solution)/shard_map/ppermute | solution.py:204
  402.3 95.6 %collective-permute-start.10 = (bf16[256,2560]{1,0:T(8,128)(2,1)S(1)}, bf16[256,2560]{1,0:T(8,128)(2,1)S(1)}, u32[]{:S(2)}, u32[]{:S(2)}) collective-permute-start(bf16[256,2560]{1,0:T(8,128)(2,1)S(1)} %slice.206), channel_id=1, source_target_pairs={{0,1},{1,0},{2,3},{3,2},{4,5},{5,4},{6,7},{7,6},{8,9},{9,8},{10,11... | collective-permute-start | bytes 3932168 | tf_op jit(solution)/shard_map/ppermute | solution.py:204
  443.6 54.3 %collective-permute-start.9 = (bf16[256,2560]{1,0:T(8,128)(2,1)S(1)}, bf16[256,2560]{1,0:T(8,128)(2,1)}, u32[]{:S(2)}, u32[]{:S(2)}) collective-permute-start(bf16[256,2560]{1,0:T(8,128)(2,1)S(1)} %slice.205), channel_id=1, source_target_pairs={{0,2},{1,3},{2,0},{3,1},{4,6},{5,7},{6,4},{7,5},{8,10},{9,11},{10,... | collective-permute-start | bytes 3932168 | tf_op jit(solution)/shard_map/ppermute | solution.py:204
  544.3 158.0 %collective-permute-start.21 = (bf16[256,2560]{1,0:T(8,128)(2,1)}, bf16[256,2560]{1,0:T(8,128)(2,1)}, u32[]{:S(2)}, u32[]{:S(2)}) collective-permute-start(bf16[256,2560]{1,0:T(8,128)(2,1)} %get-tuple-element.123), channel_id=1, source_target_pairs={{0,1},{1,0},{2,3},{3,2},{4,5},{5,4},{6,7},{7,6},{8,9},{9,8},{10,11... | collective-permute-start | bytes 3932168 | tf_op jit(solution)/shard_map/ppermute | solution.py:204
  545.8 151.3 %collective-permute-start.23 = (bf16[256,2560]{1,0:T(8,128)(2,1)}, bf16[256,2560]{1,0:T(8,128)(2,1)}, u32[]{:S(2)}, u32[]{:S(2)}) collective-permute-start(bf16[256,2560]{1,0:T(8,128)(2,1)} %get-tuple-element.124), channel_id=1, source_target_pairs={{0,2},{1,3},{2,0},{3,1},{4,6},{5,7},{6,4},{7,5},{8,10},{9,11},{10,... | collective-permute-start | bytes 3932168 | tf_op jit(solution)/shard_map/ppermute | solution.py:204
  556.6 148.6 %collective-permute-start.11 = (bf16[256,2560]{1,0:T(8,128)(2,1)}, bf16[256,2560]{1,0:T(8,128)(2,1)}, u32[]{:S(2)}, u32[]{:S(2)}) collective-permute-start(bf16[256,2560]{1,0:T(8,128)(2,1)} %get-tuple-element.125), channel_id=1, source_target_pairs={{0,1},{1,0},{2,3},{3,2},{4,5},{5,4},{6,7},{7,6},{8,9},{9,8},{10,11... | collective-permute-start | bytes 3932168 | tf_op jit(solution)/shard_map/ppermute | solution.py:204
  557.4 142.1 %collective-permute-start.13 = (bf16[256,2560]{1,0:T(8,128)(2,1)}, bf16[256,2560]{1,0:T(8,128)(2,1)}, u32[]{:S(2)}, u32[]{:S(2)}) collective-permute-start(bf16[256,2560]{1,0:T(8,128)(2,1)} %get-tuple-element.126), channel_id=1, source_target_pairs={{0,2},{1,3},{2,0},{3,1},{4,6},{5,7},{6,4},{7,5},{8,10},{9,11},{10,... | collective-permute-start | bytes 3932168 | tf_op jit(solution)/shard_map/ppermute | solution.py:204
  602.9 153.7 %collective-permute-start.17 = (bf16[256,2560]{1,0:T(8,128)(2,1)}, bf16[256,2560]{1,0:T(8,128)(2,1)S(1)}, u32[]{:S(2)}, u32[]{:S(2)}) collective-permute-start(bf16[256,2560]{1,0:T(8,128)(2,1)} %slice.215), channel_id=1, source_target_pairs={{0,1},{1,0},{2,3},{3,2},{4,5},{5,4},{6,7},{7,6},{8,9},{9,8},{10,11... | collective-permute-start | bytes 3932168 | tf_op jit(solution)/shard_map/ppermute | solution.py:204
  697.1 94.1 %collective-permute-start.7 = (bf16[256,2560]{1,0:T(8,128)(2,1)}, bf16[256,2560]{1,0:T(8,128)(2,1)}, u32[]{:S(2)}, u32[]{:S(2)}) collective-permute-start(bf16[256,2560]{1,0:T(8,128)(2,1)} %slice.201), channel_id=1, source_target_pairs={{0,1},{1,0},{2,3},{3,2},{4,5},{5,4},{6,7},{7,6},{8,9},{9,8},{10,11... | collective-permute-start | bytes 3932168 | tf_op jit(solution)/shard_map/ppermute | solution.py:204
  699.5 31.8 %collective-permute-start.25 = (bf16[256,2560]{1,0:T(8,128)(2,1)S(1)}, bf16[256,2560]{1,0:T(8,128)(2,1)S(1)}, u32[]{:S(2)}, u32[]{:S(2)}) collective-permute-start(bf16[256,2560]{1,0:T(8,128)(2,1)S(1)} %slice.222), channel_id=1, source_target_pairs={{0,2},{1,3},{2,0},{3,1},{4,6},{5,7},{6,4},{7,5},{8,10},{9,11},{10,... | collective-permute-start | bytes 3932168 | tf_op jit(solution)/shard_map/ppermute | solution.py:204
  702.3 52.0 %collective-permute-start.24 = (bf16[256,2560]{1,0:T(8,128)(2,1)S(1)}, bf16[256,2560]{1,0:T(8,128)(2,1)S(1)}, u32[]{:S(2)}, u32[]{:S(2)}) collective-permute-start(bf16[256,2560]{1,0:T(8,128)(2,1)S(1)} %add_convert_fusion.2), channel_id=1, source_target_pairs={{0,1},{1,0},{2,3},{3,2},{4,5},{5,4},{6,7},{7,6},{8,9},{9,8},{10,11... | collective-permute-start | bytes 3932168 | tf_op jit(solution)/shard_map/ppermute | solution.py:204
  705.2 54.2 %collective-permute-start.22 = (bf16[256,2560]{1,0:T(8,128)(2,1)S(1)}, bf16[256,2560]{1,0:T(8,128)(2,1)S(1)}, u32[]{:S(2)}, u32[]{:S(2)}) collective-permute-start(bf16[256,2560]{1,0:T(8,128)(2,1)S(1)} %add_convert_fusion.3), channel_id=1, source_target_pairs={{0,2},{1,3},{2,0},{3,1},{4,6},{5,7},{6,4},{7,5},{8,10},{9,11},{10,... | collective-permute-start | bytes 3932168 | tf_op jit(solution)/shard_map/ppermute | solution.py:204
  731.3 56.3 %collective-permute-start.15 = (bf16[256,2560]{1,0:T(8,128)(2,1)}, bf16[256,2560]{1,0:T(8,128)(2,1)}, u32[]{:S(2)}, u32[]{:S(2)}) collective-permute-start(bf16[256,2560]{1,0:T(8,128)(2,1)} %slice.212), channel_id=1, source_target_pairs={{0,2},{1,3},{2,0},{3,1},{4,6},{5,7},{6,4},{7,5},{8,10},{9,11},{10,... | collective-permute-start | bytes 3932168 | tf_op jit(solution)/shard_map/ppermute | solution.py:204
  754.2 33.3 %collective-permute-start.14 = (bf16[256,2560]{1,0:T(8,128)(2,1)}, bf16[256,2560]{1,0:T(8,128)(2,1)}, u32[]{:S(2)}, u32[]{:S(2)}) collective-permute-start(bf16[256,2560]{1,0:T(8,128)(2,1)} %add_convert_fusion.4), channel_id=1, source_target_pairs={{0,1},{1,0},{2,3},{3,2},{4,5},{5,4},{6,7},{7,6},{8,9},{9,8},{10,11... | collective-permute-start | bytes 3932168 | tf_op jit(solution)/shard_map/ppermute | solution.py:204
  756.5 55.8 %collective-permute-start.12 = (bf16[256,2560]{1,0:T(8,128)(2,1)}, bf16[256,2560]{1,0:T(8,128)(2,1)}, u32[]{:S(2)}, u32[]{:S(2)}) collective-permute-start(bf16[256,2560]{1,0:T(8,128)(2,1)} %add_convert_fusion.5), channel_id=1, source_target_pairs={{0,2},{1,3},{2,0},{3,1},{4,6},{5,7},{6,4},{7,5},{8,10},{9,11},{10,... | collective-permute-start | bytes 3932168 | tf_op jit(solution)/shard_map/ppermute | solution.py:204
  816.0 70.9 %copy-start.55 = (s32[640]{0:T(1024)S(1)}, s32[640]{0:T(1024)}, u32[]{:S(2)}) copy-start(s32[640]{0:T(1024)} %copy-done.54) | copy-start | bytes 7684
  831.1 55.8 %collective-permute-start.26 = (bf16[512,2560]{1,0:T(8,128)(2,1)}, bf16[512,2560]{1,0:T(8,128)(2,1)}, u32[]{:S(2)}, u32[]{:S(2)}) collective-permute-start(bf16[512,2560]{1,0:T(8,128)(2,1)} %get-tuple-element.106), channel_id=1, source_target_pairs={{0,1},{1,0},{2,3},{3,2},{4,5},{5,4},{6,7},{7,6},{8,9},{9,8},{10,11... | collective-permute-start | bytes 7864328 | tf_op jit(solution)/shard_map/ppermute | solution.py:204
  832.5 69.1 %copy-start.1 = (s32[4]{0:T(128)S(1)}, s32[4]{0:T(128)}, u32[]{:S(2)}) copy-start(s32[4]{0:T(128)} %copy-done) | copy-start | bytes 52
  991.4 77.7 %collective-permute-start.29 = (bf16[640,2560]{0,1:T(8,128)(2,1)}, bf16[640,2560]{0,1:T(8,128)(2,1)}, u32[]{:S(2)}, u32[]{:S(2)}) collective-permute-start(bf16[640,2560]{0,1:T(8,128)(2,1)} %convolution_convert_fusion.6), channel_id=1, source_target_pairs={{0,2},{1,3},{2,0},{3,1},{4,6},{5,7},{6,4},{7,5},{8,10},{9,11},{10,... | collective-permute-start | bytes 9830408 | tf_op jit(solution)/shard_map/ppermute | solution.py:204
  1015.8 351.3 %reduce-scatter.10.cloned.1.call-start = ((), (), s32[]{:S(2)}) async-start(), calls=%async_computation.10 | async-start | bytes 3686400 | tf_op jit(solution)/shard_map/reduce_scatter | solution.py:367
  1073.5 295.6 %reduce-scatter.14.cloned.1.call-start = ((), (), s32[]{:S(2)}) async-start(), calls=%async_computation.12 | async-start | bytes 10321920 | tf_op jit(solution)/shard_map/reduce_scatter | solution.py:342
  1100.5 271.4 %reduce-scatter.8.cloned.1.call-start = ((), (), s32[]{:S(2)}) async-start(), calls=%async_computation.9 | async-start | bytes 5898240 | tf_op jit(solution)/shard_map/reduce_scatter | solution.py:366
  1110.9 113.5 %collective-permute-start.28 = (bf16[2560,960]{0,1:T(8,128)(2,1)S(1)}, bf16[2560,960]{0,1:T(8,128)(2,1)}, u32[]{:S(2)}, u32[]{:S(2)}) collective-permute-start(bf16[2560,960]{0,1:T(8,128)(2,1)S(1)} %convolution_convert_fusion.5), channel_id=1, source_target_pairs={{0,2},{1,3},{2,0},{3,1},{4,6},{5,7},{6,4},{7,5},{8,10},{9,11},{10,... | collective-permute-start | bytes 14745608 | tf_op jit(solution)/shard_map/ppermute | solution.py:204
  1241.5 296.8 %reduce-scatter.12.cloned.1.call-start = ((), (), s32[]{:S(2)}) async-start(), calls=%async_computation.11 | async-start | bytes 19906560 | tf_op jit(solution)/shard_map/reduce_scatter | solution.py:343
  1294.2 58.8 %collective-permute-start.27 = (bf16[512,2560]{1,0:T(8,128)(2,1)}, bf16[512,2560]{1,0:T(8,128)(2,1)}, u32[]{:S(2)}, u32[]{:S(2)}) collective-permute-start(bf16[512,2560]{1,0:T(8,128)(2,1)} %dynamic-slice_convert_fusion), channel_id=1, source_target_pairs={{0,1},{1,0},{2,3},{3,2},{4,5},{5,4},{6,7},{7,6},{8,9},{9,8},{10,11... | collective-permute-start | bytes 7864328 | tf_op jit(solution)/shard_map/ppermute | solution.py:204
  1297.0 61.6 %slice-start = ((s8[5242880]{0:T(1024)(128)(4,1)}), s8[1048576]{0:T(1024)(128)(4,1)S(1)}, s32[]{:S(2)}) async-start(s8[5242880]{0:T(1024)(128)(4,1)} %bitcast.65), calls=%async_computation.14 | async-start | bytes 2097152
  (66 other events, 687.4 us)
Sparse Core Ops, SparseCore 0:
  9.7 42.0 all-gather.6
  54.0 54.8 all-gather.4
  111.1 157.3 all-gather.8
  270.1 86.7 all-gather.10
  1015.9 146.2 reduce-scatter.15
  1164.5 37.3 reduce-scatter.9
  1204.2 95.8 reduce-scatter.13
  1302.4 58.2 reduce-scatter.7
  1363.0 175.2 reduce-scatter.11

commit v2 on v1

--- a/solution.py
+++ b/solution.py
@@ -45,15 +45,8 @@
     return lax.dot_general(a, b, (((0,), (0,)), ((), ())), preferred_element_type=F32)
 
 
-def fwd_kernel(groups, scale, lo_ref, q_ref, k_ref, v_ref, c_ref, s_ref, start_ref,
-               o_ref, qr_ref, kr_ref, vb_ref, lse_ref):
-    length = q_ref.shape[0]
-    c, s = c_ref[...], s_ref[...]
-    kr_ref[...] = turn(k_ref[...], c, s).astype(BF)
-    vb_ref[...] = v_ref[...].astype(BF)
-    for g in range(groups):
-        lanes = slice(g * LANES, (g + 1) * LANES)
-        qr_ref[:, lanes] = turn(q_ref[:, lanes], c, s).astype(BF)
+def fwd_kernel(groups, scale, lo_ref, qr_ref, kr_ref, vb_ref, start_ref, o_ref, lse_ref):
+    length = qr_ref.shape[0]
     for i in range(length // BLK):
         rows = slice(i * BLK, (i + 1) * BLK)
         for j in range(i + 1):
@@ -106,36 +99,30 @@
 
 
 def attend(proj, tables, kv, groups):
-    cos_t, sin_t, start, lo = tables
+    start, lo = tables[2:]
     rows = proj.shape[0]
-    whole = lambda width: pl.BlockSpec((rows, width), lambda h, lo: (0, 0))
     at = lambda width, first: pl.BlockSpec((rows, width), lambda h, lo: (0, first + h))
     wide = groups * LANES
-    out = lambda width: jax.ShapeDtypeStruct((rows, kv * width), BF)
     return pl.pallas_call(
         functools.partial(fwd_kernel, groups, HD ** -0.5),
         grid_spec=pltpu.PrefetchScalarGridSpec(
             num_scalar_prefetch=1,
             grid=(kv,),
             in_specs=[at(wide, 0), at(LANES, kv * groups), at(LANES, kv * groups + kv),
-                      whole(LANES), whole(LANES), whole(1)],
-            out_specs=[at(wide, 0), at(wide, 0), at(LANES, 0), at(LANES, 0),
-                       pl.BlockSpec((None, rows, groups), lambda h, lo: (h, 0, 0))],
+                      pl.BlockSpec((rows, 1), lambda h, lo: (0, 0))],
+            out_specs=[at(wide, 0), pl.BlockSpec((None, rows, groups), lambda h, lo: (h, 0, 0))],
         ),
-        out_shape=[out(wide), out(wide), out(LANES), out(LANES),
-                   jax.ShapeDtypeStruct((kv, rows, groups), F32)],
+        out_shape=[jax.ShapeDtypeStruct((rows, kv * wide), BF), jax.ShapeDtypeStruct((kv, rows, groups), F32)],
         compiler_params=pltpu.CompilerParams(vmem_limit_bytes=48 * 2 ** 20),
-        cost_estimate=pl.CostEstimate(flops=int(4 * kv * groups * rows * rows * LANES * 0.6),
-                                      bytes_accessed=rows * kv * (groups + 1) * LANES * 10, transcendentals=0),
-        name="attend",
-    )(lo, proj, proj, proj, cos_t, sin_t, start)
-
-
-def attend_back(qr, kr, vb, d_o, tables, lse, kv, groups):
+        cost_estimate=cost(4 * kv * groups * rows * rows * LANES), name="attend",
+    )(lo, proj, proj, proj, start)
+
+
+def attend_back(proj, d_o, tables, lse, kv, groups):
     cos_t, sin_t, start, lo = tables
-    rows = qr.shape[0]
+    rows = proj.shape[0]
     whole = lambda width: pl.BlockSpec((rows, width), lambda h, lo: (0, 0))
-    at = lambda width: pl.BlockSpec((rows, width), lambda h, lo: (0, h))
+    at = lambda width, first=0: pl.BlockSpec((rows, width), lambda h, lo: (0, first + h))
     wide = groups * LANES
     out = lambda width: jax.ShapeDtypeStruct((rows, kv * width), BF)
     return pl.pallas_call(
@@ -143,17 +130,205 @@
         grid_spec=pltpu.PrefetchScalarGridSpec(
             num_scalar_prefetch=1,
             grid=(kv,),
-            in_specs=[at(wide), at(LANES), at(LANES), at(wide), whole(LANES), whole(LANES), whole(1),
+            in_specs=[at(wide), at(LANES, kv * groups), at(LANES, kv * groups + kv), at(wide), whole(LANES), whole(LANES), whole(1),
                       pl.BlockSpec((None, rows, groups), lambda h, lo: (h, 0, 0))],
             out_specs=[at(wide), at(LANES), at(LANES)],
             scratch_shapes=[pltpu.VMEM((rows, LANES), F32)] * 2,
         ),
         out_shape=[out(wide), out(LANES), out(LANES)],
         compiler_params=pltpu.CompilerParams(vmem_limit_bytes=48 * 2 ** 20),
-        cost_estimate=pl.CostEstimate(flops=int(10 * kv * groups * rows * rows * LANES * 0.6),
-                                      bytes_accessed=rows * kv * (groups + 1) * LANES * 10, transcendentals=0),
+        cost_estimate=cost(10 * kv * groups * rows * rows * LANES),
         name="attend_back",
-    )(lo, qr, kr, vb, d_o, cos_t, sin_t, start, lse)
+    )(lo, proj, proj, proj, d_o, cos_t, sin_t, start, lse)
+
+
+COLS = 256
+
+
+def cost(flops):
+    return pl.CostEstimate(flops=flops, bytes_accessed=0, transcendentals=0)
+
+
+def params():
+    return pltpu.CompilerParams(vmem_limit_bytes=56 * 2 ** 20)
+
+
+def project_kernel(heads, kv, n1_ref, w_ref, eq_ref, ek_ref, c_ref, s_ref, out_ref):
+    c, s = c_ref[...], s_ref[...]
+    q_width = heads * HD
+    step = pl.program_id(0)
+
+    def go(w, spread, turned, width):
+        padded = nn(w, spread).astype(BF)
+        proj = nn(n1_ref[...], padded)
+        for h in range(width):
+            lanes = slice(h * LANES, (h + 1) * LANES)
+            head = proj[:, lanes]
+            out_ref[:, lanes] = (turn(head, c, s) if h < turned else head).astype(BF)
+
+    per = 2 * kv
+
+    @pl.when(step < heads // per)
+    def _():
+        go(w_ref[:, :q_width], eq_ref[...], per, per)
+
+    @pl.when(step == heads // per)
+    def _():
+        go(w_ref[:, q_width:], ek_ref[...], kv, per)
+
+
+def project(n1, w, tables, heads, kv):
+    cos_t, sin_t = tables[:2]
+    rows, d = n1.shape
+    per = 2 * kv
+    steps = heads // per + 1
+    whole = lambda shape: pl.BlockSpec(shape, lambda i: (0, 0))
+    e_k = spread_matrix(2 * kv)
+    return pl.pallas_call(
+        functools.partial(project_kernel, heads, kv),
+        grid=(steps,),
+        in_specs=[whole((rows, d)), whole(w.shape),
+                  pl.BlockSpec((heads * HD, per * LANES), lambda i: (0, jnp.minimum(i, heads // per - 1))),
+                  whole(e_k.shape), whole(cos_t.shape), whole(sin_t.shape)],
+        out_specs=pl.BlockSpec((rows, per * LANES), lambda i: (0, i)),
+        out_shape=jax.ShapeDtypeStruct((rows, steps * per * LANES), BF),
+        compiler_params=params(), cost_estimate=cost(2 * rows * d * steps * per * LANES), name="project",
+    )(n1, w, spread_matrix(heads), e_k, cos_t, sin_t)
+
+
+def gate_up_kernel(sizes, *refs):
+    n2_refs, (wg_ref, wu_ref), outs = refs[:-3 * len(sizes) - 2], refs[-3 * len(sizes) - 2:-3 * len(sizes)], refs[-3 * len(sizes):]
+    n2_refs = list(n2_refs)
+    for i, pieces in enumerate(sizes):
+        at = 0
+        for rows in pieces:
+            a = n2_refs.pop(0)[...]
+            gate, up = nn(a, wg_ref[...]), nn(a, wu_ref[...])
+            here = slice(at, at + rows)
+            outs[3 * i][here, :] = gate.astype(BF)
+            outs[3 * i + 1][here, :] = up.astype(BF)
+            outs[3 * i + 2][here, :] = (gate / (1.0 + jnp.exp(-gate)) * up).astype(BF)
+            at += rows
+
+
+def gate_up(blocks, w_gate, w_up):
+    sizes = [[p.shape[0] for p in pieces] for pieces in blocks]
+    flat = [p for pieces in blocks for p in pieces]
+    d, ff = w_gate.shape
+    tile = lambda size: pl.BlockSpec((size, COLS), lambda i: (0, i))
+    outs = pl.pallas_call(
+        functools.partial(gate_up_kernel, sizes),
+        grid=(pl.cdiv(ff, COLS),),
+        in_specs=[pl.BlockSpec(p.shape, lambda i: (0, 0)) for p in flat] + [tile(d)] * 2,
+        out_specs=[tile(sum(pieces)) for pieces in sizes for _ in range(3)],
+        out_shape=[jax.ShapeDtypeStruct((sum(pieces), ff), BF) for pieces in sizes for _ in range(3)],
+        compiler_params=params(), cost_estimate=cost(4 * sum(map(sum, sizes)) * d * ff), name="gate_up",
+    )(*flat, w_gate, w_up)
+    return [outs[3 * i:3 * i + 3] for i in range(len(blocks))]
+
+
+def gate_up_back_kernel(ff, dy_ref, g_ref, u_ref, wg_ref, wu_ref, wd_ref, dg_ref, du_ref, *p_refs_acc):
+    *p_refs, acc = p_refs_acc
+    step, last = pl.program_id(0), pl.num_programs(0) - 1
+    d_hidden = nn(dy_ref[...], wd_ref[...])
+    gate, up = g_ref[...].astype(F32), u_ref[...].astype(F32)
+    sig = 1.0 / (1.0 + jnp.exp(-gate))
+    act = gate * sig
+    d_gate = (d_hidden * up * (sig + act * (1.0 - sig))).astype(BF)
+    d_up = (d_hidden * act).astype(BF)
+    dg_ref[...] = d_gate
+    du_ref[...] = d_up
+
+    @pl.when(step == 0)
+    def _():
+        acc[...] = jnp.zeros_like(acc)
+
+    @pl.when(step < last)
+    def _():
+        acc[...] += nt(d_gate, wg_ref[...]) + nt(d_up, wu_ref[...])
+
+    @pl.when(step == last)
+    def _():
+        def inside(v):
+            col = last * COLS + lax.broadcasted_iota(jnp.int32, v.shape, 1)
+            return jnp.where(col < ff, v, jnp.zeros_like(v))
+
+        total = acc[...] + nt(inside(d_gate), inside(wg_ref[...])) + nt(inside(d_up), inside(wu_ref[...]))
+        size = total.shape[0] // len(p_refs)
+        for i, p_ref in enumerate(p_refs):
+            p_ref[...] = total[i * size:(i + 1) * size].astype(p_ref.dtype)
+
+
+def gate_up_back(dy, gate, up, w_gate, w_up, w_down_t, out, parts):
+    (rows, d), ff = dy.shape, w_gate.shape[1]
+    tile = lambda size: pl.BlockSpec((size, COLS), lambda i: (0, i))
+    whole = pl.BlockSpec((rows, d), lambda i: (0, 0))
+    return pl.pallas_call(
+        functools.partial(gate_up_back_kernel, ff),
+        grid=(pl.cdiv(ff, COLS),),
+        in_specs=[whole, tile(rows), tile(rows), tile(d), tile(d), tile(d)],
+        out_specs=[tile(rows)] * 2 + [pl.BlockSpec((rows // parts, d), lambda i: (0, 0))] * parts,
+        out_shape=[jax.ShapeDtypeStruct((rows, ff), BF)] * 2 + [jax.ShapeDtypeStruct((rows // parts, d), out)] * parts,
+        scratch_shapes=[pltpu.VMEM((rows, d), F32)],
+        compiler_params=params(), cost_estimate=cost(6 * rows * d * ff), name="gate_up_back",
+    )(dy, gate, up, w_gate, w_up, w_down_t)
+
+
+def down_kernel(h_ref, w_ref, *out_refs):
+    out = nt(h_ref[...], w_ref[...])
+    size = out.shape[0] // len(out_refs)
+    for i, out_ref in enumerate(out_refs):
+        out_ref[...] = out[i * size:(i + 1) * size].astype(out_ref.dtype)
+
+
+def down(hidden, w_down_t, parts):
+    (rows, ff), d = hidden.shape, w_down_t.shape[0]
+    size = 512
+    return pl.pallas_call(
+        down_kernel,
+        grid=(pl.cdiv(d, size),),
+        in_specs=[pl.BlockSpec((rows, ff), lambda i: (0, 0)), pl.BlockSpec((size, ff), lambda i: (i, 0))],
+        out_specs=[pl.BlockSpec((rows // parts, size), lambda i: (0, i))] * parts,
+        out_shape=[jax.ShapeDtypeStruct((rows // parts, d), BF)] * parts,
+        compiler_params=params(), cost_estimate=cost(2 * rows * d * ff), name="down",
+    )(hidden, w_down_t)
+
+
+def wgrad_kernel(n, lists, *refs):
+    a_refs, b_refs = refs[:n], list(refs[n:n + sum(map(len, lists))])
+    outs, a_t = refs[n + len(b_refs):-1], refs[-1]
+
+    @pl.when(pl.program_id(0) == 0)
+    def _():
+        at = 0
+        for a_ref in a_refs:
+            a_t[:, at:at + a_ref.shape[0]] = a_ref[...].T
+            at += a_ref.shape[0]
+
+    for j, sizes in enumerate(lists):
+        total, at = None, 0
+        for rows in sizes:
+            part = nn(a_t[:, at:at + rows], b_refs.pop(0)[...])
+            total = part if total is None else total + part
+            at += rows
+        outs[j][...] = total.astype(BF)
+
+
+def wgrad(a_blocks, *b_lists):
+    d, ff = a_blocks[0].shape[1], b_lists[0][0].shape[1]
+    total = sum(a.shape[0] for a in a_blocks)
+    lists = [[b.shape[0] for b in bs] for bs in b_lists]
+    tile = lambda size: pl.BlockSpec((size, COLS), lambda i: (0, i))
+    return pl.pallas_call(
+        functools.partial(wgrad_kernel, len(a_blocks), lists),
+        grid=(pl.cdiv(ff, COLS),),
+        in_specs=[pl.BlockSpec(a.shape, lambda i: (0, 0), pipeline_mode=pl.Buffered(1)) for a in a_blocks]
+        + [tile(b.shape[0]) for bs in b_lists for b in bs],
+        out_specs=[tile(d)] * len(b_lists),
+        out_shape=[jax.ShapeDtypeStruct((d, ff), BF)] * len(b_lists),
+        scratch_shapes=[pltpu.VMEM((d, total), BF)],
+        compiler_params=params(), cost_estimate=cost(2 * total * d * ff * len(b_lists)), name="wgrad",
+    )(*a_blocks, *[b for bs in b_lists for b in bs])
 
 
 def doc_starts(seg_row):
@@ -208,39 +383,63 @@
     return [[first + i for i in range(size)] for first in range(0, lax.axis_size("tensor"), size)]
 
 
+def after(v, *done):
+    return lax.optimization_barrier((v, *done))[0]
+
+
+def square(size):
+    return size == 4 == lax.axis_size("tensor")
+
+
 def gather(mine, size):
     if size == 2:
-        return [mine, swap(mine, 1)]
-    if size == 4 and lax.axis_size("tensor") == 4:
+        return [[mine], [swap(mine, 1)]]
+    if square(size):
         half = mine.shape[0] // 2
         from_x, from_y = swap(mine, 1), swap(mine, 2)
-        return [mine, from_x, from_y, jnp.concatenate([swap(from_x[:half], 2), swap(from_y[half:], 1)])]
+        return [[mine], [from_x], [from_y], [swap(from_x[:half], 2), swap(from_y[half:], 1)]]
     blocks = lax.all_gather(mine, "tensor", axis=0, tiled=False, axis_index_groups=groups_of(size))
     at = lax.axis_index("tensor") % size
-    return [lax.dynamic_index_in_dim(blocks, at ^ r, 0, keepdims=False) for r in range(size)]
+    return [[lax.dynamic_index_in_dim(blocks, at ^ r, 0, keepdims=False)] for r in range(size)]
 
 
 def scatter(parts, size):
     if size == 2:
-        return swap(parts[1], 1).astype(F32)
-    if size == 4 and lax.axis_size("tensor") == 4:
-        _, p_x, p_y, p_diag = parts
-        half = p_x.shape[0] // 2
+        got = swap(jnp.concatenate(parts[1]), 1)
+        return got.astype(F32), parts[1]
+    if square(size):
+        _, (x_low, x_high), (y_low, y_high), (d_low, d_high) = parts
         add = lambda a, b: (a.astype(F32) + b.astype(F32)).astype(BF)
-        for_y = swap(p_diag[:half], 1)
-        for_x = swap(p_diag[half:], 2)
-        a1, b1 = swap(p_x[:half], 1), swap(p_y[half:], 2)
-        a2, b2 = swap(add(p_x[half:], for_x), 1), swap(add(p_y[:half], for_y), 2)
+        for_y, for_x = swap(d_low, 1), swap(d_high, 2)
+        a1, b1 = swap(x_low, 1), swap(y_high, 2)
+        x_high, y_low = add(x_high, for_x), add(y_low, for_y)
+        a2, b2 = swap(x_high, 1), swap(y_low, 2)
         low = a1.astype(F32) + b2.astype(F32)
         high = a2.astype(F32) + b1.astype(F32)
-        return jnp.concatenate([low, high])
+        return jnp.concatenate([low, high]), [x_high, y_low]
     at = lax.axis_index("tensor") % size
-    blocks = jnp.stack([jnp.zeros_like(parts[1])] + list(parts[1:]))[jnp.arange(size) ^ at]
+    whole = [jnp.concatenate(p) for p in parts[1:]]
+    blocks = jnp.stack([jnp.zeros_like(whole[0])] + whole)[jnp.arange(size) ^ at]
     summed = lax.psum_scatter(blocks, "tensor", scatter_dimension=0, tiled=False, axis_index_groups=groups_of(size))
-    return summed.astype(F32)
+    return summed.astype(F32), whole
+
+
+def scatter_rows(v):
+    for axis in ("dp", "tensor"):
+        size, at = lax.axis_size(axis), lax.axis_index(axis)
+        assert size & (size - 1) == 0
+        while size > 1:
+            size //= 2
+            bit = (at // size) % 2
+            low, high = jnp.split(v, 2)
+            theirs = lax.ppermute(jnp.where(bit == 0, high, low), axis,
+                                  [(i, i ^ size) for i in range(lax.axis_size(axis))])
+            v = jnp.where(bit == 0, low, high) + theirs
+    return v
 
 
 def in_order(blocks):
+    blocks = [pieces[0] for pieces in blocks]
     at = lax.axis_index("tensor") % len(blocks)
     if len(blocks) == 2:
         return by_place(at, *blocks)
@@ -263,16 +462,24 @@
     core = lax.axis_index("dp") % 2
 
     token_blocks = gather(tokens, group)
-    dy_blocks = gather(out_grad, places)
+    if square(places):
+        dy_y = swap(out_grad, 2)
     qkv_shard = jnp.concatenate(
         [w_query, w_key, w_value, attn_gain[:, None], mlp_gain[:, None]], axis=1)
     qkv_all = lax.all_gather(qkv_shard, "dp", axis=0, tiled=True)
+    if square(places):
+        qkv_all, token_blocks, dy_y, later = lax.optimization_barrier((qkv_all, token_blocks, dy_y, out_grad))
+        dy_x = swap(later, 1)
+        dy_blocks = [out_grad, dy_x, dy_y, swap(dy_x, 2)]
+    else:
+        dy_blocks = [pieces[0] for pieces in gather(out_grad, places)]
     qkv_w = qkv_all[:, :q_width + 2 * k_width]
     gain_one = qkv_all[:, q_width + 2 * k_width].astype(F32)
     gain_two = qkv_all[:, q_width + 2 * k_width + 1].astype(F32)
-    out_w = lax.all_gather(w_out, "dp", axis=1, tiled=True)
-    gu_w = lax.all_gather(jnp.concatenate([w_gate, w_up], axis=1), "dp", axis=0, tiled=True)
-    down_w = lax.all_gather(w_down, "dp", axis=1, tiled=True)
+    out_w = lax.all_gather(after(w_out, qkv_all), "dp", axis=1, tiled=True)
+    gate_w = lax.all_gather(after(w_gate, qkv_all), "dp", axis=0, tiled=True)
+    up_w = lax.all_gather(after(w_up, qkv_all), "dp", axis=0, tiled=True)
+    down_wt = lax.all_gather(after(w_down.T, out_w), "dp", axis=0, tiled=True)
 
     def swap_shared(v, bit):
         half = v.shape[0] // 2
@@ -284,17 +491,19 @@
     qkv_ws = [qkv_w] + [swap_shared(qkv_w, bits) for bits in others]
     out_ws = [out_w] + [swap_shared(out_w, bits) for bits in others]
 
+    def share(part, bits):
+        half = part.shape[0] // 2
+        theirs = lax.dynamic_slice_in_dim(part, (1 - core) * half, half, 0)
+        theirs = lax.ppermute(theirs, "dp", [(i, i ^ 1) for i in range(lax.axis_size("dp"))])
+        mine = lax.dynamic_slice_in_dim(part, core * half, half, 0)
+        return swap((mine.astype(F32) + theirs.astype(F32)).astype(BF), bits)
+
     seg_row = lax.dynamic_index_in_dim(segments, place // group, 0, keepdims=False)
     start = doc_starts(seg_row)
     cos_t, sin_t = head_tables(jnp.arange(length, dtype=jnp.int32) - start)
     tables = (cos_t, sin_t, start[:, None], start[::BLK] // BLK)
 
     spread_q, spread_k = spread_matrix(heads), spread_matrix(kv)
-
-    def pad_heads(w):
-        return jnp.concatenate([
-            dot(w[:, :q_width], spread_q), dot(w[:, q_width:q_width + k_width], spread_k),
-            dot(w[:, q_width + k_width:], spread_k)], axis=1)
 
     x_own = tokens.astype(F32)
     inv_own = inverse_rms(x_own)
@@ -303,21 +512,24 @@
     n1 = (x_pair * inv_pair * gain_one).astype(BF)
     kept = []
     for w in qkv_ws:
-        proj = dot(n1, pad_heads(w), F32)
-        o, qr, kr, vb, lse = attend(proj, tables, kv, groups)
-        kept.append((dot_nt(o, spread_q), qr, kr, vb, lse))
+        if kept:
+            w = after(w, kept[0][0])
+        proj = project(n1, w, tables, heads, kv)
+        o, lse = attend(proj, tables, kv, groups)
+        kept.append((dot_nt(o, spread_q), proj, lse))
     o_flat = jnp.concatenate([k[0] for k in kept], axis=1)
     out_both = jnp.concatenate(out_ws, axis=0)
 
     def rows_of(v, bits):
         return lax.dynamic_slice_in_dim(v, ((place % group) ^ bits) * row_count, row_count, 0)
 
-    branch = scatter([None] + [dot(rows_of(o_flat, bits), out_both) for bits in range(1, group)], group)
+    branch, _ = scatter([None] + [[dot(rows_of(o_flat, bits), out_both)] for bits in range(1, group)], group)
+    branch, dy_blocks = lax.optimization_barrier((branch, dy_blocks))
     h = x_own + dot(rows_of(o_flat, 0), out_both, F32) + branch
 
     inv_h = inverse_rms(h)
     n2 = (h * inv_h * gain_two).astype(BF)
-    n2s = gather(n2, places)
+    n2s = gather(after(n2, gate_w, up_w), places)
     segs = segments.reshape(-1)
 
     def masked(v, bits):
@@ -325,67 +537,74 @@
         return v * (own >= 0).astype(BF)[:, None]
 
     dys = [masked(block, bits) for bits, block in enumerate(dy_blocks)]
-    hiddens, gu_grads = [], []
-    for n2_c, dy_c in zip(n2s, dys):
-        gate_up = dot(n2_c, gu_w, F32)
-        d_hidden = dot_nt(dy_c, down_w, F32)
-        gate, up = gate_up[:, :ff], gate_up[:, ff:]
-        sig = jax.nn.sigmoid(gate)
-        act = gate * sig
-        hiddens.append((act * up).astype(BF))
-        gu_grads.append(jnp.concatenate(
-            [(d_hidden * up * sig * (1.0 + gate * (1.0 - sig))).astype(BF), (d_hidden * act).astype(BF)], axis=1))
-    d_n2 = scatter([None] + [dot_nt(g, gu_w) for g in gu_grads[1:]], places) + dot_nt(gu_grads[0], gu_w, F32)
-
-    hidden_all, gu_grad_all = jnp.concatenate(hiddens), jnp.concatenate(gu_grads)
-    n2_all, dy_all = jnp.concatenate(n2s), jnp.concatenate(dys)
-    down_grad = lax.psum_scatter(dot_t(hidden_all, dy_all), "dp", scatter_dimension=1, tiled=True)
-    gu_grad = lax.psum_scatter(dot_t(n2_all, gu_grad_all), "dp", scatter_dimension=0, tiled=True)
-    mlp = scatter([None] + [dot(v, down_w) for v in hiddens[1:]], places) + dot(hiddens[0], down_w, F32)
-    output = (h + mlp).astype(BF)
+    ups = gate_up(n2s[:1], gate_w, up_w)
+    ups += gate_up(after(n2s[1:places - 1], ups[0]), gate_w, up_w)
+    ups += gate_up(after(n2s[places - 1:], ups[1], down_wt), gate_w, up_w)
+    n2_pieces = [p for pieces in n2s for p in pieces]
+    hiddens = [u[2] for u in ups]
+    down_part, = wgrad(dys, hiddens)
+    down_grad = lax.psum_scatter(down_part, "dp", scatter_dimension=0, tiled=True)
+    backs, last = [None] * places, down_part
+    for r in reversed(range(places)):
+        backs[r] = gate_up_back(after(dys[r], last), ups[r][0], ups[r][1], gate_w, up_w, down_wt,
+                                *((BF, 2) if r else (F32, 1)))
+        last = backs[r][2]
+    d_n2, sent = scatter([v[2:] for v in backs], places)
+    d_n2 += backs[0][2]
+    gate_part, up_part = wgrad(after(n2_pieces, last, sent), [v[0] for v in backs], [v[1] for v in backs])
+    gate_grad = lax.psum_scatter(gate_part, "dp", scatter_dimension=0, tiled=True)
+    up_grad = lax.psum_scatter(up_part, "dp", scatter_dimension=0, tiled=True)
 
     gain_two_grad = jnp.sum(d_n2 * h * inv_h, axis=0)
     dh = dys[0].astype(F32) + norm_back(h, inv_h, gain_two, d_n2)
 
     dhb = dh.astype(BF)
-    dhb_pair = in_order(gather(dhb, group))
-    back, wgrads = [], []
-    for (o, qr, kr, vb, lse), w, w_o in zip(kept[::-1], qkv_ws[::-1], out_ws[::-1]):
+    hiddens = after(hiddens, dhb)
+    mlp_parts = [down(v, down_wt, 2 if r else 1) for r, v in enumerate(hiddens)]
+    dhb_pair = in_order(after(gather(dhb, group), mlp_parts, down_grad))
+    output = (h + scatter(after(mlp_parts, dhb_pair), places)[0] + mlp_parts[0][0].astype(F32)).astype(BF)
+    back, shares = [], []
+    for index in reversed(range(len(kept))):
+        (o, proj, lse), w, w_o = kept[index], qkv_ws[index], out_ws[index]
+        out_part = dot_t(dhb_pair, o)
         d_o = dot(dot_nt(dhb_pair, w_o), spread_q)
-        dq, dk, dv = attend_back(qr, kr, vb, d_o, tables, lse, kv, groups)
+        dq, dk, dv = attend_back(proj, d_o, tables, lse, kv, groups)
         d_proj = jnp.concatenate([dot_nt(dq, spread_q), dot_nt(dk, spread_k), dot_nt(dv, spread_k)], axis=1)
+        qkv_part = dot_t(n1, d_proj)
+        if index:
+            shares.append((share(qkv_part, others[index - 1]), share(out_part, others[index - 1])))
+            dhb_pair = after(dhb_pair, qkv_part, out_part)
         back.append((d_proj, w))
-        wgrads.append((dot_t(n1, d_proj), dot_t(o, dhb_pair)))
-
-    def add_shares(shares):
-        total = shares[-1].astype(F32)
-        for bits, share in zip(others[::-1], shares):
-            total += swap(share, bits).astype(F32)
-        return total.astype(BF)
-
-    qkv_grad = lax.psum_scatter(add_shares([g[0] for g in wgrads]), "dp", scatter_dimension=0, tiled=True).astype(F32)
-    out_grad_w = lax.psum_scatter(add_shares([g[1] for g in wgrads]), "dp", scatter_dimension=1, tiled=True).astype(F32)
-
+
+    def with_shares(mine, got):
+        half = mine.shape[0] // 2
+        rows = lax.dynamic_slice_in_dim(mine, core * half, half, 0).astype(F32) + sum(v.astype(F32) for v in got)
+        return lax.dynamic_update_slice_in_dim(mine, rows.astype(BF), core * half, 0)
+
+    back, output, gate_grad, up_grad = lax.optimization_barrier((back, output, gate_grad, up_grad))
+    out_grad_w = lax.psum_scatter(with_shares(out_part, [v[1] for v in shares]), "dp", scatter_dimension=0, tiled=True)
+    qkv_grad = lax.psum_scatter(with_shares(qkv_part, [v[0] for v in shares]), "dp", scatter_dimension=0, tiled=True)
+    out_grad_w, qkv_grad = out_grad_w.T.astype(F32), qkv_grad.astype(F32)
     d_n1_pair = sum(dot_nt(d, w, F32) for d, w in back)
     gain_one_grad = jnp.sum(d_n1_pair * x_pair * inv_pair, axis=0)
     d_n1 = rows_of(d_n1_pair, 0) + scatter(
-        [None] + [rows_of(d_n1_pair, bits).astype(BF) for bits in range(1, group)], group)
+        [None] + [[rows_of(d_n1_pair, bits).astype(BF)] for bits in range(1, group)], group)[0]
     input_grad = dh + norm_back(x_own, inv_own, gain_one, d_n1)
 
-    gains = lax.psum_scatter(jnp.stack([gain_one_grad, gain_two_grad], axis=1), ("dp", "tensor"),
-                             scatter_dimension=0, tiled=True)
+    gains = scatter_rows(jnp.concatenate(
+        [v.reshape(lax.axis_size("dp") * places, -1) for v in (gain_one_grad, gain_two_grad)], axis=1))[0]
     return (
         output,
         input_grad,
-        gains[:, 0],
+        gains[:gains.shape[0] // 2],
         qkv_grad[:, :q_width],
         qkv_grad[:, q_width:q_width + k_width],
         qkv_grad[:, q_width + k_width:],
         out_grad_w,
-        gains[:, 1],
-        gu_grad[:, :ff].astype(F32),
-        gu_grad[:, ff:].astype(F32),
-        down_grad.astype(F32),
+        gains[gains.shape[0] // 2:],
+        gate_grad.astype(F32),
+        up_grad.astype(F32),
+        down_grad.T.astype(F32),
     )
 
 

time: 1560 us -> 1140 us (0.73)
  waiting for transfers between devices: 783 us -> 390 us
  matrix products: 446 us -> 112 us
  Pallas kernels: 85.4 us -> 390 us
  local copies, waits for them, and re-layouts: 85.1 us -> 61.1 us
  other arithmetic: 109 us -> 126 us
  starting transfers between devices: 25.6 us -> 41.4 us
    pallas_call x0 -> x15, Pallas kernels: none -> 311 us  [the longest x4 95.6 us: gate_up_back(): pl.pallas_call(functools.partial(gate_up_back_kernel, ff), grid=(pl.cdiv(...]
    ppermute x28 -> x27, waiting for transfers between devices: 543 us -> 339 us  [swap(): lax.ppermute(v, 'tensor', [(i, i ^ bit) for i in range(lax.axis_size('ten...]
    reduce_scatter x4, waiting for transfers between devices: 162 us -> 0.01 us  [the longest x1 0.01 us: body(): lax.psum_scatter(down_part, 'dp', scatter_dimension=0, tiled=True)]
    dot_general x20 -> x4, matrix products: 194 us -> 40.9 us  [dot(): return jnp.dot(a, b, preferred_element_type=F32).astype(out)]
    dot_general x18 -> x10, matrix products: 143 us -> 41.3 us  [dot_nt(): lax.dot_general(a, b, (((1,), (1,)), ((), ())), preferred_element_type=F32)]
    dot_general x6 -> x4, matrix products: 109 us -> 30 us  [dot_t(): lax.dot_general(a, b, (((0,), (0,)), ((), ())), preferred_element_type=F32)]
    ppermute x0 -> x7, waiting for transfers between devices: none -> 50 us  [the longest x5 50 us: scatter_rows(): lax.ppermute(jnp.where(bit == 0, high, low), axis, [(i, i ^ size) for i i...]
    all_gather x1, waiting for transfers between devices: 49.6 us -> 0.01 us  [body(): qkv_all = lax.all_gather(qkv_shard, 'dp', axis=0, tiled=True)]
  transfers between devices with their start and end apart: 39 -> 46, of which waited for: 19 -> 20; matrix products, arithmetic and copies ran while one was open for 34% -> 25% of each run, Pallas kernels for 2% -> 30%
where the time goes in v2:
time: 1140 us
  waiting for transfers between devices  390 us (34%)
  Pallas kernels  390 us (34%)
  other arithmetic  126 us (11%)
  matrix products  112 us (10%)
  local copies, waits for them, and re-layouts  61.1 us (5%)
  starting transfers between devices  41.4 us (4%)
  between operations  15.7 us (1%)
    ppermute x27, waiting for transfers between devices, swap(): lax.ppermute(v, 'tensor', [(i, i ^ bit) for i in range(lax.axis_size('ten...  339 us
    pallas_call x4, Pallas kernels, gate_up_back(): pl.pallas_call(functools.partial(gate_up_back_kernel, ff), grid=(pl.cdiv(...  95.6 us
    pallas_call x2, Pallas kernels, wgrad(): pl.pallas_call(functools.partial(wgrad_kernel, len(a_blocks), lists), gri...  78.8 us
    pallas_call x3, Pallas kernels, gate_up(): pl.pallas_call(functools.partial(gate_up_kernel, sizes), grid=(pl.cdiv(ff...  56.4 us
    pallas_call x2, Pallas kernels, attend_back(): pl.pallas_call(functools.partial(bwd_kernel, groups, HD ** (-0.5)), grid_...  50.5 us
    ppermute x5, waiting for transfers between devices, scatter_rows(): lax.ppermute(jnp.where(bit == 0, high, low), axis, [(i, i ^ size) for i i...  50 us
    pallas_call x2, Pallas kernels, project(): pl.pallas_call(functools.partial(project_kernel, heads, kv), grid=(steps,...  41.5 us
    dot_general x10, matrix products, dot_nt(): lax.dot_general(a, b, (((1,), (1,)), ((), ())), preferred_element_type=F32)  41.3 us
  transfers between devices with their start and end apart: 46, of which 20 were waited for; matrix products, arithmetic and copies ran while one was open for 25% of the time, Pallas kernels for 30%

profile of v2, /device:TPU:0, one launch (start us, length us, event | category | flops | bytes accessed | tf_op | source)
XLA Modules:
  0.0 1136.2 jit_solution(9483015406863965401)
XLA Ops:
  17.6 55.7 %collective-permute-done.1 = bf16[512,2560]{1,0:T(8,128)(2,1)} collective-permute-done((bf16[512,2560]{1,0:T(8,128)(2,1)}, bf16[512,2560]{1,0:T(8,128)(2,1)}, u32[]{:S(2)}, u32[]{:S(2)}) %collective-permute-start.1) | collective-permute-done | bytes 2621472 | tf_op jit(solution)/shard_map/ppermute | solution.py:379
  97.6 39.4 %collective-permute-done.2 = bf16[1280,960]{0,1:T(8,128)(2,1)} collective-permute-done((bf16[1280,960]{0,1:T(8,128)(2,1)}, bf16[1280,960]{0,1:T(8,128)(2,1)}, u32[]{:S(2)}, u32[]{:S(2)}) %collective-permute-start.2) | collective-permute-done | bytes 2457632 | tf_op jit(solution)/shard_map/ppermute | solution.py:379
  144.5 8.2 fusion.2.n1_ref
  152.8 20.8 %project.2.qr_ref.kr_ref.vb_ref = bf16[1024,1536]{1,0:T(8,128)(2,1)} custom-call(bf16[1024,2560]{1,0:T(8,128)(2,1)} %fusion.2.n1_ref, bf16[2560,960]{1,0:T(8,128)(2,1)} %bitcast.60, bf16[640,1024]{1,0:T(8,128)(2,1)} %fusion.19.eq_ref, bf16[320,512]{1,0:T(8,128)(2,1)} %fusion.38.ek_ref, f32[1024,128]{1,0:T(8,128)} %get-tuple-element.268.c_ref, ...), custom_call_target="tpu_custom_call" | custom-call | flops 8053063680 | tf_op jit(solution)/shard_map/project/pallas_call | solution.py:187
  173.5 14.0 %attend.2 = (bf16[1024,1024]{1,0:T(8,128)(2,1)S(1)}, f32[2,1024,4]{2,1,0:T(8,128)S(1)}) custom-call(s32[4]{0:T(128)S(1)} %and_select_fusion.2.lo_ref, bf16[1024,1536]{1,0:T(8,128)(2,1)} %project.2.qr_ref.kr_ref.vb_ref, bf16[1024,1536]{1,0:T(8,128)(2,1)} %project.2.qr_ref.kr_ref.vb_ref, bf16[1024,1536]{1,0:T(8,128)(2,1)} %project.2.qr_ref.kr_ref.vb_ref, ...), custom_call_target="tpu_custom_call" | custom-call | flops 4294967296 | tf_op jit(solution)/shard_map/attend/pallas_call | solution.py:106
  199.1 7.5 maximum_select_fusion.1.w_ref
  206.6 20.7 %project.3.qr_ref.kr_ref.vb_ref = bf16[1024,1536]{1,0:T(8,128)(2,1)} custom-call(bf16[1024,2560]{1,0:T(8,128)(2,1)} %fusion.2.n1_ref, bf16[2560,960]{1,0:T(8,128)(2,1)} %maximum_select_fusion.1.w_ref, bf16[640,1024]{1,0:T(8,128)(2,1)} %fusion.19.eq_ref, bf16[320,512]{1,0:T(8,128)(2,1)} %fusion.38.ek_ref, f32[1024,128]{1,0:T(8,128)} %get-tuple-element.268.c_ref, ...), custom_call_target="tpu_custom_call" | custom-call | flops 8053063680 | tf_op jit(solution)/shard_map/project/pallas_call | solution.py:187
  227.3 14.2 %attend.3 = (bf16[1024,1024]{1,0:T(8,128)(2,1)S(1)}, f32[2,1024,4]{2,1,0:T(8,128)S(1)}) custom-call(s32[4]{0:T(128)S(1)} %and_select_fusion.2.lo_ref, bf16[1024,1536]{1,0:T(8,128)(2,1)} %project.3.qr_ref.kr_ref.vb_ref, bf16[1024,1536]{1,0:T(8,128)(2,1)} %project.3.qr_ref.kr_ref.vb_ref, bf16[1024,1536]{1,0:T(8,128)(2,1)} %project.3.qr_ref.kr_ref.vb_ref, ...), custom_call_target="tpu_custom_call" | custom-call | flops 4294967296 | tf_op jit(solution)/shard_map/attend/pallas_call | solution.py:106
  252.0 5.7 maximum_select_fusion.3
  265.5 9.3 fusion.12
  274.8 47.6 %collective-permute-done.6 = bf16[512,2560]{1,0:T(8,128)(2,1)} collective-permute-done((bf16[512,2560]{1,0:T(8,128)(2,1)}, bf16[512,2560]{1,0:T(8,128)(2,1)}, u32[]{:S(2)}, u32[]{:S(2)}) %collective-permute-start.6) | collective-permute-done | bytes 2621472 | tf_op jit(solution)/shard_map/ppermute | solution.py:379
  328.6 5.3 broadcast_multiply_fusion.refs_3_.dy_ref
  342.0 5.3 broadcast_multiply_fusion.1
  347.3 15.9 %gate_up.3 = (bf16[512,1728]{1,0:T(8,128)(2,1)}, bf16[512,1728]{1,0:T(8,128)(2,1)}, bf16[512,1728]{1,0:T(8,128)(2,1)}) custom-call(bf16[512,2560]{1,0:T(8,128)(2,1)} %multiply_convert_fusion.refs_0_, bf16[2560,1728]{1,0:T(8,128)(2,1)} %all-gather.10.cloned.1.call-done.refs_1_.refs_2_.wg_ref, ...), custom_call_target="tpu_custom_call" | custom-call | flops 9059696640 | tf_op jit(solution)/shard_map/gate_up/pallas_call | solution.py:219
  363.2 31.3 %collective-permute-done.10.refs_1_.refs_2_ = bf16[512,2560]{1,0:T(8,128)(2,1)S(1)} collective-permute-done((bf16[512,2560]{1,0:T(8,128)(2,1)}, bf16[512,2560]{1,0:T(8,128)(2,1)S(1)}, u32[]{:S(2)}, u32[]{:S(2)}) %collective-permute-start.10) | collective-permute-done | bytes 2621472 | tf_op jit(solution)/shard_map/ppermute | solution.py:379
  398.8 24.8 %gate_up.4 = (bf16[512,1728]{1,0:T(8,128)(2,1)}, bf16[512,1728]{1,0:T(8,128)(2,1)}, bf16[512,1728]{1,0:T(8,128)(2,1)}, bf16[512,1728]{1,0:T(8,128)(2,1)}, bf16[5...) custom-call(bf16[512,2560]{1,0:T(8,128)(2,1)} %collective-permute-done.9.refs_0_.refs_1_, bf16[512,2560]{1,0:T(8,128)(2,1)} %copy-done.38, ...), custom_call_target="tpu_custom_call" | custom-call | flops 18119393280 | tf_op jit(solution)/shard_map/gate_up/pallas_call | solution.py:219
  427.2 15.7 %gate_up.5 = (bf16[512,1728]{1,0:T(8,128)(2,1)}, bf16[512,1728]{1,0:T(8,128)(2,1)}, bf16[512,1728]{1,0:T(8,128)(2,1)}) custom-call(bf16[256,2560]{1,0:T(8,128)(2,1)} %collective-permute-done.11.refs_0_.refs_3_, bf16[256,2560]{1,0:T(8,128)(2,1)} %copy-done.62, bf16[2560,1728]{1,0:T(8,128)(2,1)} %all-gather.10.cloned.1.call-done.refs_1_.refs_2_.wg_ref, ...), custom_call_target="tpu_custom_call" | custom-call | flops 9059696640 | tf_op jit(solution)/shard_map/gate_up/pallas_call | solution.py:219
  442.9 29.6 %wgrad.2 = bf16[2560,1728]{1,0:T(8,128)(2,1)} custom-call(bf16[512,2560]{1,0:T(8,128)(2,1)} %broadcast_multiply_fusion.3.refs_0_.dy_ref, bf16[512,2560]{1,0:T(8,128)(2,1)} %get-tuple-element.143.refs_1_.dy_ref, bf16[512,2560]{1,0:T(8,128)(2,1)} %get-tuple-element.139.refs_2_.dy_ref, bf16[512,2560]{1,0:T(8,128)(2,1)} %broadcast_multiply_fusion.refs_3_.dy_ref, ...), custom_call_target="tpu_custom_call" | custom-call | flops 18119393280 | tf_op jit(solution)/shard_map/wgrad/pallas_call | solution.py:322
  472.6 23.6 %gate_up_back.4 = (bf16[512,1728]{1,0:T(8,128)(2,1)}, bf16[512,1728]{1,0:T(8,128)(2,1)}, bf16[256,2560]{1,0:T(8,128)(2,1)}, bf16[256,2560]{1,0:T(8,128)(2,1)}) custom-call(bf16[512,2560]{1,0:T(8,128)(2,1)} %broadcast_multiply_fusion.refs_3_.dy_ref, bf16[512,1728]{1,0:T(8,128)(2,1)} %get-tuple-element.136.g_ref, bf16[512,1728]{1,0:T(8,128)(2,1)} %get-tuple-element.137.u_ref, ...), custom_call_target="tpu_custom_call" | custom-call | flops 13589544960 | tf_op jit(solution)/shard_map/gate_up_back/pallas_call | solution.py:266
  497.7 23.7 %gate_up_back.5 = (bf16[512,1728]{1,0:T(8,128)(2,1)}, bf16[512,1728]{1,0:T(8,128)(2,1)}, bf16[256,2560]{1,0:T(8,128)(2,1)}, bf16[256,2560]{1,0:T(8,128)(2,1)}) custom-call(bf16[512,2560]{1,0:T(8,128)(2,1)} %get-tuple-element.139.refs_2_.dy_ref, bf16[512,1728]{1,0:T(8,128)(2,1)} %get-tuple-element.140.g_ref, bf16[512,1728]{1,0:T(8,128)(2,1)} %get-tuple-element.141.u_ref, ...), custom_call_target="tpu_custom_call" | custom-call | flops 13589544960 | tf_op jit(solution)/shard_map/gate_up_back/pallas_call | solution.py:266
  521.4 23.6 %gate_up_back.6 = (bf16[512,1728]{1,0:T(8,128)(2,1)}, bf16[512,1728]{1,0:T(8,128)(2,1)}, bf16[256,2560]{1,0:T(8,128)(2,1)}, bf16[256,2560]{1,0:T(8,128)(2,1)}) custom-call(bf16[512,2560]{1,0:T(8,128)(2,1)} %get-tuple-element.143.refs_1_.dy_ref, bf16[512,1728]{1,0:T(8,128)(2,1)} %get-tuple-element.129.g_ref, bf16[512,1728]{1,0:T(8,128)(2,1)} %get-tuple-element.130.u_ref, ...), custom_call_target="tpu_custom_call" | custom-call | flops 13589544960 | tf_op jit(solution)/shard_map/gate_up_back/pallas_call | solution.py:266
  546.4 24.7 %gate_up_back.7 = (bf16[512,1728]{1,0:T(8,128)(2,1)}, bf16[512,1728]{1,0:T(8,128)(2,1)}, f32[512,2560]{1,0:T(8,128)}) custom-call(bf16[512,2560]{1,0:T(8,128)(2,1)} %broadcast_multiply_fusion.3.refs_0_.dy_ref, bf16[512,1728]{1,0:T(8,128)(2,1)} %get-tuple-element.123.g_ref, bf16[512,1728]{1,0:T(8,128)(2,1)} %get-tuple-element.124.u_ref, ...), custom_call_target="tpu_custom_call" | custom-call | flops 13589544960 | tf_op jit(solution)/shard_map/gate_up_back/pallas_call | solution.py:266
  575.2 49.2 %wgrad.3 = (bf16[2560,1728]{1,0:T(8,128)(2,1)}, bf16[2560,1728]{1,0:T(8,128)(2,1)}) custom-call(bf16[512,2560]{1,0:T(8,128)(2,1)} %multiply_convert_fusion.refs_0_, bf16[512,2560]{1,0:T(8,128)(2,1)} %collective-permute-done.9.refs_0_.refs_1_, bf16[512,2560]{1,0:T(8,128)(2,1)} %copy-done.38, bf16[256,2560]{1,0:T(8,128)(2,1)} %collective-permute-done.11.refs_0_.refs_3_, ...), custom_call_target="tpu_custom_call" | custom-call | flops 36238786560 | tf_op jit(solution)/shard_map/wgrad/pallas_call | solution.py:322
  628.9 27.9 %collective-permute-done.18 = bf16[256,2560]{1,0:T(8,128)(2,1)} collective-permute-done((bf16[256,2560]{1,0:T(8,128)(2,1)}, bf16[256,2560]{1,0:T(8,128)(2,1)}, u32[]{:S(2)}, u32[]{:S(2)}) %collective-permute-start.18) | collective-permute-done | bytes 1310752 | tf_op jit(solution)/shard_map/ppermute | solution.py:379
  660.0 21.2 %collective-permute-done.13 = bf16[256,2560]{1,0:T(8,128)(2,1)S(1)} collective-permute-done((bf16[256,2560]{1,0:T(8,128)(2,1)}, bf16[256,2560]{1,0:T(8,128)(2,1)S(1)}, u32[]{:S(2)}, u32[]{:S(2)}) %collective-permute-start.13) | collective-permute-done | bytes 1310752 | tf_op jit(solution)/shard_map/ppermute | solution.py:379
  683.0 5.1 multiply_reduce_fusion
  688.2 5.6 fusion.85
  695.3 9.9 down.4
  705.3 9.6 down.5
  714.9 9.5 down.6
  724.4 9.7 down.7
  734.1 14.2 %collective-permute-done.19 = bf16[512,2560]{1,0:T(8,128)(2,1)} collective-permute-done((bf16[512,2560]{1,0:T(8,128)(2,1)}, bf16[512,2560]{1,0:T(8,128)(2,1)}, u32[]{:S(2)}, u32[]{:S(2)}) %collective-permute-start.19) | collective-permute-done | bytes 2621472 | tf_op jit(solution)/shard_map/ppermute | solution.py:379
  748.3 5.3 maximum_select_fusion.2
  765.1 13.4 %fusion.21.do_ref = bf16[1024,1024]{1,0:T(8,128)(2,1)} fusion(s32[640]{0:T(1024)S(1)} %copy-done.58, bf16[1024,2560]{1,0:T(8,128)(2,1)} %copy-done.15, bf16[640,2560]{0,1:T(8,128)(2,1)} %copy-done.17), kind=kOutput, calls=%fused_computation.68 | convolution fusion | flops 4699979776 | bytes 10619392 | tf_op jit(solution)/shard_map/dot_general | solution.py:358
  779.8 25.2 %attend_back.2 = (bf16[1024,1024]{1,0:T(8,128)(2,1)S(1)}, bf16[1024,256]{1,0:T(8,128)(2,1)S(1)}, bf16[1024,256]{1,0:T(8,128)(2,1)S(1)}) custom-call(s32[4]{0:T(128)S(1)} %copy-done.3, bf16[1024,1536]{1,0:T(8,128)(2,1)} %project.3.qr_ref.kr_ref.vb_ref, bf16[1024,1536]{1,0:T(8,128)(2,1)} %project.3.qr_ref.kr_ref.vb_ref, ...), custom_call_target="tpu_custom_call" | custom-call | flops 10737418240 | tf_op jit(solution)/shard_map/attend_back/pallas_call | solution.py:128
  808.3 10.8 convolution_convert_fusion.1
  819.1 13.2 %fusion.22.do_ref = bf16[1024,1024]{1,0:T(8,128)(2,1)} fusion(s32[640]{0:T(1024)S(1)} %copy-done.58, bf16[1024,2560]{1,0:T(8,128)(2,1)} %copy-done.15, bf16[640,2560]{0,1:T(8,128)(2,1)} %all-gather.8.cloned.1.call-done), kind=kOutput, calls=%fused_computation.69 | convolution fusion | flops 4699979776 | bytes 10619392 | tf_op jit(solution)/shard_map/dot_general | solution.py:358
  832.4 25.3 %attend_back.3 = (bf16[1024,1024]{1,0:T(8,128)(2,1)S(1)}, bf16[1024,256]{1,0:T(8,128)(2,1)S(1)}, bf16[1024,256]{1,0:T(8,128)(2,1)S(1)}) custom-call(s32[4]{0:T(128)S(1)} %copy-done.3, bf16[1024,1536]{1,0:T(8,128)(2,1)} %project.2.qr_ref.kr_ref.vb_ref, bf16[1024,1536]{1,0:T(8,128)(2,1)} %project.2.qr_ref.kr_ref.vb_ref, ...), custom_call_target="tpu_custom_call" | custom-call | flops 10737418240 | tf_op jit(solution)/shard_map/attend_back/pallas_call | solution.py:128
  872.2 26.4 %collective-permute-done.35 = bf16[1280,640]{1,0:T(8,128)(2,1)S(1)} collective-permute-done((bf16[1280,640]{1,0:T(8,128)(2,1)S(1)}, bf16[1280,640]{1,0:T(8,128)(2,1)S(1)}, u32[]{:S(2)}, u32[]{:S(2)}) %collective-permute-start.35) | collective-permute-done | bytes 1638432 | tf_op jit(solution)/shard_map/ppermute | solution.py:379
  900.9 9.6 convolution_convert_fusion
  926.3 22.1 %collective-permute-done.22 = bf16[256,2560]{1,0:T(8,128)(2,1)S(1)} collective-permute-done((bf16[256,2560]{1,0:T(8,128)(2,1)S(1)}, bf16[256,2560]{1,0:T(8,128)(2,1)S(1)}, u32[]{:S(2)}, u32[]{:S(2)}) %collective-permute-start.22) | collective-permute-done | bytes 1310752 | tf_op jit(solution)/shard_map/ppermute | solution.py:379
  955.5 45.2 %collective-permute-done.33 = bf16[1280,960]{0,1:T(8,128)(2,1)} collective-permute-done((bf16[1280,960]{0,1:T(8,128)(2,1)}, bf16[1280,960]{0,1:T(8,128)(2,1)}, u32[]{:S(2)}, u32[]{:S(2)}) %collective-permute-start.33) | collective-permute-done | bytes 2457632 | tf_op jit(solution)/shard_map/ppermute | solution.py:379
  1005.3 7.9 copy.89
  1013.2 11.2 fusion.89
  1024.5 17.8 %fusion.4 = (f32[2560]{0:T(1024)S(1)}, f32[1024,2560]{1,0:T(8,128)}) fusion(f32[1024]{0:T(1024)S(1)} %copy-done.55, bf16[512,2560]{1,0:T(8,128)(2,1)S(1)} %copy-done.10, bf16[512,2560]{1,0:T(8,128)(2,1)} %collective-permute-done, pred[]{:T(512)S(6)} %eq.172, f32[1024,2560]{1,0:T(8,128)} %fusion.89, bf16[1024,960]{0,1:T(8,128)(2,1)S(1)} %copy-done.21, ...), kind=kOutput, calls=%fused_computation.7 | convolution fusion | flops 5069862400 | bytes 33110016 | tf_op jit(solution)/shard_map/dot_general | solution.py:366
  1042.5 5.2 collective-permute-start.27
  1069.1 41.4 %collective-permute-done.31 = f32[1,160]{1,0:T(1,128)S(1)} collective-permute-done((f32[1,160]{1,0:T(1,128)S(1)}, f32[1,160]{1,0:T(1,128)S(1)}, u32[]{:S(2)}, u32[]{:S(2)}) %collective-permute-start.31) | collective-permute-done | bytes 672 | tf_op jit(solution)/shard_map/ppermute | solution.py:435
  1116.3 7.3 fusion.9
  (350 shorter events, 204.5 us)
Async XLA Ops:
  7.2 67.3 %all-gather.6.cloned.1.call-start = ((), (), s32[]{:S(2)}) async-start(), calls=%async_computation.5 | async-start | bytes 5898240 | tf_op jit(solution)/shard_map/all_gather | solution.py:469
  13.0 124.0 %all-gather.8.cloned.1.call-start = ((), (), s32[]{:S(2)}) async-start(), calls=%async_computation.6 | async-start | bytes 3686400 | tf_op jit(solution)/shard_map/all_gather | solution.py:479
  13.1 60.2 %collective-permute-start.1 = (bf16[512,2560]{1,0:T(8,128)(2,1)}, bf16[512,2560]{1,0:T(8,128)(2,1)}, u32[]{:S(2)}, u32[]{:S(2)}) collective-permute-start(bf16[512,2560]{1,0:T(8,128)(2,1)} %param.23), channel_id=1, source_target_pairs={{0,2},{1,3},{2,0},{3,1},{4,6},{5,7},{6,4},{7,5},{8,10},{9,11},{10,... | collective-permute-start | bytes 7864328 | tf_op jit(solution)/shard_map/ppermute | solution.py:379
  16.1 58.4 %collective-permute-start = (bf16[512,2560]{1,0:T(8,128)(2,1)S(1)}, bf16[512,2560]{1,0:T(8,128)(2,1)}, u32[]{:S(2)}, u32[]{:S(2)}) collective-permute-start(bf16[512,2560]{1,0:T(8,128)(2,1)S(1)} %copy-done.7), channel_id=1, source_target_pairs={{0,1},{1,0},{2,3},{3,2},{4,5},{5,4},{6,7},{7,6},{8,9},{9,8},{10,11... | collective-permute-start | bytes 7864328 | tf_op jit(solution)/shard_map/ppermute | solution.py:379
  74.6 261.4 %all-gather.12.cloned.1.call-start = ((), (), s32[]{:S(2)}) async-start(), calls=%async_computation.8 | async-start | bytes 10321920 | tf_op jit(solution)/shard_map/all_gather | solution.py:481
  75.3 260.6 %all-gather.10.cloned.1.call-start = ((), (), s32[]{:S(2)}) async-start(), calls=%async_computation.7 | async-start | bytes 10321920 | tf_op jit(solution)/shard_map/all_gather | solution.py:480
  75.9 351.3 %all-gather.14.cloned.1.call-start = ((), (), s32[]{:S(2)}) async-start(), calls=%async_computation.9 | async-start | bytes 10321920 | tf_op jit(solution)/shard_map/all_gather | solution.py:482
  82.8 54.2 %collective-permute-start.2 = (bf16[1280,960]{0,1:T(8,128)(2,1)}, bf16[1280,960]{0,1:T(8,128)(2,1)}, u32[]{:S(2)}, u32[]{:S(2)}) collective-permute-start(bf16[1280,960]{0,1:T(8,128)(2,1)} %copy.73), channel_id=1, source_target_pairs={{0,2},{1,3},{2,0},{3,1},{4,6},{5,7},{6,4},{7,5},{8,10},{9,11},{10,... | collective-permute-start | bytes 7372808 | tf_op jit(solution)/shard_map/ppermute | solution.py:379
  86.9 140.4 %copy-start.2 = (s32[4]{0:T(128)}, s32[4]{0:T(128)S(1)}, u32[]{:S(2)}) copy-start(s32[4]{0:T(128)S(1)} %and_select_fusion.2.lo_ref) | copy-start | bytes 52
  89.1 175.2 %collective-permute-start.7 = (bf16[512,2560]{1,0:T(8,128)(2,1)}, bf16[512,2560]{1,0:T(8,128)(2,1)}, u32[]{:S(2)}, u32[]{:S(2)}) collective-permute-start(bf16[512,2560]{1,0:T(8,128)(2,1)} %param.23), channel_id=1, source_target_pairs={{0,1},{1,0},{2,3},{3,2},{4,5},{5,4},{6,7},{7,6},{8,9},{9,8},{10,11... | collective-permute-start | bytes 7864328 | tf_op jit(solution)/shard_map/ppermute | solution.py:379
  92.9 241.0 %copy-start.39 = (f32[2560]{0:T(1024)}, f32[2560]{0:T(1024)S(1)}, u32[]{:S(2)}) copy-start(f32[2560]{0:T(1024)S(1)} %get-tuple-element.256) | copy-start | bytes 30724
  137.0 57.7 %collective-permute-start.3 = (bf16[1280,960]{0,1:T(8,128)(2,1)}, bf16[1280,960]{0,1:T(8,128)(2,1)}, u32[]{:S(2)}, u32[]{:S(2)}) collective-permute-start(bf16[1280,960]{0,1:T(8,128)(2,1)} %collective-permute-done.2), channel_id=1, source_target_pairs={{0,4},{4,0},{8,12},{12,8},{16,20},{20,16},{24,28},{28,24},{1,5},{5... | collective-permute-start | bytes 7372808 | tf_op jit(solution)/shard_map/ppermute | solution.py:487
  143.1 56.0 %collective-permute-start.4 = (bf16[320,2560]{1,0:T(8,128)(2,1)}, bf16[320,2560]{1,0:T(8,128)(2,1)}, u32[]{:S(2)}, u32[]{:S(2)}) collective-permute-start(bf16[320,2560]{1,0:T(8,128)(2,1)} %copy.81), channel_id=1, source_target_pairs={{0,2},{1,3},{2,0},{3,1},{4,6},{5,7},{6,4},{7,5},{8,10},{9,11},{10,... | collective-permute-start | bytes 4915208 | tf_op jit(solution)/shard_map/ppermute | solution.py:379
  143.9 604.4 %reduce-scatter.8.cloned.1.call-start = ((), (), s32[]{:S(2)}) async-start(), calls=%async_computation.10 | async-start | bytes 10321920 | tf_op jit(solution)/shard_map/reduce_scatter | solution.py:546
  199.1 49.0 %collective-permute-start.5 = (bf16[320,2560]{1,0:T(8,128)(2,1)}, bf16[320,2560]{1,0:T(8,128)(2,1)}, u32[]{:S(2)}, u32[]{:S(2)}) collective-permute-start(bf16[320,2560]{1,0:T(8,128)(2,1)} %collective-permute-done.4), channel_id=1, source_target_pairs={{0,4},{4,0},{8,12},{12,8},{16,20},{20,16},{24,28},{28,24},{1,5},{5... | collective-permute-start | bytes 4915208 | tf_op jit(solution)/shard_map/ppermute | solution.py:487
  262.9 59.5 %collective-permute-start.6 = (bf16[512,2560]{1,0:T(8,128)(2,1)}, bf16[512,2560]{1,0:T(8,128)(2,1)}, u32[]{:S(2)}, u32[]{:S(2)}) collective-permute-start(bf16[512,2560]{1,0:T(8,128)(2,1)} %convolution_convert_fusion.4), channel_id=1, source_target_pairs={{0,1},{1,0},{2,3},{3,2},{4,5},{5,4},{6,7},{7,6},{8,9},{9,8},{10,11... | collective-permute-start | bytes 7864328 | tf_op jit(solution)/shard_map/ppermute | solution.py:379
  264.3 60.5 %collective-permute-start.8 = (bf16[512,2560]{1,0:T(8,128)(2,1)}, bf16[512,2560]{1,0:T(8,128)(2,1)}, u32[]{:S(2)}, u32[]{:S(2)}) collective-permute-start(bf16[512,2560]{1,0:T(8,128)(2,1)} %collective-permute-done.7), channel_id=1, source_target_pairs={{0,2},{1,3},{2,0},{3,1},{4,6},{5,7},{6,4},{7,5},{8,10},{9,11},{10,... | collective-permute-start | bytes 7864328 | tf_op jit(solution)/shard_map/ppermute | solution.py:379
  335.9 58.6 %collective-permute-start.10 = (bf16[512,2560]{1,0:T(8,128)(2,1)}, bf16[512,2560]{1,0:T(8,128)(2,1)S(1)}, u32[]{:S(2)}, u32[]{:S(2)}) collective-permute-start(bf16[512,2560]{1,0:T(8,128)(2,1)} %multiply_convert_fusion.refs_0_), channel_id=1, source_target_pairs={{0,2},{1,3},{2,0},{3,1},{4,6},{5,7},{6,4},{7,5},{8,10},{9,11},{10,... | collective-permute-start | bytes 7864328 | tf_op jit(solution)/shard_map/ppermute | solution.py:379
  337.0 59.1 %collective-permute-start.9 = (bf16[512,2560]{1,0:T(8,128)(2,1)}, bf16[512,2560]{1,0:T(8,128)(2,1)}, u32[]{:S(2)}, u32[]{:S(2)}) collective-permute-start(bf16[512,2560]{1,0:T(8,128)(2,1)} %multiply_convert_fusion.refs_0_), channel_id=1, source_target_pairs={{0,1},{1,0},{2,3},{3,2},{4,5},{5,4},{6,7},{7,6},{8,9},{9,8},{10,11... | collective-permute-start | bytes 7864328 | tf_op jit(solution)/shard_map/ppermute | solution.py:379
  394.6 29.6 %collective-permute-start.12 = (bf16[256,2560]{1,0:T(8,128)(2,1)S(1)}, bf16[256,2560]{1,0:T(8,128)(2,1)S(1)}, u32[]{:S(2)}, u32[]{:S(2)}) collective-permute-start(bf16[256,2560]{1,0:T(8,128)(2,1)S(1)} %slice.76), channel_id=1, source_target_pairs={{0,1},{1,0},{2,3},{3,2},{4,5},{5,4},{6,7},{7,6},{8,9},{9,8},{10,11... | collective-permute-start | bytes 3932168 | tf_op jit(solution)/shard_map/ppermute | solution.py:379
  397.5 29.7 %collective-permute-start.11 = (bf16[256,2560]{1,0:T(8,128)(2,1)S(1)}, bf16[256,2560]{1,0:T(8,128)(2,1)}, u32[]{:S(2)}, u32[]{:S(2)}) collective-permute-start(bf16[256,2560]{1,0:T(8,128)(2,1)S(1)} %slice.75), channel_id=1, source_target_pairs={{0,2},{1,3},{2,0},{3,1},{4,6},{5,7},{6,4},{7,5},{8,10},{9,11},{10,... | collective-permute-start | bytes 3932168 | tf_op jit(solution)/shard_map/ppermute | solution.py:379
  472.5 483.0 %reduce-scatter.10.cloned.1.call-start = ((), (), s32[]{:S(2)}) async-start(), calls=%async_computation.11 | async-start | bytes 10321920 | tf_op jit(solution)/shard_map/reduce_scatter | solution.py:555
  496.2 74.9 %collective-permute-start.14 = (bf16[256,2560]{1,0:T(8,128)(2,1)}, bf16[256,2560]{1,0:T(8,128)(2,1)S(1)}, u32[]{:S(2)}, u32[]{:S(2)}) collective-permute-start(bf16[256,2560]{1,0:T(8,128)(2,1)} %get-tuple-element.138), channel_id=1, source_target_pairs={{0,1},{1,0},{2,3},{3,2},{4,5},{5,4},{6,7},{7,6},{8,9},{9,8},{10,11... | collective-permute-start | bytes 3932168 | tf_op jit(solution)/shard_map/ppermute | solution.py:379
  545.1 28.7 %collective-permute-start.16 = (bf16[256,2560]{1,0:T(8,128)(2,1)}, bf16[256,2560]{1,0:T(8,128)(2,1)S(1)}, u32[]{:S(2)}, u32[]{:S(2)}) collective-permute-start(bf16[256,2560]{1,0:T(8,128)(2,1)} %get-tuple-element.146), channel_id=1, source_target_pairs={{0,2},{1,3},{2,0},{3,1},{4,6},{5,7},{6,4},{7,5},{8,10},{9,11},{10,... | collective-permute-start | bytes 3932168 | tf_op jit(solution)/shard_map/ppermute | solution.py:379
  624.4 331.1 %reduce-scatter.12.cloned.1.call-start = ((), (), s32[]{:S(2)}) async-start(), calls=%async_computation.12 | async-start | bytes 10321920 | tf_op jit(solution)/shard_map/reduce_scatter | solution.py:556
  624.7 32.1 %collective-permute-start.18 = (bf16[256,2560]{1,0:T(8,128)(2,1)}, bf16[256,2560]{1,0:T(8,128)(2,1)}, u32[]{:S(2)}, u32[]{:S(2)}) collective-permute-start(bf16[256,2560]{1,0:T(8,128)(2,1)} %get-tuple-element.147), channel_id=1, source_target_pairs={{0,2},{1,3},{2,0},{3,1},{4,6},{5,7},{6,4},{7,5},{8,10},{9,11},{10,... | collective-permute-start | bytes 3932168 | tf_op jit(solution)/shard_map/ppermute | solution.py:379
  625.8 32.0 %collective-permute-start.17 = (bf16[256,2560]{1,0:T(8,128)(2,1)}, bf16[256,2560]{1,0:T(8,128)(2,1)}, u32[]{:S(2)}, u32[]{:S(2)}) collective-permute-start(bf16[256,2560]{1,0:T(8,128)(2,1)} %add_convert_fusion.6), channel_id=1, source_target_pairs={{0,1},{1,0},{2,3},{3,2},{4,5},{5,4},{6,7},{7,6},{8,9},{9,8},{10,11... | collective-permute-start | bytes 3932168 | tf_op jit(solution)/shard_map/ppermute | solution.py:379
  626.4 54.7 %collective-permute-start.13 = (bf16[256,2560]{1,0:T(8,128)(2,1)}, bf16[256,2560]{1,0:T(8,128)(2,1)S(1)}, u32[]{:S(2)}, u32[]{:S(2)}) collective-permute-start(bf16[256,2560]{1,0:T(8,128)(2,1)} %get-tuple-element.144), channel_id=1, source_target_pairs={{0,1},{1,0},{2,3},{3,2},{4,5},{5,4},{6,7},{7,6},{8,9},{9,8},{10,11... | collective-permute-start | bytes 3932168 | tf_op jit(solution)/shard_map/ppermute | solution.py:379
  627.8 53.3 %collective-permute-start.15 = (bf16[256,2560]{1,0:T(8,128)(2,1)}, bf16[256,2560]{1,0:T(8,128)(2,1)}, u32[]{:S(2)}, u32[]{:S(2)}) collective-permute-start(bf16[256,2560]{1,0:T(8,128)(2,1)} %add_convert_fusion.7), channel_id=1, source_target_pairs={{0,2},{1,3},{2,0},{3,1},{4,6},{5,7},{6,4},{7,5},{8,10},{9,11},{10,... | collective-permute-start | bytes 3932168 | tf_op jit(solution)/shard_map/ppermute | solution.py:379
  628.8 494.8 %reduce-scatter.14.cloned.1.call-start = ((), (), s32[]{:S(2)}) async-start(), calls=%async_computation.13 | async-start | bytes 3686400 | tf_op jit(solution)/shard_map/reduce_scatter | solution.py:585
  693.8 54.6 %collective-permute-start.19 = (bf16[512,2560]{1,0:T(8,128)(2,1)}, bf16[512,2560]{1,0:T(8,128)(2,1)}, u32[]{:S(2)}, u32[]{:S(2)}) collective-permute-start(bf16[512,2560]{1,0:T(8,128)(2,1)} %fusion.85), channel_id=1, source_target_pairs={{0,1},{1,0},{2,3},{3,2},{4,5},{5,4},{6,7},{7,6},{8,9},{9,8},{10,11... | collective-permute-start | bytes 7864328 | tf_op jit(solution)/shard_map/ppermute | solution.py:379
  753.7 172.6 %collective-permute-start.20 = (bf16[256,2560]{1,0:T(8,128)(2,1)}, bf16[256,2560]{1,0:T(8,128)(2,1)}, u32[]{:S(2)}, u32[]{:S(2)}) collective-permute-start(bf16[256,2560]{1,0:T(8,128)(2,1)} %get-tuple-element.171), channel_id=1, source_target_pairs={{0,1},{1,0},{2,3},{3,2},{4,5},{5,4},{6,7},{7,6},{8,9},{9,8},{10,11... | collective-permute-start | bytes 3932168 | tf_op jit(solution)/shard_map/ppermute | solution.py:379
  755.4 158.7 %collective-permute-start.21 = (bf16[256,2560]{1,0:T(8,128)(2,1)}, bf16[256,2560]{1,0:T(8,128)(2,1)}, u32[]{:S(2)}, u32[]{:S(2)}) collective-permute-start(bf16[256,2560]{1,0:T(8,128)(2,1)} %get-tuple-element.173), channel_id=1, source_target_pairs={{0,1},{1,0},{2,3},{3,2},{4,5},{5,4},{6,7},{7,6},{8,9},{9,8},{10,11... | collective-permute-start | bytes 3932168 | tf_op jit(solution)/shard_map/ppermute | solution.py:379
  755.8 162.4 %collective-permute-start.23 = (bf16[256,2560]{1,0:T(8,128)(2,1)}, bf16[256,2560]{1,0:T(8,128)(2,1)}, u32[]{:S(2)}, u32[]{:S(2)}) collective-permute-start(bf16[256,2560]{1,0:T(8,128)(2,1)} %get-tuple-element.175), channel_id=1, source_target_pairs={{0,2},{1,3},{2,0},{3,1},{4,6},{5,7},{6,4},{7,5},{8,10},{9,11},{10,... | collective-permute-start | bytes 3932168 | tf_op jit(solution)/shard_map/ppermute | solution.py:379
  757.2 192.8 %collective-permute-start.25 = (bf16[256,2560]{1,0:T(8,128)(2,1)}, bf16[256,2560]{1,0:T(8,128)(2,1)}, u32[]{:S(2)}, u32[]{:S(2)}) collective-permute-start(bf16[256,2560]{1,0:T(8,128)(2,1)} %get-tuple-element.176), channel_id=1, source_target_pairs={{0,2},{1,3},{2,0},{3,1},{4,6},{5,7},{6,4},{7,5},{8,10},{9,11},{10,... | collective-permute-start | bytes 3932168 | tf_op jit(solution)/shard_map/ppermute | solution.py:379
  765.1 93.7 %collective-permute-start.34 = (bf16[1280,640]{1,0:T(8,128)(2,1)}, bf16[1280,640]{1,0:T(8,128)(2,1)}, u32[]{:S(2)}, u32[]{:S(2)}) collective-permute-start(bf16[1280,640]{1,0:T(8,128)(2,1)} %constant_dynamic-slice_fusion.1), channel_id=1, source_target_pairs={{0,4},{4,0},{8,12},{12,8},{16,20},{20,16},{24,28},{28,24},{1,5},{5... | collective-permute-start | bytes 4915208 | tf_op jit(solution)/shard_map/ppermute | solution.py:497
  860.8 37.8 %collective-permute-start.35 = (bf16[1280,640]{1,0:T(8,128)(2,1)S(1)}, bf16[1280,640]{1,0:T(8,128)(2,1)S(1)}, u32[]{:S(2)}, u32[]{:S(2)}) collective-permute-start(bf16[1280,640]{1,0:T(8,128)(2,1)S(1)} %add_convert_fusion.3), channel_id=1, source_target_pairs={{0,2},{1,3},{2,0},{3,1},{4,6},{5,7},{6,4},{7,5},{8,10},{9,11},{10,... | collective-permute-start | bytes 4915208 | tf_op jit(solution)/shard_map/ppermute | solution.py:379
  898.6 23.1 %collective-permute-start.32 = (bf16[1280,960]{0,1:T(8,128)(2,1)}, bf16[1280,960]{0,1:T(8,128)(2,1)}, u32[]{:S(2)}, u32[]{:S(2)}) collective-permute-start(bf16[1280,960]{0,1:T(8,128)(2,1)} %constant_dynamic-slice_fusion.2), channel_id=1, source_target_pairs={{0,4},{4,0},{8,12},{12,8},{16,20},{20,16},{24,28},{28,24},{1,5},{5... | collective-permute-start | bytes 7372808 | tf_op jit(solution)/shard_map/ppermute | solution.py:497
  900.9 224.7 %reduce-scatter.16.cloned.1.call-start = ((), (), s32[]{:S(2)}) async-start(), calls=%async_computation.14 | async-start | bytes 5898240
  916.7 31.6 %collective-permute-start.22 = (bf16[256,2560]{1,0:T(8,128)(2,1)S(1)}, bf16[256,2560]{1,0:T(8,128)(2,1)S(1)}, u32[]{:S(2)}, u32[]{:S(2)}) collective-permute-start(bf16[256,2560]{1,0:T(8,128)(2,1)S(1)} %add_convert_fusion.5), channel_id=1, source_target_pairs={{0,2},{1,3},{2,0},{3,1},{4,6},{5,7},{6,4},{7,5},{8,10},{9,11},{10,... | collective-permute-start | bytes 3932168 | tf_op jit(solution)/shard_map/ppermute | solution.py:379
  919.9 31.0 %collective-permute-start.24 = (bf16[256,2560]{1,0:T(8,128)(2,1)S(1)}, bf16[256,2560]{1,0:T(8,128)(2,1)S(1)}, u32[]{:S(2)}, u32[]{:S(2)}) collective-permute-start(bf16[256,2560]{1,0:T(8,128)(2,1)S(1)} %add_convert_fusion.4), channel_id=1, source_target_pairs={{0,1},{1,0},{2,3},{3,2},{4,5},{5,4},{6,7},{7,6},{8,9},{9,8},{10,11... | collective-permute-start | bytes 3932168 | tf_op jit(solution)/shard_map/ppermute | solution.py:379
  925.7 75.1 %collective-permute-start.33 = (bf16[1280,960]{0,1:T(8,128)(2,1)}, bf16[1280,960]{0,1:T(8,128)(2,1)}, u32[]{:S(2)}, u32[]{:S(2)}) collective-permute-start(bf16[1280,960]{0,1:T(8,128)(2,1)} %add_convert_fusion.1), channel_id=1, source_target_pairs={{0,2},{1,3},{2,0},{3,1},{4,6},{5,7},{6,4},{7,5},{8,10},{9,11},{10,... | collective-permute-start | bytes 7372808 | tf_op jit(solution)/shard_map/ppermute | solution.py:379
  1042.5 10.2 collective-permute-start.27
  1052.0 59.1 %collective-permute-start.26 = (bf16[512,2560]{1,0:T(8,128)(2,1)}, bf16[512,2560]{1,0:T(8,128)(2,1)}, u32[]{:S(2)}, u32[]{:S(2)}) collective-permute-start(bf16[512,2560]{1,0:T(8,128)(2,1)} %dynamic-slice_convert_fusion), channel_id=1, source_target_pairs={{0,1},{1,0},{2,3},{3,2},{4,5},{5,4},{6,7},{7,6},{8,9},{9,8},{10,11... | collective-permute-start | bytes 7864328 | tf_op jit(solution)/shard_map/ppermute | solution.py:379
  1052.8 4.1 collective-permute-start.28
  1056.9 1.2 collective-permute-start.29
  1058.1 3.6 collective-permute-start.30
  1061.8 48.7 %collective-permute-start.31 = (f32[1,160]{1,0:T(1,128)S(1)}, f32[1,160]{1,0:T(1,128)S(1)}, u32[]{:S(2)}, u32[]{:S(2)}) collective-permute-start(f32[1,160]{1,0:T(1,128)S(1)} %broadcast_select_fusion.2), channel_id=1, source_target_pairs={{0,1},{1,0},{2,3},{3,2},{4,5},{5,4},{6,7},{7,6},{8,9},{9,8},{10,11... | collective-permute-start | bytes 1928 | tf_op jit(solution)/shard_map/ppermute | solution.py:435
  (76 other events, 923.1 us)
Sparse Core Ops, SparseCore 0:
  13.1 58.7 all-gather.5
  74.7 39.6 all-gather.7
  116.0 87.4 all-gather.11
  205.0 88.7 all-gather.9
  295.3 87.0 all-gather.13
  472.7 97.0 reduce-scatter.7
  624.5 96.3 reduce-scatter.9
  723.2 95.3 reduce-scatter.11
  901.0 42.5 reduce-scatter.13
  1013.3 61.4 reduce-scatter.15

commit v3 on v2

--- a/solution.py
+++ b/solution.py
@@ -114,7 +114,7 @@
         ),
         out_shape=[jax.ShapeDtypeStruct((rows, kv * wide), BF), jax.ShapeDtypeStruct((kv, rows, groups), F32)],
         compiler_params=pltpu.CompilerParams(vmem_limit_bytes=48 * 2 ** 20),
-        cost_estimate=cost(4 * kv * groups * rows * rows * LANES), name="attend",
+        cost_estimate=cost(kv * groups * rows * rows * LANES), name="attend",
     )(lo, proj, proj, proj, start)
 
 
@@ -143,6 +143,7 @@
 
 
 COLS = 256
+FINISH_COST = 52 * 10 ** 9
 
 
 def cost(flops):
@@ -153,47 +154,70 @@
     return pltpu.CompilerParams(vmem_limit_bytes=56 * 2 ** 20)
 
 
-def project_kernel(heads, kv, n1_ref, w_ref, eq_ref, ek_ref, c_ref, s_ref, out_ref):
-    c, s = c_ref[...], s_ref[...]
+def project_kernel(heads, kv, parts, at_ref, n1_ref, eq_ref, ek_ref, c_ref, s_ref, *refs):
+    w_refs, out_ref = refs[:parts], refs[parts]
     q_width = heads * HD
     step = pl.program_id(0)
 
-    def go(w, spread, turned, width):
-        padded = nn(w, spread).astype(BF)
-        proj = nn(n1_ref[...], padded)
-        for h in range(width):
+    def go(columns, spread, turned):
+        proj = None
+        for i, w_ref in enumerate(w_refs):
+            depth = w_ref.shape[0]
+            a = n1_ref[...] if parts == 1 else n1_ref[:, pl.ds(pl.multiple_of(at_ref[i] * depth, depth), depth)]
+            part = nn(a, nn(w_ref[:, columns], spread).astype(BF))
+            proj = part if proj is None else proj + part
+        for h in range(proj.shape[1] // LANES):
             lanes = slice(h * LANES, (h + 1) * LANES)
             head = proj[:, lanes]
-            out_ref[:, lanes] = (turn(head, c, s) if h < turned else head).astype(BF)
-
-    per = 2 * kv
-
-    @pl.when(step < heads // per)
+            out_ref[:, lanes] = (turn(head, c_ref[...], s_ref[...]) if h < turned else head).astype(BF)
+
+    @pl.when(step < heads // (2 * kv))
     def _():
-        go(w_ref[:, :q_width], eq_ref[...], per, per)
-
-    @pl.when(step == heads // per)
+        go(slice(0, q_width), eq_ref[...], 2 * kv)
+
+    @pl.when(step == heads // (2 * kv))
     def _():
-        go(w_ref[:, q_width:], ek_ref[...], kv, per)
-
-
-def project(n1, w, tables, heads, kv):
+        go(slice(q_width, w_refs[0].shape[1]), ek_ref[...], kv)
+
+
+def project(n1, w_parts, at, tables, heads, kv):
     cos_t, sin_t = tables[:2]
     rows, d = n1.shape
     per = 2 * kv
     steps = heads // per + 1
-    whole = lambda shape: pl.BlockSpec(shape, lambda i: (0, 0))
-    e_k = spread_matrix(2 * kv)
+    whole = lambda shape: pl.BlockSpec(shape, lambda i, at: (0, 0))
+    e_k = jnp.pad(spread_matrix(2 * kv), ((0, w_parts[0].shape[1] - (heads + 2 * kv) * HD), (0, 0)))
     return pl.pallas_call(
-        functools.partial(project_kernel, heads, kv),
-        grid=(steps,),
-        in_specs=[whole((rows, d)), whole(w.shape),
-                  pl.BlockSpec((heads * HD, per * LANES), lambda i: (0, jnp.minimum(i, heads // per - 1))),
-                  whole(e_k.shape), whole(cos_t.shape), whole(sin_t.shape)],
-        out_specs=pl.BlockSpec((rows, per * LANES), lambda i: (0, i)),
+        functools.partial(project_kernel, heads, kv, len(w_parts)),
+        grid_spec=pltpu.PrefetchScalarGridSpec(
+            num_scalar_prefetch=1,
+            grid=(steps,),
+            in_specs=[whole((rows, d)),
+                      pl.BlockSpec((heads * HD, per * LANES), lambda i, at: (0, jnp.minimum(i, heads // per - 1))),
+                      whole(e_k.shape), whole(cos_t.shape), whole(sin_t.shape)] + [whole(w.shape) for w in w_parts],
+            out_specs=pl.BlockSpec((rows, per * LANES), lambda i, at: (0, i)),
+        ),
         out_shape=jax.ShapeDtypeStruct((rows, steps * per * LANES), BF),
-        compiler_params=params(), cost_estimate=cost(2 * rows * d * steps * per * LANES), name="project",
-    )(n1, w, spread_matrix(heads), e_k, cos_t, sin_t)
+        compiler_params=params(), cost_estimate=cost(rows * d * steps * per * LANES // 2), name="project",
+    )(at, n1, spread_matrix(heads), e_k, cos_t, sin_t, *w_parts)
+
+
+def heads_back_kernel(d_ref, w_ref, e_ref, out_ref):
+    out_ref[...] = nn(nn(d_ref[...], w_ref[...]).astype(BF), e_ref[...]).astype(BF)
+
+
+def heads_back(grad, w_t, heads):
+    (rows, d), size = grad.shape, 256
+    e = spread_matrix(heads)
+    return pl.pallas_call(
+        heads_back_kernel,
+        grid=(rows // size,),
+        in_specs=[pl.BlockSpec((size, d), lambda i: (i, 0)), pl.BlockSpec(w_t.shape, lambda i: (0, 0)),
+                  pl.BlockSpec(e.shape, lambda i: (0, 0))],
+        out_specs=pl.BlockSpec((size, heads * LANES), lambda i: (i, 0)),
+        out_shape=jax.ShapeDtypeStruct((rows, heads * LANES), BF),
+        compiler_params=params(), cost_estimate=cost(2 * rows * heads * HD * (d + heads * LANES)), name="heads_back",
+    )(grad, w_t, e)
 
 
 def gate_up_kernel(sizes, *refs):
@@ -227,25 +251,28 @@
     return [outs[3 * i:3 * i + 3] for i in range(len(blocks))]
 
 
-def gate_up_back_kernel(ff, dy_ref, g_ref, u_ref, wg_ref, wu_ref, wd_ref, dg_ref, du_ref, *p_refs_acc):
-    *p_refs, acc = p_refs_acc
+def gate_up_back_kernel(ff, n, parts, *refs):
+    blocks, (wg_ref, wu_ref, wd_ref), refs = refs[:3 * n], refs[3 * n:3 * n + 3], refs[3 * n + 3:]
+    d_refs, p_refs, accs = refs[:2 * n], refs[2 * n:-n], refs[-n:]
     step, last = pl.program_id(0), pl.num_programs(0) - 1
-    d_hidden = nn(dy_ref[...], wd_ref[...])
-    gate, up = g_ref[...].astype(F32), u_ref[...].astype(F32)
-    sig = 1.0 / (1.0 + jnp.exp(-gate))
-    act = gate * sig
-    d_gate = (d_hidden * up * (sig + act * (1.0 - sig))).astype(BF)
-    d_up = (d_hidden * act).astype(BF)
-    dg_ref[...] = d_gate
-    du_ref[...] = d_up
+    for i in range(n):
+        dy_ref, g_ref, u_ref = blocks[3 * i:3 * i + 3]
+        d_hidden = nn(dy_ref[...], wd_ref[...])
+        gate, up = g_ref[...].astype(F32), u_ref[...].astype(F32)
+        sig = 1.0 / (1.0 + jnp.exp(-gate))
+        act = gate * sig
+        d_refs[2 * i][...] = (d_hidden * up * (sig + act * (1.0 - sig))).astype(BF)
+        d_refs[2 * i + 1][...] = (d_hidden * act).astype(BF)
 
     @pl.when(step == 0)
     def _():
-        acc[...] = jnp.zeros_like(acc)
-
-    @pl.when(step < last)
+        for i in range(n):
+            accs[i][...] = nt(d_refs[2 * i][...], wg_ref[...]) + nt(d_refs[2 * i + 1][...], wu_ref[...])
+
+    @pl.when((step > 0) & (step < last))
     def _():
-        acc[...] += nt(d_gate, wg_ref[...]) + nt(d_up, wu_ref[...])
+        for i in range(n):
+            accs[i][...] += nt(d_refs[2 * i][...], wg_ref[...]) + nt(d_refs[2 * i + 1][...], wu_ref[...])
 
     @pl.when(step == last)
     def _():
@@ -253,25 +280,32 @@
             col = last * COLS + lax.broadcasted_iota(jnp.int32, v.shape, 1)
             return jnp.where(col < ff, v, jnp.zeros_like(v))
 
-        total = acc[...] + nt(inside(d_gate), inside(wg_ref[...])) + nt(inside(d_up), inside(wu_ref[...]))
-        size = total.shape[0] // len(p_refs)
-        for i, p_ref in enumerate(p_refs):
-            p_ref[...] = total[i * size:(i + 1) * size].astype(p_ref.dtype)
-
-
-def gate_up_back(dy, gate, up, w_gate, w_up, w_down_t, out, parts):
-    (rows, d), ff = dy.shape, w_gate.shape[1]
+        w_g, w_u = inside(wg_ref[...]), inside(wu_ref[...])
+        for i in range(n):
+            total = accs[i][...] + nt(inside(d_refs[2 * i][...]), w_g) + nt(inside(d_refs[2 * i + 1][...]), w_u)
+            size = total.shape[0] // parts
+            for j in range(parts):
+                p_refs[parts * i + j][...] = total[j * size:(j + 1) * size].astype(BF)
+
+
+def gate_up_back(blocks, w_gate, w_up, w_down_t, parts):
+    n, (rows, d), ff = len(blocks), blocks[0][0].shape, w_gate.shape[1]
+    assert pl.cdiv(ff, COLS) > 1
     tile = lambda size: pl.BlockSpec((size, COLS), lambda i: (0, i))
-    whole = pl.BlockSpec((rows, d), lambda i: (0, 0))
-    return pl.pallas_call(
-        functools.partial(gate_up_back_kernel, ff),
+    whole = pl.BlockSpec((rows, d), lambda i: (0, 0), pipeline_mode=pl.Buffered(1))
+    piece = pl.BlockSpec((rows // parts, d), lambda i: (0, 0))
+    outs = pl.pallas_call(
+        functools.partial(gate_up_back_kernel, ff, n, parts),
         grid=(pl.cdiv(ff, COLS),),
-        in_specs=[whole, tile(rows), tile(rows), tile(d), tile(d), tile(d)],
-        out_specs=[tile(rows)] * 2 + [pl.BlockSpec((rows // parts, d), lambda i: (0, 0))] * parts,
-        out_shape=[jax.ShapeDtypeStruct((rows, ff), BF)] * 2 + [jax.ShapeDtypeStruct((rows // parts, d), out)] * parts,
-        scratch_shapes=[pltpu.VMEM((rows, d), F32)],
-        compiler_params=params(), cost_estimate=cost(6 * rows * d * ff), name="gate_up_back",
-    )(dy, gate, up, w_gate, w_up, w_down_t)
+        in_specs=[whole, tile(rows), tile(rows)] * n + [tile(d)] * 3,
+        out_specs=[tile(rows)] * (2 * n) + [piece] * (parts * n),
+        out_shape=[jax.ShapeDtypeStruct((rows, ff), BF)] * (2 * n)
+        + [jax.ShapeDtypeStruct((rows // parts, d), BF)] * (parts * n),
+        scratch_shapes=[pltpu.VMEM((rows, d), F32)] * n,
+        compiler_params=pltpu.CompilerParams(vmem_limit_bytes=58 * 2 ** 20),
+        cost_estimate=cost(6 * n * rows * d * ff), name="gate_up_back",
+    )(*[v for block in blocks for v in block], w_gate, w_up, w_down_t)
+    return [(*outs[2 * i:2 * i + 2], outs[2 * n + parts * i:2 * n + parts * (i + 1)]) for i in range(n)]
 
 
 def down_kernel(h_ref, w_ref, *out_refs):
@@ -294,11 +328,11 @@
     )(hidden, w_down_t)
 
 
-def wgrad_kernel(n, lists, *refs):
-    a_refs, b_refs = refs[:n], list(refs[n:n + sum(map(len, lists))])
-    outs, a_t = refs[n + len(b_refs):-1], refs[-1]
-
-    @pl.when(pl.program_id(0) == 0)
+def wgrad_kernel(n, lists, tiles, *refs):
+    a_refs, b_refs, (out, a_t) = refs[:n], list(refs[n:-2]), refs[-2:]
+    step = pl.program_id(0)
+
+    @pl.when(step == 0)
     def _():
         at = 0
         for a_ref in a_refs:
@@ -306,29 +340,56 @@
             at += a_ref.shape[0]
 
     for j, sizes in enumerate(lists):
-        total, at = None, 0
-        for rows in sizes:
-            part = nn(a_t[:, at:at + rows], b_refs.pop(0)[...])
-            total = part if total is None else total + part
-            at += rows
-        outs[j][...] = total.astype(BF)
+        bs = [b_refs.pop(0) for _ in sizes]
+
+        @pl.when(step // tiles == j)
+        def _():
+            total, at = None, 0
+            for rows, b_ref in zip(sizes, bs):
+                part = nn(a_t[:, at:at + rows], b_ref[...])
+                total = part if total is None else total + part
+                at += rows
+            out[...] = total.astype(BF)
 
 
 def wgrad(a_blocks, *b_lists):
     d, ff = a_blocks[0].shape[1], b_lists[0][0].shape[1]
     total = sum(a.shape[0] for a in a_blocks)
     lists = [[b.shape[0] for b in bs] for bs in b_lists]
-    tile = lambda size: pl.BlockSpec((size, COLS), lambda i: (0, i))
+    tiles = pl.cdiv(ff, COLS)
+    b_spec = lambda b, j: pl.BlockSpec((b.shape[0], COLS), lambda i: (0, jnp.clip(i - j * tiles, 0, tiles - 1)))
+    width = ff if len(lists) == 1 else len(lists) * tiles * COLS
     return pl.pallas_call(
-        functools.partial(wgrad_kernel, len(a_blocks), lists),
-        grid=(pl.cdiv(ff, COLS),),
+        functools.partial(wgrad_kernel, len(a_blocks), lists, tiles),
+        grid=(len(lists) * tiles,),
         in_specs=[pl.BlockSpec(a.shape, lambda i: (0, 0), pipeline_mode=pl.Buffered(1)) for a in a_blocks]
-        + [tile(b.shape[0]) for bs in b_lists for b in bs],
-        out_specs=[tile(d)] * len(b_lists),
-        out_shape=[jax.ShapeDtypeStruct((d, ff), BF)] * len(b_lists),
+        + [b_spec(b, j) for j, bs in enumerate(b_lists) for b in bs],
+        out_specs=pl.BlockSpec((d, COLS), lambda i: (0, i)),
+        out_shape=jax.ShapeDtypeStruct((d, width), BF),
         scratch_shapes=[pltpu.VMEM((d, total), BF)],
-        compiler_params=params(), cost_estimate=cost(2 * total * d * ff * len(b_lists)), name="wgrad",
+        compiler_params=params(), cost_estimate=cost(total * d * ff * len(b_lists) // 4), name="wgrad",
     )(*a_blocks, *[b for bs in b_lists for b in bs])
+
+
+def finish_kernel(eps, x_ref, gain_ref, own_ref, got_ref, dh_ref, out_ref):
+    x = x_ref[...].astype(F32)
+    inv = lax.rsqrt(jnp.mean(x * x, axis=1, keepdims=True) + eps)
+    scaled = (own_ref[...] + got_ref[...].astype(F32)) * gain_ref[...]
+    out_ref[...] = dh_ref[...] + inv * scaled - x * (inv * inv * inv * jnp.mean(scaled * x, axis=1, keepdims=True))
+
+
+def finish(x, gain, own, got, dh):
+    rows, d = x.shape
+    size = min(128, rows)
+    at = pl.BlockSpec((size, d), lambda i: (i, 0))
+    return pl.pallas_call(
+        functools.partial(finish_kernel, EPS),
+        grid=(rows // size,),
+        in_specs=[at, pl.BlockSpec((1, d), lambda i: (0, 0)), at, at, at],
+        out_specs=at,
+        out_shape=jax.ShapeDtypeStruct((rows, d), F32),
+        compiler_params=params(), cost_estimate=cost(FINISH_COST), name="finish",
+    )(x, gain[None, :], own, got, dh)
 
 
 def doc_starts(seg_row):
@@ -405,23 +466,27 @@
 
 def scatter(parts, size):
     if size == 2:
-        got = swap(jnp.concatenate(parts[1]), 1)
-        return got.astype(F32), parts[1]
+        return [swap(jnp.concatenate(parts[1]), 1)], parts[1]
     if square(size):
         _, (x_low, x_high), (y_low, y_high), (d_low, d_high) = parts
-        add = lambda a, b: (a.astype(F32) + b.astype(F32)).astype(BF)
         for_y, for_x = swap(d_low, 1), swap(d_high, 2)
         a1, b1 = swap(x_low, 1), swap(y_high, 2)
-        x_high, y_low = add(x_high, for_x), add(y_low, for_y)
+        x_high, y_low = plus(x_high, for_x), plus(y_low, for_y)
         a2, b2 = swap(x_high, 1), swap(y_low, 2)
-        low = a1.astype(F32) + b2.astype(F32)
-        high = a2.astype(F32) + b1.astype(F32)
-        return jnp.concatenate([low, high]), [x_high, y_low]
+        return [a1, b2, a2, b1], [x_high, y_low]
     at = lax.axis_index("tensor") % size
     whole = [jnp.concatenate(p) for p in parts[1:]]
     blocks = jnp.stack([jnp.zeros_like(whole[0])] + whole)[jnp.arange(size) ^ at]
-    summed = lax.psum_scatter(blocks, "tensor", scatter_dimension=0, tiled=False, axis_index_groups=groups_of(size))
-    return summed.astype(F32), whole
+    return [lax.psum_scatter(blocks, "tensor", scatter_dimension=0, tiled=False, axis_index_groups=groups_of(size))], whole
+
+
+def plus(a, b):
+    return (a.astype(F32) + b.astype(F32)).astype(BF)
+
+
+def summed(got):
+    got = [v.astype(F32) for v in got]
+    return got[0] if len(got) == 1 else jnp.concatenate([got[0] + got[1], got[2] + got[3]])
 
 
 def scatter_rows(v):
@@ -464,39 +529,45 @@
     token_blocks = gather(tokens, group)
     if square(places):
         dy_y = swap(out_grad, 2)
+    used = q_width + 2 * k_width
+    spare = jnp.zeros((w_query.shape[0], -(used + 2) % LANES), BF)
     qkv_shard = jnp.concatenate(
-        [w_query, w_key, w_value, attn_gain[:, None], mlp_gain[:, None]], axis=1)
+        [w_query, w_key, w_value, attn_gain[:, None], mlp_gain[:, None], spare], axis=1)
     qkv_all = lax.all_gather(qkv_shard, "dp", axis=0, tiled=True)
     if square(places):
         qkv_all, token_blocks, dy_y, later = lax.optimization_barrier((qkv_all, token_blocks, dy_y, out_grad))
         dy_x = swap(later, 1)
-        dy_blocks = [out_grad, dy_x, dy_y, swap(dy_x, 2)]
     else:
-        dy_blocks = [pieces[0] for pieces in gather(out_grad, places)]
-    qkv_w = qkv_all[:, :q_width + 2 * k_width]
-    gain_one = qkv_all[:, q_width + 2 * k_width].astype(F32)
-    gain_two = qkv_all[:, q_width + 2 * k_width + 1].astype(F32)
-    out_w = lax.all_gather(after(w_out, qkv_all), "dp", axis=1, tiled=True)
+        dy_x = None
+    gain_one = qkv_all[:, used].astype(F32)
+    gain_two = qkv_all[:, used + 1].astype(F32)
+    out_wt = lax.all_gather(after(w_out.T, qkv_all), "dp", axis=0, tiled=True)
     gate_w = lax.all_gather(after(w_gate, qkv_all), "dp", axis=0, tiled=True)
     up_w = lax.all_gather(after(w_up, qkv_all), "dp", axis=0, tiled=True)
-    down_wt = lax.all_gather(after(w_down.T, out_w), "dp", axis=0, tiled=True)
-
-    def swap_shared(v, bit):
+    down_wt = lax.all_gather(after(w_down.T, out_wt), "dp", axis=0, tiled=True)
+
+    def core_half(v):
         half = v.shape[0] // 2
-        got = swap(lax.dynamic_slice_in_dim(v, core * half, half, 0), bit)
-        pair = lax.ppermute(got, "dp", [(i, i ^ 1) for i in range(lax.axis_size("dp"))])
-        return by_place(core, got, pair)
+        return lax.dynamic_slice_in_dim(v, core * half, half, 0)
+
+    def other_half(got):
+        return lax.ppermute(got, "dp", [(i, i ^ 1) for i in range(lax.axis_size("dp"))])
+
+    def joined(got, pair):
+        both = jnp.broadcast_to(pair[None], (2, *pair.shape)).reshape(-1, pair.shape[1])
+        return lax.dynamic_update_slice_in_dim(both, got, core * got.shape[0], 0)
 
     others = [group * m for m in range(1, seq_count)]
-    qkv_ws = [qkv_w] + [swap_shared(qkv_w, bits) for bits in others]
-    out_ws = [out_w] + [swap_shared(out_w, bits) for bits in others]
-
-    def share(part, bits):
+    out_sent = core_half(out_wt)
+    qkv_halves = [swap(core_half(qkv_all), bits) for bits in others]
+    out_halves = [swap(out_sent, bits) for bits in others]
+
+    def chip_half(part):
         half = part.shape[0] // 2
         theirs = lax.dynamic_slice_in_dim(part, (1 - core) * half, half, 0)
         theirs = lax.ppermute(theirs, "dp", [(i, i ^ 1) for i in range(lax.axis_size("dp"))])
         mine = lax.dynamic_slice_in_dim(part, core * half, half, 0)
-        return swap((mine.astype(F32) + theirs.astype(F32)).astype(BF), bits)
+        return plus(mine, theirs)
 
     seg_row = lax.dynamic_index_in_dim(segments, place // group, 0, keepdims=False)
     start = doc_starts(seg_row)
@@ -510,96 +581,135 @@
     x_pair = in_order(token_blocks).astype(F32)
     inv_pair = inverse_rms(x_pair)
     n1 = (x_pair * inv_pair * gain_one).astype(BF)
-    kept = []
-    for w in qkv_ws:
-        if kept:
-            w = after(w, kept[0][0])
-        proj = project(n1, w, tables, heads, kv)
+    proj = project(n1, [qkv_all], jnp.zeros((1,), jnp.int32), tables, heads, kv)
+    proj = after(proj, out_sent)
+    o, lse = attend(proj, tables, kv, groups)
+    kept, qkv_ws, out_wts = [(dot_nt(o, spread_q), proj, lse)], [qkv_all], [out_wt]
+    for qkv_got, out_got in zip(qkv_halves, out_halves):
+        qkv_got = after(qkv_got, o)
+        parts = [qkv_got, other_half(qkv_got)]
+        proj = project(n1, parts, jnp.stack([core, 1 - core]).astype(jnp.int32), tables, heads, kv)
         o, lse = attend(proj, tables, kv, groups)
+        out_got = after(out_got, o)
+        out_wts.append(joined(out_got, other_half(out_got)))
+        parts, dy_x = lax.optimization_barrier((parts, dy_x, o))[:2]
+        qkv_ws.append(joined(*parts))
         kept.append((dot_nt(o, spread_q), proj, lse))
+    if square(places):
+        dy_blocks = [out_grad, dy_x, dy_y, swap(dy_x, 2)]
+    else:
+        dy_blocks = [pieces[0] for pieces in gather(out_grad, places)]
     o_flat = jnp.concatenate([k[0] for k in kept], axis=1)
-    out_both = jnp.concatenate(out_ws, axis=0)
+    out_both = jnp.concatenate(out_wts, axis=1)
 
     def rows_of(v, bits):
         return lax.dynamic_slice_in_dim(v, ((place % group) ^ bits) * row_count, row_count, 0)
 
-    branch, _ = scatter([None] + [[dot(rows_of(o_flat, bits), out_both)] for bits in range(1, group)], group)
-    branch, dy_blocks = lax.optimization_barrier((branch, dy_blocks))
-    h = x_own + dot(rows_of(o_flat, 0), out_both, F32) + branch
+    branch, _ = scatter([None] + [[dot_nt(rows_of(o_flat, bits), out_both)] for bits in range(1, group)], group)
+    segs = segments.reshape(-1)
+
+    def masked(v, bits):
+        own = lax.dynamic_slice_in_dim(segs, (place ^ bits) * row_count, row_count, 0)
+        return v * (own >= 0).astype(BF)[:, None]
+
+    dys = [masked(block, bits) for bits, block in enumerate(dy_blocks)]
+    branch, dys = lax.optimization_barrier((branch, dys))
+    h = x_own + dot_nt(rows_of(o_flat, 0), out_both, F32) + summed(branch)
 
     inv_h = inverse_rms(h)
     n2 = (h * inv_h * gain_two).astype(BF)
     n2s = gather(after(n2, gate_w, up_w), places)
-    segs = segments.reshape(-1)
-
-    def masked(v, bits):
-        own = lax.dynamic_slice_in_dim(segs, (place ^ bits) * row_count, row_count, 0)
-        return v * (own >= 0).astype(BF)[:, None]
-
-    dys = [masked(block, bits) for bits, block in enumerate(dy_blocks)]
-    ups = gate_up(n2s[:1], gate_w, up_w)
+    first, qkv_ws = lax.optimization_barrier((n2s[:1], qkv_ws))
+    ups = gate_up(first, gate_w, up_w)
     ups += gate_up(after(n2s[1:places - 1], ups[0]), gate_w, up_w)
     ups += gate_up(after(n2s[places - 1:], ups[1], down_wt), gate_w, up_w)
     n2_pieces = [p for pieces in n2s for p in pieces]
     hiddens = [u[2] for u in ups]
-    down_part, = wgrad(dys, hiddens)
+    down_part = wgrad(dys, hiddens)
     down_grad = lax.psum_scatter(down_part, "dp", scatter_dimension=0, tiled=True)
-    backs, last = [None] * places, down_part
-    for r in reversed(range(places)):
-        backs[r] = gate_up_back(after(dys[r], last), ups[r][0], ups[r][1], gate_w, up_w, down_wt,
-                                *((BF, 2) if r else (F32, 1)))
-        last = backs[r][2]
-    d_n2, sent = scatter([v[2:] for v in backs], places)
-    d_n2 += backs[0][2]
-    gate_part, up_part = wgrad(after(n2_pieces, last, sent), [v[0] for v in backs], [v[1] for v in backs])
+    back_blocks = [(dys[r], *ups[r][:2]) for r in range(places)]
+    far = gate_up_back(after(back_blocks[places - 1:], down_part), gate_w, up_w, down_wt, 2)
+    near = []
+    for first in range(0, places - 1, 3):
+        near += gate_up_back(after(back_blocks[first:min(first + 3, places - 1)], far), gate_w, up_w, down_wt, 2)
+    backs = near + far
+    got, sent = scatter([v[2] for v in backs], places)
+    mlp_parts = [down(v, down_wt, 1)[0] for v in after(hiddens[1:], near)]
+    n2_late = after(n2_pieces, near, sent, got[:1], got[-1:], mlp_parts[:2])
+    gate_part = wgrad(n2_late, [v[0] for v in backs])
     gate_grad = lax.psum_scatter(gate_part, "dp", scatter_dimension=0, tiled=True)
+    up_part = wgrad(after(n2_late, gate_part, got), [v[1] for v in backs])
     up_grad = lax.psum_scatter(up_part, "dp", scatter_dimension=0, tiled=True)
-
+    got = after(got, up_part)
+    d_n2 = summed(got) + jnp.concatenate(backs[0][2]).astype(F32)
     gain_two_grad = jnp.sum(d_n2 * h * inv_h, axis=0)
     dh = dys[0].astype(F32) + norm_back(h, inv_h, gain_two, d_n2)
-
     dhb = dh.astype(BF)
-    hiddens = after(hiddens, dhb)
-    mlp_parts = [down(v, down_wt, 2 if r else 1) for r, v in enumerate(hiddens)]
-    dhb_pair = in_order(after(gather(dhb, group), mlp_parts, down_grad))
-    output = (h + scatter(after(mlp_parts, dhb_pair), places)[0] + mlp_parts[0][0].astype(F32)).astype(BF)
-    back, shares = [], []
+    late_hiddens, late_parts = after((hiddens[:1], mlp_parts[2:]), dhb)
+    mlp_parts = [down(late_hiddens[0], down_wt, 1)[0], *mlp_parts[:2], *late_parts]
+
+    dhb_blocks, mlp_parts, down_grad = lax.optimization_barrier((gather(dhb, group), mlp_parts, down_grad))
+    dhb_pair = in_order(dhb_blocks)
+    out_halves = [chip_half(dot_t(dhb_pair, k[0])) for k in kept[1:]]
+    dhb_pair, mlp_parts = lax.optimization_barrier((dhb_pair, mlp_parts, out_halves))[:2]
+    out_shares = [swap(v, bits) for v, bits in zip(out_halves, others)]
+    if square(places):
+        mlp_x = [swap(mlp_parts[3], 1), swap(mlp_parts[1], 1)]
+    else:
+        mlp_got = scatter([[v] for v in mlp_parts], places)[0]
+    d_projs, qkv_shares = [], []
     for index in reversed(range(len(kept))):
-        (o, proj, lse), w, w_o = kept[index], qkv_ws[index], out_ws[index]
-        out_part = dot_t(dhb_pair, o)
-        d_o = dot(dot_nt(dhb_pair, w_o), spread_q)
+        o, proj, lse = kept[index]
+        d_o = heads_back(dhb_pair, out_wts[index], heads)
         dq, dk, dv = attend_back(proj, d_o, tables, lse, kv, groups)
-        d_proj = jnp.concatenate([dot_nt(dq, spread_q), dot_nt(dk, spread_k), dot_nt(dv, spread_k)], axis=1)
-        qkv_part = dot_t(n1, d_proj)
+        if not index and square(places):
+            dq, far_got = lax.optimization_barrier((dq, mlp_x[0]))
+        spare = jnp.zeros((dq.shape[0], qkv_all.shape[1] - used), BF)
+        d_proj = jnp.concatenate([dot_nt(dq, spread_q), dot_nt(dk, spread_k), dot_nt(dv, spread_k), spare], axis=1)
+        d_projs.insert(0, d_proj)
         if index:
-            shares.append((share(qkv_part, others[index - 1]), share(out_part, others[index - 1])))
-            dhb_pair = after(dhb_pair, qkv_part, out_part)
-        back.append((d_proj, w))
+            half = chip_half(dot_t(n1, d_proj))
+            qkv_shares.append(swap(half, others[index - 1]))
+            dhb_pair = after(dhb_pair, half)
 
     def with_shares(mine, got):
         half = mine.shape[0] // 2
         rows = lax.dynamic_slice_in_dim(mine, core * half, half, 0).astype(F32) + sum(v.astype(F32) for v in got)
         return lax.dynamic_update_slice_in_dim(mine, rows.astype(BF), core * half, 0)
 
-    back, output, gate_grad, up_grad = lax.optimization_barrier((back, output, gate_grad, up_grad))
-    out_grad_w = lax.psum_scatter(with_shares(out_part, [v[1] for v in shares]), "dp", scatter_dimension=0, tiled=True)
-    qkv_grad = lax.psum_scatter(with_shares(qkv_part, [v[0] for v in shares]), "dp", scatter_dimension=0, tiled=True)
-    out_grad_w, qkv_grad = out_grad_w.T.astype(F32), qkv_grad.astype(F32)
-    d_n1_pair = sum(dot_nt(d, w, F32) for d, w in back)
-    gain_one_grad = jnp.sum(d_n1_pair * x_pair * inv_pair, axis=0)
-    d_n1 = rows_of(d_n1_pair, 0) + scatter(
-        [None] + [[rows_of(d_n1_pair, bits).astype(BF)] for bits in range(1, group)], group)[0]
-    input_grad = dh + norm_back(x_own, inv_own, gain_one, d_n1)
-
+    out_part = dot_t(after(dhb_pair, d_projs[0]), kept[0][0])
+    out_grad_w = lax.psum_scatter(with_shares(out_part, out_shares), "dp", scatter_dimension=0, tiled=True)
+    d_all, w_all = jnp.concatenate(d_projs, axis=1), jnp.concatenate(qkv_ws, axis=1)
+    d_n1_parts = [dot_nt(rows_of(d_all, bits), w_all) for bits in range(1, group)]
+    d_n1_got, sent = scatter([None] + [[v] for v in d_n1_parts], group)
+    d_n1_own = dot_nt(rows_of(d_all, 0), w_all, F32)
+    gain_one_grad = jnp.sum(d_n1_own * x_own * inv_own, axis=0) + sum(
+        jnp.sum(v.astype(F32) * token_blocks[bits][0].astype(F32) * rows_of(inv_pair, bits), axis=0)
+        for bits, v in zip(range(1, group), d_n1_parts))
+    if square(places):
+        last_sum = plus(mlp_parts[2], far_got)
+        mlp_got = [mlp_x[1], swap(last_sum, 2)]
+        n1_late = after(n1, sent, mlp_x[1], last_sum, gain_one_grad)
+    else:
+        n1_late = after(n1, sent, gain_one_grad)
+    qkv_part = dot_t(n1_late, d_projs[0])
+
+    qkv_grad = lax.psum_scatter(with_shares(qkv_part, qkv_shares), "dp", scatter_dimension=0, tiled=True)
     gains = scatter_rows(jnp.concatenate(
         [v.reshape(lax.axis_size("dp") * places, -1) for v in (gain_one_grad, gain_two_grad)], axis=1))[0]
+    d_n1_got, mlp_got, gains = lax.optimization_barrier((d_n1_got, mlp_got, gains))
+    output = (h + sum(v.astype(F32) for v in mlp_got) + mlp_parts[0].astype(F32)).astype(BF)
+    input_grad = finish(tokens, gain_one, d_n1_own, summed(d_n1_got) if len(d_n1_got) > 1 else d_n1_got[0], dh)
+    gate_grad, up_grad, out_grad_w, qkv_grad = after((gate_grad, up_grad, out_grad_w, qkv_grad), input_grad)
+    out_grad_w, qkv_grad = out_grad_w.T.astype(F32), qkv_grad.astype(F32)
+
     return (
         output,
         input_grad,
         gains[:gains.shape[0] // 2],
         qkv_grad[:, :q_width],
         qkv_grad[:, q_width:q_width + k_width],
-        qkv_grad[:, q_width + k_width:],
+        qkv_grad[:, q_width + k_width:used],
         out_grad_w,
         gains[gains.shape[0] // 2:],
         gate_grad.astype(F32),

time: 1140 us -> 1030 us (0.904)
  waiting for transfers between devices: 390 us -> 293 us
  Pallas kernels: 390 us -> 453 us
  matrix products: 112 us -> 72.1 us
  other arithmetic: 126 us -> 89.6 us
    ppermute x27 -> x24, waiting for transfers between devices: 339 us -> 241 us  [swap(): lax.ppermute(v, 'tensor', [(i, i ^ bit) for i in range(lax.axis_size('ten...]
    dot_general x4 -> x0, matrix products: 40.9 us -> none  [dot(): return jnp.dot(a, b, preferred_element_type=F32).astype(out)]
    pallas_call x8 -> x10, Pallas kernels: 216 us -> 242 us  [the longest x3 88.1 us: wgrad(): pl.pallas_call(functools.partial(wgrad_kernel, len(a_blocks), lists, tile...]
    pallas_call x2, Pallas kernels: 50.5 us -> 75.3 us  [attend_back(): pl.pallas_call(functools.partial(bwd_kernel, groups, HD ** (-0.5)), grid_...]
    ppermute x4 -> x0, local copies, waits for them, and re-layouts: 16.7 us -> none  [the longest x2 8.36 us: swap(): lax.ppermute(v, 'tensor', [(i, i ^ bit) for i in range(lax.axis_size('ten...]
    select_n x3 -> x1, other arithmetic: 18.6 us -> 4.69 us  [by_place(): jnp.where(bit == 0, jnp.concatenate([mine, other]), jnp.concatenate([othe...]
    pallas_call x2, Pallas kernels: 28.2 us -> 40 us  [attend(): pl.pallas_call(functools.partial(fwd_kernel, groups, HD ** (-0.5)), grid_...]
    ppermute x27 -> x24, starting transfers between devices: 33.2 us -> 32.9 us  [swap(): lax.ppermute(v, 'tensor', [(i, i ^ bit) for i in range(lax.axis_size('ten...]
  transfers between devices with their start and end apart: 46 -> 43, of which waited for: 20 -> 24; matrix products, arithmetic and copies ran while one was open for 25% -> 19% of each run, Pallas kernels for 30% -> 40%
where the time goes in v3:
time: 1030 us; the launch traced here: 1020 us
  Pallas kernels  453 us (44%)
  waiting for transfers between devices  293 us (28%)
  other arithmetic  89.6 us (9%)
  matrix products  72.1 us (7%)
  local copies, waits for them, and re-layouts  59.5 us (6%)
  starting transfers between devices  36.7 us (4%)
  between operations  15.5 us (2%)
    ppermute x24, waiting for transfers between devices, swap(): lax.ppermute(v, 'tensor', [(i, i ^ bit) for i in range(lax.axis_size('ten...  241 us
    pallas_call x3, Pallas kernels, wgrad(): pl.pallas_call(functools.partial(wgrad_kernel, len(a_blocks), lists, tile...  88.1 us
    pallas_call x2, Pallas kernels, gate_up_back(): pl.pallas_call(functools.partial(gate_up_back_kernel, ff, n, parts), grid...  81.8 us
    pallas_call x2, Pallas kernels, attend_back(): pl.pallas_call(functools.partial(bwd_kernel, groups, HD ** (-0.5)), grid_...  75.3 us
    pallas_call x3, Pallas kernels, gate_up(): pl.pallas_call(functools.partial(gate_up_kernel, sizes), grid=(pl.cdiv(ff...  56.6 us
    ppermute x5, waiting for transfers between devices, scatter_rows(): lax.ppermute(jnp.where(bit == 0, high, low), axis, [(i, i ^ size) for i i...  42.1 us
    pallas_call x2, Pallas kernels, project(): pl.pallas_call(functools.partial(project_kernel, heads, kv, len(w_parts))...  41.9 us
    dot_general x12, matrix products, dot_nt(): lax.dot_general(a, b, (((1,), (1,)), ((), ())), preferred_element_type=F32)  41.6 us
  transfers between devices with their start and end apart: 43, of which 24 were waited for; matrix products, arithmetic and copies ran while one was open for 19% of the time, Pallas kernels for 40%

profile of v3, /device:TPU:0, one launch (start us, length us, event | category | flops | bytes accessed | tf_op | source)
XLA Modules:
  0.0 1018.8 jit_solution(3995532135175802810)
XLA Ops:
  17.6 55.3 %collective-permute-done = bf16[512,2560]{1,0:T(8,128)(2,1)S(1)} collective-permute-done((bf16[512,2560]{1,0:T(8,128)(2,1)S(1)}, bf16[512,2560]{1,0:T(8,128)(2,1)S(1)}, u32[]{:S(2)}, u32[]{:S(2)}) %collective-permute-start) | collective-permute-done | bytes 2621472 | tf_op jit(solution)/shard_map/ppermute | solution.py:440
  91.3 9.0 fusion.2.n1_ref
  100.3 20.5 %project.2.qr_ref.kr_ref.vb_ref = bf16[1024,1536]{1,0:T(8,128)(2,1)} custom-call(s32[1]{0:T(128)} %constant.225.clone.1.at_ref, bf16[1024,2560]{1,0:T(8,128)(2,1)} %fusion.2.n1_ref, bf16[640,1024]{1,0:T(8,128)(2,1)} %fusion.12.eq_ref.e_ref, bf16[384,512]{1,0:T(8,128)(2,1)} %pad_convert_fusion.ek_ref, f32[1024,128]{1,0:T(8,128)} %get-tuple-element.299.c_ref, ...), custom_call_target="tpu_custom_call" | custom-call | flops 2013265920 | tf_op jit(solution)/shard_map/project/pallas_call | solution.py:190
  123.7 25.9 %attend.2 = (bf16[1024,1024]{1,0:T(8,128)(2,1)S(1)}, f32[2,1024,4]{2,1,0:T(8,128)S(1)}) custom-call(s32[4]{0:T(128)S(1)} %and_select_fusion.2.lo_ref, bf16[1024,1536]{1,0:T(8,128)(2,1)} %project.2.qr_ref.kr_ref.vb_ref, bf16[1024,1536]{1,0:T(8,128)(2,1)} %project.2.qr_ref.kr_ref.vb_ref, bf16[1024,1536]{1,0:T(8,128)(2,1)} %project.2.qr_ref.kr_ref.vb_ref, ...), custom_call_target="tpu_custom_call" | custom-call | flops 1073741824 | tf_op jit(solution)/shard_map/attend/pallas_call | solution.py:106
  155.8 21.4 %project.3.qr_ref.kr_ref.vb_ref = bf16[1024,1536]{1,0:T(8,128)(2,1)} custom-call(s32[2]{0:T(128)} %pad_add_fusion.at_ref, bf16[1024,2560]{1,0:T(8,128)(2,1)} %fusion.2.n1_ref, bf16[640,1024]{1,0:T(8,128)(2,1)} %fusion.12.eq_ref.e_ref, bf16[384,512]{1,0:T(8,128)(2,1)} %pad_convert_fusion.ek_ref, f32[1024,128]{1,0:T(8,128)} %get-tuple-element.299.c_ref, ...), custom_call_target="tpu_custom_call" | custom-call | flops 2013265920 | tf_op jit(solution)/shard_map/project/pallas_call | solution.py:190
  177.2 14.1 %attend.3 = (bf16[1024,1024]{1,0:T(8,128)(2,1)S(1)}, f32[2,1024,4]{2,1,0:T(8,128)S(1)}) custom-call(s32[4]{0:T(128)S(1)} %and_select_fusion.2.lo_ref, bf16[1024,1536]{1,0:T(8,128)(2,1)} %project.3.qr_ref.kr_ref.vb_ref, bf16[1024,1536]{1,0:T(8,128)(2,1)} %project.3.qr_ref.kr_ref.vb_ref, bf16[1024,1536]{1,0:T(8,128)(2,1)} %project.3.qr_ref.kr_ref.vb_ref, ...), custom_call_target="tpu_custom_call" | custom-call | flops 1073741824 | tf_op jit(solution)/shard_map/attend/pallas_call | solution.py:106
  195.4 15.2 %collective-permute-done.7 = bf16[512,2560]{1,0:T(8,128)(2,1)} collective-permute-done((bf16[512,2560]{1,0:T(8,128)(2,1)}, bf16[512,2560]{1,0:T(8,128)(2,1)}, u32[]{:S(2)}, u32[]{:S(2)}) %collective-permute-start.7) | collective-permute-done | bytes 2621472 | tf_op jit(solution)/shard_map/ppermute | solution.py:440
  218.4 5.0 convolution_convert_fusion.5
  235.8 32.8 %collective-permute-done.8 = bf16[512,2560]{1,0:T(8,128)(2,1)S(1)} collective-permute-done((bf16[512,2560]{1,0:T(8,128)(2,1)}, bf16[512,2560]{1,0:T(8,128)(2,1)S(1)}, u32[]{:S(2)}, u32[]{:S(2)}) %collective-permute-start.8) | collective-permute-done | bytes 2621472 | tf_op jit(solution)/shard_map/ppermute | solution.py:440
  270.3 11.2 %collective-permute-done.6 = bf16[512,2560]{1,0:T(8,128)(2,1)} collective-permute-done((bf16[512,2560]{1,0:T(8,128)(2,1)}, bf16[512,2560]{1,0:T(8,128)(2,1)}, u32[]{:S(2)}, u32[]{:S(2)}) %collective-permute-start.6) | collective-permute-done | bytes 2621472 | tf_op jit(solution)/shard_map/ppermute | solution.py:440
  281.6 6.1 multiply_reduce_fusion.3
  296.2 4.8 broadcast_in_dim.52
  304.7 16.1 %gate_up.3 = (bf16[512,1728]{1,0:T(8,128)(2,1)}, bf16[512,1728]{1,0:T(8,128)(2,1)}, bf16[512,1728]{1,0:T(8,128)(2,1)}) custom-call(bf16[512,2560]{1,0:T(8,128)(2,1)} %copy-done.12, bf16[2560,1728]{1,0:T(8,128)(2,1)} %all-gather.10.cloned.1.call-done.refs_1_.refs_2_.refs_3_.refs_9_, ...), custom_call_target="tpu_custom_call" | custom-call | flops 9059696640 | tf_op jit(solution)/shard_map/gate_up/pallas_call | solution.py:243
  320.9 31.3 %collective-permute-done.10.refs_1_.refs_2_ = bf16[512,2560]{1,0:T(8,128)(2,1)S(1)} collective-permute-done((bf16[512,2560]{1,0:T(8,128)(2,1)S(1)}, bf16[512,2560]{1,0:T(8,128)(2,1)S(1)}, u32[]{:S(2)}, u32[]{:S(2)}) %collective-permute-start.10) | collective-permute-done | bytes 2621472 | tf_op jit(solution)/shard_map/ppermute | solution.py:440
  358.8 24.7 %gate_up.4 = (bf16[512,1728]{1,0:T(8,128)(2,1)}, bf16[512,1728]{1,0:T(8,128)(2,1)}, bf16[512,1728]{1,0:T(8,128)(2,1)}, bf16[512,1728]{1,0:T(8,128)(2,1)}, bf16[5...) custom-call(bf16[512,2560]{1,0:T(8,128)(2,1)} %collective-permute-done.9.refs_0_.refs_1_, bf16[512,2560]{1,0:T(8,128)(2,1)} %copy-done.18, ...), custom_call_target="tpu_custom_call" | custom-call | flops 18119393280 | tf_op jit(solution)/shard_map/gate_up/pallas_call | solution.py:243
  388.6 15.7 %gate_up.5 = (bf16[512,1728]{1,0:T(8,128)(2,1)}, bf16[512,1728]{1,0:T(8,128)(2,1)}, bf16[512,1728]{1,0:T(8,128)(2,1)}) custom-call(bf16[256,2560]{1,0:T(8,128)(2,1)} %copy-done.22, bf16[256,2560]{1,0:T(8,128)(2,1)} %copy-done.23, bf16[2560,1728]{1,0:T(8,128)(2,1)} %all-gather.10.cloned.1.call-done.refs_1_.refs_2_.refs_3_.refs_9_, ...), custom_call_target="tpu_custom_call" | custom-call | flops 9059696640 | tf_op jit(solution)/shard_map/gate_up/pallas_call | solution.py:243
  404.3 29.3 %wgrad.3 = bf16[2560,1728]{1,0:T(8,128)(2,1)} custom-call(bf16[512,2560]{1,0:T(8,128)(2,1)} %broadcast_multiply_fusion.3.refs_0_, bf16[512,2560]{1,0:T(8,128)(2,1)} %broadcast_multiply_fusion.2.refs_1_.refs_3_, bf16[512,2560]{1,0:T(8,128)(2,1)} %broadcast_multiply_fusion.1.refs_2_.refs_6_, bf16[512,2560]{1,0:T(8,128)(2,1)} %broadcast_multiply_fusion.refs_3_.refs_0_, ...), custom_call_target="tpu_custom_call" | custom-call | flops 2264924160 | tf_op jit(solution)/shard_map/wgrad/pallas_call | solution.py:362
  433.7 23.2 %gate_up_back.2 = (bf16[512,1728]{1,0:T(8,128)(2,1)}, bf16[512,1728]{1,0:T(8,128)(2,1)}, bf16[256,2560]{1,0:T(8,128)(2,1)}, bf16[256,2560]{1,0:T(8,128)(2,1)}) custom-call(bf16[512,2560]{1,0:T(8,128)(2,1)} %broadcast_multiply_fusion.refs_3_.refs_0_, bf16[512,1728]{1,0:T(8,128)(2,1)} %get-tuple-element.174.refs_1_, ...), custom_call_target="tpu_custom_call" | custom-call | flops 13589544960 | tf_op jit(solution)/shard_map/gate_up_back/pallas_call | solution.py:297
  458.9 58.6 %gate_up_back.3 = (bf16[512,1728]{1,0:T(8,128)(2,1)}, bf16[512,1728]{1,0:T(8,128)(2,1)}, bf16[512,1728]{1,0:T(8,128)(2,1)}, bf16[512,1728]{1,0:T(8,128)(2,1)}, b...) custom-call(bf16[512,2560]{1,0:T(8,128)(2,1)} %broadcast_multiply_fu, ...), custom_call_target="tpu_custom_call" | custom-call | flops 40768634880 | tf_op jit(solution)/shard_map/gate_up_back/pallas_call | solution.py:297
  519.6 9.7 down.5
  529.3 9.9 down.4
  540.9 5.6 collective-permute-done.13
  546.8 29.3 %wgrad.4 = bf16[2560,1728]{1,0:T(8,128)(2,1)} custom-call(bf16[512,2560]{1,0:T(8,128)(2,1)} %copy-done.12, bf16[512,2560]{1,0:T(8,128)(2,1)} %collective-permute-done.9.refs_0_.refs_1_, bf16[512,2560]{1,0:T(8,128)(2,1)} %copy-done.18, bf16[256,2560]{1,0:T(8,128)(2,1)} %copy-done.22, bf16[256,2560]{1,0:T(8,128)(2,1)} %copy-done.23, ...), custom_call_target="tpu_custom_call" | custom-call | flops 2264924160 | tf_op jit(solution)/shard_map/wgrad/pallas_call | solution.py:362
  579.0 25.0 %collective-permute-done.17 = bf16[256,2560]{1,0:T(8,128)(2,1)} collective-permute-done((bf16[256,2560]{1,0:T(8,128)(2,1)S(1)}, bf16[256,2560]{1,0:T(8,128)(2,1)}, u32[]{:S(2)}, u32[]{:S(2)}) %collective-permute-start.17) | collective-permute-done | bytes 1310752 | tf_op jit(solution)/shard_map/ppermute | solution.py:440
  605.0 29.5 %wgrad.5 = bf16[2560,1728]{1,0:T(8,128)(2,1)} custom-call(bf16[512,2560]{1,0:T(8,128)(2,1)} %copy-done.12, bf16[512,2560]{1,0:T(8,128)(2,1)} %collective-permute-done.9.refs_0_.refs_1_, bf16[512,2560]{1,0:T(8,128)(2,1)} %copy-done.18, bf16[256,2560]{1,0:T(8,128)(2,1)} %copy-done.22, bf16[256,2560]{1,0:T(8,128)(2,1)} %copy-done.23, ...), custom_call_target="tpu_custom_call" | custom-call | flops 2264924160 | tf_op jit(solution)/shard_map/wgrad/pallas_call | solution.py:362
  643.8 6.1 fusion.82
  650.8 9.8 down.6
  660.5 9.7 down.7
  670.3 34.1 %collective-permute-done.19 = bf16[512,2560]{1,0:T(8,128)(2,1)} collective-permute-done((bf16[512,2560]{1,0:T(8,128)(2,1)S(1)}, bf16[512,2560]{1,0:T(8,128)(2,1)}, u32[]{:S(2)}, u32[]{:S(2)}) %collective-permute-start.19) | collective-permute-done | bytes 2621472 | tf_op jit(solution)/shard_map/ppermute | solution.py:440
  704.4 4.7 maximum_select_fusion.1.d_ref
  709.1 4.6 convolution_convert_fusion.3
  718.1 10.1 heads_back.2.do_ref
  728.2 34.5 %attend_back.2 = (bf16[1024,1024]{1,0:T(8,128)(2,1)S(1)}, bf16[1024,256]{1,0:T(8,128)(2,1)S(1)}, bf16[1024,256]{1,0:T(8,128)(2,1)S(1)}) custom-call(s32[4]{0:T(128)S(1)} %copy-done.3, bf16[1024,1536]{1,0:T(8,128)(2,1)} %project.3.qr_ref.kr_ref.vb_ref, bf16[1024,1536]{1,0:T(8,128)(2,1)} %project.3.qr_ref.kr_ref.vb_ref, ...), custom_call_target="tpu_custom_call" | custom-call | flops 10737418240 | tf_op jit(solution)/shard_map/attend_back/pallas_call | solution.py:128
  765.0 10.7 %convolution_convert_fusion.1 = bf16[2560,1024]{1,0:T(8,128)(2,1)S(1)} fusion(bf16[1024,2560]{1,0:T(8,128)(2,1)} %fusion.2.n1_ref, bf16[1024,64]{0,1:T(8,128)(2,1)S(1)} %broadcast.306, bf16[1024,160]{0,1:T(8,128)(2,1)S(1)} %convolution_convert_fusion.8, bf16[1024,160]{0,1:T(8,128)(2,1)S(1)} %convolution_convert_fusion.9, bf16[1024,640]{0,1:T(8,128)(2,1)S(1)} %fusion.24), kind=kOutput, calls=%fused_computation.10 | convolution fusion | flops 5379719168 | bytes 12582912 | tf_op jit(solution)/shard_map/dot_general | solution.py:423
  795.4 6.5 add_convert_fusion.3
  802.5 5.7 convolution_convert_fusion.2
  808.2 18.5 %collective-permute-done.31 = bf16[1280,640]{1,0:T(8,128)(2,1)} collective-permute-done((bf16[1280,640]{1,0:T(8,128)(2,1)S(1)}, bf16[1280,640]{1,0:T(8,128)(2,1)}, u32[]{:S(2)}, u32[]{:S(2)}) %collective-permute-start.31) | collective-permute-done | bytes 1638432 | tf_op jit(solution)/shard_map/ppermute | solution.py:440
  830.3 10.0 heads_back.3.do_ref
  840.3 40.8 %attend_back.3 = (bf16[1024,1024]{1,0:T(8,128)(2,1)S(1)}, bf16[1024,256]{1,0:T(8,128)(2,1)S(1)}, bf16[1024,256]{1,0:T(8,128)(2,1)S(1)}) custom-call(s32[4]{0:T(128)S(1)} %copy-done.3, bf16[1024,1536]{1,0:T(8,128)(2,1)} %project.2.qr_ref.kr_ref.vb_ref, bf16[1024,1536]{1,0:T(8,128)(2,1)} %project.2.qr_ref.kr_ref.vb_ref, ...), custom_call_target="tpu_custom_call" | custom-call | flops 10737418240 | tf_op jit(solution)/shard_map/attend_back/pallas_call | solution.py:128
  894.3 9.1 multiply_reduce_fusion.1
  903.4 5.0 collective-permute-done.24
  908.4 9.5 convolution_convert_fusion
  917.9 5.3 fusion.7
  925.4 11.3 %fusion.5 = (f32[2560]{0:T(1024)S(1)}, f32[512,2560]{1,0:T(8,128)}) fusion(bf16[512,2560]{1,0:T(8,128)(2,1)S(1)} %copy-done.17, f32[512]{0:T(512)S(1)} %add_rsqrt_fusion.1, bf16[2560,2048]{1,0:T(8,128)(2,1)} %copy-done.32, bf16[1024,2048]{0,1:T(8,128)(2,1)} %broadcast_dynamic-update-slice_fusion.1, s32[]{:T(128)S(6)} %select_n.351), kind=kOutput, calls=%fused_computation.13 | convolution fusion | flops 5373949440 | bytes 20459524 | tf_op jit(solution)/shard_map/dot_general | solution.py:427
  937.7 4.5 collective-permute-done.26
  949.7 32.2 %collective-permute-done.29 = f32[2,160]{1,0:T(2,128)S(1)} collective-permute-done((f32[2,160]{1,0:T(2,128)S(1)}, f32[2,160]{1,0:T(2,128)S(1)}, u32[]{:S(2)}, u32[]{:S(2)}) %collective-permute-start.29) | collective-permute-done | bytes 1312 | tf_op jit(solution)/shard_map/ppermute | solution.py:500
  986.2 6.9 add_convert_fusion.1
  993.1 9.7 finish.1
  (340 shorter events, 174.9 us)
Async XLA Ops:
  7.2 67.6 %all-gather.6.cloned.1.call-start = ((), (), s32[]{:S(2)}) async-start(), calls=%async_computation.5 | async-start | bytes 5898240 | tf_op jit(solution)/shard_map/all_gather | solution.py:536
  10.2 66.0 %copy-start.50 = (s32[2,1024]{1,0:T(2,128)S(1)}, s32[2,1024]{1,0:T(2,128)}, u32[]{:S(2)}) copy-start(s32[2,1024]{1,0:T(2,128)} %param.13) | copy-start | bytes 24580
  13.1 107.8 %all-gather.8.cloned.1.call-start = ((), (), s32[]{:S(2)}) async-start(), calls=%async_computation.6 | async-start | bytes 3686400 | tf_op jit(solution)/shard_map/all_gather | solution.py:544
  13.1 59.9 %collective-permute-start = (bf16[512,2560]{1,0:T(8,128)(2,1)S(1)}, bf16[512,2560]{1,0:T(8,128)(2,1)S(1)}, u32[]{:S(2)}, u32[]{:S(2)}) collective-permute-start(bf16[512,2560]{1,0:T(8,128)(2,1)S(1)} %copy-done.14), channel_id=1, source_target_pairs={{0,1},{1,0},{2,3},{3,2},{4,5},{5,4},{6,7},{7,6},{8,9},{9,8},{10,11... | collective-permute-start | bytes 7864328 | tf_op jit(solution)/shard_map/ppermute | solution.py:440
  16.1 58.6 %collective-permute-start.1 = (bf16[512,2560]{1,0:T(8,128)(2,1)}, bf16[512,2560]{1,0:T(8,128)(2,1)}, u32[]{:S(2)}, u32[]{:S(2)}) collective-permute-start(bf16[512,2560]{1,0:T(8,128)(2,1)} %param.23), channel_id=1, source_target_pairs={{0,2},{1,3},{2,0},{3,1},{4,6},{5,7},{6,4},{7,5},{8,10},{9,11},{10,... | collective-permute-start | bytes 7864328 | tf_op jit(solution)/shard_map/ppermute | solution.py:440
  74.8 215.7 %all-gather.10.cloned.1.call-start = ((), (), s32[]{:S(2)}) async-start(), calls=%async_computation.7 | async-start | bytes 10321920 | tf_op jit(solution)/shard_map/all_gather | solution.py:545
  75.5 217.7 %all-gather.12.cloned.1.call-start = ((), (), s32[]{:S(2)}) async-start(), calls=%async_computation.8 | async-start | bytes 10321920 | tf_op jit(solution)/shard_map/all_gather | solution.py:546
  76.1 311.4 %all-gather.14.cloned.1.call-start = ((), (), s32[]{:S(2)}) async-start(), calls=%async_computation.9 | async-start | bytes 10321920 | tf_op jit(solution)/shard_map/all_gather | solution.py:547
  78.4 133.5 %copy-start.53 = (s32[640]{0:T(1024)}, s32[640]{0:T(1024)S(1)}, u32[]{:S(2)}) copy-start(s32[640]{0:T(1024)S(1)} %fusion.54) | copy-start | bytes 7684
  82.0 95.2 %copy-start.2 = (s32[4]{0:T(128)}, s32[4]{0:T(128)S(1)}, u32[]{:S(2)}) copy-start(s32[4]{0:T(128)S(1)} %and_select_fusion.2.lo_ref) | copy-start | bytes 52
  85.3 65.3 %collective-permute-start.2 = (bf16[1280,1024]{1,0:T(8,128)(2,1)}, bf16[1280,1024]{1,0:T(8,128)(2,1)}, u32[]{:S(2)}, u32[]{:S(2)}) collective-permute-start(bf16[1280,1024]{1,0:T(8,128)(2,1)} %constant_dynamic-slice_fusion.4), channel_id=1, source_target_pairs={{0,2},{1,3},{2,0},{3,1},{4,6},{5,7},{6,4},{7,5},{8,10},{9,11},{10,... | collective-permute-start | bytes 7864328 | tf_op jit(solution)/shard_map/ppermute | solution.py:440
  123.6 580.8 %reduce-scatter.6.cloned.1.call-start = ((), (), s32[]{:S(2)}) async-start(), calls=%async_computation.10 | async-start | bytes 10321920 | tf_op jit(solution)/shard_map/reduce_scatter | solution.py:629
  150.5 5.3 collective-permute-start.3
  150.6 43.0 %collective-permute-start.4 = (bf16[1280,640]{1,0:T(8,128)(2,1)}, bf16[1280,640]{1,0:T(8,128)(2,1)}, u32[]{:S(2)}, u32[]{:S(2)}) collective-permute-start(bf16[1280,640]{1,0:T(8,128)(2,1)} %constant_dynamic-slice_fusion.5), channel_id=1, source_target_pairs={{0,2},{1,3},{2,0},{3,1},{4,6},{5,7},{6,4},{7,5},{8,10},{9,11},{10,... | collective-permute-start | bytes 4915208 | tf_op jit(solution)/shard_map/ppermute | solution.py:440
  151.8 58.8 %collective-permute-start.7 = (bf16[512,2560]{1,0:T(8,128)(2,1)}, bf16[512,2560]{1,0:T(8,128)(2,1)}, u32[]{:S(2)}, u32[]{:S(2)}) collective-permute-start(bf16[512,2560]{1,0:T(8,128)(2,1)} %param.23), channel_id=1, source_target_pairs={{0,1},{1,0},{2,3},{3,2},{4,5},{5,4},{6,7},{7,6},{8,9},{9,8},{10,11... | collective-permute-start | bytes 7864328 | tf_op jit(solution)/shard_map/ppermute | solution.py:440
  193.5 20.0 %collective-permute-start.5 = (bf16[1280,640]{1,0:T(8,128)(2,1)}, bf16[1280,640]{1,0:T(8,128)(2,1)}, u32[]{:S(2)}, u32[]{:S(2)}) collective-permute-start(bf16[1280,640]{1,0:T(8,128)(2,1)} %collective-permute-done.4), channel_id=1, source_target_pairs={{0,4},{4,0},{8,12},{12,8},{16,20},{20,16},{24,28},{28,24},{1,5},{5... | collective-permute-start | bytes 4915208 | tf_op jit(solution)/shard_map/ppermute | solution.py:554
  210.6 58.0 %collective-permute-start.8 = (bf16[512,2560]{1,0:T(8,128)(2,1)}, bf16[512,2560]{1,0:T(8,128)(2,1)S(1)}, u32[]{:S(2)}, u32[]{:S(2)}) collective-permute-start(bf16[512,2560]{1,0:T(8,128)(2,1)} %collective-permute-done.7), channel_id=1, source_target_pairs={{0,2},{1,3},{2,0},{3,1},{4,6},{5,7},{6,4},{7,5},{8,10},{9,11},{10,... | collective-permute-start | bytes 7864328 | tf_op jit(solution)/shard_map/ppermute | solution.py:440
  223.4 58.1 %collective-permute-start.6 = (bf16[512,2560]{1,0:T(8,128)(2,1)}, bf16[512,2560]{1,0:T(8,128)(2,1)}, u32[]{:S(2)}, u32[]{:S(2)}) collective-permute-start(bf16[512,2560]{1,0:T(8,128)(2,1)} %convolution_convert_fusion.5), channel_id=1, source_target_pairs={{0,1},{1,0},{2,3},{3,2},{4,5},{5,4},{6,7},{7,6},{8,9},{9,8},{10,11... | collective-permute-start | bytes 7864328 | tf_op jit(solution)/shard_map/ppermute | solution.py:440
  293.2 59.0 %collective-permute-start.10 = (bf16[512,2560]{1,0:T(8,128)(2,1)S(1)}, bf16[512,2560]{1,0:T(8,128)(2,1)S(1)}, u32[]{:S(2)}, u32[]{:S(2)}) collective-permute-start(bf16[512,2560]{1,0:T(8,128)(2,1)S(1)} %multiply_convert_fusion.refs_0_), channel_id=1, source_target_pairs={{0,2},{1,3},{2,0},{3,1},{4,6},{5,7},{6,4},{7,5},{8,10},{9,11},{10,... | collective-permute-start | bytes 7864328 | tf_op jit(solution)/shard_map/ppermute | solution.py:440
  294.7 58.8 %collective-permute-start.9 = (bf16[512,2560]{1,0:T(8,128)(2,1)S(1)}, bf16[512,2560]{1,0:T(8,128)(2,1)}, u32[]{:S(2)}, u32[]{:S(2)}) collective-permute-start(bf16[512,2560]{1,0:T(8,128)(2,1)S(1)} %multiply_convert_fusion.refs_0_), channel_id=1, source_target_pairs={{0,1},{1,0},{2,3},{3,2},{4,5},{5,4},{6,7},{7,6},{8,9},{9,8},{10,11... | collective-permute-start | bytes 7864328 | tf_op jit(solution)/shard_map/ppermute | solution.py:440
  355.0 29.9 %collective-permute-start.11 = (bf16[256,2560]{1,0:T(8,128)(2,1)S(1)}, bf16[256,2560]{1,0:T(8,128)(2,1)S(1)}, u32[]{:S(2)}, u32[]{:S(2)}) collective-permute-start(bf16[256,2560]{1,0:T(8,128)(2,1)S(1)} %slice.63), channel_id=1, source_target_pairs={{0,2},{1,3},{2,0},{3,1},{4,6},{5,7},{6,4},{7,5},{8,10},{9,11},{10,... | collective-permute-start | bytes 3932168 | tf_op jit(solution)/shard_map/ppermute | solution.py:440
  357.3 30.2 %collective-permute-start.12 = (bf16[256,2560]{1,0:T(8,128)(2,1)}, bf16[256,2560]{1,0:T(8,128)(2,1)S(1)}, u32[]{:S(2)}, u32[]{:S(2)}) collective-permute-start(bf16[256,2560]{1,0:T(8,128)(2,1)} %slice.64), channel_id=1, source_target_pairs={{0,1},{1,0},{2,3},{3,2},{4,5},{5,4},{6,7},{7,6},{8,9},{9,8},{10,11... | collective-permute-start | bytes 3932168 | tf_op jit(solution)/shard_map/ppermute | solution.py:440
  433.6 569.1 %reduce-scatter.8.cloned.1.call-start = ((), (), s32[]{:S(2)}) async-start(), calls=%async_computation.11 | async-start | bytes 10321920 | tf_op jit(solution)/shard_map/reduce_scatter | solution.py:640
  456.9 82.3 %collective-permute-start.16 = (bf16[256,2560]{1,0:T(8,128)(2,1)}, bf16[256,2560]{1,0:T(8,128)(2,1)S(1)}, u32[]{:S(2)}, u32[]{:S(2)}) collective-permute-start(bf16[256,2560]{1,0:T(8,128)(2,1)} %get-tuple-element.179), channel_id=1, source_target_pairs={{0,2},{1,3},{2,0},{3,1},{4,6},{5,7},{6,4},{7,5},{8,10},{9,11},{10,... | collective-permute-start | bytes 3932168 | tf_op jit(solution)/shard_map/ppermute | solution.py:440
  457.4 82.2 %collective-permute-start.14 = (bf16[256,2560]{1,0:T(8,128)(2,1)}, bf16[256,2560]{1,0:T(8,128)(2,1)S(1)}, u32[]{:S(2)}, u32[]{:S(2)}) collective-permute-start(bf16[256,2560]{1,0:T(8,128)(2,1)} %get-tuple-element.178), channel_id=1, source_target_pairs={{0,1},{1,0},{2,3},{3,2},{4,5},{5,4},{6,7},{7,6},{8,9},{9,8},{10,11... | collective-permute-start | bytes 3932168 | tf_op jit(solution)/shard_map/ppermute | solution.py:440
  517.4 29.1 %collective-permute-start.13 = (bf16[256,2560]{1,0:T(8,128)(2,1)}, bf16[256,2560]{1,0:T(8,128)(2,1)}, u32[]{:S(2)}, u32[]{:S(2)}) collective-permute-start(bf16[256,2560]{1,0:T(8,128)(2,1)} %get-tuple-element.189), channel_id=1, source_target_pairs={{0,1},{1,0},{2,3},{3,2},{4,5},{5,4},{6,7},{7,6},{8,9},{9,8},{10,11... | collective-permute-start | bytes 3932168 | tf_op jit(solution)/shard_map/ppermute | solution.py:440
  518.0 28.8 %collective-permute-start.18 = (bf16[256,2560]{1,0:T(8,128)(2,1)}, bf16[256,2560]{1,0:T(8,128)(2,1)}, u32[]{:S(2)}, u32[]{:S(2)}) collective-permute-start(bf16[256,2560]{1,0:T(8,128)(2,1)} %get-tuple-element.192), channel_id=1, source_target_pairs={{0,2},{1,3},{2,0},{3,1},{4,6},{5,7},{6,4},{7,5},{8,10},{9,11},{10,... | collective-permute-start | bytes 3932168 | tf_op jit(solution)/shard_map/ppermute | solution.py:440
  576.2 426.6 %reduce-scatter.10.cloned.1.call-start = ((), (), s32[]{:S(2)}) async-start(), calls=%async_computation.12 | async-start | bytes 10321920 | tf_op jit(solution)/shard_map/reduce_scatter | solution.py:642
  576.2 27.8 %collective-permute-start.17 = (bf16[256,2560]{1,0:T(8,128)(2,1)S(1)}, bf16[256,2560]{1,0:T(8,128)(2,1)}, u32[]{:S(2)}, u32[]{:S(2)}) collective-permute-start(bf16[256,2560]{1,0:T(8,128)(2,1)S(1)} %add_convert_fusion.6), channel_id=1, source_target_pairs={{0,1},{1,0},{2,3},{3,2},{4,5},{5,4},{6,7},{7,6},{8,9},{9,8},{10,11... | collective-permute-start | bytes 3932168 | tf_op jit(solution)/shard_map/ppermute | solution.py:440
  577.7 27.3 %collective-permute-start.15 = (bf16[256,2560]{1,0:T(8,128)(2,1)S(1)}, bf16[256,2560]{1,0:T(8,128)(2,1)}, u32[]{:S(2)}, u32[]{:S(2)}) collective-permute-start(bf16[256,2560]{1,0:T(8,128)(2,1)S(1)} %add_convert_fusion.7), channel_id=1, source_target_pairs={{0,2},{1,3},{2,0},{3,1},{4,6},{5,7},{6,4},{7,5},{8,10},{9,11},{10,... | collective-permute-start | bytes 3932168 | tf_op jit(solution)/shard_map/ppermute | solution.py:440
  634.5 368.3 %reduce-scatter.12.cloned.1.call-start = ((), (), s32[]{:S(2)}) async-start(), calls=%async_computation.13 | async-start | bytes 3686400 | tf_op jit(solution)/shard_map/reduce_scatter | solution.py:681
  649.9 54.5 %collective-permute-start.19 = (bf16[512,2560]{1,0:T(8,128)(2,1)S(1)}, bf16[512,2560]{1,0:T(8,128)(2,1)}, u32[]{:S(2)}, u32[]{:S(2)}) collective-permute-start(bf16[512,2560]{1,0:T(8,128)(2,1)S(1)} %get-tuple-element.220), channel_id=1, source_target_pairs={{0,1},{1,0},{2,3},{3,2},{4,5},{5,4},{6,7},{7,6},{8,9},{9,8},{10,11... | collective-permute-start | bytes 7864328 | tf_op jit(solution)/shard_map/ppermute | solution.py:440
  713.8 3.8 collective-permute-start.20
  778.9 16.5 %collective-permute-start.21 = (bf16[1280,1024]{1,0:T(8,128)(2,1)}, bf16[1280,1024]{1,0:T(8,128)(2,1)}, u32[]{:S(2)}, u32[]{:S(2)}) collective-permute-start(bf16[1280,1024]{1,0:T(8,128)(2,1)} %constant_dynamic-slice_fusion), channel_id=1, source_target_pairs={{0,4},{4,0},{8,12},{12,8},{16,20},{20,16},{24,28},{28,24},{1,5},{5... | collective-permute-start | bytes 7864328 | tf_op jit(solution)/shard_map/ppermute | solution.py:568
  786.1 40.6 %collective-permute-start.31 = (bf16[1280,640]{1,0:T(8,128)(2,1)S(1)}, bf16[1280,640]{1,0:T(8,128)(2,1)}, u32[]{:S(2)}, u32[]{:S(2)}) collective-permute-start(bf16[1280,640]{1,0:T(8,128)(2,1)S(1)} %add_convert_fusion.5), channel_id=1, source_target_pairs={{0,2},{1,3},{2,0},{3,1},{4,6},{5,7},{6,4},{7,5},{8,10},{9,11},{10,... | collective-permute-start | bytes 4915208 | tf_op jit(solution)/shard_map/ppermute | solution.py:440
  793.3 87.8 %collective-permute-start.22 = (bf16[512,2560]{1,0:T(8,128)(2,1)}, bf16[512,2560]{1,0:T(8,128)(2,1)}, u32[]{:S(2)}, u32[]{:S(2)}) collective-permute-start(bf16[512,2560]{1,0:T(8,128)(2,1)} %down.6), channel_id=1, source_target_pairs={{0,1},{1,0},{2,3},{3,2},{4,5},{5,4},{6,7},{7,6},{8,9},{9,8},{10,11... | collective-permute-start | bytes 7864328 | tf_op jit(solution)/shard_map/ppermute | solution.py:440
  793.9 114.5 %collective-permute-start.24 = (bf16[512,2560]{1,0:T(8,128)(2,1)}, bf16[512,2560]{1,0:T(8,128)(2,1)}, u32[]{:S(2)}, u32[]{:S(2)}) collective-permute-start(bf16[512,2560]{1,0:T(8,128)(2,1)} %down.4), channel_id=1, source_target_pairs={{0,1},{1,0},{2,3},{3,2},{4,5},{5,4},{6,7},{7,6},{8,9},{9,8},{10,11... | collective-permute-start | bytes 7864328 | tf_op jit(solution)/shard_map/ppermute | solution.py:440
  801.9 116.0 %collective-permute-start.32 = (bf16[1280,1024]{1,0:T(8,128)(2,1)}, bf16[1280,1024]{1,0:T(8,128)(2,1)}, u32[]{:S(2)}, u32[]{:S(2)}) collective-permute-start(bf16[1280,1024]{1,0:T(8,128)(2,1)} %add_convert_fusion.3), channel_id=1, source_target_pairs={{0,2},{1,3},{2,0},{3,1},{4,6},{5,7},{6,4},{7,5},{8,10},{9,11},{10,... | collective-permute-start | bytes 7864328 | tf_op jit(solution)/shard_map/ppermute | solution.py:440
  830.2 172.6 %reduce-scatter.14.cloned.1.call-start = ((), (), s32[]{:S(2)}) async-start(), calls=%async_computation.14 | async-start | bytes 5898240 | tf_op jit(solution)/shard_map/reduce_scatter | solution.py:697
  840.3 53.9 %slice-start.8 = ((s8[10485760]{0:T(1024)(128)(4,1)}), s8[4194304]{0:T(1024)(128)(4,1)S(1)}, s32[]{:S(2)}) async-start(s8[10485760]{0:T(1024)(128)(4,1)} %bitcast.52), calls=%async_computation.23 | async-start | bytes 8388608
  840.3 53.9 %slice-start.9 = ((s8[10485760]{0:T(1024)(128)(4,1)}), s8[4194304]{0:T(1024)(128)(4,1)S(1)}, s32[]{:S(2)}) async-start(s8[10485760]{0:T(1024)(128)(4,1)} %bitcast.52), calls=%async_computation.24 | async-start | bytes 8388608
  924.0 61.6 %collective-permute-start.25 = (bf16[512,2560]{1,0:T(8,128)(2,1)}, bf16[512,2560]{1,0:T(8,128)(2,1)}, u32[]{:S(2)}, u32[]{:S(2)}) collective-permute-start(bf16[512,2560]{1,0:T(8,128)(2,1)} %add_convert_fusion.2), channel_id=1, source_target_pairs={{0,2},{1,3},{2,0},{3,1},{4,6},{5,7},{6,4},{7,5},{8,10},{9,11},{10,... | collective-permute-start | bytes 7864328 | tf_op jit(solution)/shard_map/ppermute | solution.py:440
  924.9 60.7 %collective-permute-start.23 = (bf16[512,2560]{1,0:T(8,128)(2,1)}, bf16[512,2560]{1,0:T(8,128)(2,1)}, u32[]{:S(2)}, u32[]{:S(2)}) collective-permute-start(bf16[512,2560]{1,0:T(8,128)(2,1)} %get-tuple-element.320), channel_id=1, source_target_pairs={{0,1},{1,0},{2,3},{3,2},{4,5},{5,4},{6,7},{7,6},{8,9},{9,8},{10,11... | collective-permute-start | bytes 7864328 | tf_op jit(solution)/shard_map/ppermute | solution.py:440
  936.9 5.3 collective-permute-start.26
  942.3 4.1 collective-permute-start.27
  946.4 1.2 collective-permute-start.28
  947.6 34.3 %collective-permute-start.29 = (f32[2,160]{1,0:T(2,128)S(1)}, f32[2,160]{1,0:T(2,128)S(1)}, u32[]{:S(2)}, u32[]{:S(2)}) collective-permute-start(f32[2,160]{1,0:T(2,128)S(1)} %broadcast_select_fusion.1), channel_id=1, source_target_pairs={{0,2},{1,3},{2,0},{3,1},{4,6},{5,7},{6,4},{7,5},{8,10},{9,11},{10,... | collective-permute-start | bytes 3848 | tf_op jit(solution)/shard_map/ppermute | solution.py:500
  981.9 3.6 collective-permute-start.30
  (71 other events, 746.5 us)
Sparse Core Ops, SparseCore 0:
  13.2 58.7 all-gather.5
  74.9 40.5 all-gather.7
  117.2 87.4 all-gather.9
  206.1 87.0 all-gather.11
  294.7 87.0 all-gather.13
  433.8 94.5 reduce-scatter.5
  576.3 96.0 reduce-scatter.7
  674.7 95.3 reduce-scatter.9
  830.4 39.1 reduce-scatter.11
  923.4 57.0 reduce-scatter.13

commit v4 on v3

--- a/solution.py
+++ b/solution.py
@@ -15,6 +15,7 @@
 NEG = -1e30
 LOG2E = 1.4426950408889634
 BLK = 256
+HEADS_AT_ONCE = 1
 BF = jnp.bfloat16
 F32 = jnp.float32
 
@@ -56,8 +57,10 @@
             @pl.when(lo_ref[i] == j)
             def _():
                 ok = allowed(start_ref[rows, :], i * BLK, BLK, j * BLK, width)
-                for g in range(groups):
-                    lanes = slice(g * LANES, (g + 1) * LANES)
+
+                @pl.loop(0, groups, unroll=HEADS_AT_ONCE)
+                def _(g):
+                    lanes = pl.ds(pl.multiple_of(g * LANES, LANES), LANES)
                     scores = nt(qr_ref[rows, lanes], kr_ref[cols, :]) * (scale * LOG2E)
                     scores = jnp.where(ok, scores, NEG)
                     top = jnp.max(scores, axis=1, keepdims=True)
@@ -65,7 +68,9 @@
                     total = jnp.sum(e, axis=1, keepdims=True)
                     mixed = nn(e.astype(BF), vb_ref[cols, :])
                     o_ref[rows, lanes] = (mixed / total).astype(BF)
-                    lse_ref[rows, g:g + 1] = top + jnp.log2(total)
+                    lse = lse_ref[rows, :]
+                    here = lax.broadcasted_iota(jnp.int32, lse.shape, 1) == g
+                    lse_ref[rows, :] = jnp.where(here, top + jnp.log2(total), lse)
 
 
 def bwd_kernel(groups, scale, lo_ref, qr_ref, kr_ref, vb_ref, do_ref, c_ref, s_ref, start_ref, lse_ref,
@@ -82,12 +87,17 @@
             @pl.when(lo_ref[i] == j)
             def _():
                 ok = allowed(start_ref[rows, :], i * BLK, BLK, j * BLK, width)
-                for g in range(groups):
-                    lanes = slice(g * LANES, (g + 1) * LANES)
+
+                @pl.loop(0, groups, unroll=HEADS_AT_ONCE)
+                def _(g):
+                    lanes = pl.ds(pl.multiple_of(g * LANES, LANES), LANES)
+                    lse = lse_ref[rows, :]
+                    here = lax.broadcasted_iota(jnp.int32, lse.shape, 1) == g
+                    lse = jnp.sum(jnp.where(here, lse, 0.0), axis=1, keepdims=True)
                     q, do = qr_ref[rows, lanes], do_ref[rows, lanes]
                     k, v = kr_ref[cols, :], vb_ref[cols, :]
                     scores = nt(q, k) * (scale * LOG2E)
-                    p = jnp.exp2(jnp.where(ok, scores, NEG) - lse_ref[rows, g:g + 1])
+                    p = jnp.exp2(jnp.where(ok, scores, NEG) - lse)
                     pd = p * nt(do, v)
                     ds = (pd - p * jnp.sum(pd, axis=1, keepdims=True)).astype(BF)
                     dq = nn(ds, k) * scale
@@ -137,7 +147,7 @@
         ),
         out_shape=[out(wide), out(LANES), out(LANES)],
         compiler_params=pltpu.CompilerParams(vmem_limit_bytes=48 * 2 ** 20),
-        cost_estimate=cost(10 * kv * groups * rows * rows * LANES),
+        cost_estimate=cost(4 * kv * groups * rows * rows * LANES),
         name="attend_back",
     )(lo, proj, proj, proj, d_o, cos_t, sin_t, start, lse)
 
@@ -586,14 +596,13 @@
     o, lse = attend(proj, tables, kv, groups)
     kept, qkv_ws, out_wts = [(dot_nt(o, spread_q), proj, lse)], [qkv_all], [out_wt]
     for qkv_got, out_got in zip(qkv_halves, out_halves):
-        qkv_got = after(qkv_got, o)
+        qkv_got, dy_x = lax.optimization_barrier((qkv_got, dy_x, o))[:2]
         parts = [qkv_got, other_half(qkv_got)]
         proj = project(n1, parts, jnp.stack([core, 1 - core]).astype(jnp.int32), tables, heads, kv)
         o, lse = attend(proj, tables, kv, groups)
         out_got = after(out_got, o)
         out_wts.append(joined(out_got, other_half(out_got)))
-        parts, dy_x = lax.optimization_barrier((parts, dy_x, o))[:2]
-        qkv_ws.append(joined(*parts))
+        qkv_ws.append(joined(*after(parts, o)))
         kept.append((dot_nt(o, spread_q), proj, lse))
     if square(places):
         dy_blocks = [out_grad, dy_x, dy_y, swap(dy_x, 2)]
@@ -618,7 +627,7 @@
 
     inv_h = inverse_rms(h)
     n2 = (h * inv_h * gain_two).astype(BF)
-    n2s = gather(after(n2, gate_w, up_w), places)
+    n2s = gather(after(n2, gate_w), places)
     first, qkv_ws = lax.optimization_barrier((n2s[:1], qkv_ws))
     ups = gate_up(first, gate_w, up_w)
     ups += gate_up(after(n2s[1:places - 1], ups[0]), gate_w, up_w)
@@ -662,13 +671,15 @@
         o, proj, lse = kept[index]
         d_o = heads_back(dhb_pair, out_wts[index], heads)
         dq, dk, dv = attend_back(proj, d_o, tables, lse, kv, groups)
-        if not index and square(places):
-            dq, far_got = lax.optimization_barrier((dq, mlp_x[0]))
         spare = jnp.zeros((dq.shape[0], qkv_all.shape[1] - used), BF)
         d_proj = jnp.concatenate([dot_nt(dq, spread_q), dot_nt(dk, spread_k), dot_nt(dv, spread_k), spare], axis=1)
         d_projs.insert(0, d_proj)
+        last_dq = dq
         if index:
-            half = chip_half(dot_t(n1, d_proj))
+            part = dot_t(n1, d_proj)
+            if square(places):
+                part, far_got, out_shares = lax.optimization_barrier((part, mlp_x[0], out_shares))
+            half = chip_half(part)
             qkv_shares.append(swap(half, others[index - 1]))
             dhb_pair = after(dhb_pair, half)
 
@@ -677,9 +688,10 @@
         rows = lax.dynamic_slice_in_dim(mine, core * half, half, 0).astype(F32) + sum(v.astype(F32) for v in got)
         return lax.dynamic_update_slice_in_dim(mine, rows.astype(BF), core * half, 0)
 
-    out_part = dot_t(after(dhb_pair, d_projs[0]), kept[0][0])
+    out_part = dot_t(after(dhb_pair, last_dq), kept[0][0])
     out_grad_w = lax.psum_scatter(with_shares(out_part, out_shares), "dp", scatter_dimension=0, tiled=True)
     d_all, w_all = jnp.concatenate(d_projs, axis=1), jnp.concatenate(qkv_ws, axis=1)
+    d_all, qkv_shares = lax.optimization_barrier((d_all, qkv_shares))
     d_n1_parts = [dot_nt(rows_of(d_all, bits), w_all) for bits in range(1, group)]
     d_n1_got, sent = scatter([None] + [[v] for v in d_n1_parts], group)
     d_n1_own = dot_nt(rows_of(d_all, 0), w_all, F32)
@@ -689,15 +701,16 @@
     if square(places):
         last_sum = plus(mlp_parts[2], far_got)
         mlp_got = [mlp_x[1], swap(last_sum, 2)]
-        n1_late = after(n1, sent, mlp_x[1], last_sum, gain_one_grad)
+        n1_late = after(n1, sent, mlp_x[1], last_sum, d_n1_own)
     else:
-        n1_late = after(n1, sent, gain_one_grad)
+        n1_late = after(n1, sent, d_n1_own)
     qkv_part = dot_t(n1_late, d_projs[0])
 
     qkv_grad = lax.psum_scatter(with_shares(qkv_part, qkv_shares), "dp", scatter_dimension=0, tiled=True)
+    d_n1_got, mlp_got = lax.optimization_barrier((d_n1_got, mlp_got))
+    gain_one_grad, gain_two_grad = after((gain_one_grad, gain_two_grad), d_n1_got)
     gains = scatter_rows(jnp.concatenate(
         [v.reshape(lax.axis_size("dp") * places, -1) for v in (gain_one_grad, gain_two_grad)], axis=1))[0]
-    d_n1_got, mlp_got, gains = lax.optimization_barrier((d_n1_got, mlp_got, gains))
     output = (h + sum(v.astype(F32) for v in mlp_got) + mlp_parts[0].astype(F32)).astype(BF)
     input_grad = finish(tokens, gain_one, d_n1_own, summed(d_n1_got) if len(d_n1_got) > 1 else d_n1_got[0], dh)
     gate_grad, up_grad, out_grad_w, qkv_grad = after((gate_grad, up_grad, out_grad_w, qkv_grad), input_grad)

time: 1030 us -> 979 us (0.950)
  Pallas kernels: 453 us -> 436 us
  waiting for transfers between devices: 293 us -> 278 us
    ppermute x5, waiting for transfers between devices: 42.1 us -> 8.42 us  [scatter_rows(): lax.ppermute(jnp.where(bit == 0, high, low), axis, [(i, i ^ size) for i i...]
    pallas_call x2, Pallas kernels: 75.3 us -> 58.9 us  [attend_back(): pl.pallas_call(functools.partial(bwd_kernel, groups, HD ** (-0.5)), grid_...]
    all_gather x1, waiting for transfers between devices: 0.01 us -> 14 us  [body(): down_wt = lax.all_gather(after(w_down.T, out_wt), 'dp', axis=0, tiled=True)]
    unnamed x162 -> x154, local copies, waits for them, and re-layouts: 24.1 us -> 22.2 us
  transfers between devices with their start and end apart: 43 -> 43, of which waited for: 24 -> 22; matrix products, arithmetic and copies ran while one was open for 19% -> 19% of each run, Pallas kernels for 40% -> 40%
where the time goes in v4:
time: 979 us; the launch traced here: 971 us
  Pallas kernels  436 us (45%)
  waiting for transfers between devices  278 us (28%)
  other arithmetic  84.4 us (9%)
  matrix products  72.1 us (7%)
  local copies, waits for them, and re-layouts  56.7 us (6%)
  starting transfers between devices  28.2 us (3%)
  between operations  15.6 us (2%)
    ppermute x24, waiting for transfers between devices, swap(): lax.ppermute(v, 'tensor', [(i, i ^ bit) for i in range(lax.axis_size('ten...  240 us
    pallas_call x3, Pallas kernels, wgrad(): pl.pallas_call(functools.partial(wgrad_kernel, len(a_blocks), lists, tile...  88.4 us
    pallas_call x2, Pallas kernels, gate_up_back(): pl.pallas_call(functools.partial(gate_up_back_kernel, ff, n, parts), grid...  81.8 us
    pallas_call x2, Pallas kernels, attend_back(): pl.pallas_call(functools.partial(bwd_kernel, groups, HD ** (-0.5)), grid_...  58.9 us
    pallas_call x3, Pallas kernels, gate_up(): pl.pallas_call(functools.partial(gate_up_kernel, sizes), grid=(pl.cdiv(ff...  56.6 us
    pallas_call x2, Pallas kernels, project(): pl.pallas_call(functools.partial(project_kernel, heads, kv, len(w_parts))...  42 us
    pallas_call x4, Pallas kernels, down(): pl.pallas_call(down_kernel, grid=(pl.cdiv(d, size),), in_specs=[pl.BlockS...  39.4 us
    pallas_call x2, Pallas kernels, attend(): pl.pallas_call(functools.partial(fwd_kernel, groups, HD ** (-0.5)), grid_...  38.9 us
  transfers between devices with their start and end apart: 43, of which 22 were waited for; matrix products, arithmetic and copies ran while one was open for 19% of the time, Pallas kernels for 40%

profile of v4, /device:TPU:0, one launch (start us, length us, event | category | flops | bytes accessed | tf_op | source)
XLA Modules:
  0.0 971.2 jit_solution(16905723552084775332)
XLA Ops:
  17.6 55.3 %collective-permute-done = bf16[512,2560]{1,0:T(8,128)(2,1)S(1)} collective-permute-done((bf16[512,2560]{1,0:T(8,128)(2,1)S(1)}, bf16[512,2560]{1,0:T(8,128)(2,1)S(1)}, u32[]{:S(2)}, u32[]{:S(2)}) %collective-permute-start) | collective-permute-done | bytes 2621472 | tf_op jit(solution)/shard_map/ppermute | solution.py:450
  92.6 9.0 fusion.2.n1_ref
  101.6 20.5 %project.2.qr_ref.kr_ref.vb_ref = bf16[1024,1536]{1,0:T(8,128)(2,1)} custom-call(s32[1]{0:T(128)} %constant.225.clone.1.at_ref, bf16[1024,2560]{1,0:T(8,128)(2,1)} %fusion.2.n1_ref, bf16[640,1024]{1,0:T(8,128)(2,1)} %fusion.12.eq_ref.e_ref, bf16[384,512]{1,0:T(8,128)(2,1)} %pad_convert_fusion.ek_ref, f32[1024,128]{1,0:T(8,128)} %get-tuple-element.307.c_ref, ...), custom_call_target="tpu_custom_call" | custom-call | flops 2013265920 | tf_op jit(solution)/shard_map/project/pallas_call | solution.py:200
  125.1 19.4 %attend.2 = (bf16[1024,1024]{1,0:T(8,128)(2,1)S(1)}, f32[2,1024,4]{2,1,0:T(8,128)S(1)}) custom-call(s32[4]{0:T(128)S(1)} %and_select_fusion.2.lo_ref, bf16[1024,1536]{1,0:T(8,128)(2,1)} %project.2.qr_ref.kr_ref.vb_ref, bf16[1024,1536]{1,0:T(8,128)(2,1)} %project.2.qr_ref.kr_ref.vb_ref, bf16[1024,1536]{1,0:T(8,128)(2,1)} %project.2.qr_ref.kr_ref.vb_ref, ...), custom_call_target="tpu_custom_call" | custom-call | flops 1073741824 | tf_op jit(solution)/shard_map/attend/pallas_call | solution.py:116
  150.8 21.5 %project.3.qr_ref.kr_ref.vb_ref = bf16[1024,1536]{1,0:T(8,128)(2,1)} custom-call(s32[2]{0:T(128)} %pad_add_fusion.at_ref, bf16[1024,2560]{1,0:T(8,128)(2,1)} %fusion.2.n1_ref, bf16[640,1024]{1,0:T(8,128)(2,1)} %fusion.12.eq_ref.e_ref, bf16[384,512]{1,0:T(8,128)(2,1)} %pad_convert_fusion.ek_ref, f32[1024,128]{1,0:T(8,128)} %get-tuple-element.307.c_ref, ...), custom_call_target="tpu_custom_call" | custom-call | flops 2013265920 | tf_op jit(solution)/shard_map/project/pallas_call | solution.py:200
  172.3 19.5 %attend.3 = (bf16[1024,1024]{1,0:T(8,128)(2,1)S(1)}, f32[2,1024,4]{2,1,0:T(8,128)S(1)}) custom-call(s32[4]{0:T(128)S(1)} %and_select_fusion.2.lo_ref, bf16[1024,1536]{1,0:T(8,128)(2,1)} %project.3.qr_ref.kr_ref.vb_ref, bf16[1024,1536]{1,0:T(8,128)(2,1)} %project.3.qr_ref.kr_ref.vb_ref, bf16[1024,1536]{1,0:T(8,128)(2,1)} %project.3.qr_ref.kr_ref.vb_ref, ...), custom_call_target="tpu_custom_call" | custom-call | flops 1073741824 | tf_op jit(solution)/shard_map/attend/pallas_call | solution.py:116
  202.6 5.3 convolution_convert_fusion.5
  219.6 34.3 %collective-permute-done.8 = bf16[512,2560]{1,0:T(8,128)(2,1)} collective-permute-done((bf16[512,2560]{1,0:T(8,128)(2,1)}, bf16[512,2560]{1,0:T(8,128)(2,1)}, u32[]{:S(2)}, u32[]{:S(2)}) %collective-permute-start.8) | collective-permute-done | bytes 2621472 | tf_op jit(solution)/shard_map/ppermute | solution.py:450
  257.5 9.6 collective-permute-done.7
  267.1 5.9 multiply_reduce_fusion.3
  278.2 4.8 broadcast_in_dim.52
  286.5 6.7 all-gather.12.cloned.1.call-done.refs_2_.refs_3_.refs_4_.refs_10_
  293.2 16.0 %gate_up.3 = (bf16[512,1728]{1,0:T(8,128)(2,1)}, bf16[512,1728]{1,0:T(8,128)(2,1)}, bf16[512,1728]{1,0:T(8,128)(2,1)}) custom-call(bf16[512,2560]{1,0:T(8,128)(2,1)} %copy-done.14, bf16[2560,1728]{1,0:T(8,128)(2,1)} %all-gather.10.cloned.1.call-done.refs_1_.refs_2_.refs_3_.refs_9_, ...), custom_call_target="tpu_custom_call" | custom-call | flops 9059696640 | tf_op jit(solution)/shard_map/gate_up/pallas_call | solution.py:253
  309.2 25.0 %collective-permute-done.10.refs_1_.refs_2_ = bf16[512,2560]{1,0:T(8,128)(2,1)} collective-permute-done((bf16[512,2560]{1,0:T(8,128)(2,1)S(1)}, bf16[512,2560]{1,0:T(8,128)(2,1)}, u32[]{:S(2)}, u32[]{:S(2)}) %collective-permute-start.10) | collective-permute-done | bytes 2621472 | tf_op jit(solution)/shard_map/ppermute | solution.py:450
  339.6 24.8 %gate_up.4 = (bf16[512,1728]{1,0:T(8,128)(2,1)}, bf16[512,1728]{1,0:T(8,128)(2,1)}, bf16[512,1728]{1,0:T(8,128)(2,1)}, bf16[512,1728]{1,0:T(8,128)(2,1)}, bf16[5...) custom-call(bf16[512,2560]{1,0:T(8,128)(2,1)} %collective-permute-done.9.refs_0_.refs_1_, ...), custom_call_target="tpu_custom_call" | custom-call | flops 18119393280 | tf_op jit(solution)/shard_map/gate_up/pallas_call | solution.py:253
  367.7 14.0 %all-gather.14.cloned.1.call-done.refs_5_.refs_11_.w_ref = bf16[2560,1728]{1,0:T(8,128)(2,1)} async-done(((bf16[320,1728]{1,0:T(8,128)(2,1)}), bf16[2560,1728]{1,0:T(8,128)(2,1)}) %all-gather.14.cloned.1.call-update) | async-done | bytes 8847376 | tf_op jit(solution)/shard_map/all_gather | solution.py:557
  381.8 15.8 %gate_up.5 = (bf16[512,1728]{1,0:T(8,128)(2,1)}, bf16[512,1728]{1,0:T(8,128)(2,1)}, bf16[512,1728]{1,0:T(8,128)(2,1)}) custom-call(bf16[256,2560]{1,0:T(8,128)(2,1)} %copy-done.23, bf16[256,2560]{1,0:T(8,128)(2,1)} %copy-done.24, bf16[2560,1728]{1,0:T(8,128)(2,1)} %all-gather.10.cloned.1.call-done.refs_1_.refs_2_.refs_3_.refs_9_, ...), custom_call_target="tpu_custom_call" | custom-call | flops 9059696640 | tf_op jit(solution)/shard_map/gate_up/pallas_call | solution.py:253
  397.5 29.6 %wgrad.3 = bf16[2560,1728]{1,0:T(8,128)(2,1)} custom-call(bf16[512,2560]{1,0:T(8,128)(2,1)} %broadcast_multiply_fusion.3.refs_0_, bf16[512,2560]{1,0:T(8,128)(2,1)} %broadcast_multiply_fusion.2.refs_1_.refs_3_, bf16[512,2560]{1,0:T(8,128)(2,1)} %broadcast_multiply_fusion.1.refs_2_.refs_6_, bf16[512,2560]{1,0:T(8,128)(2,1)} %broadcast_multiply_fusion.refs_3_.refs_0_, ...), custom_call_target="tpu_custom_call" | custom-call | flops 2264924160 | tf_op jit(solution)/shard_map/wgrad/pallas_call | solution.py:372
  427.2 23.1 %gate_up_back.2 = (bf16[512,1728]{1,0:T(8,128)(2,1)}, bf16[512,1728]{1,0:T(8,128)(2,1)}, bf16[256,2560]{1,0:T(8,128)(2,1)}, bf16[256,2560]{1,0:T(8,128)(2,1)}) custom-call(bf16[512,2560]{1,0:T(8,128)(2,1)} %broadcast_multiply_fusion.refs_3_.refs_0_, bf16[512,1728]{1,0:T(8,128)(2,1)} %get-tuple-element.178.refs_1_, ...), custom_call_target="tpu_custom_call" | custom-call | flops 13589544960 | tf_op jit(solution)/shard_map/gate_up_back/pallas_call | solution.py:307
  453.4 58.7 %gate_up_back.3 = (bf16[512,1728]{1,0:T(8,128)(2,1)}, bf16[512,1728]{1,0:T(8,128)(2,1)}, bf16[512,1728]{1,0:T(8,128)(2,1)}, bf16[512,1728]{1,0:T(8,128)(2,1)}, b...) custom-call(bf16[512,2560]{1,0:T(8,128)(2,1)} %broadcast_multiply_fu, ...), custom_call_target="tpu_custom_call" | custom-call | flops 40768634880 | tf_op jit(solution)/shard_map/gate_up_back/pallas_call | solution.py:307
  513.1 9.9 %down.5 = bf16[512,2560]{1,0:T(8,128)(2,1)} custom-call(bf16[512,1728]{1,0:T(8,128)(2,1)} %get-tuple-element.206.refs_6_.h_ref, bf16[2560,1728]{1,0:T(8,128)(2,1)} %all-gather.14.cloned.1.call-done.refs_5_.refs_11_.w_ref), custom_call_target="tpu_custom_call" | custom-call | flops 4529848320 | tf_op jit(solution)/shard_map/down/pallas_call | solution.py:331
  523.0 9.8 %down.4 = bf16[512,2560]{1,0:T(8,128)(2,1)} custom-call(bf16[512,1728]{1,0:T(8,128)(2,1)} %get-tuple-element.205.refs_5_.h_ref, bf16[2560,1728]{1,0:T(8,128)(2,1)} %all-gather.14.cloned.1.call-done.refs_5_.refs_11_.w_ref), custom_call_target="tpu_custom_call" | custom-call | flops 4529848320 | tf_op jit(solution)/shard_map/down/pallas_call | solution.py:331
  534.5 8.2 collective-permute-done.13
  543.0 29.3 %wgrad.4 = bf16[2560,1728]{1,0:T(8,128)(2,1)} custom-call(bf16[512,2560]{1,0:T(8,128)(2,1)} %copy-done.14, bf16[512,2560]{1,0:T(8,128)(2,1)} %collective-permute-done.9.refs_0_.refs_1_, bf16[512,2560]{1,0:T(8,128)(2,1)} %collective-permute-done.10.refs_1_.refs_2_, bf16[256,2560]{1,0:T(8,128)(2,1)} %copy-done.23, bf16[256,2560]{1,0:T(8,128)(2,1)} %copy-done.24, ...), custom_call_target="tpu_custom_call" | custom-call | flops 2264924160 | tf_op jit(solution)/shard_map/wgrad/pallas_call | solution.py:372
  574.5 27.3 %collective-permute-done.17 = bf16[256,2560]{1,0:T(8,128)(2,1)} collective-permute-done((bf16[256,2560]{1,0:T(8,128)(2,1)S(1)}, bf16[256,2560]{1,0:T(8,128)(2,1)}, u32[]{:S(2)}, u32[]{:S(2)}) %collective-permute-start.17) | collective-permute-done | bytes 1310752 | tf_op jit(solution)/shard_map/ppermute | solution.py:450
  602.8 29.5 %wgrad.5 = bf16[2560,1728]{1,0:T(8,128)(2,1)} custom-call(bf16[512,2560]{1,0:T(8,128)(2,1)} %copy-done.14, bf16[512,2560]{1,0:T(8,128)(2,1)} %collective-permute-done.9.refs_0_.refs_1_, bf16[512,2560]{1,0:T(8,128)(2,1)} %collective-permute-done.10.refs_1_.refs_2_, bf16[256,2560]{1,0:T(8,128)(2,1)} %copy-done.23, bf16[256,2560]{1,0:T(8,128)(2,1)} %copy-done.24, ...), custom_call_target="tpu_custom_call" | custom-call | flops 2264924160 | tf_op jit(solution)/shard_map/wgrad/pallas_call | solution.py:372
  641.8 6.0 fusion.88
  648.4 9.9 %down.6 = bf16[512,2560]{1,0:T(8,128)(2,1)} custom-call(bf16[512,1728]{1,0:T(8,128)(2,1)} %get-tuple-element.221.refs_7_.h_ref, bf16[2560,1728]{1,0:T(8,128)(2,1)} %all-gather.14.cloned.1.call-done.refs_5_.refs_11_.w_ref), custom_call_target="tpu_custom_call" | custom-call | flops 4529848320 | tf_op jit(solution)/shard_map/down/pallas_call | solution.py:331
  658.3 9.8 %down.7 = bf16[512,2560]{1,0:T(8,128)(2,1)} custom-call(bf16[512,1728]{1,0:T(8,128)(2,1)} %get-tuple-element.222.refs_4_.h_ref, bf16[2560,1728]{1,0:T(8,128)(2,1)} %all-gather.14.cloned.1.call-done.refs_5_.refs_11_.w_ref), custom_call_target="tpu_custom_call" | custom-call | flops 4529848320 | tf_op jit(solution)/shard_map/down/pallas_call | solution.py:331
  668.0 35.6 %collective-permute-done.19 = bf16[512,2560]{1,0:T(8,128)(2,1)} collective-permute-done((bf16[512,2560]{1,0:T(8,128)(2,1)S(1)}, bf16[512,2560]{1,0:T(8,128)(2,1)}, u32[]{:S(2)}, u32[]{:S(2)}) %collective-permute-start.19) | collective-permute-done | bytes 2621472 | tf_op jit(solution)/shard_map/ppermute | solution.py:450
  720.1 10.0 %heads_back.2.do_ref = bf16[1024,1024]{1,0:T(8,128)(2,1)} custom-call(bf16[1024,2560]{1,0:T(8,128)(2,1)} %copy-done.29, bf16[2560,640]{1,0:T(8,128)(2,1)} %copy-done.30, bf16[640,1024]{1,0:T(8,128)(2,1)} %fusion.12.eq_ref.e_ref), custom_call_target="tpu_custom_call" | custom-call | flops 4697620480 | tf_op jit(solution)/shard_map/heads_back/pallas_call | solution.py:222
  730.0 29.4 %attend_back.2 = (bf16[1024,1024]{1,0:T(8,128)(2,1)S(1)}, bf16[1024,256]{1,0:T(8,128)(2,1)S(1)}, bf16[1024,256]{1,0:T(8,128)(2,1)S(1)}) custom-call(s32[4]{0:T(128)S(1)} %and_select_fusion.2.lo_ref, bf16[1024,1536]{1,0:T(8,128)(2,1)} %project.3.qr_ref.kr_ref.vb_ref, bf16[1024,1536]{1,0:T(8,128)(2,1)} %project.3.qr_ref.kr_ref.vb_ref, ...), custom_call_target="tpu_custom_call" | custom-call | flops 4294967296 | tf_op jit(solution)/shard_map/attend_back/pallas_call | solution.py:138
  762.5 10.4 %convolution_convert_fusion.1 = bf16[2560,1024]{1,0:T(8,128)(2,1)S(1)} fusion(bf16[1024,2560]{1,0:T(8,128)(2,1)} %fusion.2.n1_ref, bf16[1024,64]{0,1:T(8,128)(2,1)S(1)} %broadcast.306, bf16[1024,160]{0,1:T(8,128)(2,1)S(1)} %convolution_convert_fusion.8, bf16[1024,160]{0,1:T(8,128)(2,1)S(1)} %convolution_convert_fusion.9, bf16[1024,640]{0,1:T(8,128)(2,1)S(1)} %fusion.29), kind=kOutput, calls=%fused_computation.10 | convolution fusion | flops 5379719168 | bytes 12582912 | tf_op jit(solution)/shard_map/dot_general | solution.py:433
  772.9 5.2 collective-permute-done.21
  783.3 5.5 constant_dynamic-update-slice_fusion.6
  793.5 9.9 %heads_back.3.do_ref = bf16[1024,1024]{1,0:T(8,128)(2,1)} custom-call(bf16[1024,2560]{1,0:T(8,128)(2,1)} %copy-done.29, bf16[2560,640]{1,0:T(8,128)(2,1)} %all-gather.8.cloned.1.call-done.w_ref, bf16[640,1024]{1,0:T(8,128)(2,1)} %fusion.12.eq_ref.e_ref), custom_call_target="tpu_custom_call" | custom-call | flops 4697620480 | tf_op jit(solution)/shard_map/heads_back/pallas_call | solution.py:222
  803.5 29.4 %attend_back.3 = (bf16[1024,1024]{1,0:T(8,128)(2,1)S(1)}, bf16[1024,256]{1,0:T(8,128)(2,1)S(1)}, bf16[1024,256]{1,0:T(8,128)(2,1)S(1)}) custom-call(s32[4]{0:T(128)S(1)} %copy-done.3, bf16[1024,1536]{1,0:T(8,128)(2,1)} %project.2.qr_ref.kr_ref.vb_ref, bf16[1024,1536]{1,0:T(8,128)(2,1)} %project.2.qr_ref.kr_ref.vb_ref, ...), custom_call_target="tpu_custom_call" | custom-call | flops 4294967296 | tf_op jit(solution)/shard_map/attend_back/pallas_call | solution.py:138
  832.9 9.3 convolution_convert_fusion.2
  845.8 4.8 add_convert_fusion.2
  856.6 9.9 %multiply_reduce_fusion.1 = (f32[2560]{0:T(1024)S(1)}, bf16[512,2560]{1,0:T(8,128)(2,1)}) fusion(bf16[512,2560]{1,0:T(8,128)(2,1)S(1)} %copy-done.22, f32[512]{0:T(512)S(1)} %dynamic-slice.3, bf16[2560,2048]{1,0:T(8,128)(2,1)S(1)} %bitcast.56, bf16[1024,2048]{0,1:T(8,128)(2,1)} %copy-done.55, s32[]{:T(128)S(6)} %select_n.352), kind=kOutput, calls=%fused_computation.20 | convolution fusion | flops 5376570880 | bytes 17838084 | tf_op jit(solution)/shard_map/dot_general | solution.py:437
  867.9 9.6 fusion.5
  877.5 9.7 convolution_convert_fusion
  887.2 5.4 fusion.7
  892.6 16.0 %collective-permute-done.27 = bf16[512,2560]{1,0:T(8,128)(2,1)} collective-permute-done((bf16[512,2560]{1,0:T(8,128)(2,1)}, bf16[512,2560]{1,0:T(8,128)(2,1)}, u32[]{:S(2)}, u32[]{:S(2)}) %collective-permute-start.27) | collective-permute-done | bytes 2621472 | tf_op jit(solution)/shard_map/ppermute | solution.py:450
  908.6 16.8 %collective-permute-done.25.got_ref = bf16[512,2560]{1,0:T(8,128)(2,1)} collective-permute-done((bf16[512,2560]{1,0:T(8,128)(2,1)}, bf16[512,2560]{1,0:T(8,128)(2,1)}, u32[]{:S(2)}, u32[]{:S(2)}) %collective-permute-start.25) | collective-permute-done | bytes 2621472 | tf_op jit(solution)/shard_map/ppermute | solution.py:450
  926.0 5.0 collective-permute-done.28
  937.2 10.5 %finish.1 = f32[512,2560]{1,0:T(8,128)} custom-call(bf16[512,2560]{1,0:T(8,128)(2,1)} %x_ref.1, f32[1,2560]{1,0:T(1,128)} %reshape.250.gain_ref, f32[512,2560]{1,0:T(8,128)} %get-tuple-element.326.own_ref, bf16[512,2560]{1,0:T(8,128)(2,1)} %collective-permute-done.25.got_ref, f32[512,2560]{1,0:T(8,128)} %get-tuple-element.301.dh_ref), custom_call_target="tpu_custom_call" | custom-call | flops 51999997952 | tf_op jit(solution)/shard_map/finish/pallas_call | solution.py:395
  949.1 5.4 add_convert_fusion.1
  (332 shorter events, 159.6 us)
Async XLA Ops:
  7.2 67.6 %all-gather.6.cloned.1.call-start = ((), (), s32[]{:S(2)}) async-start(), calls=%async_computation.5 | async-start | bytes 5898240 | tf_op jit(solution)/shard_map/all_gather | solution.py:546
  10.2 66.0 %copy-start.50 = (s32[2,1024]{1,0:T(2,128)S(1)}, s32[2,1024]{1,0:T(2,128)}, u32[]{:S(2)}) copy-start(s32[2,1024]{1,0:T(2,128)} %param.13) | copy-start | bytes 24580
  13.1 109.1 %all-gather.8.cloned.1.call-start = ((), (), s32[]{:S(2)}) async-start(), calls=%async_computation.6 | async-start | bytes 3686400 | tf_op jit(solution)/shard_map/all_gather | solution.py:554
  13.1 59.9 %collective-permute-start = (bf16[512,2560]{1,0:T(8,128)(2,1)S(1)}, bf16[512,2560]{1,0:T(8,128)(2,1)S(1)}, u32[]{:S(2)}, u32[]{:S(2)}) collective-permute-start(bf16[512,2560]{1,0:T(8,128)(2,1)S(1)} %copy-done.16), channel_id=1, source_target_pairs={{0,1},{1,0},{2,3},{3,2},{4,5},{5,4},{6,7},{7,6},{8,9},{9,8},{10,11... | collective-permute-start | bytes 7864328 | tf_op jit(solution)/shard_map/ppermute | solution.py:450
  16.1 58.6 %collective-permute-start.1 = (bf16[512,2560]{1,0:T(8,128)(2,1)}, bf16[512,2560]{1,0:T(8,128)(2,1)}, u32[]{:S(2)}, u32[]{:S(2)}) collective-permute-start(bf16[512,2560]{1,0:T(8,128)(2,1)} %param.23), channel_id=1, source_target_pairs={{0,2},{1,3},{2,0},{3,1},{4,6},{5,7},{6,4},{7,5},{8,10},{9,11},{10,... | collective-permute-start | bytes 7864328 | tf_op jit(solution)/shard_map/ppermute | solution.py:450
  74.8 201.1 %all-gather.10.cloned.1.call-start = ((), (), s32[]{:S(2)}) async-start(), calls=%async_computation.7 | async-start | bytes 10321920 | tf_op jit(solution)/shard_map/all_gather | solution.py:555
  75.5 217.7 %all-gather.12.cloned.1.call-start = ((), (), s32[]{:S(2)}) async-start(), calls=%async_computation.8 | async-start | bytes 10321920 | tf_op jit(solution)/shard_map/all_gather | solution.py:556
  76.1 305.7 %all-gather.14.cloned.1.call-start = ((), (), s32[]{:S(2)}) async-start(), calls=%async_computation.9 | async-start | bytes 10321920 | tf_op jit(solution)/shard_map/all_gather | solution.py:557
  78.4 117.9 %copy-start.53 = (s32[640]{0:T(1024)}, s32[640]{0:T(1024)S(1)}, u32[]{:S(2)}) copy-start(s32[640]{0:T(1024)S(1)} %fusion.59) | copy-start | bytes 7684
  82.0 648.0 %copy-start.2 = (s32[4]{0:T(128)}, s32[4]{0:T(128)S(1)}, u32[]{:S(2)}) copy-start(s32[4]{0:T(128)S(1)} %and_select_fusion.2.lo_ref) | copy-start | bytes 52
  85.3 60.2 %collective-permute-start.2 = (bf16[1280,1024]{1,0:T(8,128)(2,1)}, bf16[1280,1024]{1,0:T(8,128)(2,1)}, u32[]{:S(2)}, u32[]{:S(2)}) collective-permute-start(bf16[1280,1024]{1,0:T(8,128)(2,1)} %constant_dynamic-slice_fusion.4), channel_id=1, source_target_pairs={{0,2},{1,3},{2,0},{3,1},{4,6},{5,7},{6,4},{7,5},{8,10},{9,11},{10,... | collective-permute-start | bytes 7864328 | tf_op jit(solution)/shard_map/ppermute | solution.py:450
  86.9 58.7 %collective-permute-start.3 = (bf16[512,2560]{1,0:T(8,128)(2,1)}, bf16[512,2560]{1,0:T(8,128)(2,1)}, u32[]{:S(2)}, u32[]{:S(2)}) collective-permute-start(bf16[512,2560]{1,0:T(8,128)(2,1)} %param.23), channel_id=1, source_target_pairs={{0,1},{1,0},{2,3},{3,2},{4,5},{5,4},{6,7},{7,6},{8,9},{9,8},{10,11... | collective-permute-start | bytes 7864328 | tf_op jit(solution)/shard_map/ppermute | solution.py:450
  125.1 578.5 %reduce-scatter.6.cloned.1.call-start = ((), (), s32[]{:S(2)}) async-start(), calls=%async_computation.10 | async-start | bytes 10321920 | tf_op jit(solution)/shard_map/reduce_scatter | solution.py:638
  145.6 5.3 collective-permute-start.4
  145.6 48.5 %collective-permute-start.5 = (bf16[1280,640]{1,0:T(8,128)(2,1)}, bf16[1280,640]{1,0:T(8,128)(2,1)}, u32[]{:S(2)}, u32[]{:S(2)}) collective-permute-start(bf16[1280,640]{1,0:T(8,128)(2,1)} %constant_dynamic-slice_fusion.5), channel_id=1, source_target_pairs={{0,2},{1,3},{2,0},{3,1},{4,6},{5,7},{6,4},{7,5},{8,10},{9,11},{10,... | collective-permute-start | bytes 4915208 | tf_op jit(solution)/shard_map/ppermute | solution.py:450
  194.1 3.9 collective-permute-start.6
  194.2 59.6 %collective-permute-start.8 = (bf16[512,2560]{1,0:T(8,128)(2,1)}, bf16[512,2560]{1,0:T(8,128)(2,1)}, u32[]{:S(2)}, u32[]{:S(2)}) collective-permute-start(bf16[512,2560]{1,0:T(8,128)(2,1)} %collective-permute-done.3), channel_id=1, source_target_pairs={{0,2},{1,3},{2,0},{3,1},{4,6},{5,7},{6,4},{7,5},{8,10},{9,11},{10,... | collective-permute-start | bytes 7864328 | tf_op jit(solution)/shard_map/ppermute | solution.py:450
  198.0 69.1 %copy-start.59 = (bf16[1024,640]{0,1:T(8,128)(2,1)}, bf16[1024,640]{0,1:T(8,128)(2,1)S(1)}, u32[]{:S(2)}) copy-start(bf16[1024,640]{0,1:T(8,128)(2,1)S(1)} %fusion.28) | copy-start | bytes 3932164
  207.9 59.1 %collective-permute-start.7 = (bf16[512,2560]{1,0:T(8,128)(2,1)}, bf16[512,2560]{1,0:T(8,128)(2,1)}, u32[]{:S(2)}, u32[]{:S(2)}) collective-permute-start(bf16[512,2560]{1,0:T(8,128)(2,1)} %convolution_convert_fusion.5), channel_id=1, source_target_pairs={{0,1},{1,0},{2,3},{3,2},{4,5},{5,4},{6,7},{7,6},{8,9},{9,8},{10,11... | collective-permute-start | bytes 7864328 | tf_op jit(solution)/shard_map/ppermute | solution.py:450
  215.9 51.2 %copy-start.44 = (bf16[2560,640]{1,0:T(8,128)(2,1)S(1)}, bf16[2560,640]{1,0:T(8,128)(2,1)}, u32[]{:S(2)}) copy-start(bf16[2560,640]{1,0:T(8,128)(2,1)} %all-gather.8.cloned.1.call-done.w_ref) | copy-start | bytes 9830404
  275.9 58.3 %collective-permute-start.10 = (bf16[512,2560]{1,0:T(8,128)(2,1)S(1)}, bf16[512,2560]{1,0:T(8,128)(2,1)}, u32[]{:S(2)}, u32[]{:S(2)}) collective-permute-start(bf16[512,2560]{1,0:T(8,128)(2,1)S(1)} %multiply_convert_fusion.refs_0_), channel_id=1, source_target_pairs={{0,2},{1,3},{2,0},{3,1},{4,6},{5,7},{6,4},{7,5},{8,10},{9,11},{10,... | collective-permute-start | bytes 7864328 | tf_op jit(solution)/shard_map/ppermute | solution.py:450
  277.7 57.9 %collective-permute-start.9 = (bf16[512,2560]{1,0:T(8,128)(2,1)S(1)}, bf16[512,2560]{1,0:T(8,128)(2,1)}, u32[]{:S(2)}, u32[]{:S(2)}) collective-permute-start(bf16[512,2560]{1,0:T(8,128)(2,1)S(1)} %multiply_convert_fusion.refs_0_), channel_id=1, source_target_pairs={{0,1},{1,0},{2,3},{3,2},{4,5},{5,4},{6,7},{7,6},{8,9},{9,8},{10,11... | collective-permute-start | bytes 7864328 | tf_op jit(solution)/shard_map/ppermute | solution.py:450
  337.1 28.9 %collective-permute-start.11 = (bf16[256,2560]{1,0:T(8,128)(2,1)S(1)}, bf16[256,2560]{1,0:T(8,128)(2,1)S(1)}, u32[]{:S(2)}, u32[]{:S(2)}) collective-permute-start(bf16[256,2560]{1,0:T(8,128)(2,1)S(1)} %slice.71), channel_id=1, source_target_pairs={{0,2},{1,3},{2,0},{3,1},{4,6},{5,7},{6,4},{7,5},{8,10},{9,11},{10,... | collective-permute-start | bytes 3932168 | tf_op jit(solution)/shard_map/ppermute | solution.py:450
  338.9 28.8 %collective-permute-start.12 = (bf16[256,2560]{1,0:T(8,128)(2,1)S(1)}, bf16[256,2560]{1,0:T(8,128)(2,1)S(1)}, u32[]{:S(2)}, u32[]{:S(2)}) collective-permute-start(bf16[256,2560]{1,0:T(8,128)(2,1)S(1)} %slice.72), channel_id=1, source_target_pairs={{0,1},{1,0},{2,3},{3,2},{4,5},{5,4},{6,7},{7,6},{8,9},{9,8},{10,11... | collective-permute-start | bytes 3932168 | tf_op jit(solution)/shard_map/ppermute | solution.py:450
  427.1 528.0 %reduce-scatter.8.cloned.1.call-start = ((), (), s32[]{:S(2)}) async-start(), calls=%async_computation.11 | async-start | bytes 10321920 | tf_op jit(solution)/shard_map/reduce_scatter | solution.py:649
  450.3 82.5 %collective-permute-start.16 = (bf16[256,2560]{1,0:T(8,128)(2,1)}, bf16[256,2560]{1,0:T(8,128)(2,1)S(1)}, u32[]{:S(2)}, u32[]{:S(2)}) collective-permute-start(bf16[256,2560]{1,0:T(8,128)(2,1)} %get-tuple-element.183), channel_id=1, source_target_pairs={{0,2},{1,3},{2,0},{3,1},{4,6},{5,7},{6,4},{7,5},{8,10},{9,11},{10,... | collective-permute-start | bytes 3932168 | tf_op jit(solution)/shard_map/ppermute | solution.py:450
  451.9 81.3 %collective-permute-start.14 = (bf16[256,2560]{1,0:T(8,128)(2,1)}, bf16[256,2560]{1,0:T(8,128)(2,1)S(1)}, u32[]{:S(2)}, u32[]{:S(2)}) collective-permute-start(bf16[256,2560]{1,0:T(8,128)(2,1)} %get-tuple-element.182), channel_id=1, source_target_pairs={{0,1},{1,0},{2,3},{3,2},{4,5},{5,4},{6,7},{7,6},{8,9},{9,8},{10,11... | collective-permute-start | bytes 3932168 | tf_op jit(solution)/shard_map/ppermute | solution.py:450
  512.1 30.7 %collective-permute-start.13 = (bf16[256,2560]{1,0:T(8,128)(2,1)}, bf16[256,2560]{1,0:T(8,128)(2,1)}, u32[]{:S(2)}, u32[]{:S(2)}) collective-permute-start(bf16[256,2560]{1,0:T(8,128)(2,1)} %get-tuple-element.193), channel_id=1, source_target_pairs={{0,1},{1,0},{2,3},{3,2},{4,5},{5,4},{6,7},{7,6},{8,9},{9,8},{10,11... | collective-permute-start | bytes 3932168 | tf_op jit(solution)/shard_map/ppermute | solution.py:450
  512.6 30.4 %collective-permute-start.18 = (bf16[256,2560]{1,0:T(8,128)(2,1)}, bf16[256,2560]{1,0:T(8,128)(2,1)}, u32[]{:S(2)}, u32[]{:S(2)}) collective-permute-start(bf16[256,2560]{1,0:T(8,128)(2,1)} %get-tuple-element.196), channel_id=1, source_target_pairs={{0,2},{1,3},{2,0},{3,1},{4,6},{5,7},{6,4},{7,5},{8,10},{9,11},{10,... | collective-permute-start | bytes 3932168 | tf_op jit(solution)/shard_map/ppermute | solution.py:450
  572.4 382.8 %reduce-scatter.10.cloned.1.call-start = ((), (), s32[]{:S(2)}) async-start(), calls=%async_computation.12 | async-start | bytes 10321920 | tf_op jit(solution)/shard_map/reduce_scatter | solution.py:651
  572.4 29.3 %collective-permute-start.17 = (bf16[256,2560]{1,0:T(8,128)(2,1)S(1)}, bf16[256,2560]{1,0:T(8,128)(2,1)}, u32[]{:S(2)}, u32[]{:S(2)}) collective-permute-start(bf16[256,2560]{1,0:T(8,128)(2,1)S(1)} %add_convert_fusion.6), channel_id=1, source_target_pairs={{0,1},{1,0},{2,3},{3,2},{4,5},{5,4},{6,7},{7,6},{8,9},{9,8},{10,11... | collective-permute-start | bytes 3932168 | tf_op jit(solution)/shard_map/ppermute | solution.py:450
  573.9 28.9 %collective-permute-start.15 = (bf16[256,2560]{1,0:T(8,128)(2,1)S(1)}, bf16[256,2560]{1,0:T(8,128)(2,1)}, u32[]{:S(2)}, u32[]{:S(2)}) collective-permute-start(bf16[256,2560]{1,0:T(8,128)(2,1)S(1)} %add_convert_fusion.7), channel_id=1, source_target_pairs={{0,2},{1,3},{2,0},{3,1},{4,6},{5,7},{6,4},{7,5},{8,10},{9,11},{10,... | collective-permute-start | bytes 3932168 | tf_op jit(solution)/shard_map/ppermute | solution.py:450
  632.4 322.8 %reduce-scatter.12.cloned.1.call-start = ((), (), s32[]{:S(2)}) async-start(), calls=%async_computation.13 | async-start | bytes 3686400 | tf_op jit(solution)/shard_map/reduce_scatter | solution.py:692
  647.8 55.8 %collective-permute-start.19 = (bf16[512,2560]{1,0:T(8,128)(2,1)S(1)}, bf16[512,2560]{1,0:T(8,128)(2,1)}, u32[]{:S(2)}, u32[]{:S(2)}) collective-permute-start(bf16[512,2560]{1,0:T(8,128)(2,1)S(1)} %get-tuple-element.224), channel_id=1, source_target_pairs={{0,1},{1,0},{2,3},{3,2},{4,5},{5,4},{6,7},{7,6},{8,9},{9,8},{10,11... | collective-permute-start | bytes 7864328 | tf_op jit(solution)/shard_map/ppermute | solution.py:450
  713.0 3.6 collective-permute-start.20
  718.2 54.7 %collective-permute-start.22 = (bf16[1280,640]{1,0:T(8,128)(2,1)}, bf16[1280,640]{1,0:T(8,128)(2,1)}, u32[]{:S(2)}, u32[]{:S(2)}) collective-permute-start(bf16[1280,640]{1,0:T(8,128)(2,1)} %add_convert_fusion.5), channel_id=1, source_target_pairs={{0,2},{1,3},{2,0},{3,1},{4,6},{5,7},{6,4},{7,5},{8,10},{9,11},{10,... | collective-permute-start | bytes 4915208 | tf_op jit(solution)/shard_map/ppermute | solution.py:450
  719.3 58.8 %collective-permute-start.21 = (bf16[512,2560]{1,0:T(8,128)(2,1)}, bf16[512,2560]{1,0:T(8,128)(2,1)S(1)}, u32[]{:S(2)}, u32[]{:S(2)}) collective-permute-start(bf16[512,2560]{1,0:T(8,128)(2,1)} %down.6), channel_id=1, source_target_pairs={{0,1},{1,0},{2,3},{3,2},{4,5},{5,4},{6,7},{7,6},{8,9},{9,8},{10,11... | collective-permute-start | bytes 7864328 | tf_op jit(solution)/shard_map/ppermute | solution.py:450
  779.6 10.0 %collective-permute-start.23 = (bf16[1280,1024]{1,0:T(8,128)(2,1)S(1)}, bf16[1280,1024]{1,0:T(8,128)(2,1)S(1)}, u32[]{:S(2)}, u32[]{:S(2)}) collective-permute-start(bf16[1280,1024]{1,0:T(8,128)(2,1)S(1)} %constant_dynamic-slice_fusion), channel_id=1, source_target_pairs={{0,4},{4,0},{8,12},{12,8},{16,20},{20,16},{24,28},{28,24},{1,5},{5... | collective-permute-start | bytes 7864328 | tf_op jit(solution)/shard_map/ppermute | solution.py:578
  788.8 88.7 %collective-permute-start.26 = (bf16[512,2560]{1,0:T(8,128)(2,1)}, bf16[512,2560]{1,0:T(8,128)(2,1)}, u32[]{:S(2)}, u32[]{:S(2)}) collective-permute-start(bf16[512,2560]{1,0:T(8,128)(2,1)} %down.4), channel_id=1, source_target_pairs={{0,1},{1,0},{2,3},{3,2},{4,5},{5,4},{6,7},{7,6},{8,9},{9,8},{10,11... | collective-permute-start | bytes 7864328 | tf_op jit(solution)/shard_map/ppermute | solution.py:450
  792.3 64.3 %collective-permute-start.24 = (bf16[1280,1024]{1,0:T(8,128)(2,1)}, bf16[1280,1024]{1,0:T(8,128)(2,1)}, u32[]{:S(2)}, u32[]{:S(2)}) collective-permute-start(bf16[1280,1024]{1,0:T(8,128)(2,1)} %add_convert_fusion.3), channel_id=1, source_target_pairs={{0,2},{1,3},{2,0},{3,1},{4,6},{5,7},{6,4},{7,5},{8,10},{9,11},{10,... | collective-permute-start | bytes 7864328 | tf_op jit(solution)/shard_map/ppermute | solution.py:450
  845.7 109.5 %reduce-scatter.14.cloned.1.call-start = ((), (), s32[]{:S(2)}) async-start(), calls=%async_computation.14 | async-start | bytes 5898240 | tf_op jit(solution)/shard_map/reduce_scatter | solution.py:709
  850.6 58.0 %collective-permute-start.27 = (bf16[512,2560]{1,0:T(8,128)(2,1)}, bf16[512,2560]{1,0:T(8,128)(2,1)}, u32[]{:S(2)}, u32[]{:S(2)}) collective-permute-start(bf16[512,2560]{1,0:T(8,128)(2,1)} %add_convert_fusion.2), channel_id=1, source_target_pairs={{0,2},{1,3},{2,0},{3,1},{4,6},{5,7},{6,4},{7,5},{8,10},{9,11},{10,... | collective-permute-start | bytes 7864328 | tf_op jit(solution)/shard_map/ppermute | solution.py:450
  866.5 58.9 %collective-permute-start.25 = (bf16[512,2560]{1,0:T(8,128)(2,1)}, bf16[512,2560]{1,0:T(8,128)(2,1)}, u32[]{:S(2)}, u32[]{:S(2)}) collective-permute-start(bf16[512,2560]{1,0:T(8,128)(2,1)} %get-tuple-element.328), channel_id=1, source_target_pairs={{0,1},{1,0},{2,3},{3,2},{4,5},{5,4},{6,7},{7,6},{8,9},{9,8},{10,11... | collective-permute-start | bytes 7864328 | tf_op jit(solution)/shard_map/ppermute | solution.py:450
  925.7 5.3 collective-permute-start.28
  931.1 4.1 collective-permute-start.29
  935.2 1.6 collective-permute-start.30
  936.9 10.8 %collective-permute-start.31 = (f32[2,160]{1,0:T(2,128)S(1)}, f32[2,160]{1,0:T(2,128)S(1)}, u32[]{:S(2)}, u32[]{:S(2)}) collective-permute-start(f32[2,160]{1,0:T(2,128)S(1)} %broadcast_select_fusion.1), channel_id=1, source_target_pairs={{0,2},{1,3},{2,0},{3,1},{4,6},{5,7},{6,4},{7,5},{8,10},{9,11},{10,... | collective-permute-start | bytes 3848 | tf_op jit(solution)/shard_map/ppermute | solution.py:510
  947.7 6.9 collective-permute-start.32
  (67 other events, 612.7 us)
Sparse Core Ops, SparseCore 0:
  13.2 58.7 all-gather.5
  74.9 40.5 all-gather.7
  117.2 87.4 all-gather.9
  206.1 87.0 all-gather.11
  294.7 87.0 all-gather.13
  427.2 95.5 reduce-scatter.5
  572.5 95.1 reduce-scatter.7
  670.0 95.3 reduce-scatter.9
  845.8 42.7 reduce-scatter.11
  892.7 60.8 reduce-scatter.13

commit v5 on v4

--- a/solution.py
+++ b/solution.py
@@ -334,7 +334,7 @@
         in_specs=[pl.BlockSpec((rows, ff), lambda i: (0, 0)), pl.BlockSpec((size, ff), lambda i: (i, 0))],
         out_specs=[pl.BlockSpec((rows // parts, size), lambda i: (0, i))] * parts,
         out_shape=[jax.ShapeDtypeStruct((rows // parts, d), BF)] * parts,
-        compiler_params=params(), cost_estimate=cost(2 * rows * d * ff), name="down",
+        compiler_params=params(), cost_estimate=cost(0), name="down",
     )(hidden, w_down_t)
 
 
@@ -631,7 +631,7 @@
     first, qkv_ws = lax.optimization_barrier((n2s[:1], qkv_ws))
     ups = gate_up(first, gate_w, up_w)
     ups += gate_up(after(n2s[1:places - 1], ups[0]), gate_w, up_w)
-    ups += gate_up(after(n2s[places - 1:], ups[1], down_wt), gate_w, up_w)
+    ups += gate_up(after(n2s[places - 1:], ups[1]), gate_w, up_w)
     n2_pieces = [p for pieces in n2s for p in pieces]
     hiddens = [u[2] for u in ups]
     down_part = wgrad(dys, hiddens)
@@ -639,15 +639,16 @@
     back_blocks = [(dys[r], *ups[r][:2]) for r in range(places)]
     far = gate_up_back(after(back_blocks[places - 1:], down_part), gate_w, up_w, down_wt, 2)
     near = []
-    for first in range(0, places - 1, 3):
-        near += gate_up_back(after(back_blocks[first:min(first + 3, places - 1)], far), gate_w, up_w, down_wt, 2)
-    backs = near + far
-    got, sent = scatter([v[2] for v in backs], places)
-    mlp_parts = [down(v, down_wt, 1)[0] for v in after(hiddens[1:], near)]
-    n2_late = after(n2_pieces, near, sent, got[:1], got[-1:], mlp_parts[:2])
+    for first in range(1, places - 1, 2):
+        near += gate_up_back(after(back_blocks[first:min(first + 2, places - 1)], far), gate_w, up_w, down_wt, 2)
+    got, sent = scatter([None, *(v[2] for v in near + far)], places)
+    own = gate_up_back(after(back_blocks[:1], near, sent), gate_w, up_w, down_wt, 2)
+    backs = own + near + far
+    mlp_parts = [down(v, down_wt, 1)[0] for v in after(hiddens[1:], own)]
+    n2_late, got = lax.optimization_barrier((n2_pieces, got, own, mlp_parts[:2]))[:2]
     gate_part = wgrad(n2_late, [v[0] for v in backs])
     gate_grad = lax.psum_scatter(gate_part, "dp", scatter_dimension=0, tiled=True)
-    up_part = wgrad(after(n2_late, gate_part, got), [v[1] for v in backs])
+    up_part = wgrad(after(n2_late, gate_part), [v[1] for v in backs])
     up_grad = lax.psum_scatter(up_part, "dp", scatter_dimension=0, tiled=True)
     got = after(got, up_part)
     d_n2 = summed(got) + jnp.concatenate(backs[0][2]).astype(F32)

time: 979 us -> 947 us (0.967)
  waiting for transfers between devices: 278 us -> 234 us
  Pallas kernels: 436 us -> 454 us
    ppermute x24, waiting for transfers between devices: 240 us -> 211 us  [swap(): lax.ppermute(v, 'tensor', [(i, i ^ bit) for i in range(lax.axis_size('ten...]
    all_gather x1, waiting for transfers between devices: 14 us -> 0.02 us  [body(): down_wt = lax.all_gather(after(w_down.T, out_wt), 'dp', axis=0, tiled=True)]
    pallas_call x2 -> x3, Pallas kernels: 81.8 us -> 88.7 us  [gate_up_back(): pl.pallas_call(functools.partial(gate_up_back_kernel, ff, n, parts), grid...]
    unnamed x154 -> x152, local copies, waits for them, and re-layouts: 22.2 us -> 22.4 us
  transfers between devices with their start and end apart: 43 -> 43, of which waited for: 22 -> 19; matrix products, arithmetic and copies ran while one was open for 19% -> 19% of each run, Pallas kernels for 40% -> 48%
where the time goes in v5:
time: 947 us; the launch traced here: 943 us
  Pallas kernels  454 us (48%)
  waiting for transfers between devices  234 us (25%)
  other arithmetic  85.9 us (9%)
  matrix products  71.5 us (8%)
  local copies, waits for them, and re-layouts  56.4 us (6%)
  starting transfers between devices  25.4 us (3%)
  between operations  15.6 us (2%)
    ppermute x24, waiting for transfers between devices, swap(): lax.ppermute(v, 'tensor', [(i, i ^ bit) for i in range(lax.axis_size('ten...  211 us
    pallas_call x3, Pallas kernels, gate_up_back(): pl.pallas_call(functools.partial(gate_up_back_kernel, ff, n, parts), grid...  88.7 us
    pallas_call x3, Pallas kernels, wgrad(): pl.pallas_call(functools.partial(wgrad_kernel, len(a_blocks), lists, tile...  88.3 us
    pallas_call x2, Pallas kernels, attend_back(): pl.pallas_call(functools.partial(bwd_kernel, groups, HD ** (-0.5)), grid_...  65.6 us
    pallas_call x3, Pallas kernels, gate_up(): pl.pallas_call(functools.partial(gate_up_kernel, sizes), grid=(pl.cdiv(ff...  57.1 us
    pallas_call x2, Pallas kernels, attend(): pl.pallas_call(functools.partial(fwd_kernel, groups, HD ** (-0.5)), grid_...  42.7 us
    pallas_call x2, Pallas kernels, project(): pl.pallas_call(functools.partial(project_kernel, heads, kv, len(w_parts))...  42.1 us
    pallas_call x4, Pallas kernels, down(): pl.pallas_call(down_kernel, grid=(pl.cdiv(d, size),), in_specs=[pl.BlockS...  39.2 us
  transfers between devices with their start and end apart: 43, of which 19 were waited for; matrix products, arithmetic and copies ran while one was open for 19% of the time, Pallas kernels for 48%

profile of v5, /device:TPU:0, one launch (start us, length us, event | category | flops | bytes accessed | tf_op | source)
XLA Modules:
  0.0 942.7 jit_solution(14398801935998360165)
XLA Ops:
  17.6 55.3 %collective-permute-done = bf16[512,2560]{1,0:T(8,128)(2,1)S(1)} collective-permute-done((bf16[512,2560]{1,0:T(8,128)(2,1)S(1)}, bf16[512,2560]{1,0:T(8,128)(2,1)S(1)}, u32[]{:S(2)}, u32[]{:S(2)}) %collective-permute-start) | collective-permute-done | bytes 2621472 | tf_op jit(solution)/shard_map/ppermute | solution.py:450
  92.5 9.0 fusion.2.n1_ref
  101.5 20.5 %project.2.qr_ref.kr_ref.vb_ref = bf16[1024,1536]{1,0:T(8,128)(2,1)} custom-call(s32[1]{0:T(128)} %constant.225.clone.1.at_ref, bf16[1024,2560]{1,0:T(8,128)(2,1)} %fusion.2.n1_ref, bf16[640,1024]{1,0:T(8,128)(2,1)} %fusion.12.eq_ref.e_ref, bf16[384,512]{1,0:T(8,128)(2,1)} %pad_convert_fusion.ek_ref, f32[1024,128]{1,0:T(8,128)} %get-tuple-element.315.c_ref, ...), custom_call_target="tpu_custom_call" | custom-call | flops 2013265920 | tf_op jit(solution)/shard_map/project/pallas_call | solution.py:200
  125.0 21.5 %attend.2 = (bf16[1024,1024]{1,0:T(8,128)(2,1)S(1)}, f32[2,1024,4]{2,1,0:T(8,128)S(1)}) custom-call(s32[4]{0:T(128)S(1)} %and_select_fusion.2.lo_ref, bf16[1024,1536]{1,0:T(8,128)(2,1)} %project.2.qr_ref.kr_ref.vb_ref, bf16[1024,1536]{1,0:T(8,128)(2,1)} %project.2.qr_ref.kr_ref.vb_ref, bf16[1024,1536]{1,0:T(8,128)(2,1)} %project.2.qr_ref.kr_ref.vb_ref, ...), custom_call_target="tpu_custom_call" | custom-call | flops 1073741824 | tf_op jit(solution)/shard_map/attend/pallas_call | solution.py:116
  148.2 4.5 collective-permute-done.4.refs_1_
  152.7 21.5 %project.3.qr_ref.kr_ref.vb_ref = bf16[1024,1536]{1,0:T(8,128)(2,1)} custom-call(s32[2]{0:T(128)} %pad_add_fusion.at_ref, bf16[1024,2560]{1,0:T(8,128)(2,1)} %fusion.2.n1_ref, bf16[640,1024]{1,0:T(8,128)(2,1)} %fusion.12.eq_ref.e_ref, bf16[384,512]{1,0:T(8,128)(2,1)} %pad_convert_fusion.ek_ref, f32[1024,128]{1,0:T(8,128)} %get-tuple-element.315.c_ref, ...), custom_call_target="tpu_custom_call" | custom-call | flops 2013265920 | tf_op jit(solution)/shard_map/project/pallas_call | solution.py:200
  174.2 21.2 %attend.3 = (bf16[1024,1024]{1,0:T(8,128)(2,1)S(1)}, f32[2,1024,4]{2,1,0:T(8,128)S(1)}) custom-call(s32[4]{0:T(128)S(1)} %and_select_fusion.2.lo_ref, bf16[1024,1536]{1,0:T(8,128)(2,1)} %project.3.qr_ref.kr_ref.vb_ref, bf16[1024,1536]{1,0:T(8,128)(2,1)} %project.3.qr_ref.kr_ref.vb_ref, bf16[1024,1536]{1,0:T(8,128)(2,1)} %project.3.qr_ref.kr_ref.vb_ref, ...), custom_call_target="tpu_custom_call" | custom-call | flops 1073741824 | tf_op jit(solution)/shard_map/attend/pallas_call | solution.py:116
  205.9 5.0 convolution_convert_fusion.5
  222.2 35.3 %collective-permute-done.8 = bf16[512,2560]{1,0:T(8,128)(2,1)} collective-permute-done((bf16[512,2560]{1,0:T(8,128)(2,1)}, bf16[512,2560]{1,0:T(8,128)(2,1)}, u32[]{:S(2)}, u32[]{:S(2)}) %collective-permute-start.8) | collective-permute-done | bytes 2621472 | tf_op jit(solution)/shard_map/ppermute | solution.py:450
  261.1 9.1 collective-permute-done.7
  270.3 5.9 multiply_reduce_fusion.3
  281.4 4.8 broadcast_in_dim.52
  293.2 16.3 %gate_up.3 = (bf16[512,1728]{1,0:T(8,128)(2,1)}, bf16[512,1728]{1,0:T(8,128)(2,1)}, bf16[512,1728]{1,0:T(8,128)(2,1)}) custom-call(bf16[512,2560]{1,0:T(8,128)(2,1)} %copy-done.14, bf16[2560,1728]{1,0:T(8,128)(2,1)} %all-gather.10.cloned.1.call-done.refs_1_.refs_2_.refs_3_.refs_6_, ...), custom_call_target="tpu_custom_call" | custom-call | flops 9059696640 | tf_op jit(solution)/shard_map/gate_up/pallas_call | solution.py:253
  309.5 27.9 %collective-permute-done.10.refs_1_.refs_2_ = bf16[512,2560]{1,0:T(8,128)(2,1)} collective-permute-done((bf16[512,2560]{1,0:T(8,128)(2,1)S(1)}, bf16[512,2560]{1,0:T(8,128)(2,1)}, u32[]{:S(2)}, u32[]{:S(2)}) %collective-permute-start.10) | collective-permute-done | bytes 2621472 | tf_op jit(solution)/shard_map/ppermute | solution.py:450
  342.9 25.0 %gate_up.4 = (bf16[512,1728]{1,0:T(8,128)(2,1)}, bf16[512,1728]{1,0:T(8,128)(2,1)}, bf16[512,1728]{1,0:T(8,128)(2,1)}, bf16[512,1728]{1,0:T(8,128)(2,1)}, bf16[5...) custom-call(bf16[512,2560]{1,0:T(8,128)(2,1)} %collective-permute-done.9.refs_0_.refs_1_, ...), custom_call_target="tpu_custom_call" | custom-call | flops 18119393280 | tf_op jit(solution)/shard_map/gate_up/pallas_call | solution.py:253
  372.0 15.8 %gate_up.5 = (bf16[512,1728]{1,0:T(8,128)(2,1)}, bf16[512,1728]{1,0:T(8,128)(2,1)}, bf16[512,1728]{1,0:T(8,128)(2,1)}) custom-call(bf16[256,2560]{1,0:T(8,128)(2,1)} %copy-done.24, bf16[256,2560]{1,0:T(8,128)(2,1)} %copy-done.25, bf16[2560,1728]{1,0:T(8,128)(2,1)} %all-gather.10.cloned.1.call-done.refs_1_.refs_2_.refs_3_.refs_6_, ...), custom_call_target="tpu_custom_call" | custom-call | flops 9059696640 | tf_op jit(solution)/shard_map/gate_up/pallas_call | solution.py:253
  387.9 29.3 %wgrad.3 = bf16[2560,1728]{1,0:T(8,128)(2,1)} custom-call(bf16[512,2560]{1,0:T(8,128)(2,1)} %broadcast_multiply_fusion.3.refs_0_, bf16[512,2560]{1,0:T(8,128)(2,1)} %broadcast_multiply_fusion.2.refs_1_.refs_0_, bf16[512,2560]{1,0:T(8,128)(2,1)} %broadcast_multiply_fusion.1.refs_2_.refs_3_, bf16[512,2560]{1,0:T(8,128)(2,1)} %broadcast_multiply_fusion.refs_3_.refs_0_, ...), custom_call_target="tpu_custom_call" | custom-call | flops 2264924160 | tf_op jit(solution)/shard_map/wgrad/pallas_call | solution.py:372
  417.2 23.4 %gate_up_back.3 = (bf16[512,1728]{1,0:T(8,128)(2,1)}, bf16[512,1728]{1,0:T(8,128)(2,1)}, bf16[256,2560]{1,0:T(8,128)(2,1)}, bf16[256,2560]{1,0:T(8,128)(2,1)}) custom-call(bf16[512,2560]{1,0:T(8,128)(2,1)} %broadcast_multiply_fusion.refs_3_.refs_0_, bf16[512,1728]{1,0:T(8,128)(2,1)} %get-tuple-element.181.refs_1_, ...), custom_call_target="tpu_custom_call" | custom-call | flops 13589544960 | tf_op jit(solution)/shard_map/gate_up_back/pallas_call | solution.py:307
  442.4 41.9 %gate_up_back.4 = (bf16[512,1728]{1,0:T(8,128)(2,1)}, bf16[512,1728]{1,0:T(8,128)(2,1)}, bf16[512,1728]{1,0:T(8,128)(2,1)}, bf16[512,1728]{1,0:T(8,128)(2,1)}, b...) custom-call(bf16[512,2560]{1,0:T(8,128)(2,1)} %broadcast_multiply_fu, ...), custom_call_target="tpu_custom_call" | custom-call | flops 27179089920 | tf_op jit(solution)/shard_map/gate_up_back/pallas_call | solution.py:307
  490.6 23.4 %gate_up_back.5 = (bf16[512,1728]{1,0:T(8,128)(2,1)}, bf16[512,1728]{1,0:T(8,128)(2,1)}, bf16[256,2560]{1,0:T(8,128)(2,1)}, bf16[256,2560]{1,0:T(8,128)(2,1)}) custom-call(bf16[512,2560]{1,0:T(8,128)(2,1)} %broadcast_multiply_fusion.3.refs_0_, bf16[512,1728]{1,0:T(8,128)(2,1)} %get-tuple-element.203.refs_1_, bf16[512,1728]{1,0:T(8,128)(2,1)} %get-tuple-element.204.refs_2_, ...), custom_call_target="tpu_custom_call" | custom-call | flops 13589544960 | tf_op jit(solution)/shard_map/gate_up_back/pallas_call | solution.py:307
  514.0 9.8 %down.5 = bf16[512,2560]{1,0:T(8,128)(2,1)} custom-call(bf16[512,1728]{1,0:T(8,128)(2,1)} %get-tuple-element.210.refs_6_.h_ref, bf16[2560,1728]{1,0:T(8,128)(2,1)} %all-gather.14.cloned.1.call-done.refs_5_.refs_8_.w_ref), custom_call_target="tpu_custom_call" | custom-call | tf_op jit(solution)/shard_map/down/pallas_call | solution.py:331
  523.8 9.8 %down.4 = bf16[512,2560]{1,0:T(8,128)(2,1)} custom-call(bf16[512,1728]{1,0:T(8,128)(2,1)} %get-tuple-element.209.refs_5_.h_ref, bf16[2560,1728]{1,0:T(8,128)(2,1)} %all-gather.14.cloned.1.call-done.refs_5_.refs_8_.w_ref), custom_call_target="tpu_custom_call" | custom-call | tf_op jit(solution)/shard_map/down/pallas_call | solution.py:331
  533.5 8.1 collective-permute-done.15
  541.7 29.3 %wgrad.4 = bf16[2560,1728]{1,0:T(8,128)(2,1)} custom-call(bf16[512,2560]{1,0:T(8,128)(2,1)} %copy-done.14, bf16[512,2560]{1,0:T(8,128)(2,1)} %collective-permute-done.9.refs_0_.refs_1_, bf16[512,2560]{1,0:T(8,128)(2,1)} %collective-permute-done.10.refs_1_.refs_2_, bf16[256,2560]{1,0:T(8,128)(2,1)} %copy-done.24, bf16[256,2560]{1,0:T(8,128)(2,1)} %copy-done.25, ...), custom_call_target="tpu_custom_call" | custom-call | flops 2264924160 | tf_op jit(solution)/shard_map/wgrad/pallas_call | solution.py:372
  571.0 29.7 %wgrad.5 = bf16[2560,1728]{1,0:T(8,128)(2,1)} custom-call(bf16[512,2560]{1,0:T(8,128)(2,1)} %copy-done.14, bf16[512,2560]{1,0:T(8,128)(2,1)} %collective-permute-done.9.refs_0_.refs_1_, bf16[512,2560]{1,0:T(8,128)(2,1)} %collective-permute-done.10.refs_1_.refs_2_, bf16[256,2560]{1,0:T(8,128)(2,1)} %copy-done.24, bf16[256,2560]{1,0:T(8,128)(2,1)} %copy-done.25, ...), custom_call_target="tpu_custom_call" | custom-call | flops 2264924160 | tf_op jit(solution)/shard_map/wgrad/pallas_call | solution.py:372
  610.9 6.0 fusion.88
  617.8 9.9 %down.6 = bf16[512,2560]{1,0:T(8,128)(2,1)} custom-call(bf16[512,1728]{1,0:T(8,128)(2,1)} %get-tuple-element.229.refs_7_.h_ref, bf16[2560,1728]{1,0:T(8,128)(2,1)} %all-gather.14.cloned.1.call-done.refs_5_.refs_8_.w_ref), custom_call_target="tpu_custom_call" | custom-call | tf_op jit(solution)/shard_map/down/pallas_call | solution.py:331
  627.7 9.8 %down.7 = bf16[512,2560]{1,0:T(8,128)(2,1)} custom-call(bf16[512,1728]{1,0:T(8,128)(2,1)} %get-tuple-element.230.refs_4_.h_ref, bf16[2560,1728]{1,0:T(8,128)(2,1)} %all-gather.14.cloned.1.call-done.refs_5_.refs_8_.w_ref), custom_call_target="tpu_custom_call" | custom-call | tf_op jit(solution)/shard_map/down/pallas_call | solution.py:331
  637.4 34.6 %collective-permute-done.19 = bf16[512,2560]{1,0:T(8,128)(2,1)} collective-permute-done((bf16[512,2560]{1,0:T(8,128)(2,1)S(1)}, bf16[512,2560]{1,0:T(8,128)(2,1)}, u32[]{:S(2)}, u32[]{:S(2)}) %collective-permute-start.19) | collective-permute-done | bytes 2621472 | tf_op jit(solution)/shard_map/ppermute | solution.py:450
  672.0 4.7 maximum_select_fusion.1.d_ref
  676.7 4.6 convolution_convert_fusion.3
  689.3 9.9 %heads_back.2.do_ref = bf16[1024,1024]{1,0:T(8,128)(2,1)} custom-call(bf16[1024,2560]{1,0:T(8,128)(2,1)} %copy-done.30, bf16[2560,640]{1,0:T(8,128)(2,1)} %copy-done.31, bf16[640,1024]{1,0:T(8,128)(2,1)} %fusion.12.eq_ref.e_ref), custom_call_target="tpu_custom_call" | custom-call | flops 4697620480 | tf_op jit(solution)/shard_map/heads_back/pallas_call | solution.py:222
  699.3 32.5 %attend_back.2 = (bf16[1024,1024]{1,0:T(8,128)(2,1)S(1)}, bf16[1024,256]{1,0:T(8,128)(2,1)S(1)}, bf16[1024,256]{1,0:T(8,128)(2,1)S(1)}) custom-call(s32[4]{0:T(128)S(1)} %and_select_fusion.2.lo_ref, bf16[1024,1536]{1,0:T(8,128)(2,1)} %project.3.qr_ref.kr_ref.vb_ref, bf16[1024,1536]{1,0:T(8,128)(2,1)} %project.3.qr_ref.kr_ref.vb_ref, ...), custom_call_target="tpu_custom_call" | custom-call | flops 4294967296 | tf_op jit(solution)/shard_map/attend_back/pallas_call | solution.py:138
  734.8 10.4 %convolution_convert_fusion.1 = bf16[2560,1024]{1,0:T(8,128)(2,1)S(1)} fusion(bf16[1024,2560]{1,0:T(8,128)(2,1)} %fusion.2.n1_ref, bf16[1024,64]{0,1:T(8,128)(2,1)S(1)} %broadcast.306, bf16[1024,160]{0,1:T(8,128)(2,1)S(1)} %convolution_convert_fusion.8, bf16[1024,160]{0,1:T(8,128)(2,1)S(1)} %convolution_convert_fusion.9, bf16[1024,640]{0,1:T(8,128)(2,1)S(1)} %fusion.29), kind=kOutput, calls=%fused_computation.10 | convolution fusion | flops 5379719168 | bytes 12582912 | tf_op jit(solution)/shard_map/dot_general | solution.py:433
  751.8 5.5 constant_dynamic-update-slice_fusion.6
  762.3 10.0 %heads_back.3.do_ref = bf16[1024,1024]{1,0:T(8,128)(2,1)} custom-call(bf16[1024,2560]{1,0:T(8,128)(2,1)} %copy-done.30, bf16[2560,640]{1,0:T(8,128)(2,1)} %all-gather.8.cloned.1.call-done.w_ref, bf16[640,1024]{1,0:T(8,128)(2,1)} %fusion.12.eq_ref.e_ref), custom_call_target="tpu_custom_call" | custom-call | flops 4697620480 | tf_op jit(solution)/shard_map/heads_back/pallas_call | solution.py:222
  772.3 33.1 %attend_back.3 = (bf16[1024,1024]{1,0:T(8,128)(2,1)S(1)}, bf16[1024,256]{1,0:T(8,128)(2,1)S(1)}, bf16[1024,256]{1,0:T(8,128)(2,1)S(1)}) custom-call(s32[4]{0:T(128)S(1)} %copy-done.3, bf16[1024,1536]{1,0:T(8,128)(2,1)} %project.2.qr_ref.kr_ref.vb_ref, bf16[1024,1536]{1,0:T(8,128)(2,1)} %project.2.qr_ref.kr_ref.vb_ref, ...), custom_call_target="tpu_custom_call" | custom-call | flops 4294967296 | tf_op jit(solution)/shard_map/attend_back/pallas_call | solution.py:138
  805.4 9.2 convolution_convert_fusion.2
  818.3 4.9 add_convert_fusion.2
  828.5 9.5 %multiply_reduce_fusion.1 = (f32[2560]{0:T(1024)S(1)}, bf16[512,2560]{1,0:T(8,128)(2,1)}) fusion(bf16[512,2560]{1,0:T(8,128)(2,1)S(1)} %copy-done.22, f32[512]{0:T(512)S(1)} %dynamic-slice.3, bf16[2560,2048]{1,0:T(8,128)(2,1)S(1)} %bitcast.56, bf16[1024,2048]{0,1:T(8,128)(2,1)} %copy-done.54, s32[]{:T(128)S(6)} %select_n.352), kind=kOutput, calls=%fused_computation.20 | convolution fusion | flops 5376570880 | bytes 17838084 | tf_op jit(solution)/shard_map/dot_general | solution.py:437
  838.5 9.5 %fusion.5 = (f32[2560]{0:T(1024)S(1)}, f32[512,2560]{1,0:T(8,128)}) fusion(bf16[512,2560]{1,0:T(8,128)(2,1)S(1)} %copy-done.19, f32[512]{0:T(512)S(1)} %add_rsqrt_fusion.1, bf16[2560,2048]{1,0:T(8,128)(2,1)S(1)} %bitcast.56, bf16[1024,2048]{0,1:T(8,128)(2,1)} %copy-done.54, s32[]{:T(128)S(6)} %select_n.351), kind=kOutput, calls=%fused_computation.13 | convolution fusion | flops 5373949440 | bytes 20459524 | tf_op jit(solution)/shard_map/dot_general | solution.py:437
  848.1 9.8 %convolution_convert_fusion = bf16[2560,1024]{1,0:T(8,128)(2,1)} fusion(bf16[1024,2560]{1,0:T(8,128)(2,1)S(1)} %bitcast.51, bf16[1024,64]{0,1:T(8,128)(2,1)S(1)} %copy-done.46, bf16[1024,160]{0,1:T(8,128)(2,1)S(1)} %get-tuple-element.332, bf16[1024,160]{0,1:T(8,128)(2,1)S(1)} %get-tuple-element.330, bf16[1024,640]{0,1:T(8,128)(2,1)S(1)} %get-tuple-element.328), kind=kOutput, calls=%fused_computation.9 | convolution fusion | flops 5379719168 | bytes 12582912 | tf_op jit(solution)/shard_map/dot_general | solution.py:433
  857.9 5.2 fusion.7
  863.2 18.3 %collective-permute-done.27 = bf16[512,2560]{1,0:T(8,128)(2,1)} collective-permute-done((bf16[512,2560]{1,0:T(8,128)(2,1)}, bf16[512,2560]{1,0:T(8,128)(2,1)}, u32[]{:S(2)}, u32[]{:S(2)}) %collective-permute-start.27) | collective-permute-done | bytes 2621472 | tf_op jit(solution)/shard_map/ppermute | solution.py:450
  881.5 16.1 %collective-permute-done.25.got_ref = bf16[512,2560]{1,0:T(8,128)(2,1)} collective-permute-done((bf16[512,2560]{1,0:T(8,128)(2,1)}, bf16[512,2560]{1,0:T(8,128)(2,1)}, u32[]{:S(2)}, u32[]{:S(2)}) %collective-permute-start.25) | collective-permute-done | bytes 2621472 | tf_op jit(solution)/shard_map/ppermute | solution.py:450
  897.9 5.3 collective-permute-done.28
  909.6 10.4 %finish.1 = f32[512,2560]{1,0:T(8,128)} custom-call(bf16[512,2560]{1,0:T(8,128)(2,1)} %x_ref.1, f32[1,2560]{1,0:T(1,128)} %reshape.250.gain_ref, f32[512,2560]{1,0:T(8,128)} %get-tuple-element.334.own_ref, bf16[512,2560]{1,0:T(8,128)(2,1)} %collective-permute-done.25.got_ref, f32[512,2560]{1,0:T(8,128)} %get-tuple-element.309.dh_ref), custom_call_target="tpu_custom_call" | custom-call | flops 51999997952 | tf_op jit(solution)/shard_map/finish/pallas_call | solution.py:395
  920.6 5.4 add_convert_fusion.1
  (331 shorter events, 149.0 us)
Async XLA Ops:
  7.2 67.6 %all-gather.6.cloned.1.call-start = ((), (), s32[]{:S(2)}) async-start(), calls=%async_computation.5 | async-start | bytes 5898240 | tf_op jit(solution)/shard_map/all_gather | solution.py:546
  10.2 66.0 %copy-start.49 = (s32[2,1024]{1,0:T(2,128)S(1)}, s32[2,1024]{1,0:T(2,128)}, u32[]{:S(2)}) copy-start(s32[2,1024]{1,0:T(2,128)} %param.13) | copy-start | bytes 24580
  13.1 109.0 %all-gather.8.cloned.1.call-start = ((), (), s32[]{:S(2)}) async-start(), calls=%async_computation.6 | async-start | bytes 3686400 | tf_op jit(solution)/shard_map/all_gather | solution.py:554
  13.1 59.9 %collective-permute-start = (bf16[512,2560]{1,0:T(8,128)(2,1)S(1)}, bf16[512,2560]{1,0:T(8,128)(2,1)S(1)}, u32[]{:S(2)}, u32[]{:S(2)}) collective-permute-start(bf16[512,2560]{1,0:T(8,128)(2,1)S(1)} %copy-done.16), channel_id=1, source_target_pairs={{0,1},{1,0},{2,3},{3,2},{4,5},{5,4},{6,7},{7,6},{8,9},{9,8},{10,11... | collective-permute-start | bytes 7864328 | tf_op jit(solution)/shard_map/ppermute | solution.py:450
  16.1 58.6 %collective-permute-start.1 = (bf16[512,2560]{1,0:T(8,128)(2,1)}, bf16[512,2560]{1,0:T(8,128)(2,1)}, u32[]{:S(2)}, u32[]{:S(2)}) collective-permute-start(bf16[512,2560]{1,0:T(8,128)(2,1)} %param.23), channel_id=1, source_target_pairs={{0,2},{1,3},{2,0},{3,1},{4,6},{5,7},{6,4},{7,5},{8,10},{9,11},{10,... | collective-permute-start | bytes 7864328 | tf_op jit(solution)/shard_map/ppermute | solution.py:450
  74.8 204.2 %all-gather.10.cloned.1.call-start = ((), (), s32[]{:S(2)}) async-start(), calls=%async_computation.7 | async-start | bytes 10321920 | tf_op jit(solution)/shard_map/all_gather | solution.py:555
  75.5 217.7 %all-gather.12.cloned.1.call-start = ((), (), s32[]{:S(2)}) async-start(), calls=%async_computation.8 | async-start | bytes 10321920 | tf_op jit(solution)/shard_map/all_gather | solution.py:556
  76.1 341.1 %all-gather.14.cloned.1.call-start = ((), (), s32[]{:S(2)}) async-start(), calls=%async_computation.9 | async-start | bytes 10321920 | tf_op jit(solution)/shard_map/all_gather | solution.py:557
  78.4 121.1 %copy-start.52 = (s32[640]{0:T(1024)}, s32[640]{0:T(1024)S(1)}, u32[]{:S(2)}) copy-start(s32[640]{0:T(1024)S(1)} %fusion.59) | copy-start | bytes 7684
  82.0 617.2 %copy-start.2 = (s32[4]{0:T(128)}, s32[4]{0:T(128)S(1)}, u32[]{:S(2)}) copy-start(s32[4]{0:T(128)S(1)} %and_select_fusion.2.lo_ref) | copy-start | bytes 52
  85.2 62.2 %collective-permute-start.2 = (bf16[1280,1024]{1,0:T(8,128)(2,1)}, bf16[1280,1024]{1,0:T(8,128)(2,1)}, u32[]{:S(2)}, u32[]{:S(2)}) collective-permute-start(bf16[1280,1024]{1,0:T(8,128)(2,1)} %constant_dynamic-slice_fusion.4), channel_id=1, source_target_pairs={{0,2},{1,3},{2,0},{3,1},{4,6},{5,7},{6,4},{7,5},{8,10},{9,11},{10,... | collective-permute-start | bytes 7864328 | tf_op jit(solution)/shard_map/ppermute | solution.py:450
  86.8 60.7 %collective-permute-start.3 = (bf16[512,2560]{1,0:T(8,128)(2,1)}, bf16[512,2560]{1,0:T(8,128)(2,1)}, u32[]{:S(2)}, u32[]{:S(2)}) collective-permute-start(bf16[512,2560]{1,0:T(8,128)(2,1)} %param.23), channel_id=1, source_target_pairs={{0,1},{1,0},{2,3},{3,2},{4,5},{5,4},{6,7},{7,6},{8,9},{9,8},{10,11... | collective-permute-start | bytes 7864328 | tf_op jit(solution)/shard_map/ppermute | solution.py:450
  147.5 5.3 collective-permute-start.4
  147.5 524.5 %reduce-scatter.6.cloned.1.call-start = ((), (), s32[]{:S(2)}) async-start(), calls=%async_computation.10 | async-start | bytes 10321920 | tf_op jit(solution)/shard_map/reduce_scatter | solution.py:638
  147.5 50.2 %collective-permute-start.5 = (bf16[1280,640]{1,0:T(8,128)(2,1)}, bf16[1280,640]{1,0:T(8,128)(2,1)}, u32[]{:S(2)}, u32[]{:S(2)}) collective-permute-start(bf16[1280,640]{1,0:T(8,128)(2,1)} %constant_dynamic-slice_fusion.5), channel_id=1, source_target_pairs={{0,2},{1,3},{2,0},{3,1},{4,6},{5,7},{6,4},{7,5},{8,10},{9,11},{10,... | collective-permute-start | bytes 4915208 | tf_op jit(solution)/shard_map/ppermute | solution.py:450
  197.7 4.1 collective-permute-start.6
  197.8 59.6 %collective-permute-start.8 = (bf16[512,2560]{1,0:T(8,128)(2,1)}, bf16[512,2560]{1,0:T(8,128)(2,1)}, u32[]{:S(2)}, u32[]{:S(2)}) collective-permute-start(bf16[512,2560]{1,0:T(8,128)(2,1)} %collective-permute-done.3), channel_id=1, source_target_pairs={{0,2},{1,3},{2,0},{3,1},{4,6},{5,7},{6,4},{7,5},{8,10},{9,11},{10,... | collective-permute-start | bytes 7864328 | tf_op jit(solution)/shard_map/ppermute | solution.py:450
  201.1 69.1 %copy-start.58 = (bf16[1024,640]{0,1:T(8,128)(2,1)}, bf16[1024,640]{0,1:T(8,128)(2,1)S(1)}, u32[]{:S(2)}) copy-start(bf16[1024,640]{0,1:T(8,128)(2,1)S(1)} %fusion.28) | copy-start | bytes 3932164
  210.9 59.4 %collective-permute-start.7 = (bf16[512,2560]{1,0:T(8,128)(2,1)}, bf16[512,2560]{1,0:T(8,128)(2,1)}, u32[]{:S(2)}, u32[]{:S(2)}) collective-permute-start(bf16[512,2560]{1,0:T(8,128)(2,1)} %convolution_convert_fusion.5), channel_id=1, source_target_pairs={{0,1},{1,0},{2,3},{3,2},{4,5},{5,4},{6,7},{7,6},{8,9},{9,8},{10,11... | collective-permute-start | bytes 7864328 | tf_op jit(solution)/shard_map/ppermute | solution.py:450
  218.6 51.7 %copy-start.43 = (bf16[2560,640]{1,0:T(8,128)(2,1)S(1)}, bf16[2560,640]{1,0:T(8,128)(2,1)}, u32[]{:S(2)}) copy-start(bf16[2560,640]{1,0:T(8,128)(2,1)} %all-gather.8.cloned.1.call-done.w_ref) | copy-start | bytes 9830404
  279.0 58.4 %collective-permute-start.10 = (bf16[512,2560]{1,0:T(8,128)(2,1)S(1)}, bf16[512,2560]{1,0:T(8,128)(2,1)}, u32[]{:S(2)}, u32[]{:S(2)}) collective-permute-start(bf16[512,2560]{1,0:T(8,128)(2,1)S(1)} %multiply_convert_fusion.refs_0_), channel_id=1, source_target_pairs={{0,2},{1,3},{2,0},{3,1},{4,6},{5,7},{6,4},{7,5},{8,10},{9,11},{10,... | collective-permute-start | bytes 7864328 | tf_op jit(solution)/shard_map/ppermute | solution.py:450
  280.8 58.0 %collective-permute-start.9 = (bf16[512,2560]{1,0:T(8,128)(2,1)S(1)}, bf16[512,2560]{1,0:T(8,128)(2,1)}, u32[]{:S(2)}, u32[]{:S(2)}) collective-permute-start(bf16[512,2560]{1,0:T(8,128)(2,1)S(1)} %multiply_convert_fusion.refs_0_), channel_id=1, source_target_pairs={{0,1},{1,0},{2,3},{3,2},{4,5},{5,4},{6,7},{7,6},{8,9},{9,8},{10,11... | collective-permute-start | bytes 7864328 | tf_op jit(solution)/shard_map/ppermute | solution.py:450
  340.3 28.9 %collective-permute-start.11 = (bf16[256,2560]{1,0:T(8,128)(2,1)S(1)}, bf16[256,2560]{1,0:T(8,128)(2,1)S(1)}, u32[]{:S(2)}, u32[]{:S(2)}) collective-permute-start(bf16[256,2560]{1,0:T(8,128)(2,1)S(1)} %slice.71), channel_id=1, source_target_pairs={{0,2},{1,3},{2,0},{3,1},{4,6},{5,7},{6,4},{7,5},{8,10},{9,11},{10,... | collective-permute-start | bytes 3932168 | tf_op jit(solution)/shard_map/ppermute | solution.py:450
  342.1 28.8 %collective-permute-start.12 = (bf16[256,2560]{1,0:T(8,128)(2,1)S(1)}, bf16[256,2560]{1,0:T(8,128)(2,1)S(1)}, u32[]{:S(2)}, u32[]{:S(2)}) collective-permute-start(bf16[256,2560]{1,0:T(8,128)(2,1)S(1)} %slice.72), channel_id=1, source_target_pairs={{0,1},{1,0},{2,3},{3,2},{4,5},{5,4},{6,7},{7,6},{8,9},{9,8},{10,11... | collective-permute-start | bytes 3932168 | tf_op jit(solution)/shard_map/ppermute | solution.py:450
  417.2 509.5 %reduce-scatter.10.cloned.1.call-start = ((), (), s32[]{:S(2)}) async-start(), calls=%async_computation.12 | async-start | bytes 10321920 | tf_op jit(solution)/shard_map/reduce_scatter | solution.py:652
  440.7 46.1 %collective-permute-start.14 = (bf16[256,2560]{1,0:T(8,128)(2,1)}, bf16[256,2560]{1,0:T(8,128)(2,1)S(1)}, u32[]{:S(2)}, u32[]{:S(2)}) collective-permute-start(bf16[256,2560]{1,0:T(8,128)(2,1)} %get-tuple-element.186), channel_id=1, source_target_pairs={{0,1},{1,0},{2,3},{3,2},{4,5},{5,4},{6,7},{7,6},{8,9},{9,8},{10,11... | collective-permute-start | bytes 3932168 | tf_op jit(solution)/shard_map/ppermute | solution.py:450
  441.2 48.6 %collective-permute-start.16 = (bf16[256,2560]{1,0:T(8,128)(2,1)}, bf16[256,2560]{1,0:T(8,128)(2,1)S(1)}, u32[]{:S(2)}, u32[]{:S(2)}) collective-permute-start(bf16[256,2560]{1,0:T(8,128)(2,1)} %get-tuple-element.187), channel_id=1, source_target_pairs={{0,2},{1,3},{2,0},{3,1},{4,6},{5,7},{6,4},{7,5},{8,10},{9,11},{10,... | collective-permute-start | bytes 3932168 | tf_op jit(solution)/shard_map/ppermute | solution.py:450
  484.4 49.2 %collective-permute-start.13 = (bf16[256,2560]{1,0:T(8,128)(2,1)}, bf16[256,2560]{1,0:T(8,128)(2,1)}, u32[]{:S(2)}, u32[]{:S(2)}) collective-permute-start(bf16[256,2560]{1,0:T(8,128)(2,1)} %get-tuple-element.194), channel_id=1, source_target_pairs={{0,1},{1,0},{2,3},{3,2},{4,5},{5,4},{6,7},{7,6},{8,9},{9,8},{10,11... | collective-permute-start | bytes 3932168 | tf_op jit(solution)/shard_map/ppermute | solution.py:450
  486.0 47.5 %collective-permute-start.18 = (bf16[256,2560]{1,0:T(8,128)(2,1)}, bf16[256,2560]{1,0:T(8,128)(2,1)}, u32[]{:S(2)}, u32[]{:S(2)}) collective-permute-start(bf16[256,2560]{1,0:T(8,128)(2,1)} %get-tuple-element.197), channel_id=1, source_target_pairs={{0,2},{1,3},{2,0},{3,1},{4,6},{5,7},{6,4},{7,5},{8,10},{9,11},{10,... | collective-permute-start | bytes 3932168 | tf_op jit(solution)/shard_map/ppermute | solution.py:450
  488.4 53.2 %collective-permute-start.15 = (bf16[256,2560]{1,0:T(8,128)(2,1)S(1)}, bf16[256,2560]{1,0:T(8,128)(2,1)}, u32[]{:S(2)}, u32[]{:S(2)}) collective-permute-start(bf16[256,2560]{1,0:T(8,128)(2,1)S(1)} %add_convert_fusion.7), channel_id=1, source_target_pairs={{0,2},{1,3},{2,0},{3,1},{4,6},{5,7},{6,4},{7,5},{8,10},{9,11},{10,... | collective-permute-start | bytes 3932168 | tf_op jit(solution)/shard_map/ppermute | solution.py:450
  490.2 51.5 %collective-permute-start.17 = (bf16[256,2560]{1,0:T(8,128)(2,1)S(1)}, bf16[256,2560]{1,0:T(8,128)(2,1)}, u32[]{:S(2)}, u32[]{:S(2)}) collective-permute-start(bf16[256,2560]{1,0:T(8,128)(2,1)S(1)} %add_convert_fusion.6), channel_id=1, source_target_pairs={{0,1},{1,0},{2,3},{3,2},{4,5},{5,4},{6,7},{7,6},{8,9},{9,8},{10,11... | collective-permute-start | bytes 3932168 | tf_op jit(solution)/shard_map/ppermute | solution.py:450
  600.8 325.9 %reduce-scatter.8.cloned.1.call-start = ((), (), s32[]{:S(2)}) async-start(), calls=%async_computation.11 | async-start | bytes 10321920 | tf_op jit(solution)/shard_map/reduce_scatter | solution.py:650
  601.5 325.1 %reduce-scatter.12.cloned.1.call-start = ((), (), s32[]{:S(2)}) async-start(), calls=%async_computation.13 | async-start | bytes 3686400 | tf_op jit(solution)/shard_map/reduce_scatter | solution.py:693
  616.9 55.1 %collective-permute-start.19 = (bf16[512,2560]{1,0:T(8,128)(2,1)S(1)}, bf16[512,2560]{1,0:T(8,128)(2,1)}, u32[]{:S(2)}, u32[]{:S(2)}) collective-permute-start(bf16[512,2560]{1,0:T(8,128)(2,1)S(1)} %get-tuple-element.232), channel_id=1, source_target_pairs={{0,1},{1,0},{2,3},{3,2},{4,5},{5,4},{6,7},{7,6},{8,9},{9,8},{10,11... | collective-permute-start | bytes 7864328 | tf_op jit(solution)/shard_map/ppermute | solution.py:450
  681.5 3.6 collective-permute-start.20
  686.7 58.6 %collective-permute-start.22 = (bf16[1280,640]{1,0:T(8,128)(2,1)}, bf16[1280,640]{1,0:T(8,128)(2,1)}, u32[]{:S(2)}, u32[]{:S(2)}) collective-permute-start(bf16[1280,640]{1,0:T(8,128)(2,1)} %add_convert_fusion.5), channel_id=1, source_target_pairs={{0,2},{1,3},{2,0},{3,1},{4,6},{5,7},{6,4},{7,5},{8,10},{9,11},{10,... | collective-permute-start | bytes 4915208 | tf_op jit(solution)/shard_map/ppermute | solution.py:450
  687.8 58.8 %collective-permute-start.21 = (bf16[512,2560]{1,0:T(8,128)(2,1)}, bf16[512,2560]{1,0:T(8,128)(2,1)S(1)}, u32[]{:S(2)}, u32[]{:S(2)}) collective-permute-start(bf16[512,2560]{1,0:T(8,128)(2,1)} %down.6), channel_id=1, source_target_pairs={{0,1},{1,0},{2,3},{3,2},{4,5},{5,4},{6,7},{7,6},{8,9},{9,8},{10,11... | collective-permute-start | bytes 7864328 | tf_op jit(solution)/shard_map/ppermute | solution.py:450
  748.1 10.7 %collective-permute-start.23 = (bf16[1280,1024]{1,0:T(8,128)(2,1)S(1)}, bf16[1280,1024]{1,0:T(8,128)(2,1)S(1)}, u32[]{:S(2)}, u32[]{:S(2)}) collective-permute-start(bf16[1280,1024]{1,0:T(8,128)(2,1)S(1)} %constant_dynamic-slice_fusion), channel_id=1, source_target_pairs={{0,4},{4,0},{8,12},{12,8},{16,20},{20,16},{24,28},{28,24},{1,5},{5... | collective-permute-start | bytes 7864328 | tf_op jit(solution)/shard_map/ppermute | solution.py:578
  757.3 90.8 %collective-permute-start.26 = (bf16[512,2560]{1,0:T(8,128)(2,1)}, bf16[512,2560]{1,0:T(8,128)(2,1)}, u32[]{:S(2)}, u32[]{:S(2)}) collective-permute-start(bf16[512,2560]{1,0:T(8,128)(2,1)} %down.4), channel_id=1, source_target_pairs={{0,1},{1,0},{2,3},{3,2},{4,5},{5,4},{6,7},{7,6},{8,9},{9,8},{10,11... | collective-permute-start | bytes 7864328 | tf_op jit(solution)/shard_map/ppermute | solution.py:450
  761.6 66.9 %collective-permute-start.24 = (bf16[1280,1024]{1,0:T(8,128)(2,1)}, bf16[1280,1024]{1,0:T(8,128)(2,1)}, u32[]{:S(2)}, u32[]{:S(2)}) collective-permute-start(bf16[1280,1024]{1,0:T(8,128)(2,1)} %add_convert_fusion.3), channel_id=1, source_target_pairs={{0,2},{1,3},{2,0},{3,1},{4,6},{5,7},{6,4},{7,5},{8,10},{9,11},{10,... | collective-permute-start | bytes 7864328 | tf_op jit(solution)/shard_map/ppermute | solution.py:450
  818.2 108.5 %reduce-scatter.14.cloned.1.call-start = ((), (), s32[]{:S(2)}) async-start(), calls=%async_computation.14 | async-start | bytes 5898240 | tf_op jit(solution)/shard_map/reduce_scatter | solution.py:710
  823.3 58.3 %collective-permute-start.27 = (bf16[512,2560]{1,0:T(8,128)(2,1)}, bf16[512,2560]{1,0:T(8,128)(2,1)}, u32[]{:S(2)}, u32[]{:S(2)}) collective-permute-start(bf16[512,2560]{1,0:T(8,128)(2,1)} %add_convert_fusion.2), channel_id=1, source_target_pairs={{0,2},{1,3},{2,0},{3,1},{4,6},{5,7},{6,4},{7,5},{8,10},{9,11},{10,... | collective-permute-start | bytes 7864328 | tf_op jit(solution)/shard_map/ppermute | solution.py:450
  838.0 59.5 %collective-permute-start.25 = (bf16[512,2560]{1,0:T(8,128)(2,1)}, bf16[512,2560]{1,0:T(8,128)(2,1)}, u32[]{:S(2)}, u32[]{:S(2)}) collective-permute-start(bf16[512,2560]{1,0:T(8,128)(2,1)} %get-tuple-element.336), channel_id=1, source_target_pairs={{0,1},{1,0},{2,3},{3,2},{4,5},{5,4},{6,7},{7,6},{8,9},{9,8},{10,11... | collective-permute-start | bytes 7864328 | tf_op jit(solution)/shard_map/ppermute | solution.py:450
  897.8 5.3 collective-permute-start.28
  903.2 4.1 collective-permute-start.29
  907.4 1.6 collective-permute-start.30
  909.0 11.0 %collective-permute-start.31 = (f32[2,160]{1,0:T(2,128)S(1)}, f32[2,160]{1,0:T(2,128)S(1)}, u32[]{:S(2)}, u32[]{:S(2)}) collective-permute-start(f32[2,160]{1,0:T(2,128)S(1)} %broadcast_select_fusion.1), channel_id=1, source_target_pairs={{0,2},{1,3},{2,0},{3,1},{4,6},{5,7},{6,4},{7,5},{8,10},{9,11},{10,... | collective-permute-start | bytes 3848 | tf_op jit(solution)/shard_map/ppermute | solution.py:510
  920.0 6.0 collective-permute-start.32
  (66 other events, 568.6 us)
Sparse Core Ops, SparseCore 0:
  13.2 58.7 all-gather.5
  74.9 40.5 all-gather.7
  117.2 87.4 all-gather.9
  206.1 87.0 all-gather.11
  294.7 87.0 all-gather.13
  417.3 94.2 reduce-scatter.5
  600.9 94.1 reduce-scatter.9
  697.4 95.3 reduce-scatter.7
  818.4 37.8 reduce-scatter.11
  863.3 58.8 reduce-scatter.13

commit v6 on v5

--- a/solution.py
+++ b/solution.py
@@ -646,11 +646,9 @@
     backs = own + near + far
     mlp_parts = [down(v, down_wt, 1)[0] for v in after(hiddens[1:], own)]
     n2_late, got = lax.optimization_barrier((n2_pieces, got, own, mlp_parts[:2]))[:2]
-    gate_part = wgrad(n2_late, [v[0] for v in backs])
-    gate_grad = lax.psum_scatter(gate_part, "dp", scatter_dimension=0, tiled=True)
-    up_part = wgrad(after(n2_late, gate_part), [v[1] for v in backs])
-    up_grad = lax.psum_scatter(up_part, "dp", scatter_dimension=0, tiled=True)
-    got = after(got, up_part)
+    gu_part = wgrad(n2_late, [v[0] for v in backs], [v[1] for v in backs])
+    gu_grad = lax.psum_scatter(gu_part, "dp", scatter_dimension=0, tiled=True)
+    got = after(got, gu_part)
     d_n2 = summed(got) + jnp.concatenate(backs[0][2]).astype(F32)
     gain_two_grad = jnp.sum(d_n2 * h * inv_h, axis=0)
     dh = dys[0].astype(F32) + norm_back(h, inv_h, gain_two, d_n2)
@@ -714,7 +712,8 @@
         [v.reshape(lax.axis_size("dp") * places, -1) for v in (gain_one_grad, gain_two_grad)], axis=1))[0]
     output = (h + sum(v.astype(F32) for v in mlp_got) + mlp_parts[0].astype(F32)).astype(BF)
     input_grad = finish(tokens, gain_one, d_n1_own, summed(d_n1_got) if len(d_n1_got) > 1 else d_n1_got[0], dh)
-    gate_grad, up_grad, out_grad_w, qkv_grad = after((gate_grad, up_grad, out_grad_w, qkv_grad), input_grad)
+    gu_grad, out_grad_w, qkv_grad = after((gu_grad, out_grad_w, qkv_grad), input_grad)
+    gate_grad, up_grad = gu_grad[:, :ff], gu_grad[:, gu_grad.shape[1] // 2:gu_grad.shape[1] // 2 + ff]
     out_grad_w, qkv_grad = out_grad_w.T.astype(F32), qkv_grad.astype(F32)
 
     return (

time: 947 us -> 1130 us (1.19)
  waiting for transfers between devices: 234 us -> 416 us
  Pallas kernels: 454 us -> 425 us
  starting transfers between devices: 25.4 us -> 41.7 us
    reduce_scatter x2 -> x1, waiting for transfers between devices: 0.01 us -> 152 us  [body(): gu_grad = lax.psum_scatter(gu_part, 'dp', scatter_dimension=0, tiled=True)]
    ppermute x24, waiting for transfers between devices: 211 us -> 245 us  [swap(): lax.ppermute(v, 'tensor', [(i, i ^ bit) for i in range(lax.axis_size('ten...]
    pallas_call x2, Pallas kernels: 65.6 us -> 52.6 us  [attend_back(): pl.pallas_call(functools.partial(bwd_kernel, groups, HD ** (-0.5)), grid_...]
    pallas_call x3 -> x2, Pallas kernels: 88.3 us -> 80.5 us  [wgrad(): pl.pallas_call(functools.partial(wgrad_kernel, len(a_blocks), lists, tile...]
  transfers between devices with their start and end apart: 43 -> 42, of which waited for: 19 -> 20; matrix products, arithmetic and copies ran while one was open for 19% -> 16% of each run, Pallas kernels for 48% -> 38%
where the time goes in v6:
time: 1130 us; the launch traced here: 1120 us
  Pallas kernels  425 us (38%)
  waiting for transfers between devices  416 us (37%)
  other arithmetic  85.1 us (8%)
  matrix products  74.1 us (7%)
  local copies, waits for them, and re-layouts  58.9 us (5%)
  starting transfers between devices  41.7 us (4%)
  between operations  15.1 us (1%)
    ppermute x24, waiting for transfers between devices, swap(): lax.ppermute(v, 'tensor', [(i, i ^ bit) for i in range(lax.axis_size('ten...  245 us
    reduce_scatter x1, waiting for transfers between devices, body(): gu_grad = lax.psum_scatter(gu_part, 'dp', scatter_dimension=0, tiled=True)  152 us
    pallas_call x3, Pallas kernels, gate_up_back(): pl.pallas_call(functools.partial(gate_up_back_kernel, ff, n, parts), grid...  88.9 us
    pallas_call x2, Pallas kernels, wgrad(): pl.pallas_call(functools.partial(wgrad_kernel, len(a_blocks), lists, tile...  80.5 us
    pallas_call x3, Pallas kernels, gate_up(): pl.pallas_call(functools.partial(gate_up_kernel, sizes), grid=(pl.cdiv(ff...  57.1 us
    pallas_call x2, Pallas kernels, attend_back(): pl.pallas_call(functools.partial(bwd_kernel, groups, HD ** (-0.5)), grid_...  52.6 us
    dot_general x12, matrix products, dot_nt(): lax.dot_general(a, b, (((1,), (1,)), ((), ())), preferred_element_type=F32)  43 us
    pallas_call x2, Pallas kernels, project(): pl.pallas_call(functools.partial(project_kernel, heads, kv, len(w_parts))...  41.9 us
  transfers between devices with their start and end apart: 42, of which 20 were waited for; matrix products, arithmetic and copies ran while one was open for 16% of the time, Pallas kernels for 38%

profile of v6, /device:TPU:0, one launch (start us, length us, event | category | flops | bytes accessed | tf_op | source)
XLA Modules:
  0.0 1116.5 jit_solution(4381977314074305605)
XLA Ops:
  17.6 55.3 %collective-permute-done = bf16[512,2560]{1,0:T(8,128)(2,1)S(1)} collective-permute-done((bf16[512,2560]{1,0:T(8,128)(2,1)S(1)}, bf16[512,2560]{1,0:T(8,128)(2,1)S(1)}, u32[]{:S(2)}, u32[]{:S(2)}) %collective-permute-start) | collective-permute-done | bytes 2621472 | tf_op jit(solution)/shard_map/ppermute | solution.py:450
  92.7 9.0 fusion.2.n1_ref
  101.7 20.5 %project.2.qr_ref.kr_ref.vb_ref = bf16[1024,1536]{1,0:T(8,128)(2,1)} custom-call(s32[1]{0:T(128)} %constant.225.clone.1.at_ref, bf16[1024,2560]{1,0:T(8,128)(2,1)} %fusion.2.n1_ref, bf16[640,1024]{1,0:T(8,128)(2,1)} %fusion.12.eq_ref.e_ref, bf16[384,512]{1,0:T(8,128)(2,1)} %pad_convert_fusion.ek_ref, f32[1024,128]{1,0:T(8,128)} %get-tuple-element.305.c_ref, ...), custom_call_target="tpu_custom_call" | custom-call | flops 2013265920 | tf_op jit(solution)/shard_map/project/pallas_call | solution.py:200
  125.1 17.9 %attend.2 = (bf16[1024,1024]{1,0:T(8,128)(2,1)S(1)}, f32[2,1024,4]{2,1,0:T(8,128)S(1)}) custom-call(s32[4]{0:T(128)S(1)} %and_select_fusion.2.lo_ref, bf16[1024,1536]{1,0:T(8,128)(2,1)} %project.2.qr_ref.kr_ref.vb_ref, bf16[1024,1536]{1,0:T(8,128)(2,1)} %project.2.qr_ref.kr_ref.vb_ref, bf16[1024,1536]{1,0:T(8,128)(2,1)} %project.2.qr_ref.kr_ref.vb_ref, ...), custom_call_target="tpu_custom_call" | custom-call | flops 1073741824 | tf_op jit(solution)/shard_map/attend/pallas_call | solution.py:116
  149.9 21.3 %project.3.qr_ref.kr_ref.vb_ref = bf16[1024,1536]{1,0:T(8,128)(2,1)} custom-call(s32[2]{0:T(128)} %pad_add_fusion.at_ref, bf16[1024,2560]{1,0:T(8,128)(2,1)} %fusion.2.n1_ref, bf16[640,1024]{1,0:T(8,128)(2,1)} %fusion.12.eq_ref.e_ref, bf16[384,512]{1,0:T(8,128)(2,1)} %pad_convert_fusion.ek_ref, f32[1024,128]{1,0:T(8,128)} %get-tuple-element.305.c_ref, ...), custom_call_target="tpu_custom_call" | custom-call | flops 2013265920 | tf_op jit(solution)/shard_map/project/pallas_call | solution.py:200
  171.2 17.4 %attend.3 = (bf16[1024,1024]{1,0:T(8,128)(2,1)S(1)}, f32[2,1024,4]{2,1,0:T(8,128)S(1)}) custom-call(s32[4]{0:T(128)S(1)} %and_select_fusion.2.lo_ref, bf16[1024,1536]{1,0:T(8,128)(2,1)} %project.3.qr_ref.kr_ref.vb_ref, bf16[1024,1536]{1,0:T(8,128)(2,1)} %project.3.qr_ref.kr_ref.vb_ref, bf16[1024,1536]{1,0:T(8,128)(2,1)} %project.3.qr_ref.kr_ref.vb_ref, ...), custom_call_target="tpu_custom_call" | custom-call | flops 1073741824 | tf_op jit(solution)/shard_map/attend/pallas_call | solution.py:116
  202.6 5.0 convolution_convert_fusion.5
  218.9 33.4 %collective-permute-done.8 = bf16[512,2560]{1,0:T(8,128)(2,1)} collective-permute-done((bf16[512,2560]{1,0:T(8,128)(2,1)}, bf16[512,2560]{1,0:T(8,128)(2,1)}, u32[]{:S(2)}, u32[]{:S(2)}) %collective-permute-start.8) | collective-permute-done | bytes 2621472 | tf_op jit(solution)/shard_map/ppermute | solution.py:450
  256.0 10.7 collective-permute-done.7
  266.6 5.9 multiply_reduce_fusion.3
  277.2 4.8 broadcast_in_dim.52
  285.4 7.8 all-gather.12.cloned.1.call-done.refs_2_.refs_3_.refs_4_.refs_7_
  293.2 16.4 %gate_up.3 = (bf16[512,1728]{1,0:T(8,128)(2,1)}, bf16[512,1728]{1,0:T(8,128)(2,1)}, bf16[512,1728]{1,0:T(8,128)(2,1)}) custom-call(bf16[512,2560]{1,0:T(8,128)(2,1)} %copy-done.23, bf16[2560,1728]{1,0:T(8,128)(2,1)} %all-gather.10.cloned.1.call-done.refs_1_.refs_2_.refs_3_.refs_6_, ...), custom_call_target="tpu_custom_call" | custom-call | flops 9059696640 | tf_op jit(solution)/shard_map/gate_up/pallas_call | solution.py:253
  309.5 23.9 %collective-permute-done.10.refs_1_.refs_2_ = bf16[512,2560]{1,0:T(8,128)(2,1)} collective-permute-done((bf16[512,2560]{1,0:T(8,128)(2,1)S(1)}, bf16[512,2560]{1,0:T(8,128)(2,1)}, u32[]{:S(2)}, u32[]{:S(2)}) %collective-permute-start.10) | collective-permute-done | bytes 2621472 | tf_op jit(solution)/shard_map/ppermute | solution.py:450
  338.7 24.9 %gate_up.4 = (bf16[512,1728]{1,0:T(8,128)(2,1)}, bf16[512,1728]{1,0:T(8,128)(2,1)}, bf16[512,1728]{1,0:T(8,128)(2,1)}, bf16[512,1728]{1,0:T(8,128)(2,1)}, bf16[5...) custom-call(bf16[512,2560]{1,0:T(8,128)(2,1)} %collective-permute-done.9.refs_0_.refs_1_, ...), custom_call_target="tpu_custom_call" | custom-call | flops 18119393280 | tf_op jit(solution)/shard_map/gate_up/pallas_call | solution.py:253
  367.4 15.8 %gate_up.5 = (bf16[512,1728]{1,0:T(8,128)(2,1)}, bf16[512,1728]{1,0:T(8,128)(2,1)}, bf16[512,1728]{1,0:T(8,128)(2,1)}) custom-call(bf16[256,2560]{1,0:T(8,128)(2,1)} %copy-done.38, bf16[256,2560]{1,0:T(8,128)(2,1)} %copy-done.39, bf16[2560,1728]{1,0:T(8,128)(2,1)} %all-gather.10.cloned.1.call-done.refs_1_.refs_2_.refs_3_.refs_6_, ...), custom_call_target="tpu_custom_call" | custom-call | flops 9059696640 | tf_op jit(solution)/shard_map/gate_up/pallas_call | solution.py:253
  383.2 29.3 %wgrad.2 = bf16[2560,1728]{1,0:T(8,128)(2,1)} custom-call(bf16[512,2560]{1,0:T(8,128)(2,1)} %broadcast_multiply_fusion.3.refs_0_, bf16[512,2560]{1,0:T(8,128)(2,1)} %broadcast_multiply_fusion.2.refs_1_.refs_0_, bf16[512,2560]{1,0:T(8,128)(2,1)} %broadcast_multiply_fusion.1.refs_2_.refs_3_, bf16[512,2560]{1,0:T(8,128)(2,1)} %broadcast_multiply_fusion.refs_3_.refs_0_, ...), custom_call_target="tpu_custom_call" | custom-call | flops 2264924160 | tf_op jit(solution)/shard_map/wgrad/pallas_call | solution.py:372
  412.6 23.8 %gate_up_back.3 = (bf16[512,1728]{1,0:T(8,128)(2,1)}, bf16[512,1728]{1,0:T(8,128)(2,1)}, bf16[256,2560]{1,0:T(8,128)(2,1)}, bf16[256,2560]{1,0:T(8,128)(2,1)}) custom-call(bf16[512,2560]{1,0:T(8,128)(2,1)} %broadcast_multiply_fusion.refs_3_.refs_0_, bf16[512,1728]{1,0:T(8,128)(2,1)} %get-tuple-element.175.refs_1_, ...), custom_call_target="tpu_custom_call" | custom-call | flops 13589544960 | tf_op jit(solution)/shard_map/gate_up_back/pallas_call | solution.py:307
  437.4 41.7 %gate_up_back.4 = (bf16[512,1728]{1,0:T(8,128)(2,1)}, bf16[512,1728]{1,0:T(8,128)(2,1)}, bf16[512,1728]{1,0:T(8,128)(2,1)}, bf16[512,1728]{1,0:T(8,128)(2,1)}, b...) custom-call(bf16[512,2560]{1,0:T(8,128)(2,1)} %broadcast_multiply_fu, ...), custom_call_target="tpu_custom_call" | custom-call | flops 27179089920 | tf_op jit(solution)/shard_map/gate_up_back/pallas_call | solution.py:307
  487.9 23.4 %gate_up_back.5 = (bf16[512,1728]{1,0:T(8,128)(2,1)}, bf16[512,1728]{1,0:T(8,128)(2,1)}, bf16[256,2560]{1,0:T(8,128)(2,1)}, bf16[256,2560]{1,0:T(8,128)(2,1)}) custom-call(bf16[512,2560]{1,0:T(8,128)(2,1)} %broadcast_multiply_fusion.3.refs_0_, bf16[512,1728]{1,0:T(8,128)(2,1)} %get-tuple-element.197.refs_1_, bf16[512,1728]{1,0:T(8,128)(2,1)} %get-tuple-element.198.refs_2_, ...), custom_call_target="tpu_custom_call" | custom-call | flops 13589544960 | tf_op jit(solution)/shard_map/gate_up_back/pallas_call | solution.py:307
  511.3 9.8 down.5
  521.1 9.8 down.4
  530.8 4.9 collective-permute-done.15
  535.7 51.2 %wgrad.3 = bf16[2560,3584]{1,0:T(8,128)(2,1)} custom-call(bf16[512,2560]{1,0:T(8,128)(2,1)} %copy-done.23, bf16[512,2560]{1,0:T(8,128)(2,1)} %collective-permute-done.9.refs_0_.refs_1_, bf16[512,2560]{1,0:T(8,128)(2,1)} %collective-permute-done.10.refs_1_.refs_2_, bf16[256,2560]{1,0:T(8,128)(2,1)} %copy-done.38, bf16[256,2560]{1,0:T(8,128)(2,1)} %copy-done.39, ...), custom_call_target="tpu_custom_call" | custom-call | flops 4529848320 | tf_op jit(solution)/shard_map/wgrad/pallas_call | solution.py:372
  593.2 4.0 fusion.88
  598.1 9.8 down.6
  607.9 9.8 down.7
  617.7 33.9 %collective-permute-done.19 = bf16[512,2560]{1,0:T(8,128)(2,1)S(1)} collective-permute-done((bf16[512,2560]{1,0:T(8,128)(2,1)}, bf16[512,2560]{1,0:T(8,128)(2,1)S(1)}, u32[]{:S(2)}, u32[]{:S(2)}) %collective-permute-start.19) | collective-permute-done | bytes 2621472 | tf_op jit(solution)/shard_map/ppermute | solution.py:450
  651.6 5.2 maximum_select_fusion.1.d_ref
  656.8 4.6 convolution_convert_fusion.3
  667.3 10.1 heads_back.2.do_ref
  678.6 26.1 %attend_back.2 = (bf16[1024,1024]{1,0:T(8,128)(2,1)S(1)}, bf16[1024,256]{1,0:T(8,128)(2,1)S(1)}, bf16[1024,256]{1,0:T(8,128)(2,1)S(1)}) custom-call(s32[4]{0:T(128)S(1)} %and_select_fusion.2.lo_ref, bf16[1024,1536]{1,0:T(8,128)(2,1)} %project.3.qr_ref.kr_ref.vb_ref, bf16[1024,1536]{1,0:T(8,128)(2,1)} %project.3.qr_ref.kr_ref.vb_ref, ...), custom_call_target="tpu_custom_call" | custom-call | flops 4294967296 | tf_op jit(solution)/shard_map/attend_back/pallas_call | solution.py:138
  707.0 8.1 convolution_convert_fusion.1
  715.2 21.1 %collective-permute-done.21 = bf16[512,2560]{1,0:T(8,128)(2,1)S(1)} collective-permute-done((bf16[512,2560]{1,0:T(8,128)(2,1)}, bf16[512,2560]{1,0:T(8,128)(2,1)S(1)}, u32[]{:S(2)}, u32[]{:S(2)}) %collective-permute-start.21) | collective-permute-done | bytes 2621472 | tf_op jit(solution)/shard_map/ppermute | solution.py:450
  741.7 5.4 constant_dynamic-update-slice_fusion.6
  752.2 9.9 heads_back.3.do_ref
  762.1 26.5 %attend_back.3 = (bf16[1024,1024]{1,0:T(8,128)(2,1)S(1)}, bf16[1024,256]{1,0:T(8,128)(2,1)S(1)}, bf16[1024,256]{1,0:T(8,128)(2,1)S(1)}) custom-call(s32[4]{0:T(128)S(1)} %copy-done.3, bf16[1024,1536]{1,0:T(8,128)(2,1)} %project.2.qr_ref.kr_ref.vb_ref, bf16[1024,1536]{1,0:T(8,128)(2,1)} %project.2.qr_ref.kr_ref.vb_ref, ...), custom_call_target="tpu_custom_call" | custom-call | flops 4294967296 | tf_op jit(solution)/shard_map/attend_back/pallas_call | solution.py:138
  788.7 9.2 convolution_convert_fusion.2
  801.5 4.8 add_convert_fusion.2
  815.8 12.1 %fusion.5 = (f32[2560]{0:T(1024)S(1)}, f32[512,2560]{1,0:T(8,128)}) fusion(bf16[512,2560]{1,0:T(8,128)(2,1)S(1)} %copy-done.19, f32[512]{0:T(512)S(1)} %add_rsqrt_fusion.1, bf16[2560,2048]{1,0:T(8,128)(2,1)} %constant_dynamic-update-slice_fusion.6, bf16[1024,2048]{0,1:T(8,128)(2,1)} %broadcast_dynamic-update-slice_fusion.1, s32[]{:T(128)S(6)} %select_n.351), kind=kOutput, calls=%fused_computation.13 | convolution fusion | flops 5373949440 | bytes 20459524 | tf_op jit(solution)/shard_map/dot_general | solution.py:437
  828.0 9.2 multiply_reduce_fusion.1
  837.2 9.2 convolution_convert_fusion
  846.4 5.3 fusion.7
  858.2 56.8 %collective-permute-done.27 = bf16[512,2560]{1,0:T(8,128)(2,1)} collective-permute-done((bf16[512,2560]{1,0:T(8,128)(2,1)S(1)}, bf16[512,2560]{1,0:T(8,128)(2,1)}, u32[]{:S(2)}, u32[]{:S(2)}) %collective-permute-start.27) | collective-permute-done | bytes 2621472 | tf_op jit(solution)/shard_map/ppermute | solution.py:450
  921.3 4.1 collective-permute-start.29
  930.8 10.1 finish.1
  942.5 6.6 add_convert_fusion.1
  949.7 151.8 %reduce-scatter.7.cloned.1.call-done = bf16[320,3584]{1,0:T(8,128)(2,1)} async-done(((bf16[2560,3584]{1,0:T(8,128)(2,1)}), bf16[320,3584]{1,0:T(8,128)(2,1)}) %reduce-scatter.7.cloned.1.call-update) | async-done | bytes 2293776 | tf_op jit(solution)/shard_map/reduce_scatter | solution.py:650
  (327 shorter events, 163.8 us)
Async XLA Ops:
  7.2 67.6 %all-gather.6.cloned.1.call-start = ((), (), s32[]{:S(2)}) async-start(), calls=%async_computation.4 | async-start | bytes 5898240 | tf_op jit(solution)/shard_map/all_gather | solution.py:546
  10.2 66.0 %copy-start.47 = (s32[2,1024]{1,0:T(2,128)S(1)}, s32[2,1024]{1,0:T(2,128)}, u32[]{:S(2)}) copy-start(s32[2,1024]{1,0:T(2,128)} %param.13) | copy-start | bytes 24580
  13.1 109.1 %all-gather.8.cloned.1.call-start = ((), (), s32[]{:S(2)}) async-start(), calls=%async_computation.5 | async-start | bytes 3686400 | tf_op jit(solution)/shard_map/all_gather | solution.py:554
  13.1 59.9 %collective-permute-start = (bf16[512,2560]{1,0:T(8,128)(2,1)S(1)}, bf16[512,2560]{1,0:T(8,128)(2,1)S(1)}, u32[]{:S(2)}, u32[]{:S(2)}) collective-permute-start(bf16[512,2560]{1,0:T(8,128)(2,1)S(1)} %copy-done.15), channel_id=1, source_target_pairs={{0,1},{1,0},{2,3},{3,2},{4,5},{5,4},{6,7},{7,6},{8,9},{9,8},{10,11... | collective-permute-start | bytes 7864328 | tf_op jit(solution)/shard_map/ppermute | solution.py:450
  16.1 58.6 %collective-permute-start.1 = (bf16[512,2560]{1,0:T(8,128)(2,1)}, bf16[512,2560]{1,0:T(8,128)(2,1)}, u32[]{:S(2)}, u32[]{:S(2)}) collective-permute-start(bf16[512,2560]{1,0:T(8,128)(2,1)} %param.23), channel_id=1, source_target_pairs={{0,2},{1,3},{2,0},{3,1},{4,6},{5,7},{6,4},{7,5},{8,10},{9,11},{10,... | collective-permute-start | bytes 7864328 | tf_op jit(solution)/shard_map/ppermute | solution.py:450
  74.8 200.6 %all-gather.10.cloned.1.call-start = ((), (), s32[]{:S(2)}) async-start(), calls=%async_computation.6 | async-start | bytes 10321920 | tf_op jit(solution)/shard_map/all_gather | solution.py:555
  75.5 217.7 %all-gather.12.cloned.1.call-start = ((), (), s32[]{:S(2)}) async-start(), calls=%async_computation.7 | async-start | bytes 10321920 | tf_op jit(solution)/shard_map/all_gather | solution.py:556
  76.1 336.5 %all-gather.14.cloned.1.call-start = ((), (), s32[]{:S(2)}) async-start(), calls=%async_computation.8 | async-start | bytes 10321920 | tf_op jit(solution)/shard_map/all_gather | solution.py:557
  78.4 117.9 %copy-start.50 = (s32[640]{0:T(1024)}, s32[640]{0:T(1024)S(1)}, u32[]{:S(2)}) copy-start(s32[640]{0:T(1024)S(1)} %fusion.59) | copy-start | bytes 7684
  82.0 596.6 %copy-start.2 = (s32[4]{0:T(128)}, s32[4]{0:T(128)S(1)}, u32[]{:S(2)}) copy-start(s32[4]{0:T(128)S(1)} %and_select_fusion.2.lo_ref) | copy-start | bytes 52
  85.3 58.7 %collective-permute-start.2 = (bf16[1280,1024]{1,0:T(8,128)(2,1)}, bf16[1280,1024]{1,0:T(8,128)(2,1)}, u32[]{:S(2)}, u32[]{:S(2)}) collective-permute-start(bf16[1280,1024]{1,0:T(8,128)(2,1)} %constant_dynamic-slice_fusion.4), channel_id=1, source_target_pairs={{0,2},{1,3},{2,0},{3,1},{4,6},{5,7},{6,4},{7,5},{8,10},{9,11},{10,... | collective-permute-start | bytes 7864328 | tf_op jit(solution)/shard_map/ppermute | solution.py:450
  86.8 57.8 %collective-permute-start.3 = (bf16[512,2560]{1,0:T(8,128)(2,1)}, bf16[512,2560]{1,0:T(8,128)(2,1)}, u32[]{:S(2)}, u32[]{:S(2)}) collective-permute-start(bf16[512,2560]{1,0:T(8,128)(2,1)} %param.23), channel_id=1, source_target_pairs={{0,1},{1,0},{2,3},{3,2},{4,5},{5,4},{6,7},{7,6},{8,9},{9,8},{10,11... | collective-permute-start | bytes 7864328 | tf_op jit(solution)/shard_map/ppermute | solution.py:450
  144.6 5.3 collective-permute-start.4
  144.7 506.9 %reduce-scatter.5.cloned.1.call-start = ((), (), s32[]{:S(2)}) async-start(), calls=%async_computation.9 | async-start | bytes 10321920 | tf_op jit(solution)/shard_map/reduce_scatter | solution.py:638
  144.7 46.2 %collective-permute-start.5 = (bf16[1280,640]{1,0:T(8,128)(2,1)}, bf16[1280,640]{1,0:T(8,128)(2,1)}, u32[]{:S(2)}, u32[]{:S(2)}) collective-permute-start(bf16[1280,640]{1,0:T(8,128)(2,1)} %constant_dynamic-slice_fusion.5), channel_id=1, source_target_pairs={{0,2},{1,3},{2,0},{3,1},{4,6},{5,7},{6,4},{7,5},{8,10},{9,11},{10,... | collective-permute-start | bytes 4915208 | tf_op jit(solution)/shard_map/ppermute | solution.py:450
  191.0 7.0 collective-permute-start.6
  193.0 59.3 %collective-permute-start.8 = (bf16[512,2560]{1,0:T(8,128)(2,1)}, bf16[512,2560]{1,0:T(8,128)(2,1)}, u32[]{:S(2)}, u32[]{:S(2)}) collective-permute-start(bf16[512,2560]{1,0:T(8,128)(2,1)} %collective-permute-done.3), channel_id=1, source_target_pairs={{0,2},{1,3},{2,0},{3,1},{4,6},{5,7},{6,4},{7,5},{8,10},{9,11},{10,... | collective-permute-start | bytes 7864328 | tf_op jit(solution)/shard_map/ppermute | solution.py:450
  197.9 68.7 %copy-start.56 = (bf16[1024,640]{0,1:T(8,128)(2,1)}, bf16[1024,640]{0,1:T(8,128)(2,1)S(1)}, u32[]{:S(2)}) copy-start(bf16[1024,640]{0,1:T(8,128)(2,1)S(1)} %fusion.28) | copy-start | bytes 3932164
  207.6 59.0 %collective-permute-start.7 = (bf16[512,2560]{1,0:T(8,128)(2,1)}, bf16[512,2560]{1,0:T(8,128)(2,1)}, u32[]{:S(2)}, u32[]{:S(2)}) collective-permute-start(bf16[512,2560]{1,0:T(8,128)(2,1)} %convolution_convert_fusion.5), channel_id=1, source_target_pairs={{0,1},{1,0},{2,3},{3,2},{4,5},{5,4},{6,7},{7,6},{8,9},{9,8},{10,11... | collective-permute-start | bytes 7864328 | tf_op jit(solution)/shard_map/ppermute | solution.py:450
  215.2 51.4 %copy-start.41 = (bf16[2560,640]{1,0:T(8,128)(2,1)S(1)}, bf16[2560,640]{1,0:T(8,128)(2,1)}, u32[]{:S(2)}) copy-start(bf16[2560,640]{1,0:T(8,128)(2,1)} %all-gather.8.cloned.1.call-done.w_ref) | copy-start | bytes 9830404
  275.4 58.0 %collective-permute-start.10 = (bf16[512,2560]{1,0:T(8,128)(2,1)S(1)}, bf16[512,2560]{1,0:T(8,128)(2,1)}, u32[]{:S(2)}, u32[]{:S(2)}) collective-permute-start(bf16[512,2560]{1,0:T(8,128)(2,1)S(1)} %multiply_convert_fusion.refs_0_), channel_id=1, source_target_pairs={{0,2},{1,3},{2,0},{3,1},{4,6},{5,7},{6,4},{7,5},{8,10},{9,11},{10,... | collective-permute-start | bytes 7864328 | tf_op jit(solution)/shard_map/ppermute | solution.py:450
  275.8 57.7 %collective-permute-start.9 = (bf16[512,2560]{1,0:T(8,128)(2,1)S(1)}, bf16[512,2560]{1,0:T(8,128)(2,1)}, u32[]{:S(2)}, u32[]{:S(2)}) collective-permute-start(bf16[512,2560]{1,0:T(8,128)(2,1)S(1)} %multiply_convert_fusion.refs_0_), channel_id=1, source_target_pairs={{0,1},{1,0},{2,3},{3,2},{4,5},{5,4},{6,7},{7,6},{8,9},{9,8},{10,11... | collective-permute-start | bytes 7864328 | tf_op jit(solution)/shard_map/ppermute | solution.py:450
  334.9 28.8 %collective-permute-start.11 = (bf16[256,2560]{1,0:T(8,128)(2,1)S(1)}, bf16[256,2560]{1,0:T(8,128)(2,1)S(1)}, u32[]{:S(2)}, u32[]{:S(2)}) collective-permute-start(bf16[256,2560]{1,0:T(8,128)(2,1)S(1)} %slice.79), channel_id=1, source_target_pairs={{0,2},{1,3},{2,0},{3,1},{4,6},{5,7},{6,4},{7,5},{8,10},{9,11},{10,... | collective-permute-start | bytes 3932168 | tf_op jit(solution)/shard_map/ppermute | solution.py:450
  338.0 28.3 %collective-permute-start.12 = (bf16[256,2560]{1,0:T(8,128)(2,1)S(1)}, bf16[256,2560]{1,0:T(8,128)(2,1)S(1)}, u32[]{:S(2)}, u32[]{:S(2)}) collective-permute-start(bf16[256,2560]{1,0:T(8,128)(2,1)S(1)} %slice.80), channel_id=1, source_target_pairs={{0,1},{1,0},{2,3},{3,2},{4,5},{5,4},{6,7},{7,6},{8,9},{9,8},{10,11... | collective-permute-start | bytes 3932168 | tf_op jit(solution)/shard_map/ppermute | solution.py:450
  412.5 537.2 %reduce-scatter.9.cloned.1.call-start = ((), (), s32[]{:S(2)}) async-start(), calls=%async_computation.11 | async-start | bytes 3686400 | tf_op jit(solution)/shard_map/reduce_scatter | solution.py:691
  436.4 45.9 %collective-permute-start.14 = (bf16[256,2560]{1,0:T(8,128)(2,1)}, bf16[256,2560]{1,0:T(8,128)(2,1)S(1)}, u32[]{:S(2)}, u32[]{:S(2)}) collective-permute-start(bf16[256,2560]{1,0:T(8,128)(2,1)} %get-tuple-element.180), channel_id=1, source_target_pairs={{0,1},{1,0},{2,3},{3,2},{4,5},{5,4},{6,7},{7,6},{8,9},{9,8},{10,11... | collective-permute-start | bytes 3932168 | tf_op jit(solution)/shard_map/ppermute | solution.py:450
  436.7 48.9 %collective-permute-start.16 = (bf16[256,2560]{1,0:T(8,128)(2,1)}, bf16[256,2560]{1,0:T(8,128)(2,1)S(1)}, u32[]{:S(2)}, u32[]{:S(2)}) collective-permute-start(bf16[256,2560]{1,0:T(8,128)(2,1)} %get-tuple-element.181), channel_id=1, source_target_pairs={{0,2},{1,3},{2,0},{3,1},{4,6},{5,7},{6,4},{7,5},{8,10},{9,11},{10,... | collective-permute-start | bytes 3932168 | tf_op jit(solution)/shard_map/ppermute | solution.py:450
  479.1 51.7 %collective-permute-start.13 = (bf16[256,2560]{1,0:T(8,128)(2,1)}, bf16[256,2560]{1,0:T(8,128)(2,1)S(1)}, u32[]{:S(2)}, u32[]{:S(2)}) collective-permute-start(bf16[256,2560]{1,0:T(8,128)(2,1)} %get-tuple-element.188), channel_id=1, source_target_pairs={{0,1},{1,0},{2,3},{3,2},{4,5},{5,4},{6,7},{7,6},{8,9},{9,8},{10,11... | collective-permute-start | bytes 3932168 | tf_op jit(solution)/shard_map/ppermute | solution.py:450
  480.3 50.5 %collective-permute-start.18 = (bf16[256,2560]{1,0:T(8,128)(2,1)}, bf16[256,2560]{1,0:T(8,128)(2,1)}, u32[]{:S(2)}, u32[]{:S(2)}) collective-permute-start(bf16[256,2560]{1,0:T(8,128)(2,1)} %get-tuple-element.191), channel_id=1, source_target_pairs={{0,2},{1,3},{2,0},{3,1},{4,6},{5,7},{6,4},{7,5},{8,10},{9,11},{10,... | collective-permute-start | bytes 3932168 | tf_op jit(solution)/shard_map/ppermute | solution.py:450
  485.4 50.3 %collective-permute-start.15 = (bf16[256,2560]{1,0:T(8,128)(2,1)S(1)}, bf16[256,2560]{1,0:T(8,128)(2,1)}, u32[]{:S(2)}, u32[]{:S(2)}) collective-permute-start(bf16[256,2560]{1,0:T(8,128)(2,1)S(1)} %add_convert_fusion.7), channel_id=1, source_target_pairs={{0,2},{1,3},{2,0},{3,1},{4,6},{5,7},{6,4},{7,5},{8,10},{9,11},{10,... | collective-permute-start | bytes 3932168 | tf_op jit(solution)/shard_map/ppermute | solution.py:450
  487.0 48.7 %collective-permute-start.17 = (bf16[256,2560]{1,0:T(8,128)(2,1)}, bf16[256,2560]{1,0:T(8,128)(2,1)}, u32[]{:S(2)}, u32[]{:S(2)}) collective-permute-start(bf16[256,2560]{1,0:T(8,128)(2,1)} %add_convert_fusion.6), channel_id=1, source_target_pairs={{0,1},{1,0},{2,3},{3,2},{4,5},{5,4},{6,7},{7,6},{8,9},{9,8},{10,11... | collective-permute-start | bytes 3932168 | tf_op jit(solution)/shard_map/ppermute | solution.py:450
  597.3 54.3 %collective-permute-start.19 = (bf16[512,2560]{1,0:T(8,128)(2,1)}, bf16[512,2560]{1,0:T(8,128)(2,1)S(1)}, u32[]{:S(2)}, u32[]{:S(2)}) collective-permute-start(bf16[512,2560]{1,0:T(8,128)(2,1)} %get-tuple-element.221), channel_id=1, source_target_pairs={{0,1},{1,0},{2,3},{3,2},{4,5},{5,4},{6,7},{7,6},{8,9},{9,8},{10,11... | collective-permute-start | bytes 7864328 | tf_op jit(solution)/shard_map/ppermute | solution.py:450
  661.5 3.6 collective-permute-start.20
  666.7 48.5 %collective-permute-start.22 = (bf16[1280,640]{1,0:T(8,128)(2,1)}, bf16[1280,640]{1,0:T(8,128)(2,1)}, u32[]{:S(2)}, u32[]{:S(2)}) collective-permute-start(bf16[1280,640]{1,0:T(8,128)(2,1)} %add_convert_fusion.5), channel_id=1, source_target_pairs={{0,2},{1,3},{2,0},{3,1},{4,6},{5,7},{6,4},{7,5},{8,10},{9,11},{10,... | collective-permute-start | bytes 4915208 | tf_op jit(solution)/shard_map/ppermute | solution.py:450
  677.4 58.9 %collective-permute-start.21 = (bf16[512,2560]{1,0:T(8,128)(2,1)}, bf16[512,2560]{1,0:T(8,128)(2,1)S(1)}, u32[]{:S(2)}, u32[]{:S(2)}) collective-permute-start(bf16[512,2560]{1,0:T(8,128)(2,1)} %down.6), channel_id=1, source_target_pairs={{0,1},{1,0},{2,3},{3,2},{4,5},{5,4},{6,7},{7,6},{8,9},{9,8},{10,11... | collective-permute-start | bytes 7864328 | tf_op jit(solution)/shard_map/ppermute | solution.py:450
  738.0 10.3 collective-permute-start.23
  747.2 90.0 %collective-permute-start.26 = (bf16[512,2560]{1,0:T(8,128)(2,1)}, bf16[512,2560]{1,0:T(8,128)(2,1)}, u32[]{:S(2)}, u32[]{:S(2)}) collective-permute-start(bf16[512,2560]{1,0:T(8,128)(2,1)} %down.4), channel_id=1, source_target_pairs={{0,1},{1,0},{2,3},{3,2},{4,5},{5,4},{6,7},{7,6},{8,9},{9,8},{10,11... | collective-permute-start | bytes 7864328 | tf_op jit(solution)/shard_map/ppermute | solution.py:450
  751.1 64.6 %collective-permute-start.24 = (bf16[1280,1024]{1,0:T(8,128)(2,1)}, bf16[1280,1024]{1,0:T(8,128)(2,1)}, u32[]{:S(2)}, u32[]{:S(2)}) collective-permute-start(bf16[1280,1024]{1,0:T(8,128)(2,1)} %add_convert_fusion.3), channel_id=1, source_target_pairs={{0,2},{1,3},{2,0},{3,1},{4,6},{5,7},{6,4},{7,5},{8,10},{9,11},{10,... | collective-permute-start | bytes 7864328 | tf_op jit(solution)/shard_map/ppermute | solution.py:450
  801.4 148.2 %reduce-scatter.11.cloned.1.call-start = ((), (), s32[]{:S(2)}) async-start(), calls=%async_computation.12 | async-start | bytes 5898240 | tf_op jit(solution)/shard_map/reduce_scatter | solution.py:708
  851.7 73.6 %copy-start.46 = (f32[2560]{0:T(1024)S(1)}, f32[2560]{0:T(1024)}, u32[]{:S(2)}) copy-start(f32[2560]{0:T(1024)} %copy-done.45) | copy-start | bytes 30724
  851.8 249.7 %reduce-scatter.7.cloned.1.call-start = ((), (), s32[]{:S(2)}) async-start(), calls=%async_computation.10 | async-start | bytes 20643840 | tf_op jit(solution)/shard_map/reduce_scatter | solution.py:650
  853.5 61.6 %collective-permute-start.27 = (bf16[512,2560]{1,0:T(8,128)(2,1)S(1)}, bf16[512,2560]{1,0:T(8,128)(2,1)}, u32[]{:S(2)}, u32[]{:S(2)}) collective-permute-start(bf16[512,2560]{1,0:T(8,128)(2,1)S(1)} %copy-done.29), channel_id=1, source_target_pairs={{0,2},{1,3},{2,0},{3,1},{4,6},{5,7},{6,4},{7,5},{8,10},{9,11},{10,... | collective-permute-start | bytes 7864328 | tf_op jit(solution)/shard_map/ppermute | solution.py:450
  857.3 59.0 %collective-permute-start.25 = (bf16[512,2560]{1,0:T(8,128)(2,1)}, bf16[512,2560]{1,0:T(8,128)(2,1)}, u32[]{:S(2)}, u32[]{:S(2)}) collective-permute-start(bf16[512,2560]{1,0:T(8,128)(2,1)} %get-tuple-element.326), channel_id=1, source_target_pairs={{0,1},{1,0},{2,3},{3,2},{4,5},{5,4},{6,7},{7,6},{8,9},{9,8},{10,11... | collective-permute-start | bytes 7864328 | tf_op jit(solution)/shard_map/ppermute | solution.py:450
  916.6 4.6 collective-permute-start.28
  921.3 5.7 collective-permute-start.29
  927.0 2.9 collective-permute-start.30
  929.9 11.0 collective-permute-start.31
  940.9 8.1 collective-permute-start.32
  (65 other events, 638.4 us)
Sparse Core Ops, SparseCore 0:
  13.2 58.7 all-gather.5
  74.9 40.5 all-gather.7
  117.2 87.4 all-gather.9
  206.1 87.0 all-gather.11
  294.7 87.1 all-gather.13
  412.6 98.2 reduce-scatter.4
  801.6 46.9 reduce-scatter.8
  851.8 65.5 reduce-scatter.10
  919.9 181.4 reduce-scatter.6
